TPU v7x, 32 devices: a whole 2x2x4 slice. The times are simulated.
32 devices in a mesh: dp: 8 (over y, x, core), mp: 4 (over z).
Axes of the slice: x: 2, y: 2, z: 4, core: 2. Of those that a mesh axis runs over, the one named last changes fastest.
Arguments:
- tokens: bfloat16 [2, 8, 1024, 768], P(None, 'dp', 'mp'), may hold values from -6 to 6
- cotangent: bfloat16 [2, 8, 1024, 768], P(None, 'dp', 'mp'), may hold values from -0.078125 to 0.078125
- segment_ids: int32 [2, 8, 1024], P(None, 'dp'), may hold values from 0 to 7, never falling along the last dimension, each value on 1 to 512 neighbouring positions
- targets: int32 [2, 8, 8], P(None, 'dp'), may hold values from 0 to 62
- attention_weights: float32 [4, 768, 768], P(None, 'dp', 'mp')
- feedforward_weights: float32 [2, 768, 3072], P(None, 'dp', 'mp')
- projection: float32 [768, 768], P('dp', 'mp'), may hold values from -0.21875 to 0.21875
- norm_gains: float32 [3, 768], replicated
- bias_table: float32 [32, 12], replicated, may hold values from -4 to 4
- attention_first: float32 [4, 768, 768], P(None, 'dp', 'mp'), may hold values from -0.00061035156 to 0.00061035156
- attention_second: float32 [4, 768, 768], P(None, 'dp', 'mp'), may hold values from 1.303713e-10 to 5.214852e-10
- feedforward_first: float32 [2, 768, 3072], P(None, 'dp', 'mp'), may hold values from -0.00061035156 to 0.00061035156
- feedforward_second: float32 [2, 768, 3072], P(None, 'dp', 'mp'), may hold values from 1.303713e-10 to 5.214852e-10
- projection_first: float32 [768, 768], P('dp', 'mp'), may hold values from -0.00061035156 to 0.00061035156
- projection_second: float32 [768, 768], P('dp', 'mp'), may hold values from 1.303713e-10 to 5.214852e-10
- gains_first: float32 [3, 768], replicated, may hold values from -0.00061035156 to 0.00061035156
- gains_second: float32 [3, 768], replicated, may hold values from 1.303713e-10 to 5.214852e-10
- bias_first: float32 [32, 12], replicated, may hold values from -0.00061035156 to 0.00061035156
- bias_second: float32 [32, 12], replicated, may hold values from 1.303713e-10 to 5.214852e-10
Outputs:
- output: bfloat16 [2, 8, 1024, 768], P(None, 'dp', 'mp')
- tokens_grad: float32 [2, 8, 1024, 768], P(None, 'dp', 'mp')
- grad_norm: float32 [], replicated
- attention_new: float32 [4, 768, 768], P(None, 'dp', 'mp')
- attention_first_new: float32 [4, 768, 768], P(None, 'dp', 'mp')
- attention_second_new: float32 [4, 768, 768], P(None, 'dp', 'mp')
- feedforward_new: float32 [2, 768, 3072], P(None, 'dp', 'mp')
- feedforward_first_new: float32 [2, 768, 3072], P(None, 'dp', 'mp')
- feedforward_second_new: float32 [2, 768, 3072], P(None, 'dp', 'mp')
- projection_new: float32 [768, 768], P('dp', 'mp')
- projection_first_new: float32 [768, 768], P('dp', 'mp')
- projection_second_new: float32 [768, 768], P('dp', 'mp')
- gains_new: float32 [3, 768], replicated
- gains_first_new: float32 [3, 768], replicated
- gains_second_new: float32 [3, 768], replicated
- bias_new: float32 [32, 12], replicated
- bias_first_new: float32 [32, 12], replicated
- bias_second_new: float32 [32, 12], replicated
Inputs may be any that keep to these rules, and one draw needn't show every extreme that they name: `segment_ids`: along every row the segment numbers never fall; each of the 8 numbers occurs, at most 512 times, one exactly 512 times.
All inputs are finite; a program needn't handle non-finite values.
Results may differ from a plain program's by a relative error of at most 0.015.
Values may be sent and summed in bfloat16 or wider, within the bound.
No kernel may reach another device: no remote copies, remote signals or barrier semaphores. Data moves between devices by JAX's collectives and lax.ppermute only.
A program may use at most 192 MiB of HBM per device.

v0:
```python
import jax
import jax.numpy as jnp
from jax import lax
from jax.sharding import PartitionSpec as P

D = 768
HD = 64
STEP = 10


EPS_NORM = 1e-06
EPS_ADAM = 1e-08
SIM_SCALE = 50.0
NEG_FILL = -1000000000.0
BETA_ONE = 0.9
BETA_TWO = 0.999
CLIP_NORM = 1.0
RATE_MATRIX = 0.05
RATE_SMALL = 0.2
DECAY_MATRIX = 0.01
LIMITS = (12, 16, 23, 32, 46, 64, 91)
HIGHEST = lax.Precision.HIGHEST
CONTRACT_LAST = (((1,), (1,)), ((), ()))
CONTRACT_FIRST = (((0,), (0,)), ((), ()))


def bucket_of(relative):
    distance = jnp.abs(relative)
    far_bucket = 8 + sum(((distance >= threshold).astype(jnp.int32) for threshold in LIMITS))
    near_bucket = jnp.where(distance < 8, distance, far_bucket)
    return near_bucket + 16 * (relative > 0).astype(jnp.int32)


def norm_factor(values):
    return lax.rsqrt(jnp.mean(values * values, axis=-1, keepdims=True) + EPS_NORM)


def norm_back(values, factor, upstream):
    return factor * upstream - values * (factor * factor * factor) * jnp.mean(
        upstream * values, axis=-1, keepdims=True
    )


def bias_from(table_in, buckets):
    head_count = table_in.shape[1]
    value = jnp.broadcast_to(table_in[0][:, None, None], (head_count,) + buckets.shape)
    for number in range(1, table_in.shape[0]):
        value = jnp.where((buckets == number)[None], table_in[number][:, None, None], value)
    return value


def bias_grad(score_grad, buckets, bucket_total):
    nothing = jnp.zeros((), score_grad.dtype)
    return jnp.stack(
        [
            jnp.sum(
                jnp.where((buckets == number)[None], score_grad, nothing),
                axis=(1, 2),
                dtype=jnp.float32,
            )
            for number in range(bucket_total)
        ]
    )


def adam_update(weight_now, clipped, first_old, second_old, step_rate, weight_decay):
    first_new = BETA_ONE * first_old + (1.0 - BETA_ONE) * clipped
    second_new = BETA_TWO * second_old + (1.0 - BETA_TWO) * clipped * clipped
    first_hat = first_new / (1.0 - BETA_ONE**STEP)
    second_hat = second_new / (1.0 - BETA_TWO**STEP)
    weight_new = weight_now - step_rate * (
        first_hat / (jnp.sqrt(second_hat) + EPS_ADAM) + weight_decay * weight_now
    )
    return (weight_new, first_new, second_new)


def local(
    tokens,
    cotangent,
    segment_ids,
    targets,
    attention_weights,
    feedforward_weights,
    projection,
    norm_gains,
    bias_table,
    attention_first,
    attention_second,
    feedforward_first,
    feedforward_second,
    projection_first,
    projection_second,
    gains_first,
    gains_second,
    bias_first,
    bias_second,
):
    wide_count = lax.axis_size("dp")
    wide_rank = lax.axis_index("dp")
    narrow_rank = lax.axis_index("mp")
    micro_count = tokens.shape[0]
    part_rows = tokens.shape[2]
    row_length = segment_ids.shape[2]
    segment_count = targets.shape[2]
    heads_here = attention_weights.shape[2] // HD
    all_segments = segment_count * wide_count
    block_rows = min(512, row_length)
    block_count = row_length // block_rows
    score_scale = HD ** (-0.5)
    own_start = narrow_rank * part_rows
    table_here = lax.dynamic_slice_in_dim(bias_table, narrow_rank * heads_here, heads_here, 1)
    spots = jnp.arange(row_length, dtype=jnp.int32)
    block_spots = jnp.arange(block_rows, dtype=jnp.int32)
    block_starts = jnp.arange(block_count, dtype=jnp.int32) * block_rows
    segment_numbers = jnp.arange(segment_count, dtype=jnp.int32)
    all_numbers = jnp.arange(all_segments, dtype=jnp.int32)
    own_index = wide_rank * segment_count + segment_numbers
    is_self = own_index[:, None] == all_numbers[None, :]
    attention_low = attention_weights.astype(jnp.bfloat16)
    feedforward_low = feedforward_weights.astype(jnp.bfloat16)
    projection_low = projection.astype(jnp.bfloat16)

    def bucket_block(block_start):
        return bucket_of(spots[None, :] - (block_start + block_spots)[:, None])

    def rows_all(values):
        return lax.all_gather(values, "mp", axis=0, tiled=True)

    def rows_sum(factor_pairs):
        running = jnp.zeros((lax.axis_size("mp") * part_rows, D), jnp.float32)
        for left_rows, right_matrix in factor_pairs:
            running = running + lax.dot_general(
                left_rows, right_matrix, CONTRACT_LAST, preferred_element_type=jnp.float32
            )
        return lax.psum_scatter(
            running.astype(jnp.bfloat16), "mp", scatter_dimension=0, tiled=True
        ).astype(jnp.float32)

    def feature_total(values):
        return lax.psum(values, "mp")

    attn_reduced = jnp.zeros_like(attention_weights)
    ffn_reduced = jnp.zeros_like(feedforward_weights)
    proj_reduced = jnp.zeros_like(projection)
    gains_acc = jnp.zeros_like(norm_gains)
    table_acc = jnp.zeros_like(table_here)
    output_rows = []
    input_grads = []
    for micro_index in range(micro_count):
        attn_low, ffn_low, proj_low = (
            lax.all_gather(attention_low, "dp", axis=1, tiled=True),
            lax.all_gather(feedforward_low, "dp", axis=1, tiled=True),
            lax.all_gather(projection_low, "dp", axis=0, tiled=True),
        )
        token_rows = tokens[micro_index, 0].astype(jnp.float32)
        segments = segment_ids[micro_index, 0]
        factor_one = norm_factor(token_rows)
        normed_one = (token_rows * factor_one * norm_gains[0]).astype(jnp.bfloat16)
        normed_all = rows_all(normed_one)
        projected = jnp.einsum(
            "rd,cde->cre", normed_all, attn_low[:3], preferred_element_type=jnp.float32
        ).astype(jnp.bfloat16)
        queries = projected[0].reshape(row_length, heads_here, HD)
        keys_all = projected[1].reshape(row_length, heads_here, HD)
        values_all = projected[2].reshape(row_length, heads_here, HD)

        def block_scores(block_start, bias_block):
            query_block = lax.dynamic_slice_in_dim(queries, block_start, block_rows, 0)
            raw_scores = (
                jnp.einsum(
                    "qhd,khd->hqk", query_block, keys_all, preferred_element_type=jnp.float32
                )
                * score_scale
            )
            segment_block = lax.dynamic_slice_in_dim(segments, block_start, block_rows, 0)
            same_segment = segment_block[:, None] == segments[None, :]
            return (query_block, jnp.where(same_segment[None], raw_scores + bias_block, NEG_FILL))

        def forward_block(block_start):
            query_block, scores = block_scores(
                block_start, bias_from(table_here, bucket_block(block_start))
            )
            peak = jnp.max(scores, axis=-1, keepdims=True)
            shifted = jnp.exp(scores - peak)
            row_total = jnp.sum(shifted, axis=-1, keepdims=True)
            probs = shifted / row_total
            mixed_block = jnp.einsum(
                "hqk,khd->qhd",
                probs.astype(jnp.bfloat16),
                values_all,
                preferred_element_type=jnp.float32,
            )
            return (mixed_block, peak + jnp.log(row_total))

        mixed, log_totals = lax.map(forward_block, block_starts)
        mixed = mixed.reshape(row_length, heads_here * HD).astype(jnp.bfloat16)
        hidden_one = token_rows + lax.psum_scatter(
            lax.dot_general(mixed, attn_low[3], CONTRACT_LAST, preferred_element_type=jnp.float32),
            "mp",
            scatter_dimension=0,
            tiled=True,
        )
        factor_two = norm_factor(hidden_one)
        normed_two = (hidden_one * factor_two * norm_gains[1]).astype(jnp.bfloat16)
        normed_all_two = lax.all_gather(normed_two, "mp", axis=0, tiled=True)
        pre_act = jnp.dot(normed_all_two, ffn_low[0], preferred_element_type=jnp.float32)
        activated, gelu_pull = jax.vjp(jax.nn.gelu, pre_act)
        activated = activated.astype(jnp.bfloat16)
        hidden_two = hidden_one + rows_sum(((activated, ffn_low[1]),))
        output_rows.append(hidden_two.astype(jnp.bfloat16))
        factor_three = norm_factor(hidden_two)
        unit_three = hidden_two * factor_three
        normed_three = unit_three * norm_gains[2]
        segments_here = lax.dynamic_slice_in_dim(segments, own_start, part_rows, 0)
        member_here = (segment_numbers[:, None] == segments_here[None, :]).astype(jnp.float32)
        counts = jnp.sum(
            (segment_numbers[:, None] == segments[None, :]).astype(jnp.float32),
            axis=1,
            keepdims=True,
        )
        pooled = (
            feature_total(
                jnp.dot(
                    member_here, normed_three, precision=HIGHEST, preferred_element_type=jnp.float32
                )
            )
            / counts
        )
        pooled_low = pooled.astype(jnp.bfloat16)
        embedded = jnp.dot(pooled_low, proj_low, preferred_element_type=jnp.float32)
        emb_squares = feature_total(jnp.sum(embedded * embedded, axis=1, keepdims=True))
        inverse = lax.rsqrt(emb_squares + EPS_NORM)
        unit = (embedded * inverse).astype(jnp.bfloat16)
        unit_all = lax.all_gather(unit, "dp", axis=0, tiled=True)
        sims = feature_total(
            lax.dot_general(unit, unit_all, CONTRACT_LAST, preferred_element_type=jnp.float32)
        )
        logits = jnp.where(is_self, NEG_FILL, SIM_SCALE * sims)
        picked = targets[micro_index, 0]
        picked = picked + (picked >= own_index).astype(jnp.int32)
        sim_probs = jax.nn.softmax(logits, axis=-1)
        logit_grad = (
            sim_probs - (picked[:, None] == all_numbers[None, :]).astype(jnp.float32)
        ).astype(jnp.bfloat16)
        attn_back, ffn_back, proj_back = (
            lax.all_gather(attention_low, "dp", axis=1, tiled=True),
            lax.all_gather(feedforward_low, "dp", axis=1, tiled=True),
            lax.all_gather(projection_low, "dp", axis=0, tiled=True),
        )
        query_side = jnp.dot(logit_grad, unit_all, preferred_element_type=jnp.float32) * SIM_SCALE
        key_side = (
            lax.dot_general(logit_grad, unit, CONTRACT_FIRST, preferred_element_type=jnp.float32)
            * SIM_SCALE
        )
        unit_grad = query_side + lax.psum_scatter(key_side, "dp", scatter_dimension=0, tiled=True)
        unit_grad = unit_grad.astype(jnp.bfloat16).astype(jnp.float32)
        emb_dot = feature_total(jnp.sum(unit_grad * embedded, axis=1, keepdims=True))
        embed_grad = (
            inverse * unit_grad - embedded * (inverse * inverse * inverse) * emb_dot
        ).astype(jnp.bfloat16)
        proj_part = lax.dot_general(
            pooled_low, embed_grad, CONTRACT_FIRST, preferred_element_type=jnp.float32
        )
        pooled_grad = (
            feature_total(
                lax.dot_general(
                    embed_grad, proj_back, CONTRACT_LAST, preferred_element_type=jnp.float32
                )
            )
            / counts
        )
        normed_three_grad = lax.dot_general(
            member_here,
            pooled_grad,
            CONTRACT_FIRST,
            precision=HIGHEST,
            preferred_element_type=jnp.float32,
        )
        gain_three = jnp.sum(normed_three_grad * unit_three, axis=0)
        hidden_two_grad = cotangent[micro_index, 0].astype(jnp.float32) + norm_back(
            hidden_two, factor_three, normed_three_grad * norm_gains[2]
        )
        ffn_out_all = rows_all(hidden_two_grad.astype(jnp.bfloat16))
        act_grad = jnp.dot(ffn_out_all, ffn_back[1], preferred_element_type=jnp.float32)
        down_part = lax.dot_general(
            ffn_out_all, activated, CONTRACT_FIRST, preferred_element_type=jnp.float32
        )
        pre_grad = gelu_pull(act_grad)[0].astype(jnp.bfloat16)
        up_part = lax.dot_general(
            normed_all_two, pre_grad, CONTRACT_FIRST, preferred_element_type=jnp.float32
        )
        normed_two_grad = rows_sum(((pre_grad, ffn_back[0]),))
        gain_two = jnp.sum(normed_two_grad * hidden_one * factor_two, axis=0)
        hidden_one_grad = hidden_two_grad + norm_back(
            hidden_one, factor_two, normed_two_grad * norm_gains[1]
        )
        attn_out_all = rows_all(hidden_one_grad.astype(jnp.bfloat16))
        mixed_grad = jnp.dot(attn_out_all, attn_back[3], preferred_element_type=jnp.float32).astype(
            jnp.bfloat16
        )
        out_part = lax.dot_general(
            attn_out_all, mixed, CONTRACT_FIRST, preferred_element_type=jnp.float32
        )
        mixed_grad_heads = mixed_grad.reshape(row_length, heads_here, HD)

        def backward_block(carry, block_args):
            key_grad, value_grad, table_grad = carry
            block_start, log_block = block_args
            buckets = bucket_block(block_start)
            query_block, scores = block_scores(block_start, bias_from(table_here, buckets))
            probs = jnp.exp(scores - log_block)
            out_block = lax.dynamic_slice_in_dim(mixed_grad_heads, block_start, block_rows, 0)
            prob_grad = jnp.einsum(
                "qhd,khd->hqk", out_block, values_all, preferred_element_type=jnp.float32
            )
            row_delta = jnp.sum(probs * prob_grad, axis=-1, keepdims=True)
            score_grad = (probs * (prob_grad - row_delta)).astype(jnp.bfloat16)
            query_grad = (
                jnp.einsum("hqk,khd->qhd", score_grad, keys_all, preferred_element_type=jnp.float32)
                * score_scale
            )
            key_grad = (
                key_grad
                + jnp.einsum(
                    "hqk,qhd->khd", score_grad, query_block, preferred_element_type=jnp.float32
                )
                * score_scale
            )
            value_grad = value_grad + jnp.einsum(
                "hqk,qhd->khd",
                probs.astype(jnp.bfloat16),
                out_block,
                preferred_element_type=jnp.float32,
            )
            table_grad = table_grad + bias_grad(score_grad, buckets, table_here.shape[0])
            return ((key_grad, value_grad, table_grad), query_grad)

        zero_heads = jnp.zeros((row_length, heads_here, HD), jnp.float32)
        carry_out, query_grads = lax.scan(
            backward_block,
            (zero_heads, zero_heads, jnp.zeros_like(table_here)),
            (block_starts, log_totals),
        )
        key_grad, value_grad, table_grad = carry_out
        stacked_grad = jnp.stack(
            [
                query_grads.reshape(row_length, heads_here * HD),
                key_grad.reshape(row_length, heads_here * HD),
                value_grad.reshape(row_length, heads_here * HD),
            ]
        ).astype(jnp.bfloat16)
        qkv_part = jnp.einsum(
            "rd,cre->cde", normed_all, stacked_grad, preferred_element_type=jnp.float32
        )
        normed_one_grad = rows_sum(
            (
                (stacked_grad[0], attn_back[0]),
                (stacked_grad[1], attn_back[1]),
                (stacked_grad[2], attn_back[2]),
            )
        )
        gain_one = jnp.sum(normed_one_grad * token_rows * factor_one, axis=0)
        input_grads.append(
            hidden_one_grad + norm_back(token_rows, factor_one, normed_one_grad * norm_gains[0])
        )
        attn_part = jnp.concatenate([qkv_part, out_part[None]], axis=0)
        ffn_part = jnp.stack([up_part, down_part])
        attn_piece, ffn_piece, proj_piece = (
            lax.psum_scatter(attn_part, "dp", scatter_dimension=1, tiled=True),
            lax.psum_scatter(ffn_part, "dp", scatter_dimension=1, tiled=True),
            lax.psum_scatter(proj_part, "dp", scatter_dimension=0, tiled=True),
        )
        attn_reduced = attn_reduced + attn_piece
        ffn_reduced = ffn_reduced + ffn_piece
        proj_reduced = proj_reduced + proj_piece
        gains_acc = gains_acc + jnp.stack([gain_one, gain_two, gain_three])
        table_acc = table_acc + table_grad
    full_table = lax.dynamic_update_slice_in_dim(
        jnp.zeros_like(bias_table), table_acc, narrow_rank * heads_here, 1
    )
    gains_grad, table_full_grad = lax.psum((gains_acc, full_table), ("dp", "mp"))
    local_squares = (
        jnp.sum(attn_reduced * attn_reduced)
        + jnp.sum(ffn_reduced * ffn_reduced)
        + jnp.sum(proj_reduced * proj_reduced)
    )
    total_squares = (
        lax.psum(local_squares, ("dp", "mp"))
        + jnp.sum(gains_grad * gains_grad)
        + jnp.sum(table_full_grad * table_full_grad)
    )
    grad_norm = jnp.sqrt(total_squares)
    factor = jnp.minimum(1.0, CLIP_NORM / (grad_norm + 1e-06))
    attn_new = adam_update(
        attention_weights,
        attn_reduced * factor,
        attention_first,
        attention_second,
        RATE_MATRIX,
        DECAY_MATRIX,
    )
    ffn_new = adam_update(
        feedforward_weights,
        ffn_reduced * factor,
        feedforward_first,
        feedforward_second,
        RATE_MATRIX,
        DECAY_MATRIX,
    )
    proj_new = adam_update(
        projection,
        proj_reduced * factor,
        projection_first,
        projection_second,
        RATE_MATRIX,
        DECAY_MATRIX,
    )
    gains_new = adam_update(
        norm_gains, gains_grad * factor, gains_first, gains_second, RATE_SMALL, 0.0
    )
    table_new = adam_update(
        bias_table, table_full_grad * factor, bias_first, bias_second, RATE_SMALL, 0.0
    )
    output = jnp.stack(output_rows)[:, None]
    tokens_grad = jnp.stack(input_grads)[:, None]
    return (
        output,
        tokens_grad,
        grad_norm,
        attn_new[0],
        attn_new[1],
        attn_new[2],
        ffn_new[0],
        ffn_new[1],
        ffn_new[2],
        proj_new[0],
        proj_new[1],
        proj_new[2],
        gains_new[0],
        gains_new[1],
        gains_new[2],
        table_new[0],
        table_new[1],
        table_new[2],
    )


def solution(mesh):
    return jax.shard_map(
        local,
        mesh=mesh,
        in_specs=(
            P(None, "dp", "mp", None),
            P(None, "dp", "mp", None),
            P(None, "dp", None),
            P(None, "dp", None),
            P(None, "dp", "mp"),
            P(None, "dp", "mp"),
            P("dp", "mp"),
            P(),
            P(),
            P(None, "dp", "mp"),
            P(None, "dp", "mp"),
            P(None, "dp", "mp"),
            P(None, "dp", "mp"),
            P("dp", "mp"),
            P("dp", "mp"),
            P(),
            P(),
            P(),
            P(),
        ),
        out_specs=(
            P(None, "dp", "mp", None),
            P(None, "dp", "mp", None),
            P(),
            P(None, "dp", "mp"),
            P(None, "dp", "mp"),
            P(None, "dp", "mp"),
            P(None, "dp", "mp"),
            P(None, "dp", "mp"),
            P(None, "dp", "mp"),
            P("dp", "mp"),
            P("dp", "mp"),
            P("dp", "mp"),
            P(),
            P(),
            P(),
            P(),
            P(),
            P(),
        ),
        check_vma=False,
    )
```

profile of v0, /device:TPU:0, one launch (start us, length us, event | category | flops | bytes accessed | tf_op | source)
XLA Modules:
  0.0 1670.9 jit_solution(13338193621622566950)
XLA Ops:
  17.7 21.2 %all-gather.13.cloned.1.call-done = bf16[4,768,192]{2,0,1:T(4,128)(2,1)} async-done(((bf16[4,96,192]{2,0,1:T(4,128)(2,1)}), bf16[4,768,192]{2,0,1:T(4,128)(2,1)}) %all-gather.13.cloned.1.call-update) | async-done | bytes 1179664 | tf_op jit(solution)/shard_map/all_gather | solution.py:151
  41.6 3.4 fusion.259
  46.6 31.6 %all-gather.19.cloned.1.call-done = bf16[1024,768]{1,0:T(8,128)(2,1)} async-done(((bf16[256,768]{1,0:T(8,128)(2,1)}), bf16[1024,768]{1,0:T(8,128)(2,1)}) %all-gather.19.cloned.1.call-update) | async-done | bytes 1572880 | tf_op jit(solution)/shard_map/all_gather | solution.py:127
  83.3 115.2 %while.61 = (s32[]{:T(128)}, bf16[2,512,3,64]{1,3,2,0:T(8,128)(2,1)}, f32[2,3,512,1]{2,1,3,0:T(4,128)}, s32[2]{0:T(128)}, s32[1024]{0:T(1024)}, /*index=5*/s32[1...) while((s32[]{:T(128)}, ...), condition=%wide.region_12.13_spmd.clone, body=%wide.region_9.12_spmd.clone.sunk | while | flops 497024000 | bytes 79180856 | solution.py:195
  91.6 14.2 broadcast_compare_fusion.140
  105.8 26.8 %fusion.372 = (f32[3,512]{1,0:T(4,128)}, f32[3,512,1024]{2,1,0:T(8,128)}) fusion(f32[3]{0:T(128)} %get-tuple-element.1767, f32[3]{0:T(128)} %get-tuple-element.1768, pred[512,1024]{1,0:T(8,128)(4,1)} %get-tuple-element.1769, f32[3]{0:T(128)} %get-tuple-element.1770, pred[512,1024]{1,0:T(8,128)(4,1)} %get-tuple-element.1771, ...), kind=kOutput, calls=%fused_computation.733.clone.1 | convolution fusion | flops 256375296 | bytes 23681028 | tf_op jit(solution)/shard_map/while/body/eval_jaxpr/qhd,khd->hqk/dot_general | solution.py:170
  132.6 4.1 fusion.373
  148.9 14.2 broadcast_compare_fusion.140
  163.1 26.8 %fusion.372 = (f32[3,512]{1,0:T(4,128)}, f32[3,512,1024]{2,1,0:T(8,128)}) fusion(f32[3]{0:T(128)} %get-tuple-element.1767, f32[3]{0:T(128)} %get-tuple-element.1768, pred[512,1024]{1,0:T(8,128)(4,1)} %get-tuple-element.1769, f32[3]{0:T(128)} %get-tuple-element.1770, pred[512,1024]{1,0:T(8,128)(4,1)} %get-tuple-element.1771, ...), kind=kOutput, calls=%fused_computation.733.clone.1 | convolution fusion | flops 256375296 | bytes 23681028 | tf_op jit(solution)/shard_map/while/body/eval_jaxpr/qhd,khd->hqk/dot_general | solution.py:170
  189.9 4.1 fusion.373
  208.0 115.3 %while.60 = (s32[]{:T(128)}, bf16[2,512,3,64]{1,3,2,0:T(8,128)(2,1)}, f32[2,3,512,1]{2,1,3,0:T(4,128)}, s32[2]{0:T(128)}, s32[1024]{0:T(1024)}, /*index=5*/s32[1...) while((s32[]{:T(128)}, ...), condition=%wide.region_4.5_spmd.clone, body=%wide.region_1.4_spmd.clone.sunk | while | flops 497024000 | bytes 79180856 | solution.py:195
  215.9 14.2 broadcast_compare_fusion.138
  230.2 26.8 %fusion.367 = (f32[3,512]{1,0:T(4,128)}, f32[3,512,1024]{2,1,0:T(8,128)}) fusion(f32[3]{0:T(128)} %get-tuple-element.1692, f32[3]{0:T(128)} %get-tuple-element.1693, pred[512,1024]{1,0:T(8,128)(4,1)} %get-tuple-element.1694, f32[3]{0:T(128)} %get-tuple-element.1695, pred[512,1024]{1,0:T(8,128)(4,1)} %get-tuple-element.1696, ...), kind=kOutput, calls=%fused_computation.732.clone.1 | convolution fusion | flops 256375296 | bytes 23681028 | tf_op jit(solution)/shard_map/while/body/eval_jaxpr/qhd,khd->hqk/dot_general | solution.py:170
  256.9 4.1 fusion.368
  273.3 14.2 broadcast_compare_fusion.138
  287.5 26.7 %fusion.367 = (f32[3,512]{1,0:T(4,128)}, f32[3,512,1024]{2,1,0:T(8,128)}) fusion(f32[3]{0:T(128)} %get-tuple-element.1692, f32[3]{0:T(128)} %get-tuple-element.1693, pred[512,1024]{1,0:T(8,128)(4,1)} %get-tuple-element.1694, f32[3]{0:T(128)} %get-tuple-element.1695, pred[512,1024]{1,0:T(8,128)(4,1)} %get-tuple-element.1696, ...), kind=kOutput, calls=%fused_computation.732.clone.1 | convolution fusion | flops 256375296 | bytes 23681028 | tf_op jit(solution)/shard_map/while/body/eval_jaxpr/qhd,khd->hqk/dot_general | solution.py:170
  314.3 4.1 fusion.368
  324.9 3.4 fusion.216
  329.2 58.4 %reduce-scatter.16.cloned.1.call-done = f32[256,768]{1,0:T(8,128)} async-done(((f32[1024,768]{1,0:T(8,128)}), f32[256,768]{1,0:T(8,128)}) %reduce-scatter.16.cloned.1.call-update) | async-done | bytes 786448 | tf_op jit(solution)/shard_map/reduce_scatter | solution.py:197
  392.4 26.7 %all-gather.17.cloned.1.call-done = bf16[2,768,768]{2,1,0:T(8,128)(2,1)} async-done(((bf16[2,96,768]{2,1,0:T(8,128)(2,1)}), bf16[2,768,768]{2,1,0:T(8,128)(2,1)}) %all-gather.17.cloned.1.call-update) | async-done | bytes 2359312 | tf_op jit(solution)/shard_map/all_gather | solution.py:152
  419.0 39.3 %all-gather.21.cloned.1.call-done = bf16[1024,768]{1,0:T(8,128)(2,1)} async-done(((bf16[256,768]{1,0:T(8,128)(2,1)}), bf16[1024,768]{1,0:T(8,128)(2,1)}) %all-gather.21.cloned.1.call-update) | async-done | bytes 1572880 | tf_op jit(solution)/shard_map/all_gather | solution.py:205
  466.5 29.9 %all-gather.15.cloned.1.call-done = bf16[1024,768]{1,0:T(8,128)(2,1)} async-done(((bf16[256,768]{1,0:T(8,128)(2,1)}), bf16[1024,768]{1,0:T(8,128)(2,1)}) %all-gather.15.cloned.1.call-update) | async-done | bytes 1572880 | tf_op jit(solution)/shard_map/all_gather | solution.py:205
  504.6 9.5 all_gather.54
  520.4 12.5 reduce-scatter.22.cloned.1.call-done
  534.7 35.2 %reduce-scatter.18.cloned.1.call-done = bf16[256,768]{1,0:T(8,128)(2,1)} async-done(((bf16[1024,768]{1,0:T(8,128)(2,1)}), bf16[256,768]{1,0:T(8,128)(2,1)}) %reduce-scatter.18.cloned.1.call-update) | async-done | bytes 393232 | tf_op jit(solution)/shard_map/reduce_scatter | solution.py:135
  575.3 18.6 %all-reduce.5 = (f32[8,768]{1,0:T(8,128)}, f32[8,768]{1,0:T(8,128)}) all-reduce(f32[8,768]{1,0:T(8,128)} %fusion.186, f32[8,768]{1,0:T(8,128)} %fusion.188), channel_id=1, replica_groups=mesh['dp'=8,'mp'=4] {'mp'}, use_global_device_ids=true, to_apply=%region_69.70 | all-reduce | flops 12288 | bytes 98304 | tf_op jit(solution)/shard_map/psum | solution.py:140
  598.2 9.5 all-reduce.4
  610.9 9.0 all_gather.58
  622.0 9.0 all_gather.55
  632.4 10.6 all-reduce.3
  649.9 28.8 %reduce-scatter.24.cloned.1.call-done = f32[8,192]{1,0:T(8,128)} async-done(((f32[64,192]{1,0:T(8,128)}), f32[8,192]{1,0:T(8,128)}) %reduce-scatter.24.cloned.1.call-update) | async-done | bytes 6160 | tf_op jit(solution)/shard_map/reduce_scatter | solution.py:255
  680.9 34.8 %reduce-scatter.30.cloned.1.call-done = f32[8,192]{1,0:T(8,128)} async-done(((f32[64,192]{1,0:T(8,128)}), f32[8,192]{1,0:T(8,128)}) %reduce-scatter.30.cloned.1.call-update) | async-done | bytes 6160 | tf_op jit(solution)/shard_map/reduce_scatter | solution.py:255
  717.9 12.4 all-reduce.2
  734.3 16.8 %all-reduce.1 = (f32[8,768]{1,0:T(8,128)S(1)}, f32[8,768]{1,0:T(8,128)S(1)}) all-reduce(f32[8,768]{1,0:T(8,128)} %fusion.268, f32[8,768]{1,0:T(8,128)} %fusion.266), channel_id=1, replica_groups=mesh['dp'=8,'mp'=4] {'mp'}, use_global_device_ids=true, to_apply=%region_79.80 | all-reduce | flops 12288 | bytes 98304 | tf_op jit(solution)/shard_map/psum | solution.py:140
  757.4 35.1 %all-gather.27.cloned.1.call-done = bf16[1024,768]{1,0:T(8,128)(2,1)} async-done(((bf16[256,768]{1,0:T(8,128)(2,1)}), bf16[1024,768]{1,0:T(8,128)(2,1)}) %all-gather.27.cloned.1.call-update) | async-done | bytes 1572880 | tf_op jit(solution)/shard_map/all_gather | solution.py:127
  792.5 5.6 fusion.123
  802.0 28.5 %all-gather.23.cloned.1.call-done = bf16[1024,768]{1,0:T(8,128)(2,1)} async-done(((bf16[256,768]{1,0:T(8,128)(2,1)}), bf16[1024,768]{1,0:T(8,128)(2,1)}) %all-gather.23.cloned.1.call-update) | async-done | bytes 1572880 | tf_op jit(solution)/shard_map/all_gather | solution.py:127
  830.5 5.6 fusion.116
  839.9 26.9 %reduce-scatter.32.cloned.1.call-done = bf16[256,768]{1,0:T(8,128)(2,1)} async-done(((bf16[1024,768]{1,0:T(8,128)(2,1)}), bf16[256,768]{1,0:T(8,128)(2,1)}) %reduce-scatter.32.cloned.1.call-update) | async-done | bytes 393232 | tf_op jit(solution)/shard_map/reduce_scatter | solution.py:135
  866.8 37.0 %reduce-scatter.26.cloned.1.call-done = bf16[256,768]{1,0:T(8,128)(2,1)} async-done(((bf16[1024,768]{1,0:T(8,128)(2,1)}), bf16[256,768]{1,0:T(8,128)(2,1)}) %reduce-scatter.26.cloned.1.call-update) | async-done | bytes 393232 | tf_op jit(solution)/shard_map/reduce_scatter | solution.py:135
  906.2 3.5 fusion.251
  918.7 4.1 convolution_bitcast_fusion
  931.5 13.7 all-gather.29.cloned.1.call-done
  948.8 277.3 %while.63 = (s32[]{:T(128)}, f32[1024,3,64]{0,2,1:T(8,128)}, f32[1024,3,64]{0,2,1:T(8,128)}, f32[32,3]{0,1:T(4,128)}, bf16[2,512,3,64]{1,3,2,0:T(8,128)(2,1)}, /...) while((s32[]{:T(128)}, f32[1024,3,64]{0,2,1:T(8,128)}, ...), condition=%wide.region_117.118_spmd.clone, body=%wide.region_83.117_spmd.clone.sunk | while | flops 1255177216 | bytes 137162704 | solution.py:339
  959.7 14.1 broadcast_compare_fusion.144
  973.8 26.8 %multiply_reduce_fusion.22 = (f32[3,512]{1,0:T(4,128)S(1)}, f32[3,512,1024]{2,1,0:T(8,128)S(1)}) fusion(f32[3,512,1024]{2,1,0:T(8,128)S(1)} %fusion.397, f32[3,512]{1,0:T(4,128)S(1)} %dynamic-slice_bitcast_fusion.5, f32[3]{0:T(128)S(1)} %get-tuple-element.1977, f32[3]{0:T(128)S(1)} %get-tuple-element.1978, ...), kind=kOutput, calls=%fused_computation.349.clone.1 | convolution fusion | flops 259521024 | bytes 29974128 | tf_op jit(solution)/shard_map/while/body/eval_jaxpr/qhd,khd->hqk/dot_general | solution.py:170
  1000.6 22.9 %convert_reduce_fusion.72 = (f32[3]{0:T(128)}, f32[3]{0:T(128)}, f32[3]{0:T(128)}, f32[3]{0:T(128)}, f32[3]{0:T(128)}, /*index=5*/f32[3]{0:T(128)}, f32[3]{0:T(1...) fusion(pred[512,1024]{1,0:T(8,128)(4,1)} %get-tuple-element.195, ...), kind=kLoop, calls=%fused_computation.316.clone.1 | loop fusion | flops 89653200 | bytes 25172184 | tf_op jit(solution)/shard_map/while/body/eval_jaxpr/reduce_sum | solution.py:56
  1025.4 14.2 convert_reduce_fusion.73
  1098.2 14.1 broadcast_compare_fusion.144
  1112.4 26.7 %multiply_reduce_fusion.22 = (f32[3,512]{1,0:T(4,128)S(1)}, f32[3,512,1024]{2,1,0:T(8,128)S(1)}) fusion(f32[3,512,1024]{2,1,0:T(8,128)S(1)} %fusion.397, f32[3,512]{1,0:T(4,128)S(1)} %dynamic-slice_bitcast_fusion.5, f32[3]{0:T(128)S(1)} %get-tuple-element.1977, f32[3]{0:T(128)S(1)} %get-tuple-element.1978, ...), kind=kOutput, calls=%fused_computation.349.clone.1 | convolution fusion | flops 259521024 | bytes 29974128 | tf_op jit(solution)/shard_map/while/body/eval_jaxpr/qhd,khd->hqk/dot_general | solution.py:170
  1139.2 22.9 %convert_reduce_fusion.72 = (f32[3]{0:T(128)}, f32[3]{0:T(128)}, f32[3]{0:T(128)}, f32[3]{0:T(128)}, f32[3]{0:T(128)}, /*index=5*/f32[3]{0:T(128)}, f32[3]{0:T(1...) fusion(pred[512,1024]{1,0:T(8,128)(4,1)} %get-tuple-element.195, ...), kind=kLoop, calls=%fused_computation.316.clone.1 | loop fusion | flops 89653200 | bytes 25172184 | tf_op jit(solution)/shard_map/while/body/eval_jaxpr/reduce_sum | solution.py:56
  1163.9 14.2 convert_reduce_fusion.73
  1237.2 277.4 %while.62 = (s32[]{:T(128)}, f32[1024,3,64]{0,2,1:T(8,128)}, f32[1024,3,64]{0,2,1:T(8,128)}, f32[32,3]{0,1:T(4,128)}, bf16[2,512,3,64]{1,3,2,0:T(8,128)(2,1)}, /...) while((s32[]{:T(128)}, f32[1024,3,64]{0,2,1:T(8,128)}, ...), condition=%wide.region_65.66_spmd.clone, body=%wide.region_31.65_spmd.clone.sunk | while | flops 1255177216 | bytes 137162704 | solution.py:339
  1248.3 14.1 broadcast_compare_fusion.142
  1262.5 26.8 %multiply_reduce_fusion.21 = (f32[3,512]{1,0:T(4,128)S(1)}, f32[3,512,1024]{2,1,0:T(8,128)S(1)}) fusion(f32[3,512,1024]{2,1,0:T(8,128)S(1)} %fusion.384, f32[3,512]{1,0:T(4,128)S(1)} %dynamic-slice_bitcast_fusion.4, f32[3]{0:T(128)S(1)} %get-tuple-element.1864, f32[3]{0:T(128)S(1)} %get-tuple-element.1865, ...), kind=kOutput, calls=%fused_computation.215.clone.1 | convolution fusion | flops 259521024 | bytes 29974128 | tf_op jit(solution)/shard_map/while/body/eval_jaxpr/qhd,khd->hqk/dot_general | solution.py:170
  1289.3 22.9 %convert_reduce_fusion.70 = (f32[3]{0:T(128)}, f32[3]{0:T(128)}, f32[3]{0:T(128)}, f32[3]{0:T(128)}, f32[3]{0:T(128)}, /*index=5*/f32[3]{0:T(128)}, f32[3]{0:T(1...) fusion(pred[512,1024]{1,0:T(8,128)(4,1)} %get-tuple-element.184, ...), kind=kLoop, calls=%fused_computation.182.clone.1 | loop fusion | flops 89653200 | bytes 25172184 | tf_op jit(solution)/shard_map/while/body/eval_jaxpr/reduce_sum | solution.py:56
  1314.0 14.2 convert_reduce_fusion.71
  1386.7 14.1 broadcast_compare_fusion.142
  1400.9 26.7 %multiply_reduce_fusion.21 = (f32[3,512]{1,0:T(4,128)S(1)}, f32[3,512,1024]{2,1,0:T(8,128)S(1)}) fusion(f32[3,512,1024]{2,1,0:T(8,128)S(1)} %fusion.384, f32[3,512]{1,0:T(4,128)S(1)} %dynamic-slice_bitcast_fusion.4, f32[3]{0:T(128)S(1)} %get-tuple-element.1864, f32[3]{0:T(128)S(1)} %get-tuple-element.1865, ...), kind=kOutput, calls=%fused_computation.215.clone.1 | convolution fusion | flops 259521024 | bytes 29974128 | tf_op jit(solution)/shard_map/while/body/eval_jaxpr/qhd,khd->hqk/dot_general | solution.py:170
  1427.7 22.9 %convert_reduce_fusion.70 = (f32[3]{0:T(128)}, f32[3]{0:T(128)}, f32[3]{0:T(128)}, f32[3]{0:T(128)}, f32[3]{0:T(128)}, /*index=5*/f32[3]{0:T(128)}, f32[3]{0:T(1...) fusion(pred[512,1024]{1,0:T(8,128)(4,1)} %get-tuple-element.184, ...), kind=kLoop, calls=%fused_computation.182.clone.1 | loop fusion | flops 89653200 | bytes 25172184 | tf_op jit(solution)/shard_map/while/body/eval_jaxpr/reduce_sum | solution.py:56
  1452.4 14.2 convert_reduce_fusion.71
  1547.0 10.0 reduce-scatter.28.cloned.1.call-done
  1561.3 40.8 %reduce-scatter.40.cloned.1.call-done = f32[96,768]{1,0:T(8,128)} async-done(((f32[768,768]{1,0:T(8,128)}), f32[96,768]{1,0:T(8,128)}) %reduce-scatter.40.cloned.1.call-update) | async-done | bytes 294928
  1607.5 40.1 %all-reduce = (f32[]{:T(128)}, f32[3,768]{1,0:T(4,128)S(1)}, f32[32,12]{0,1:T(8,128)S(1)}) all-reduce(f32[]{:T(128)S(6)} %add.3655, f32[3,768]{1,0:T(4,128)S(1)} %copy-done.90, f32[32,12]{0,1:T(8,128)} %copy-done.100), channel_id=1, replica_groups=mesh['dp'=8,'mp'=4] {'dp','mp'}, use_global_device_ids=true, to_apply=%region_129.130 | all-reduce | flops 2689 | bytes 21512 | tf_op jit(solution)/shard_map/psum | solution.py:388
  (764 shorter events, 468.2 us)
Async XLA Ops:
  7.2 31.7 %all-gather.13.cloned.1.call-start = ((), (), s32[]{:S(2)}) async-start(), calls=%async_computation.14 | async-start | bytes 1769472 | tf_op jit(solution)/shard_map/all_gather | solution.py:151
  9.2 69.0 %all-gather.19.cloned.1.call-start = ((), (), s32[]{:S(2)}) async-start(), calls=%async_computation.19 | async-start | bytes 1966080 | tf_op jit(solution)/shard_map/all_gather | solution.py:127
  14.9 185.2 %all-gather.11.cloned.1.call-start = ((), (), s32[]{:S(2)}) async-start(), calls=%async_computation.13 | async-start | bytes 1966080 | tf_op jit(solution)/shard_map/all_gather | solution.py:127
  15.7 313.6 %reduce-scatter.20.cloned.1.call-start = ((), (), s32[]{:S(2)}) async-start(), calls=%async_computation.20 | async-start | bytes 3932160 | tf_op jit(solution)/shard_map/reduce_scatter | solution.py:197
  41.6 36.6 %copy-start.66 = (bf16[3,768,192]{1,2,0:T(8,128)(2,1)}, bf16[3,768,192]{1,2,0:T(8,128)(2,1)S(1)}, u32[]{:S(2)}) copy-start(bf16[3,768,192]{1,2,0:T(8,128)(2,1)S(1)} %copy.327) | copy-start | bytes 2654212
  206.5 181.1 %reduce-scatter.16.cloned.1.call-start = ((), (), s32[]{:S(2)}) async-start(), calls=%async_computation.15 | async-start | bytes 3932160 | tf_op jit(solution)/shard_map/reduce_scatter | solution.py:197
  324.9 62.8 %copy-start.24 = (bf16[2,1,256,768]{3,2,1,0:T(8,128)(2,1)S(1)}, bf16[2,1,256,768]{3,2,1,0:T(8,128)(2,1)}, u32[]{:S(2)}) copy-start(bf16[2,1,256,768]{3,2,1,0:T(8,128)(2,1)} %param.27) | copy-start | bytes 2359300
  328.3 62.1 %copy-start.88 = (f32[768]{0:T(1024)S(1)}, f32[768]{0:T(1024)}, u32[]{:S(2)}) copy-start(f32[768]{0:T(1024)} %get-tuple-element.641) | copy-start | bytes 9220
  328.3 90.7 %all-gather.17.cloned.1.call-start = ((), (), s32[]{:S(2)}) async-start(), calls=%async_computation.17 | async-start | bytes 2654208 | tf_op jit(solution)/shard_map/all_gather | solution.py:152
  329.2 129.1 %all-gather.21.cloned.1.call-start = ((), (), s32[]{:S(2)}) async-start(), calls=%async_computation.21 | async-start | bytes 1966080 | tf_op jit(solution)/shard_map/all_gather | solution.py:205
  389.9 71.7 %copy-start.104 = (f32[256]{0:T(256)}, f32[256]{0:T(256)S(1)}, u32[]{:S(2)}) copy-start(f32[256]{0:T(256)S(1)} %get-tuple-element.1086) | copy-start | bytes 3076
  390.5 71.1 %copy-start.106 = (f32[256]{0:T(256)}, f32[256]{0:T(256)S(1)}, u32[]{:S(2)}) copy-start(f32[256]{0:T(256)S(1)} %get-tuple-element.1090) | copy-start | bytes 3076
  391.6 104.9 %all-gather.15.cloned.1.call-start = ((), (), s32[]{:S(2)}) async-start(), calls=%async_computation.16 | async-start | bytes 1966080 | tf_op jit(solution)/shard_map/all_gather | solution.py:205
  392.3 140.6 %reduce-scatter.22.cloned.1.call-start = ((), (), s32[]{:S(2)}) async-start(), calls=%async_computation.22 | async-start | bytes 1966080 | tf_op jit(solution)/shard_map/reduce_scatter | solution.py:135
  466.5 103.4 %reduce-scatter.18.cloned.1.call-start = ((), (), s32[]{:S(2)}) async-start(), calls=%async_computation.18 | async-start | bytes 1966080 | tf_op jit(solution)/shard_map/reduce_scatter | solution.py:135
  504.6 174.2 %reduce-scatter.24.cloned.1.call-start = ((), (), s32[]{:S(2)}) async-start(), calls=%async_computation.23 | async-start | bytes 73728 | tf_op jit(solution)/shard_map/reduce_scatter | solution.py:255
  648.1 67.6 %reduce-scatter.30.cloned.1.call-start = ((), (), s32[]{:S(2)}) async-start(), calls=%async_computation.28 | async-start | bytes 73728 | tf_op jit(solution)/shard_map/reduce_scatter | solution.py:255
  649.8 142.7 %all-gather.27.cloned.1.call-start = ((), (), s32[]{:S(2)}) async-start(), calls=%async_computation.29 | async-start | bytes 1966080 | tf_op jit(solution)/shard_map/all_gather | solution.py:127
  756.8 73.7 %all-gather.23.cloned.1.call-start = ((), (), s32[]{:S(2)}) async-start(), calls=%async_computation.24 | async-start | bytes 1966080 | tf_op jit(solution)/shard_map/all_gather | solution.py:127
  757.4 109.4 %reduce-scatter.32.cloned.1.call-start = ((), (), s32[]{:S(2)}) async-start(), calls=%async_computation.30 | async-start | bytes 1966080 | tf_op jit(solution)/shard_map/reduce_scatter | solution.py:135
  801.9 101.9 %reduce-scatter.26.cloned.1.call-start = ((), (), s32[]{:S(2)}) async-start(), calls=%async_computation.25 | async-start | bytes 1966080 | tf_op jit(solution)/shard_map/reduce_scatter | solution.py:135
  837.3 66.5 %copy-start.89 = (f32[768]{0:T(1024)S(1)}, f32[768]{0:T(1024)}, u32[]{:S(2)}) copy-start(f32[768]{0:T(1024)} %get-tuple-element.641) | copy-start | bytes 9220
  837.3 66.5 %copy-start.105 = (f32[256]{0:T(256)S(1)}, f32[256]{0:T(256)}, u32[]{:S(2)}) copy-start(f32[256]{0:T(256)} %copy-done.104) | copy-start | bytes 3076
  837.3 66.5 %copy-start.107 = (f32[256]{0:T(256)S(1)}, f32[256]{0:T(256)}, u32[]{:S(2)}) copy-start(f32[256]{0:T(256)} %copy-done.106) | copy-start | bytes 3076
  839.9 66.3 %copy-start.114 = (f32[256]{0:T(256)S(1)}, f32[256]{0:T(256)}, u32[]{:S(2)}) copy-start(f32[256]{0:T(256)} %get-tuple-element.1085) | copy-start | bytes 3076
  839.9 66.3 %copy-start.115 = (f32[256]{0:T(256)S(1)}, f32[256]{0:T(256)}, u32[]{:S(2)}) copy-start(f32[256]{0:T(256)} %get-tuple-element.1089) | copy-start | bytes 3076
  839.9 105.3 %all-gather.29.cloned.1.call-start = ((), (), s32[]{:S(2)}) async-start(), calls=%async_computation.31 | async-start | bytes 1966080 | tf_op jit(solution)/shard_map/all_gather | solution.py:127
  909.7 323.9 %all-gather.25.cloned.1.call-start = ((), (), s32[]{:S(2)}) async-start(), calls=%async_computation.26 | async-start | bytes 1966080 | tf_op jit(solution)/shard_map/all_gather | solution.py:127
  910.3 631.7 %reduce-scatter.38.cloned.1.call-start = ((), (), s32[]{:S(2)}) async-start(), calls=%async_computation.34 | async-start | bytes 884736 | tf_op jit(solution)/shard_map/reduce_scatter | solution.py:371
  918.7 626.5 %reduce-scatter.36.cloned.1.call-start = ((), (), s32[]{:S(2)}) async-start(), calls=%async_computation.33 | async-start | bytes 5308416 | tf_op jit(solution)/shard_map/reduce_scatter | solution.py:370
  931.5 615.5 %reduce-scatter.34.cloned.1.call-start = ((), (), s32[]{:S(2)}) async-start(), calls=%async_computation.32 | async-start | bytes 1966080 | tf_op jit(solution)/shard_map/reduce_scatter | solution.py:135
  973.7 26.8 %copy-start.2 = (pred[512,1024]{1,0:T(8,128)(4,1)}, pred[512,1024]{1,0:T(8,128)(4,1)S(1)}, u32[]{:S(2)}) copy-start(pred[512,1024]{1,0:T(8,128)(4,1)S(1)} %get-tuple-element.1961) | copy-start | bytes 1572868 | tf_op jit(solution)/shard_map/while
  973.7 26.8 %copy-start.3 = (pred[512,1024]{1,0:T(8,128)(4,1)}, pred[512,1024]{1,0:T(8,128)(4,1)S(1)}, u32[]{:S(2)}) copy-start(pred[512,1024]{1,0:T(8,128)(4,1)S(1)} %get-tuple-element.1962) | copy-start | bytes 1572868 | tf_op jit(solution)/shard_map/while
  973.7 26.8 %copy-start.4 = (pred[512,1024]{1,0:T(8,128)(4,1)}, pred[512,1024]{1,0:T(8,128)(4,1)S(1)}, u32[]{:S(2)}) copy-start(pred[512,1024]{1,0:T(8,128)(4,1)S(1)} %get-tuple-element.1963) | copy-start | bytes 1572868 | tf_op jit(solution)/shard_map/while
  973.8 26.8 %copy-start.5 = (pred[512,1024]{1,0:T(8,128)(4,1)}, pred[512,1024]{1,0:T(8,128)(4,1)S(1)}, u32[]{:S(2)}) copy-start(pred[512,1024]{1,0:T(8,128)(4,1)S(1)} %get-tuple-element.1964) | copy-start | bytes 1572868 | tf_op jit(solution)/shard_map/while
  973.8 26.8 %copy-start.6 = (pred[512,1024]{1,0:T(8,128)(4,1)}, pred[512,1024]{1,0:T(8,128)(4,1)S(1)}, u32[]{:S(2)}) copy-start(pred[512,1024]{1,0:T(8,128)(4,1)S(1)} %get-tuple-element.1965) | copy-start | bytes 1572868 | tf_op jit(solution)/shard_map/while
  973.8 26.8 %copy-start.7 = (pred[512,1024]{1,0:T(8,128)(4,1)}, pred[512,1024]{1,0:T(8,128)(4,1)S(1)}, u32[]{:S(2)}) copy-start(pred[512,1024]{1,0:T(8,128)(4,1)S(1)} %get-tuple-element.1966) | copy-start | bytes 1572868 | tf_op jit(solution)/shard_map/while
  973.8 26.8 %copy-start.8 = (pred[512,1024]{1,0:T(8,128)(4,1)}, pred[512,1024]{1,0:T(8,128)(4,1)S(1)}, u32[]{:S(2)}) copy-start(pred[512,1024]{1,0:T(8,128)(4,1)S(1)} %get-tuple-element.1967) | copy-start | bytes 1572868 | tf_op jit(solution)/shard_map/while
  1025.3 58.8 %copy-start.29 = (bf16[1024,3,64]{0,2,1:T(8,128)(2,1)S(1)}, bf16[1024,3,64]{0,2,1:T(8,128)(2,1)}, u32[]{:S(2)}) copy-start(bf16[1024,3,64]{0,2,1:T(8,128)(2,1)} %get-tuple-element.2230) | copy-start | bytes 1179652 | tf_op jit(solution)/shard_map/while
  1112.3 26.8 %copy-start.3 = (pred[512,1024]{1,0:T(8,128)(4,1)}, pred[512,1024]{1,0:T(8,128)(4,1)S(1)}, u32[]{:S(2)}) copy-start(pred[512,1024]{1,0:T(8,128)(4,1)S(1)} %get-tuple-element.1962) | copy-start | bytes 1572868 | tf_op jit(solution)/shard_map/while
  1112.3 26.8 %copy-start.4 = (pred[512,1024]{1,0:T(8,128)(4,1)}, pred[512,1024]{1,0:T(8,128)(4,1)S(1)}, u32[]{:S(2)}) copy-start(pred[512,1024]{1,0:T(8,128)(4,1)S(1)} %get-tuple-element.1963) | copy-start | bytes 1572868 | tf_op jit(solution)/shard_map/while
  1112.3 26.8 %copy-start.5 = (pred[512,1024]{1,0:T(8,128)(4,1)}, pred[512,1024]{1,0:T(8,128)(4,1)S(1)}, u32[]{:S(2)}) copy-start(pred[512,1024]{1,0:T(8,128)(4,1)S(1)} %get-tuple-element.1964) | copy-start | bytes 1572868 | tf_op jit(solution)/shard_map/while
  1112.3 26.8 %copy-start.6 = (pred[512,1024]{1,0:T(8,128)(4,1)}, pred[512,1024]{1,0:T(8,128)(4,1)S(1)}, u32[]{:S(2)}) copy-start(pred[512,1024]{1,0:T(8,128)(4,1)S(1)} %get-tuple-element.1965) | copy-start | bytes 1572868 | tf_op jit(solution)/shard_map/while
  1112.3 26.8 %copy-start.7 = (pred[512,1024]{1,0:T(8,128)(4,1)}, pred[512,1024]{1,0:T(8,128)(4,1)S(1)}, u32[]{:S(2)}) copy-start(pred[512,1024]{1,0:T(8,128)(4,1)S(1)} %get-tuple-element.1966) | copy-start | bytes 1572868 | tf_op jit(solution)/shard_map/while
  1112.4 26.8 %copy-start.8 = (pred[512,1024]{1,0:T(8,128)(4,1)}, pred[512,1024]{1,0:T(8,128)(4,1)S(1)}, u32[]{:S(2)}) copy-start(pred[512,1024]{1,0:T(8,128)(4,1)S(1)} %get-tuple-element.1967) | copy-start | bytes 1572868 | tf_op jit(solution)/shard_map/while
  1163.9 58.8 %copy-start.29 = (bf16[1024,3,64]{0,2,1:T(8,128)(2,1)S(1)}, bf16[1024,3,64]{0,2,1:T(8,128)(2,1)}, u32[]{:S(2)}) copy-start(bf16[1024,3,64]{0,2,1:T(8,128)(2,1)} %get-tuple-element.2230) | copy-start | bytes 1179652 | tf_op jit(solution)/shard_map/while
  1233.5 323.4 %reduce-scatter.28.cloned.1.call-start = ((), (), s32[]{:S(2)}) async-start(), calls=%async_computation.27 | async-start | bytes 1966080 | tf_op jit(solution)/shard_map/reduce_scatter | solution.py:135
  1262.4 26.8 %copy-start.9 = (pred[512,1024]{1,0:T(8,128)(4,1)}, pred[512,1024]{1,0:T(8,128)(4,1)S(1)}, u32[]{:S(2)}) copy-start(pred[512,1024]{1,0:T(8,128)(4,1)S(1)} %get-tuple-element.1848) | copy-start | bytes 1572868 | tf_op jit(solution)/shard_map/while
  1262.4 26.8 %copy-start.10 = (pred[512,1024]{1,0:T(8,128)(4,1)}, pred[512,1024]{1,0:T(8,128)(4,1)S(1)}, u32[]{:S(2)}) copy-start(pred[512,1024]{1,0:T(8,128)(4,1)S(1)} %get-tuple-element.1849) | copy-start | bytes 1572868 | tf_op jit(solution)/shard_map/while
  1262.4 26.8 %copy-start.11 = (pred[512,1024]{1,0:T(8,128)(4,1)}, pred[512,1024]{1,0:T(8,128)(4,1)S(1)}, u32[]{:S(2)}) copy-start(pred[512,1024]{1,0:T(8,128)(4,1)S(1)} %get-tuple-element.1850) | copy-start | bytes 1572868 | tf_op jit(solution)/shard_map/while
  1262.4 26.8 %copy-start.12 = (pred[512,1024]{1,0:T(8,128)(4,1)}, pred[512,1024]{1,0:T(8,128)(4,1)S(1)}, u32[]{:S(2)}) copy-start(pred[512,1024]{1,0:T(8,128)(4,1)S(1)} %get-tuple-element.1851) | copy-start | bytes 1572868 | tf_op jit(solution)/shard_map/while
  1262.4 26.8 %copy-start.13 = (pred[512,1024]{1,0:T(8,128)(4,1)}, pred[512,1024]{1,0:T(8,128)(4,1)S(1)}, u32[]{:S(2)}) copy-start(pred[512,1024]{1,0:T(8,128)(4,1)S(1)} %get-tuple-element.1852) | copy-start | bytes 1572868 | tf_op jit(solution)/shard_map/while
  1262.4 26.8 %copy-start.14 = (pred[512,1024]{1,0:T(8,128)(4,1)}, pred[512,1024]{1,0:T(8,128)(4,1)S(1)}, u32[]{:S(2)}) copy-start(pred[512,1024]{1,0:T(8,128)(4,1)S(1)} %get-tuple-element.1853) | copy-start | bytes 1572868 | tf_op jit(solution)/shard_map/while
  1262.4 26.8 %copy-start.15 = (pred[512,1024]{1,0:T(8,128)(4,1)}, pred[512,1024]{1,0:T(8,128)(4,1)S(1)}, u32[]{:S(2)}) copy-start(pred[512,1024]{1,0:T(8,128)(4,1)S(1)} %get-tuple-element.1854) | copy-start | bytes 1572868 | tf_op jit(solution)/shard_map/while
  1314.0 58.6 %copy-start.27 = (bf16[1024,3,64]{0,2,1:T(8,128)(2,1)S(1)}, bf16[1024,3,64]{0,2,1:T(8,128)(2,1)}, u32[]{:S(2)}) copy-start(bf16[1024,3,64]{0,2,1:T(8,128)(2,1)} %get-tuple-element.2179) | copy-start | bytes 1179652 | tf_op jit(solution)/shard_map/while
  1400.8 26.8 %copy-start.11 = (pred[512,1024]{1,0:T(8,128)(4,1)}, pred[512,1024]{1,0:T(8,128)(4,1)S(1)}, u32[]{:S(2)}) copy-start(pred[512,1024]{1,0:T(8,128)(4,1)S(1)} %get-tuple-element.1850) | copy-start | bytes 1572868 | tf_op jit(solution)/shard_map/while
  1400.8 26.8 %copy-start.12 = (pred[512,1024]{1,0:T(8,128)(4,1)}, pred[512,1024]{1,0:T(8,128)(4,1)S(1)}, u32[]{:S(2)}) copy-start(pred[512,1024]{1,0:T(8,128)(4,1)S(1)} %get-tuple-element.1851) | copy-start | bytes 1572868 | tf_op jit(solution)/shard_map/while
  1452.4 58.6 %copy-start.27 = (bf16[1024,3,64]{0,2,1:T(8,128)(2,1)S(1)}, bf16[1024,3,64]{0,2,1:T(8,128)(2,1)}, u32[]{:S(2)}) copy-start(bf16[1024,3,64]{0,2,1:T(8,128)(2,1)} %get-tuple-element.2179) | copy-start | bytes 1179652 | tf_op jit(solution)/shard_map/while
  1521.8 80.3 %reduce-scatter.40.cloned.1.call-start = ((), (), s32[]{:S(2)}) async-start(), calls=%async_computation.35 | async-start | bytes 2654208
  1561.2 46.2 %copy-start.90 = (f32[3,768]{1,0:T(4,128)S(1)}, f32[3,768]{1,0:T(4,128)}, u32[]{:S(2)}) copy-start(f32[3,768]{1,0:T(4,128)} %maximum_add_fusion.2) | copy-start | bytes 27652
  1561.3 89.6 %copy-start.64 = (f32[4,96,192]{1,2,0:T(8,128)S(1)}, f32[4,96,192]{1,2,0:T(8,128)}, u32[]{:S(2)}) copy-start(f32[4,96,192]{1,2,0:T(8,128)} %copy.319) | copy-start | bytes 884740
  1561.3 89.6 %copy-start.65 = (f32[4,96,192]{1,2,0:T(8,128)S(1)}, f32[4,96,192]{1,2,0:T(8,128)}, u32[]{:S(2)}) copy-start(f32[4,96,192]{1,2,0:T(8,128)} %copy.317) | copy-start | bytes 884740
  1607.5 52.8 %copy-start.52 = (f32[2,96,768]{2,1,0:T(8,128)S(1)}, f32[2,96,768]{2,1,0:T(8,128)}, u32[]{:S(2)}) copy-start(f32[2,96,768]{2,1,0:T(8,128)} %param.32) | copy-start | bytes 1769476
  1607.5 52.8 %copy-start.53 = (f32[2,96,768]{2,1,0:T(8,128)S(1)}, f32[2,96,768]{2,1,0:T(8,128)}, u32[]{:S(2)}) copy-start(f32[2,96,768]{2,1,0:T(8,128)} %reduce-scatter.36.cloned.1.call-done) | copy-start | bytes 1769476
  (133 other events, 911.0 us)
Sparse Core Ops, SparseCore 0:
  10.5 28.3 all-gather.12
  41.1 37.0 all-gather.18
  80.3 35.9 all-gather.10
  206.7 59.0 reduce-scatter.19
  328.4 59.1 reduce-scatter.15
  390.0 29.0 all-gather.16
  421.2 37.0 all-gather.20
  460.4 35.9 all-gather.14
  498.7 34.1 reduce-scatter.21
  535.6 34.2 reduce-scatter.17
  648.3 30.4 reduce-scatter.23
  682.4 33.2 reduce-scatter.29
  756.9 35.5 all-gather.26
  794.5 35.9 all-gather.22
  832.6 34.1 reduce-scatter.31
  869.5 34.2 reduce-scatter.25
  909.9 35.3 all-gather.28
  947.2 36.6 all-gather.24
  987.1 33.8 reduce-scatter.37
  1024.3 53.9 reduce-scatter.35
  1233.7 34.8 reduce-scatter.33
  1521.9 34.9 reduce-scatter.27
  1560.6 41.4 reduce-scatter.39
where the time goes:
time: 1680 us; the launch traced here: 1670 us
  waiting for transfers between devices  513 us (31%)
  other arithmetic  366 us (22%)
  matrix products  343 us (20%)
  local copies, waits for them, and re-layouts  273 us (16%)
  blocking collectives  136 us (8%)
  between operations  20.7 us (1%)
  loops' own time  18.3 us (1%)
    dot_general x8, matrix products, block_scores(): jnp.einsum('qhd,khd->hqk', query_block, keys_all, preferred_element_type=...  214 us
    another operation x132, local copies, waits for them, and re-layouts, bias_grad(): jnp.stack([jnp.sum(jnp.where((buckets == number)[None], score_grad, nothi...  173 us
    reduce_sum x8, other arithmetic, bias_grad(): jnp.sum(jnp.where((buckets == number)[None], score_grad, nothing), axis=(...  148 us
    reduce_scatter x6, waiting for transfers between devices, rows_sum(): lax.psum_scatter(running.astype(jnp.bfloat16), 'mp', scatter_dimension=0,...  122 us
    all_gather x6, waiting for transfers between devices, rows_all(): return lax.all_gather(values, 'mp', axis=0, tiled=True)  109 us
    all_gather x2, waiting for transfers between devices, local(): normed_all_two = lax.all_gather(normed_two, 'mp', axis=0, tiled=True)  69.2 us
    psum x5, blocking collectives, feature_total(): return lax.psum(values, 'mp')  67.9 us
    reduce_scatter x2, waiting for transfers between devices, local(): lax.psum_scatter(key_side, 'dp', scatter_dimension=0, tiled=True)  63.6 us
  transfers between devices with their start and end apart: 23, of which 17 were waited for; matrix products, arithmetic and copies ran while one was open for 54% of the time, Pallas kernels for 0%

commit v1 on v0

v1 whole, which is shorter than its diff:
```python
import functools

import jax
import jax.numpy as jnp
from jax import lax
from jax.experimental import pallas as pl
from jax.experimental.pallas import tpu as pltpu
from jax.sharding import PartitionSpec as P

D = 768
HD = 64
STEP = 10
SEG_MOST = 512

EPS_NORM = 1e-06
EPS_ADAM = 1e-08
SIM_SCALE = 50.0
NEG_FILL = -1000000000.0
BETA_ONE = 0.9
BETA_TWO = 0.999
CLIP_NORM = 1.0
RATE_MATRIX = 0.05
RATE_SMALL = 0.2
DECAY_MATRIX = 0.01
LIMITS = (12, 16, 23, 32, 46, 64, 91)
FAR = LIMITS[-1]
MASKED = -float(2**30)
HIGHEST = lax.Precision.HIGHEST
BF16 = jnp.bfloat16
F32 = jnp.float32
NN = (((1,), (0,)), ((), ()))
NT = (((1,), (1,)), ((), ()))
TN = (((0,), (0,)), ((), ()))
VMEM_LIMIT = 48 * 1024 * 1024


def dot(left, right, dims=NN, precision=None):
    return lax.dot_general(left, right, dims, precision=precision, preferred_element_type=F32)


def bucket_of(relative):
    distance = jnp.abs(relative)
    far_bucket = 8 + sum(((distance >= threshold).astype(jnp.int32) for threshold in LIMITS))
    near_bucket = jnp.where(distance < 8, distance, far_bucket)
    return near_bucket + 16 * (relative > 0).astype(jnp.int32)


def norm_factor(values):
    return lax.rsqrt(jnp.mean(values * values, axis=-1, keepdims=True) + EPS_NORM)


def norm_back(values, factor, upstream):
    return factor * upstream - values * (factor * factor * factor) * jnp.mean(
        upstream * values, axis=-1, keepdims=True
    )


def adam_update(weight_now, clipped, first_old, second_old, step_rate, weight_decay):
    first_new = BETA_ONE * first_old + (1.0 - BETA_ONE) * clipped
    second_new = BETA_TWO * second_old + (1.0 - BETA_TWO) * clipped * clipped
    first_hat = first_new / (1.0 - BETA_ONE**STEP)
    second_hat = second_new / (1.0 - BETA_TWO**STEP)
    weight_new = weight_now - step_rate * (
        first_hat / (jnp.sqrt(second_hat) + EPS_ADAM) + weight_decay * weight_now
    )
    return (weight_new, first_new, second_new)


def swap(values, axis, mask):
    count = lax.axis_size(axis)
    return lax.ppermute(values, axis, [(i, i ^ mask) for i in range(count)])


def shift(values, axis, step):
    count = lax.axis_size(axis)
    pairs = [(i, i + step) for i in range(count) if 0 <= i + step < count]
    return lax.ppermute(values, axis, pairs)


def outer_masks():
    return [1 << bit for bit in range(1, lax.axis_size("dp").bit_length() - 1)]


def core_masks():
    return [1] if lax.axis_size("dp") > 1 else []


def gather_columns(values):
    count = lax.axis_size("mp")
    return jnp.concatenate([values] + [swap(values, "mp", k) for k in range(1, count)], axis=-1)


def gather_rows(values, low_first):
    held = values[:, None]
    order = outer_masks()
    for mask in order if low_first else order[::-1]:
        other = swap(held, "dp", mask)
        if low_first:
            held = jnp.concatenate([held, other], axis=1)
        else:
            c, n, r, w = held.shape
            held = jnp.stack([held, other], axis=2).reshape(c, 2 * n, r, w)
    for mask in core_masks():
        held = jnp.concatenate([held, swap(held, "dp", mask)], axis=1)
    c, n, r, w = held.shape
    return held.reshape(c, n * r, w)


def reduce_rows(values, low_first):
    count = lax.axis_size("dp")
    c, _, w = values.shape
    held = values.reshape(c, count, D // count, w)
    for mask in core_masks():
        half = held.shape[1] // 2
        other = swap(held[:, half:].astype(BF16), "dp", mask)
        held = held[:, :half].astype(F32) + other.astype(F32)
    order = outer_masks()
    for mask in order if low_first else order[::-1]:
        half = held.shape[1] // 2
        if low_first:
            parts = held.reshape(c, half, 2, D // count, w)
            stay, leave = parts[:, :, 0], parts[:, :, 1]
        else:
            stay, leave = held[:, :half], held[:, half:]
        other = swap(leave.astype(BF16), "dp", mask)
        held = stay.astype(F32) + other.astype(F32)
    return held.reshape(c, D // count, w)


def reduce_columns(values):
    count = lax.axis_size("mp")
    width = values.shape[-1] // count
    parts = [values[..., k * width : (k + 1) * width] for k in range(count)]
    total = parts[0].astype(F32)
    for k in range(1, count):
        total = total + swap(parts[k].astype(BF16), "mp", k).astype(F32)
    return total


def sum_over(values, axis):
    bit = 1
    while bit < lax.axis_size(axis):
        values = values + swap(values, axis, bit)
        bit *= 2
    return values


def gather_near(values):
    bit = 1
    while bit < lax.axis_size("dp"):
        values = jnp.concatenate([values, swap(values, "dp", bit)], axis=0)
        bit *= 2
    return values


def bias_kernel(line_ref, tile_ref):
    rows = tile_ref.shape[2]
    for block in range(tile_ref.shape[1]):
        line = jnp.broadcast_to(line_ref[0, block : block + 1, :], (rows, 2 * rows))
        tile_ref[0, block] = pltpu.roll(line, 0, 1, stride=1, stride_axis=0)[:, :rows]


def bias_tiles(table, rows):
    heads = table.shape[1]
    lane = jnp.arange(2 * rows, dtype=jnp.int32)
    back = jnp.where(lane < rows, lane, lane - 2 * rows)
    relative = (jnp.arange(3, dtype=jnp.int32)[:, None] - 1) * rows - back[None, :]
    hot = (bucket_of(relative)[..., None] == jnp.arange(table.shape[0])).astype(F32)
    lines = dot(table, hot.reshape(-1, table.shape[0]), (((0,), (1,)), ((), ())), HIGHEST)
    lines = lines.reshape(heads, 3, 2 * rows)
    return pl.pallas_call(
        bias_kernel,
        grid=(heads,),
        in_specs=[pl.BlockSpec((1, 3, 2 * rows), lambda h: (h, 0, 0))],
        out_specs=pl.BlockSpec((1, 3, rows, rows), lambda h: (h, 0, 0, 0)),
        out_shape=jax.ShapeDtypeStruct((heads, 3, rows, rows), F32),
        compiler_params=pltpu.CompilerParams(vmem_limit_bytes=VMEM_LIMIT),
    )(lines)


def own_lanes(shape, part):
    lane = lax.broadcasted_iota(jnp.int32, shape, 1)
    return (lane < HD) if part == 0 else (lane >= HD)


def block_choices(reach):
    return [
        (lo, hi) for lo in range(reach + 1) for hi in range(reach + 1) if lo + hi < 2 * reach
    ]


def forward_kernel(reach, range_ref, far_ref, q_ref, k_ref, v_ref, qf_ref, kf_ref, bias_ref, o_ref, log_ref):
    pair = pl.program_id(0)
    rows = q_ref.shape[0]
    score_scale = HD ** (-0.5)

    def work(lo, hi):
        query = q_ref[...] * jnp.asarray(score_scale, BF16)
        mixed, logs = [], []
        for part in range(2):
            own_q = own_lanes((rows, 2 * HD), part)
            query_low = jnp.where(own_q, query, qf_ref[...])
            scores = []
            for block in range(-lo, hi + 1):
                spot = pl.ds((block + reach) * rows, rows)
                key_low = jnp.where(own_q, k_ref[spot, :], kf_ref[spot, :])
                score = dot(key_low, query_low, NT)
                if abs(block) <= 1:
                    score = score + bias_ref[part, block + 1]
                else:
                    score = score + far_ref[int(block > 0), 2 * pair + part]
                scores.append(score)
            peak = jnp.max(functools.reduce(jnp.maximum, scores), axis=0, keepdims=True)
            total = jnp.zeros((2 * HD, rows), F32)
            for number, block in enumerate(range(-lo, hi + 1)):
                spot = pl.ds((block + reach) * rows, rows)
                probs = jnp.exp(scores[number] - peak).astype(BF16)
                value_low = jnp.where(own_q, v_ref[spot, :], jnp.ones((), BF16))
                total = total + dot(value_low, probs, TN)
            row_sum = total[HD * (1 - part) : HD * (1 - part) + 1, :]
            mixed.append(total[HD * part : HD * (part + 1), :] / row_sum)
            logs.append(peak + jnp.log(row_sum))
        o_ref[...] = jnp.concatenate(mixed, axis=0).T.astype(BF16)
        log_ref[0] = jnp.concatenate(logs + [jnp.zeros((6, rows), F32)], axis=0)

    for lo, hi in block_choices(reach):
        pl.when((range_ref[0] == lo) & (range_ref[1] == hi))(functools.partial(work, lo, hi))


def backward_kernel(
    reach, range_ref, far_ref, q_ref, k_ref, v_ref, qf_ref, kf_ref, bias_ref, do_ref, o_ref, log_ref,
    dq_ref, dk_ref, dv_ref, db_ref,
):
    pair = pl.program_id(0)
    rows = q_ref.shape[0]
    score_scale = HD ** (-0.5)

    def work(lo, hi):
        query = q_ref[...] * jnp.asarray(score_scale, BF16)
        upstream = do_ref[...]
        products = (upstream.astype(F32) * o_ref[...].astype(F32)).T
        nothing = jnp.zeros((), BF16)
        ahead = lax.broadcasted_iota(jnp.int32, (rows, rows), 0) - lax.broadcasted_iota(
            jnp.int32, (rows, rows), 1
        )
        own, query_low, query_own, up_own, delta, log_row, dq, near, far = ([None, None] for _ in range(9))
        for part in range(2):
            own[part] = own_lanes((rows, 2 * HD), part)
            query_low[part] = jnp.where(own[part], query, qf_ref[...])
            query_own[part] = jnp.where(own[part], query, nothing)
            up_own[part] = jnp.where(own[part], upstream, nothing)
            delta[part] = jnp.sum(products[HD * part : HD * (part + 1), :], axis=0, keepdims=True)
            log_row[part] = log_ref[0, part : part + 1, :]
            dq[part] = jnp.zeros((2 * HD, rows), F32)
            near[part] = jnp.zeros((rows, rows), F32)
            far[part] = [jnp.zeros((1, rows), F32), jnp.zeros((1, rows), F32)]
        for block in range(-reach, reach + 1):
            spot = pl.ds((block + reach) * rows, rows)
            if not -lo <= block <= hi:
                dk_ref[spot, :] = jnp.zeros((rows, 2 * HD), BF16)
                dv_ref[spot, :] = jnp.zeros((rows, 2 * HD), BF16)
                continue
            dk = jnp.zeros((rows, 2 * HD), F32)
            dv = jnp.zeros((rows, 2 * HD), F32)
            for part in range(2):
                key = k_ref[spot, :]
                score = dot(jnp.where(own[part], key, kf_ref[spot, :]), query_low[part], NT)
                if abs(block) <= 1:
                    score = score + bias_ref[part, block + 1]
                else:
                    score = score + far_ref[int(block > 0), 2 * pair + part]
                probs = jnp.exp(score - log_row[part])
                dprobs = dot(v_ref[spot, :], up_own[part], NT)
                dscore = probs * (dprobs - delta[part])
                probs_low, dscore_low = probs.astype(BF16), dscore.astype(BF16)
                dv = dv + dot(probs_low, up_own[part])
                dk = dk + dot(dscore_low, query_own[part])
                dq[part] = dq[part] + dot(key, dscore_low, TN)
                if block == 0:
                    close = jnp.abs(ahead) < FAR
                    near[part] = near[part] + jnp.where(close, dscore, 0.0)
                    far[part][0] += jnp.sum(jnp.where(ahead <= -FAR, dscore, 0.0), axis=0, keepdims=True)
                    far[part][1] += jnp.sum(jnp.where(ahead >= FAR, dscore, 0.0), axis=0, keepdims=True)
                elif abs(block) == 1:
                    close = (ahead < FAR - rows) if block > 0 else (ahead > rows - FAR)
                    near[part] = near[part] + jnp.where(close, dscore, 0.0)
                    far[part][int(block > 0)] += jnp.sum(jnp.where(close, 0.0, dscore), axis=0, keepdims=True)
                else:
                    far[part][int(block > 0)] += jnp.sum(dscore, axis=0, keepdims=True)
            dk_ref[spot, :] = dk.astype(BF16)
            dv_ref[spot, :] = dv.astype(BF16)
        dq_ref[...] = (
            jnp.concatenate([dq[0][:HD], dq[1][HD:]], axis=0).T * score_scale
        ).astype(BF16)
        flip = (
            lax.broadcasted_iota(jnp.int32, (rows, rows), 0) + lax.broadcasted_iota(jnp.int32, (rows, rows), 1)
            == rows - 1
        ).astype(BF16)
        for part in range(2):
            turned = dot(flip, near[part].astype(BF16))
            turned = pltpu.roll(turned, 0, 1, stride=1, stride_axis=0)
            line = jnp.sum(turned, axis=0, keepdims=True)
            db_ref[0, part] = jnp.concatenate(
                [line, far[part][0], far[part][1], jnp.zeros((5, rows), F32)], axis=0
            )

    for lo, hi in block_choices(reach):
        pl.when((range_ref[0] == lo) & (range_ref[1] == hi))(functools.partial(work, lo, hi))


def attention_specs(rows, window, pairs):
    smem = pl.BlockSpec(memory_space=pltpu.SMEM)
    return [
        smem,
        smem,
        pl.BlockSpec((rows, 2 * HD), lambda p: (0, p)),
        pl.BlockSpec((window, 2 * HD), lambda p: (0, p)),
        pl.BlockSpec((window, 2 * HD), lambda p: (0, p)),
        pl.BlockSpec((rows, 2 * HD), lambda p: (0, 0)),
        pl.BlockSpec((window, 2 * HD), lambda p: (0, 0)),
        pl.BlockSpec((2, 3, rows, rows), lambda p: (p, 0, 0, 0)),
    ]


def attend(reach, *operands):
    rows, width = operands[2].shape
    window = operands[3].shape[0]
    pairs = width // (2 * HD)
    return pl.pallas_call(
        functools.partial(forward_kernel, reach),
        grid=(pairs,),
        in_specs=attention_specs(rows, window, pairs),
        out_specs=[
            pl.BlockSpec((rows, 2 * HD), lambda p: (0, p)),
            pl.BlockSpec((1, 8, rows), lambda p: (p, 0, 0)),
        ],
        out_shape=[
            jax.ShapeDtypeStruct((rows, width), BF16),
            jax.ShapeDtypeStruct((pairs, 8, rows), F32),
        ],
        compiler_params=pltpu.CompilerParams(vmem_limit_bytes=VMEM_LIMIT),
        name="attend",
    )(*operands)


def attend_back(reach, *operands):
    rows, width = operands[2].shape
    window = operands[3].shape[0]
    pairs = width // (2 * HD)
    tall = pl.BlockSpec((window, 2 * HD), lambda p: (0, p))
    short = pl.BlockSpec((rows, 2 * HD), lambda p: (0, p))
    return pl.pallas_call(
        functools.partial(backward_kernel, reach),
        grid=(pairs,),
        in_specs=attention_specs(rows, window, pairs)
        + [short, short, pl.BlockSpec((1, 8, rows), lambda p: (p, 0, 0))],
        out_specs=[short, tall, tall, pl.BlockSpec((1, 2, 8, rows), lambda p: (p, 0, 0, 0))],
        out_shape=[
            jax.ShapeDtypeStruct((rows, width), BF16),
            jax.ShapeDtypeStruct((window, width), BF16),
            jax.ShapeDtypeStruct((window, width), BF16),
            jax.ShapeDtypeStruct((pairs, 2, 8, rows), F32),
        ],
        compiler_params=pltpu.CompilerParams(vmem_limit_bytes=VMEM_LIMIT),
        name="attend_back",
    )(*operands)


def local(
    tokens,
    cotangent,
    segment_ids,
    targets,
    attention_weights,
    feedforward_weights,
    projection,
    norm_gains,
    bias_table,
    attention_first,
    attention_second,
    feedforward_first,
    feedforward_second,
    projection_first,
    projection_second,
    gains_first,
    gains_second,
    bias_first,
    bias_second,
):
    wide_count = lax.axis_size("dp")
    narrow_count = lax.axis_size("mp")
    wide_rank = lax.axis_index("dp")
    narrow_rank = lax.axis_index("mp")
    micro_count, _, rows, _ = tokens.shape
    segment_count = targets.shape[2]
    block = D // wide_count
    heads_part = attention_weights.shape[2] // HD
    reach = min(narrow_count - 1, -(-(SEG_MOST - 1) // rows))
    span = 2 * reach + 1

    feature = jnp.arange(D, dtype=jnp.int32)
    place = feature // block
    order = outer_masks() + core_masks()
    away = sum(((place >> bit) & 1) * mask for bit, mask in enumerate(order)) + jnp.zeros_like(place)
    source = (wide_rank ^ away) * block + feature % block
    turn = (feature[:, None] == source[None, :]).astype(BF16)
    turn_wide = turn.astype(F32)

    attention_low = attention_weights.astype(BF16)
    feedforward_low = feedforward_weights.astype(BF16)
    projection_low = projection.astype(BF16)

    token_rows = dot(tokens.reshape(micro_count * rows, D), turn)
    gains = dot(norm_gains, turn_wide, precision=HIGHEST)
    factor_one = norm_factor(token_rows)
    normed_one = (token_rows * factor_one * gains[0]).astype(BF16)
    normed_one = normed_one.reshape(micro_count, rows, D)

    attn_cols = gather_columns(attention_low)
    attn_qo = gather_rows(jnp.stack([attn_cols[0], attn_cols[3]]), True)
    attn_kv = gather_rows(attn_cols[1:3], False)
    w_query, w_out = attn_qo[0], attn_qo[1]
    w_key, w_value = attn_kv[0], attn_kv[1]

    windows = []
    for micro in range(micro_count):
        left, right = [], []
        from_left = from_right = normed_one[micro]
        for _ in range(reach):
            from_left, from_right = shift(from_left, "mp", 1), shift(from_right, "mp", -1)
            left.insert(0, from_left)
            right.append(from_right)
        windows.append(jnp.concatenate(left + [normed_one[micro]] + right, axis=0))

    ffn_cols = gather_columns(feedforward_low)
    w_up = gather_rows(ffn_cols[0:1], True)[0]
    w_down = gather_rows(ffn_cols[1:2], False)[0]
    proj_all = lax.all_gather(projection_low, ("dp", "mp"), axis=0, tiled=False)
    proj_all = proj_all.reshape(wide_count, narrow_count, block, D // narrow_count)
    proj_all = proj_all.transpose(0, 2, 1, 3).reshape(D, D)

    table = jnp.concatenate(
        [
            lax.dynamic_slice_in_dim(bias_table, (narrow_rank ^ k) * heads_part, heads_part, 1)
            for k in range(narrow_count)
        ],
        axis=1,
    )
    tiles = bias_tiles(table, rows)
    far_bias = jnp.stack([table[15], table[31]])
    lanes = jnp.arange(2 * HD, dtype=jnp.int32) % HD
    padded = jnp.pad(
        segment_ids[:, 0], ((0, 0), (reach * rows, reach * rows)), constant_values=segment_count
    )
    window_segments = lax.dynamic_slice_in_dim(padded, narrow_rank * rows, span * rows, 1)
    own_segments = window_segments[:, reach * rows : (reach + 1) * rows]
    key_marks = (window_segments[:, :, None] == lanes).astype(BF16)
    query_marks = jnp.where(
        (own_segments[:, :, None] != lanes) & (lanes <= segment_count), MASKED, 0.0
    ).astype(BF16)
    first, last = own_segments[:, 0], own_segments[:, -1]
    low_count = sum(
        (window_segments[:, (reach - n) * rows + rows - 1] == first).astype(jnp.int32)
        for n in range(1, reach + 1)
    )
    high_count = sum(
        (window_segments[:, (reach + n) * rows] == last).astype(jnp.int32)
        for n in range(1, reach + 1)
    )
    ranges = jnp.stack([low_count, high_count], axis=1)

    mixed, kept = [], []
    for micro in range(micro_count):
        queries = dot(normed_one[micro], w_query).astype(BF16)
        keys = dot(windows[micro], w_key).astype(BF16)
        values = dot(windows[micro], w_value).astype(BF16)
        operands = (
            ranges[micro], far_bias, queries, keys, values, query_marks[micro], key_marks[micro], tiles
        )
        mixed_part, logs = attend(reach, *operands)
        mixed.append(mixed_part)
        kept.append((operands, mixed_part, logs))
    mixed = jnp.concatenate(mixed, axis=0)
    hidden_one = token_rows + dot(mixed, w_out, NT)

    factor_two = norm_factor(hidden_one)
    normed_two = (hidden_one * factor_two * gains[1]).astype(BF16)
    pre_act = dot(normed_two, w_up)
    activated, gelu_pull = jax.vjp(jax.nn.gelu, pre_act)
    activated = activated.astype(BF16)
    hidden_two = hidden_one + dot(activated, w_down, NT)
    output = dot(hidden_two.astype(BF16), turn, NT).astype(BF16)

    factor_three = norm_factor(hidden_two)
    unit_three = hidden_two * factor_three
    normed_three = (unit_three * gains[2]).reshape(micro_count, rows, D)
    numbers = jnp.arange(segment_count, dtype=jnp.int32)
    member = (own_segments[:, None, :] == numbers[None, :, None]).astype(F32)
    counts = jnp.sum(
        (segment_ids[:, 0][:, None, :] == numbers[None, :, None]).astype(F32), axis=2, keepdims=True
    )
    pooled = lax.dot_general(
        member, normed_three, (((2,), (1,)), ((0,), (0,))), precision=HIGHEST, preferred_element_type=F32
    )
    pooled = sum_over(pooled, "mp") / counts
    pooled = dot(pooled.reshape(-1, D).astype(BF16), turn, NT).astype(BF16)
    pooled_all = gather_near(pooled.reshape(1, micro_count, segment_count, D))
    targets_all = gather_near(targets[:, 0].astype(F32)[None])
    every = wide_count * segment_count
    pooled_all = pooled_all.transpose(1, 0, 2, 3).reshape(micro_count, every, D)
    owner = wide_rank ^ jnp.arange(wide_count, dtype=jnp.int32)
    absolute = (owner[:, None] * segment_count + numbers[None, :]).reshape(every)
    picked = targets_all.astype(jnp.int32).transpose(1, 0, 2).reshape(micro_count, every)
    picked = picked + (picked >= absolute[None]).astype(jnp.int32)
    embedded = dot(pooled_all.reshape(-1, D), proj_all).reshape(micro_count, every, D)
    inverse = lax.rsqrt(jnp.sum(embedded * embedded, axis=2, keepdims=True) + EPS_NORM)
    unit = (embedded * inverse).astype(BF16)
    sims = lax.dot_general(
        unit, unit, (((2,), (2,)), ((0,), (0,))), preferred_element_type=F32
    )
    logits = jnp.where(jnp.eye(every, dtype=bool)[None], NEG_FILL, SIM_SCALE * sims)
    logit_grad = (
        jax.nn.softmax(logits, axis=-1) - (picked[:, :, None] == absolute[None, None, :]).astype(F32)
    ).astype(BF16)
    unit_grad = SIM_SCALE * (
        lax.dot_general(logit_grad, unit, (((2,), (1,)), ((0,), (0,))), preferred_element_type=F32)
        + lax.dot_general(logit_grad, unit, (((1,), (1,)), ((0,), (0,))), preferred_element_type=F32)
    )
    unit_grad = unit_grad.astype(BF16).astype(F32)
    along = jnp.sum(unit_grad * embedded, axis=2, keepdims=True)
    embed_grad = (
        inverse * unit_grad - embedded * (inverse * inverse * inverse) * along
    ).astype(BF16)
    proj_reduced = dot(
        lax.dynamic_slice_in_dim(pooled_all.reshape(-1, D), wide_rank * block, block, 1),
        lax.dynamic_slice_in_dim(
            embed_grad.reshape(-1, D), narrow_rank * projection.shape[1], projection.shape[1], 1
        ),
        TN,
    )
    pooled_grad = dot(embed_grad[:, :segment_count].reshape(-1, D), proj_all, NT)
    pooled_grad = dot(pooled_grad, turn_wide, precision=HIGHEST)
    pooled_grad = pooled_grad.reshape(micro_count, segment_count, D) / counts
    normed_three_grad = lax.dot_general(
        member, pooled_grad, (((1,), (1,)), ((0,), (0,))), precision=HIGHEST, preferred_element_type=F32
    ).reshape(micro_count * rows, D)
    gain_three = jnp.sum(normed_three_grad * unit_three, axis=0)

    upstream = dot(cotangent.reshape(micro_count * rows, D), turn)
    hidden_two_grad = upstream + norm_back(hidden_two, factor_three, normed_three_grad * gains[2])
    hidden_two_low = hidden_two_grad.astype(BF16)
    act_grad = dot(hidden_two_low, w_down)
    pre_grad = gelu_pull(act_grad)[0].astype(BF16)
    down_part = dot(hidden_two_low, activated, TN).astype(BF16)
    down_rows = reduce_rows(down_part[None], False)
    up_part = dot(normed_two, pre_grad, TN).astype(BF16)
    up_rows = reduce_rows(up_part[None], True)
    ffn_reduced = reduce_columns(jnp.concatenate([up_rows, down_rows]))
    normed_two_grad = dot(pre_grad, w_up, NT)
    gain_two = jnp.sum(normed_two_grad * hidden_one * factor_two, axis=0)
    hidden_one_grad = hidden_two_grad + norm_back(
        hidden_one, factor_two, normed_two_grad * gains[1]
    )
    hidden_one_low = hidden_one_grad.astype(BF16)
    mixed_grad = dot(hidden_one_low, w_out).astype(BF16).reshape(micro_count, rows, D)
    out_part = dot(hidden_one_low, mixed, TN).astype(BF16)

    query_grads, key_grads, value_grads, bias_parts, normed_one_grads = [], [], [], [], []
    for micro in range(micro_count):
        operands, mixed_part, logs = kept[micro]
        dq, dk, dv, db = attend_back(reach, *operands, mixed_grad[micro], mixed_part, logs)
        query_grads.append(dq)
        key_grads.append(dk)
        value_grads.append(dv)
        bias_parts.append(db)
        partial = (dot(dk, w_key, NT) + dot(dv, w_value, NT)).reshape(span, rows, D)
        own = partial[reach] + dot(dq, w_query, NT)
        to_left = to_right = None
        for n in range(reach, 0, -1):
            leave_left, leave_right = partial[reach - n], partial[reach + n]
            if to_left is not None:
                leave_left = leave_left + to_left
                leave_right = leave_right + to_right
            to_left = shift(leave_left.astype(BF16), "mp", -1).astype(F32)
            to_right = shift(leave_right.astype(BF16), "mp", 1).astype(F32)
        normed_one_grads.append(own + to_left + to_right)
    windows_all = jnp.concatenate(windows, axis=0)
    query_part = dot(normed_one.reshape(-1, D), jnp.concatenate(query_grads), TN).astype(BF16)
    key_part = dot(windows_all, jnp.concatenate(key_grads), TN).astype(BF16)
    value_part = dot(windows_all, jnp.concatenate(value_grads), TN).astype(BF16)
    qo_rows = reduce_rows(jnp.stack([query_part, out_part]), True)
    kv_rows = reduce_rows(jnp.stack([key_part, value_part]), False)
    attn_reduced = reduce_columns(
        jnp.concatenate([qo_rows[0:1], kv_rows, qo_rows[1:2]])
    )
    normed_one_grad = jnp.concatenate(normed_one_grads, axis=0)
    gain_one = jnp.sum(normed_one_grad * token_rows * factor_one, axis=0)
    tokens_grad = hidden_one_grad + norm_back(token_rows, factor_one, normed_one_grad * gains[0])
    tokens_grad = dot(tokens_grad, turn_wide, NT, HIGHEST)

    bias_sum = sum(bias_parts)
    heads = table.shape[1]
    bias_sum = bias_sum.reshape(heads, 8, rows)
    spot = (jnp.arange(rows, dtype=jnp.int32) + 1) % rows
    relative = jnp.where(spot < FAR, -spot, rows - spot)
    buckets = jnp.arange(table.shape[0], dtype=jnp.int32)
    near_hot = (bucket_of(relative)[:, None] == buckets[None, :]) & (
        jnp.abs(relative) < FAR
    )[:, None]
    table_grad = dot(near_hot.astype(F32), bias_sum[:, 0], (((0,), (1,)), ((), ())), HIGHEST)
    table_grad = (
        table_grad
        + (buckets == 15).astype(F32)[:, None] * jnp.sum(bias_sum[:, 1], axis=1)[None, :]
        + (buckets == 31).astype(F32)[:, None] * jnp.sum(bias_sum[:, 2], axis=1)[None, :]
    )
    full_table = jnp.zeros_like(bias_table)
    for k in range(narrow_count):
        full_table = lax.dynamic_update_slice_in_dim(
            full_table,
            table_grad[:, k * heads_part : (k + 1) * heads_part],
            (narrow_rank ^ k) * heads_part,
            1,
        )
    gains_part = dot(jnp.stack([gain_one, gain_two, gain_three]), turn_wide, NT, HIGHEST)
    small = jnp.concatenate(
        [gains_part, jnp.pad(full_table.reshape(1, -1), ((0, 0), (0, D - full_table.size)))]
    )
    small = sum_over(sum_over(small, "dp"), "mp")
    gains_grad = small[:3]
    table_full_grad = small[3, : full_table.size].reshape(full_table.shape)
    local_squares = (
        jnp.sum(attn_reduced * attn_reduced)
        + jnp.sum(ffn_reduced * ffn_reduced)
        + jnp.sum(proj_reduced * proj_reduced)
    )
    total_squares = sum_over(
        sum_over(jnp.broadcast_to(local_squares, (8, 128)), "dp"), "mp"
    )[0, 0]
    total_squares = (
        total_squares
        + jnp.sum(gains_grad * gains_grad)
        + jnp.sum(table_full_grad * table_full_grad)
    )
    grad_norm = jnp.sqrt(total_squares)
    factor = jnp.minimum(1.0, CLIP_NORM / (grad_norm + 1e-06))
    attn_new = adam_update(
        attention_weights, attn_reduced * factor, attention_first, attention_second,
        RATE_MATRIX, DECAY_MATRIX,
    )
    ffn_new = adam_update(
        feedforward_weights, ffn_reduced * factor, feedforward_first, feedforward_second,
        RATE_MATRIX, DECAY_MATRIX,
    )
    proj_new = adam_update(
        projection, proj_reduced * factor, projection_first, projection_second,
        RATE_MATRIX, DECAY_MATRIX,
    )
    gains_new = adam_update(
        norm_gains, gains_grad * factor, gains_first, gains_second, RATE_SMALL, 0.0
    )
    table_new = adam_update(
        bias_table, table_full_grad * factor, bias_first, bias_second, RATE_SMALL, 0.0
    )
    return (
        output.reshape(tokens.shape),
        tokens_grad.reshape(tokens.shape),
        grad_norm,
        *attn_new,
        *ffn_new,
        *proj_new,
        *gains_new,
        *table_new,
    )


def solution(mesh):
    return jax.shard_map(
        local,
        mesh=mesh,
        in_specs=(
            P(None, "dp", "mp", None),
            P(None, "dp", "mp", None),
            P(None, "dp", None),
            P(None, "dp", None),
            P(None, "dp", "mp"),
            P(None, "dp", "mp"),
            P("dp", "mp"),
            P(),
            P(),
            P(None, "dp", "mp"),
            P(None, "dp", "mp"),
            P(None, "dp", "mp"),
            P(None, "dp", "mp"),
            P("dp", "mp"),
            P("dp", "mp"),
            P(),
            P(),
            P(),
            P(),
        ),
        out_specs=(
            P(None, "dp", "mp", None),
            P(None, "dp", "mp", None),
            P(),
            P(None, "dp", "mp"),
            P(None, "dp", "mp"),
            P(None, "dp", "mp"),
            P(None, "dp", "mp"),
            P(None, "dp", "mp"),
            P(None, "dp", "mp"),
            P("dp", "mp"),
            P("dp", "mp"),
            P("dp", "mp"),
            P(),
            P(),
            P(),
            P(),
            P(),
            P(),
        ),
        check_vma=False,
    )
```

time: 1680 us -> 492 us (0.29)
  waiting for transfers between devices: 513 us -> 152 us
  other arithmetic: 366 us -> 45.4 us
  matrix products: 343 us -> 82.7 us
  local copies, waits for them, and re-layouts: 273 us -> 26.2 us
  blocking collectives: 136 us -> 0 us
  starting transfers between devices: 0.94 us -> 102 us
  Pallas kernels: 0 us -> 53.5 us
  loops' own time: 18.3 us -> 0 us
    dot_general x70 -> x42, matrix products: 337 us -> 82.7 us  [the longest x37 78.7 us: dot(): lax.dot_general(left, right, dims, precision=precision, preferred_element...]
    reduce_scatter x12 -> x0, waiting for transfers between devices: 244 us -> none  [the longest x6 122 us: rows_sum(): lax.psum_scatter(running.astype(jnp.bfloat16), 'mp', scatter_dimension=0,...]
    all_gather x10 -> x1, waiting for transfers between devices: 226 us -> 0.01 us  [local(): proj_all = lax.all_gather(projection_low, ('dp', 'mp'), axis=0, tiled=False)]
    another operation x149 -> x4, local copies, waits for them, and re-layouts: 185 us -> 0.01 us  [the longest x3 0.01 us: local(): jnp.stack([gain_one, gain_two, gain_three])]
    reduce_sum x21 -> x3, other arithmetic: 178 us -> 0.74 us  [the longest x1 0.47 us: local(): gain_three = jnp.sum(normed_three_grad * unit_three, axis=0)]
    ppermute x0 -> x70, waiting for transfers between devices: none -> 152 us  [the longest x54 114 us: swap(): return lax.ppermute(values, axis, [(i, i ^ mask) for i in range(count)])]
    eq x16 -> x1, other arithmetic: 128 us -> 0.01 us  [local(): jnp.eye(every, dtype=bool)[None]]
    psum x6 -> x0, blocking collectives: 108 us -> none  [the longest x5 67.9 us: feature_total(): return lax.psum(values, 'mp')]
  transfers between devices with their start and end apart: 23 -> 71, of which waited for: 17 -> 30; matrix products, arithmetic and copies ran while one was open for 54% -> 21% of each run, Pallas kernels for 0% -> 8%
where the time goes in v1:
time: 492 us; the launch traced here: 484 us
  waiting for transfers between devices  152 us (31%)
  starting transfers between devices  102 us (21%)
  matrix products  82.7 us (17%)
  Pallas kernels  53.5 us (11%)
  other arithmetic  45.4 us (9%)
  local copies, waits for them, and re-layouts  26.2 us (5%)
  between operations  22 us (4%)
    ppermute x54, waiting for transfers between devices, swap(): return lax.ppermute(values, axis, [(i, i ^ mask) for i in range(count)])  114 us
    dot_general x37, matrix products, dot(): lax.dot_general(left, right, dims, precision=precision, preferred_element...  78.7 us
    ppermute x16, starting transfers between devices, shift(): return lax.ppermute(values, axis, pairs)  51.9 us
    ppermute x54, starting transfers between devices, swap(): return lax.ppermute(values, axis, [(i, i ^ mask) for i in range(count)])  50 us
    ppermute x16, waiting for transfers between devices, shift(): return lax.ppermute(values, axis, pairs)  37.7 us
    pallas_call x2, Pallas kernels, attend_back(): pl.pallas_call(functools.partial(backward_kernel, reach), grid=(pairs,),...  26.4 us
    pallas_call x2, Pallas kernels, attend(): pl.pallas_call(functools.partial(forward_kernel, reach), grid=(pairs,), i...  19.8 us
  transfers between devices with their start and end apart: 71, of which 30 were waited for; matrix products, arithmetic and copies ran while one was open for 21% of the time, Pallas kernels for 8%

profile of v1, /device:TPU:0, one launch (start us, length us, event | category | flops | bytes accessed | tf_op | source)
XLA Modules:
  0.0 483.6 jit_solution(14167191147778846659)
XLA Ops:
  8.3 5.1 %collective-permute-start.2 = (bf16[4,96,192]{2,1,0:T(8,128)(2,1)S(1)}, bf16[4,96,192]{2,1,0:T(8,128)(2,1)S(1)}, u32[]{:S(2)}, u32[]{:S(2)}) collective-permute-start(bf16[4,96,192]{2,1,0:T(8,128)(2,1)S(1)} %convert_element_type.429), channel_id=1, source_target_pairs={{0,3},{1,2},{2,1},{3,0},{4,7},{5,6},{6,5},{7,4},{8,11},{9,10},{10,... | collective-permute-start | bytes 442376 | tf_op jit(solution)/shard_map/ppermute | solution.py:71
  15.2 3.8 collective-permute-start.19
  28.4 7.4 %shard_map.322.bias_ref = f32[12,3,256,256]{3,2,1,0:T(8,128)} custom-call(f32[12,3,512]{2,1,0:T(4,128)S(1)} %copy.134.line_ref), custom_call_target="tpu_custom_call" | custom-call | tf_op jit(solution)/shard_map/pallas_call | solution.py:171
  35.9 8.6 %collective-permute-done.1 = bf16[4,96,192]{2,1,0:T(8,128)(2,1)S(1)} collective-permute-done((bf16[4,96,192]{2,1,0:T(8,128)(2,1)S(1)}, bf16[4,96,192]{2,1,0:T(8,128)(2,1)S(1)}, u32[]{:S(2)}, u32[]{:S(2)}) %collective-permute-start.1) | collective-permute-done | bytes 147488 | tf_op jit(solution)/shard_map/ppermute | solution.py:71
  44.4 2.0 collective-permute-start.6
  48.1 10.1 %collective-permute-done.18 = bf16[2,96,768]{2,1,0:T(8,128)(2,1)S(1)} collective-permute-done((bf16[2,96,768]{2,1,0:T(8,128)(2,1)S(1)}, bf16[2,96,768]{2,1,0:T(8,128)(2,1)S(1)}, u32[]{:S(2)}, u32[]{:S(2)}) %collective-permute-start.18) | collective-permute-done | bytes 294944 | tf_op jit(solution)/shard_map/ppermute | solution.py:71
  61.3 7.3 %collective-permute-start.7 = (bf16[256,768]{1,0:T(8,128)(2,1)S(1)}, bf16[256,768]{1,0:T(8,128)(2,1)S(1)}, u32[]{:S(2)}, u32[]{:S(2)}) collective-permute-start(bf16[256,768]{1,0:T(8,128)(2,1)S(1)} %collective-permute-done.6), channel_id=1, source_target_pairs={{0,1},{1,2},{2,3},{4,5},{5,6},{6,7},{8,9},{9,10},{10,11},{12,13},{... | collective-permute-start | bytes 1179656 | tf_op jit(solution)/shard_map/ppermute | solution.py:77
  73.5 6.3 %collective-permute-done.7 = bf16[256,768]{1,0:T(8,128)(2,1)S(1)} collective-permute-done((bf16[256,768]{1,0:T(8,128)(2,1)S(1)}, bf16[256,768]{1,0:T(8,128)(2,1)S(1)}, u32[]{:S(2)}, u32[]{:S(2)}) %collective-permute-start.7) | collective-permute-done | bytes 393248 | tf_op jit(solution)/shard_map/ppermute | solution.py:77
  79.8 1.8 collective-permute-start.4
  81.8 4.8 %collective-permute-done.9 = bf16[256,768]{1,0:T(8,128)(2,1)S(1)} collective-permute-done((bf16[256,768]{1,0:T(8,128)(2,1)S(1)}, bf16[256,768]{1,0:T(8,128)(2,1)S(1)}, u32[]{:S(2)}, u32[]{:S(2)}) %collective-permute-start.9) | collective-permute-done | bytes 393248 | tf_op jit(solution)/shard_map/ppermute | solution.py:77
  86.6 3.5 collective-permute-start.13
  92.5 4.1 collective-permute-done.13
  96.5 4.4 collective-permute-start.14
  101.0 2.7 collective-permute-done.11
  108.5 10.6 %collective-permute-done.16 = bf16[256,768]{1,0:T(8,128)(2,1)S(1)} collective-permute-done((bf16[256,768]{1,0:T(8,128)(2,1)S(1)}, bf16[256,768]{1,0:T(8,128)(2,1)S(1)}, u32[]{:S(2)}, u32[]{:S(2)}) %collective-permute-start.16) | collective-permute-done | bytes 393248 | tf_op jit(solution)/shard_map/ppermute | solution.py:77
  119.1 9.2 %collective-permute-done.24 = bf16[1,2,96,3072]{3,2,1,0:T(8,128)(2,1)S(1)} collective-permute-done((bf16[1,2,96,3072]{3,2,1,0:T(8,128)(2,1)S(1)}, bf16[1,2,96,3072]{3,2,1,0:T(8,128)(2,1)S(1)}, u32[]{:S(2)}, u32[]{:S(2)}) %collective-permute-start.24) | collective-permute-done | bytes 1179680 | tf_op jit(solution)/shard_map/ppermute | solution.py:71
  140.1 9.5 %attend.2 = (bf16[256,768]{1,0:T(8,128)(2,1)S(1)}, f32[6,8,256]{2,1,0:T(8,128)S(1)}) custom-call(s32[2]{0:T(128)S(1)} %get-tuple-element.220.range_ref, f32[2,12]{1,0:T(2,128)S(1)} %pad_maximum_fusion.28.far_ref, bf16[256,768]{1,0:T(8,128)(2,1)S(1)} %convolution_convert_fusion.10.q_ref, bf16[1280,768]{1,0:T(8,128)(2,1)S(1)} %convolution_convert_fusion.5.k_ref, ...), custom_call_target="tpu_custom_call" | custom-call | tf_op jit(solution)/shard_map/attend/pallas_call | solution.py:329
  151.3 10.3 %attend.3 = (bf16[256,768]{1,0:T(8,128)(2,1)S(1)}, f32[6,8,256]{2,1,0:T(8,128)S(1)}) custom-call(s32[2]{0:T(128)S(1)} %get-tuple-element.219.range_ref, f32[2,12]{1,0:T(2,128)S(1)} %pad_maximum_fusion.28.far_ref, bf16[256,768]{1,0:T(8,128)(2,1)S(1)} %convolution_convert_fusion.9.q_ref, bf16[1280,768]{1,0:T(8,128)(2,1)S(1)} %convolution_convert_fusion.3.k_ref, ...), custom_call_target="tpu_custom_call" | custom-call | tf_op jit(solution)/shard_map/attend/pallas_call | solution.py:329
  164.4 2.8 pad_maximum_fusion
  167.2 2.7 fusion.202
  169.9 5.1 %pad_maximum_fusion.1 = bf16[1,8,96,3072]{3,2,1,0:T(8,128)(2,1)S(1)} fusion(bf16[1,4,96,3072]{3,2,1,0:T(8,128)(2,1)} %collective-permute-done.25, bf16[1,4,96,3072]{3,2,1,0:T(8,128)(2,1)} %bitcast.33), kind=kLoop, calls=%fused_computation.15 | loop fusion | flops 2359296 | bytes 9437184 | tf_op jit(solution)/shard_map/concatenate | solution.py:104
  175.0 4.0 multiply_reduce_fusion.3
  180.2 1.9 collective-permute-start.26
  186.0 3.3 collective-permute-done.27
  196.5 2.6 copy.174
  199.2 2.3 reshape.557
  201.4 2.4 reshape.576
  216.4 6.1 %fusion.8 = bf16[512,3072]{1,0:T(8,128)(2,1)S(1)} fusion(f32[512,3072]{1,0:T(8,128)S(1)} %bitcast.275, bf16[768,3072]{1,0:T(8,128)(2,1)S(1)} %bitcast.278, f32[512,768]{1,0:T(8,128)S(1)} %bitcast_add_fusion), kind=kOutput, calls=%fused_computation.10 | convolution fusion | flops 2447769600 | bytes 15728640 | tf_op jit(solution)/shard_map/dot_general | solution.py:38
  222.6 2.9 multiply_reduce_fusion
  228.4 1.8 convolution_convert_fusion.6
  230.2 4.6 convolution_convert_fusion
  234.8 4.6 convolution_convert_fusion.1
  239.4 14.7 %attend_back.3 = (bf16[256,768]{1,0:T(8,128)(2,1)S(1)}, bf16[1280,768]{1,0:T(8,128)(2,1)S(1)}, bf16[1280,768]{1,0:T(8,128)(2,1)S(1)}, f32[6,2,8,256]{3,2,1,0:T(8,128)S(1)}) custom-call(s32[2]{0:T(128)S(1)} %get-tuple-element.219.range_ref, f32[2,12]{1,0:T(2,128)S(1)} %pad_maximum_fusion.28.far_ref, bf16[256,768]{1,0:T(8,128)(2,1)S(1)} %convolution_convert_fusion.9.q_ref, ...), custom_call_target="tpu_custom_call" | custom-call | tf_op jit(solution)/shard_map/attend_back/pallas_call | solution.py:352
  255.9 3.6 fusion.222
  261.8 5.3 %collective-permute-start.40 = (bf16[256,768]{1,0:T(8,128)(2,1)}, bf16[256,768]{1,0:T(8,128)(2,1)}, u32[]{:S(2)}, u32[]{:S(2)}) collective-permute-start(bf16[256,768]{1,0:T(8,128)(2,1)} %get-tuple-element.155), channel_id=1, source_target_pairs={{0,1},{1,2},{2,3},{4,5},{5,6},{6,7},{8,9},{9,10},{10,11},{12,13},{... | collective-permute-start | bytes 1179656 | tf_op jit(solution)/shard_map/ppermute | solution.py:77
  267.1 11.7 %attend_back.2 = (bf16[256,768]{1,0:T(8,128)(2,1)S(1)}, bf16[1280,768]{1,0:T(8,128)(2,1)S(1)}, bf16[1280,768]{1,0:T(8,128)(2,1)S(1)}, f32[6,2,8,256]{3,2,1,0:T(8,128)S(1)}) custom-call(s32[2]{0:T(128)S(1)} %get-tuple-element.220.range_ref, f32[2,12]{1,0:T(2,128)S(1)} %pad_maximum_fusion.28.far_ref, bf16[256,768]{1,0:T(8,128)(2,1)S(1)} %convolution_convert_fusion.10.q_ref, ...), custom_call_target="tpu_custom_call" | custom-call | tf_op jit(solution)/shard_map/attend_back/pallas_call | solution.py:352
  278.8 3.1 fusion.224
  282.0 4.4 fusion.40
  286.4 4.3 fusion.43
  290.7 3.7 fusion.223
  296.6 10.3 %collective-permute-start.36 = (bf16[256,768]{1,0:T(8,128)(2,1)}, bf16[256,768]{1,0:T(8,128)(2,1)}, u32[]{:S(2)}, u32[]{:S(2)}) collective-permute-start(bf16[256,768]{1,0:T(8,128)(2,1)} %get-tuple-element.153), channel_id=1, source_target_pairs={{0,1},{1,2},{2,3},{4,5},{5,6},{6,7},{8,9},{9,10},{10,11},{12,13},{... | collective-permute-start | bytes 1179656 | tf_op jit(solution)/shard_map/ppermute | solution.py:77
  315.4 1.8 fusion.78
  317.2 3.5 collective-permute-start.41
  323.3 4.6 collective-permute-start.37
  330.1 4.5 collective-permute-done.39
  336.3 1.9 collective-permute-done.37
  338.2 4.1 collective-permute-done.35
  347.1 2.1 collective-permute-start.66
  349.7 2.4 multiply_reduce_fusion.9
  352.1 11.0 %collective-permute-done.66 = f32[4,768]{1,0:T(4,128)S(1)} collective-permute-done((f32[4,768]{1,0:T(4,128)S(1)}, f32[4,768]{1,0:T(4,128)S(1)}, u32[]{:S(2)}, u32[]{:S(2)}) %collective-permute-start.66) | collective-permute-done | bytes 12320 | tf_op jit(solution)/shard_map/ppermute | solution.py:71
  365.4 6.6 %collective-permute-done.44 = bf16[2,1,96,768]{3,2,0,1:T(8,128)(2,1)S(1)} collective-permute-done((bf16[2,1,96,768]{3,2,0,1:T(8,128)(2,1)S(1)}, bf16[2,1,96,768]{3,2,0,1:T(8,128)(2,1)S(1)}, u32[]{:S(2)}, u32[]{:S(2)}) %collective-permute-start.44) | collective-permute-done | bytes 294944 | tf_op jit(solution)/shard_map/ppermute | solution.py:71
  378.8 2.7 collective-permute-start.48
  381.5 18.8 %collective-permute-done.55 = bf16[1,2,96,3072]{3,2,1,0:T(8,128)(2,1)S(1)} collective-permute-done((bf16[1,2,96,3072]{3,2,1,0:T(8,128)(2,1)S(1)}, bf16[1,2,96,3072]{3,2,1,0:T(8,128)(2,1)S(1)}, u32[]{:S(2)}, u32[]{:S(2)}) %collective-permute-start.55) | collective-permute-done | bytes 1179680 | tf_op jit(solution)/shard_map/ppermute | solution.py:71
  401.6 2.6 collective-permute-done.52
  404.6 10.4 %collective-permute-done.56 = bf16[1,1,96,3072]{3,2,1,0:T(8,128)(2,1)S(1)} collective-permute-done((bf16[1,1,96,3072]{3,2,1,0:T(8,128)(2,1)S(1)}, bf16[1,1,96,3072]{3,2,1,0:T(8,128)(2,1)S(1)}, u32[]{:S(2)}, u32[]{:S(2)}) %collective-permute-start.56) | collective-permute-done | bytes 589856 | tf_op jit(solution)/shard_map/ppermute | solution.py:71
  417.4 2.7 collective-permute-start.57
  422.4 5.1 %collective-permute-done.59 = bf16[2,96,768]{2,1,0:T(8,128)(2,1)S(1)} collective-permute-done((bf16[2,96,768]{2,1,0:T(8,128)(2,1)S(1)}, bf16[2,96,768]{2,1,0:T(8,128)(2,1)S(1)}, u32[]{:S(2)}, u32[]{:S(2)}) %collective-permute-start.59) | collective-permute-done | bytes 294944 | tf_op jit(solution)/shard_map/ppermute | solution.py:71
  427.5 13.8 %collective-permute-done.58 = bf16[2,96,768]{2,1,0:T(8,128)(2,1)S(1)} collective-permute-done((bf16[2,96,768]{2,1,0:T(8,128)(2,1)S(1)}, bf16[2,96,768]{2,1,0:T(8,128)(2,1)S(1)}, u32[]{:S(2)}, u32[]{:S(2)}) %collective-permute-start.58) | collective-permute-done | bytes 294944 | tf_op jit(solution)/shard_map/ppermute | solution.py:71
  445.1 3.1 fusion.47
  448.9 3.1 collective-permute-done.68
  452.4 5.2 %fusion.21 = f32[512,768]{1,0:T(8,128)} fusion(f32[512,768]{1,0:T(8,128)} %copy-done.18, f32[768,512]{0,1:T(8,128)S(1)} %copy-done.15, s32[768]{0:T(1024)S(1)} %fusion.177, f32[256,768]{1,0:T(8,128)S(1)} %copy-done.31, f32[256,768]{1,0:T(8,128)S(1)} %copy-done.33, f32[512]{0:T(512)S(1)} %broadcast_multiply_fusion, f32[512]{0:T(512)S(1)} %copy-done.80, ...), kind=kOutput, calls=%fused_computation.55 | convolution fusion | flops 3627220992 | bytes 6303744 | tf_op jit(solution)/shard_map/dot_general | solution.py:38
  457.7 1.9 collective-permute-start.63
  461.3 2.8 collective-permute-start.64
  470.0 2.4 multiply_subtract_fusion.1
  (502 shorter events, 125.0 us)
Async XLA Ops:
  7.2 189.3 %all-gather.3.cloned.1.call-start = ((), (), s32[]{:S(2)}) async-start(), calls=%async_computation | async-start | bytes 1622016 | tf_op jit(solution)/shard_map/all_gather | solution.py:438
  8.3 18.9 %collective-permute-start.2 = (bf16[4,96,192]{2,1,0:T(8,128)(2,1)S(1)}, bf16[4,96,192]{2,1,0:T(8,128)(2,1)S(1)}, u32[]{:S(2)}, u32[]{:S(2)}) collective-permute-start(bf16[4,96,192]{2,1,0:T(8,128)(2,1)S(1)} %convert_element_type.429), channel_id=1, source_target_pairs={{0,3},{1,2},{2,1},{3,0},{4,7},{5,6},{6,5},{7,4},{8,11},{9,10},{10,... | collective-permute-start | bytes 442376 | tf_op jit(solution)/shard_map/ppermute | solution.py:71
  13.5 31.0 %collective-permute-start.1 = (bf16[4,96,192]{2,1,0:T(8,128)(2,1)S(1)}, bf16[4,96,192]{2,1,0:T(8,128)(2,1)S(1)}, u32[]{:S(2)}, u32[]{:S(2)}) collective-permute-start(bf16[4,96,192]{2,1,0:T(8,128)(2,1)S(1)} %convert_element_type.429), channel_id=1, source_target_pairs={{0,2},{1,3},{2,0},{3,1},{4,6},{5,7},{6,4},{7,5},{8,10},{9,11},{10,... | collective-permute-start | bytes 442376 | tf_op jit(solution)/shard_map/ppermute | solution.py:71
  13.5 33.0 %collective-permute-start = (bf16[4,96,192]{2,1,0:T(8,128)(2,1)S(1)}, bf16[4,96,192]{2,1,0:T(8,128)(2,1)S(1)}, u32[]{:S(2)}, u32[]{:S(2)}) collective-permute-start(bf16[4,96,192]{2,1,0:T(8,128)(2,1)S(1)} %convert_element_type.429), channel_id=1, source_target_pairs={{0,1},{1,0},{2,3},{3,2},{4,5},{5,4},{6,7},{7,6},{8,9},{9,8},{10,11... | collective-permute-start | bytes 442376 | tf_op jit(solution)/shard_map/ppermute | solution.py:71
  15.2 32.8 %collective-permute-start.19 = (bf16[2,96,768]{2,1,0:T(8,128)(2,1)S(1)}, bf16[2,96,768]{2,1,0:T(8,128)(2,1)S(1)}, u32[]{:S(2)}, u32[]{:S(2)}) collective-permute-start(bf16[2,96,768]{2,1,0:T(8,128)(2,1)S(1)} %convert_element_type.446), channel_id=1, source_target_pairs={{0,3},{1,2},{2,1},{3,0},{4,7},{5,6},{6,5},{7,4},{8,11},{9,10},{10,... | collective-permute-start | bytes 884744 | tf_op jit(solution)/shard_map/ppermute | solution.py:71
  19.0 39.2 %collective-permute-start.18 = (bf16[2,96,768]{2,1,0:T(8,128)(2,1)S(1)}, bf16[2,96,768]{2,1,0:T(8,128)(2,1)S(1)}, u32[]{:S(2)}, u32[]{:S(2)}) collective-permute-start(bf16[2,96,768]{2,1,0:T(8,128)(2,1)S(1)} %convert_element_type.446), channel_id=1, source_target_pairs={{0,2},{1,3},{2,0},{3,1},{4,6},{5,7},{6,4},{7,5},{8,10},{9,11},{10,... | collective-permute-start | bytes 884744 | tf_op jit(solution)/shard_map/ppermute | solution.py:71
  27.2 32.5 %collective-permute-start.17 = (bf16[2,96,768]{2,1,0:T(8,128)(2,1)S(1)}, bf16[2,96,768]{2,1,0:T(8,128)(2,1)S(1)}, u32[]{:S(2)}, u32[]{:S(2)}) collective-permute-start(bf16[2,96,768]{2,1,0:T(8,128)(2,1)S(1)} %convert_element_type.446), channel_id=1, source_target_pairs={{0,1},{1,0},{2,3},{3,2},{4,5},{5,4},{6,7},{7,6},{8,9},{9,8},{10,11... | collective-permute-start | bytes 884744 | tf_op jit(solution)/shard_map/ppermute | solution.py:71
  44.4 16.9 %collective-permute-start.6 = (bf16[256,768]{1,0:T(8,128)(2,1)S(1)}, bf16[256,768]{1,0:T(8,128)(2,1)S(1)}, u32[]{:S(2)}, u32[]{:S(2)}) collective-permute-start(bf16[256,768]{1,0:T(8,128)(2,1)S(1)} %slice.400), channel_id=1, source_target_pairs={{0,1},{1,2},{2,3},{4,5},{5,6},{6,7},{8,9},{9,10},{10,11},{12,13},{... | collective-permute-start | bytes 1179656 | tf_op jit(solution)/shard_map/ppermute | solution.py:77
  46.5 24.1 %collective-permute-start.8 = (bf16[256,768]{1,0:T(8,128)(2,1)S(1)}, bf16[256,768]{1,0:T(8,128)(2,1)S(1)}, u32[]{:S(2)}, u32[]{:S(2)}) collective-permute-start(bf16[256,768]{1,0:T(8,128)(2,1)S(1)} %slice.400), channel_id=1, source_target_pairs={{1,0},{2,1},{3,2},{5,4},{6,5},{7,6},{9,8},{10,9},{11,10},{13,12},{... | collective-permute-start | bytes 1179656 | tf_op jit(solution)/shard_map/ppermute | solution.py:77
  48.0 137.9 %collective-permute-start.31 = (f32[1,2,8]{2,1,0:T(2,128)S(1)}, f32[1,2,8]{2,1,0:T(2,128)S(1)}, u32[]{:S(2)}, u32[]{:S(2)}) collective-permute-start(f32[1,2,8]{2,1,0:T(2,128)S(1)} %bitcast.319), channel_id=1, source_target_pairs={{0,4},{4,0},{8,12},{12,8},{16,20},{20,16},{24,28},{28,24},{1,5},{5... | collective-permute-start | bytes 200 | tf_op jit(solution)/shard_map/ppermute | solution.py:71
  58.2 13.9 %collective-permute-start.3 = (bf16[2,1,96,768]{3,2,0,1:T(8,128)(2,1)S(1)}, bf16[2,1,96,768]{3,2,0,1:T(8,128)(2,1)S(1)}, u32[]{:S(2)}, u32[]{:S(2)}) collective-permute-start(bf16[2,1,96,768]{3,2,0,1:T(8,128)(2,1)S(1)} %get-tuple-element.173), channel_id=1, source_target_pairs={{0,8},{4,12},{8,0},{12,4},{16,24},{20,28},{24,16},{28,20},{1,9},{5... | collective-permute-start | bytes 884744 | tf_op jit(solution)/shard_map/ppermute | solution.py:71
  59.7 9.2 %collective-permute-start.10 = (bf16[2,1,96,768]{3,2,0,1:T(8,128)(2,1)S(1)}, bf16[2,1,96,768]{3,2,0,1:T(8,128)(2,1)S(1)}, u32[]{:S(2)}, u32[]{:S(2)}) collective-permute-start(bf16[2,1,96,768]{3,2,0,1:T(8,128)(2,1)S(1)} %get-tuple-element.174), channel_id=1, source_target_pairs={{0,16},{4,20},{8,24},{12,28},{16,0},{20,4},{24,8},{28,12},{1,17},{... | collective-permute-start | bytes 884744 | tf_op jit(solution)/shard_map/ppermute | solution.py:71
  61.3 18.4 %collective-permute-start.7 = (bf16[256,768]{1,0:T(8,128)(2,1)S(1)}, bf16[256,768]{1,0:T(8,128)(2,1)S(1)}, u32[]{:S(2)}, u32[]{:S(2)}) collective-permute-start(bf16[256,768]{1,0:T(8,128)(2,1)S(1)} %collective-permute-done.6), channel_id=1, source_target_pairs={{0,1},{1,2},{2,3},{4,5},{5,6},{6,7},{8,9},{9,10},{10,11},{12,13},{... | collective-permute-start | bytes 1179656 | tf_op jit(solution)/shard_map/ppermute | solution.py:77
  68.9 21.3 %collective-permute-start.23 = (bf16[1,1,96,3072]{3,2,1,0:T(8,128)(2,1)S(1)}, bf16[1,1,96,3072]{3,2,1,0:T(8,128)(2,1)S(1)}, u32[]{:S(2)}, u32[]{:S(2)}) collective-permute-start(bf16[1,1,96,3072]{3,2,1,0:T(8,128)(2,1)S(1)} %get-tuple-element.161), channel_id=1, source_target_pairs={{0,16},{4,20},{8,24},{12,28},{16,0},{20,4},{24,8},{28,12},{1,17},{... | collective-permute-start | bytes 1769480 | tf_op jit(solution)/shard_map/ppermute | solution.py:71
  70.6 20.6 %collective-permute-start.20 = (bf16[1,1,96,3072]{3,2,1,0:T(8,128)(2,1)S(1)}, bf16[1,1,96,3072]{3,2,1,0:T(8,128)(2,1)S(1)}, u32[]{:S(2)}, u32[]{:S(2)}) collective-permute-start(bf16[1,1,96,3072]{3,2,1,0:T(8,128)(2,1)S(1)} %get-tuple-element.160), channel_id=1, source_target_pairs={{0,8},{4,12},{8,0},{12,4},{16,24},{20,28},{24,16},{28,20},{1,9},{5... | collective-permute-start | bytes 1769480 | tf_op jit(solution)/shard_map/ppermute | solution.py:71
  72.1 14.5 %collective-permute-start.9 = (bf16[256,768]{1,0:T(8,128)(2,1)S(1)}, bf16[256,768]{1,0:T(8,128)(2,1)S(1)}, u32[]{:S(2)}, u32[]{:S(2)}) collective-permute-start(bf16[256,768]{1,0:T(8,128)(2,1)S(1)} %collective-permute-done.8), channel_id=1, source_target_pairs={{1,0},{2,1},{3,2},{5,4},{6,5},{7,6},{9,8},{10,9},{11,10},{13,12},{... | collective-permute-start | bytes 1179656 | tf_op jit(solution)/shard_map/ppermute | solution.py:77
  79.8 24.8 %collective-permute-start.4 = (bf16[2,2,96,768]{3,2,0,1:T(8,128)(2,1)S(1)}, bf16[2,2,96,768]{3,2,0,1:T(8,128)(2,1)S(1)}, u32[]{:S(2)}, u32[]{:S(2)}) collective-permute-start(bf16[2,2,96,768]{3,2,0,1:T(8,128)(2,1)S(1)} %pad_maximum_fusion.17), channel_id=1, source_target_pairs={{0,16},{4,20},{8,24},{12,28},{16,0},{20,4},{24,8},{28,12},{1,17},{... | collective-permute-start | bytes 1769480 | tf_op jit(solution)/shard_map/ppermute | solution.py:71
  86.6 9.9 %collective-permute-start.13 = (bf16[256,768]{1,0:T(8,128)(2,1)S(1)}, bf16[256,768]{1,0:T(8,128)(2,1)S(1)}, u32[]{:S(2)}, u32[]{:S(2)}) collective-permute-start(bf16[256,768]{1,0:T(8,128)(2,1)S(1)} %get-tuple-element.169), channel_id=1, source_target_pairs={{0,1},{1,2},{2,3},{4,5},{5,6},{6,7},{8,9},{9,10},{10,11},{12,13},{... | collective-permute-start | bytes 1179656 | tf_op jit(solution)/shard_map/ppermute | solution.py:77
  90.2 13.6 %collective-permute-start.11 = (bf16[2,2,96,768]{3,2,1,0:T(8,128)(2,1)S(1)}, bf16[2,2,96,768]{3,2,1,0:T(8,128)(2,1)S(1)}, u32[]{:S(2)}, u32[]{:S(2)}) collective-permute-start(bf16[2,2,96,768]{3,2,1,0:T(8,128)(2,1)S(1)} %get-tuple-element.183), channel_id=1, source_target_pairs={{0,8},{4,12},{8,0},{12,4},{16,24},{20,28},{24,16},{28,20},{1,9},{5... | collective-permute-start | bytes 1769480 | tf_op jit(solution)/shard_map/ppermute | solution.py:71
  91.2 14.4 %collective-permute-start.15 = (bf16[256,768]{1,0:T(8,128)(2,1)S(1)}, bf16[256,768]{1,0:T(8,128)(2,1)S(1)}, u32[]{:S(2)}, u32[]{:S(2)}) collective-permute-start(bf16[256,768]{1,0:T(8,128)(2,1)S(1)} %get-tuple-element.169), channel_id=1, source_target_pairs={{1,0},{2,1},{3,2},{5,4},{6,5},{7,6},{9,8},{10,9},{11,10},{13,12},{... | collective-permute-start | bytes 1179656 | tf_op jit(solution)/shard_map/ppermute | solution.py:77
  96.5 9.9 %collective-permute-start.14 = (bf16[256,768]{1,0:T(8,128)(2,1)S(1)}, bf16[256,768]{1,0:T(8,128)(2,1)S(1)}, u32[]{:S(2)}, u32[]{:S(2)}) collective-permute-start(bf16[256,768]{1,0:T(8,128)(2,1)S(1)} %collective-permute-done.13), channel_id=1, source_target_pairs={{0,1},{1,2},{2,3},{4,5},{5,6},{6,7},{8,9},{9,10},{10,11},{12,13},{... | collective-permute-start | bytes 1179656 | tf_op jit(solution)/shard_map/ppermute | solution.py:77
  103.8 24.6 %collective-permute-start.24 = (bf16[1,2,96,3072]{3,2,1,0:T(8,128)(2,1)S(1)}, bf16[1,2,96,3072]{3,2,1,0:T(8,128)(2,1)S(1)}, u32[]{:S(2)}, u32[]{:S(2)}) collective-permute-start(bf16[1,2,96,3072]{3,2,1,0:T(8,128)(2,1)S(1)} %get-tuple-element.164), channel_id=1, source_target_pairs={{0,8},{4,12},{8,0},{12,4},{16,24},{20,28},{24,16},{28,20},{1,9},{5... | collective-permute-start | bytes 3538952 | tf_op jit(solution)/shard_map/ppermute | solution.py:71
  104.6 25.4 %collective-permute-start.21 = (bf16[1,2,96,3072]{3,2,1,0:T(8,128)(2,1)S(1)}, bf16[1,2,96,3072]{3,2,1,0:T(8,128)(2,1)S(1)}, u32[]{:S(2)}, u32[]{:S(2)}) collective-permute-start(bf16[1,2,96,3072]{3,2,1,0:T(8,128)(2,1)S(1)} %pad_maximum_fusion.13), channel_id=1, source_target_pairs={{0,16},{4,20},{8,24},{12,28},{16,0},{20,4},{24,8},{28,12},{1,17},{... | collective-permute-start | bytes 3538952 | tf_op jit(solution)/shard_map/ppermute | solution.py:71
  105.6 26.6 %collective-permute-start.5 = (bf16[2,4,96,768]{3,2,0,1:T(8,128)(2,1)S(1)}, bf16[2,4,96,768]{3,2,0,1:T(8,128)(2,1)S(1)}, u32[]{:S(2)}, u32[]{:S(2)}) collective-permute-start(bf16[2,4,96,768]{3,2,0,1:T(8,128)(2,1)S(1)} %pad_maximum_fusion.10), channel_id=1, source_target_pairs={{0,4},{4,0},{8,12},{12,8},{16,20},{20,16},{24,28},{28,24},{1,5},{5... | collective-permute-start | bytes 3538952 | tf_op jit(solution)/shard_map/ppermute | solution.py:71
  106.4 12.7 %collective-permute-start.16 = (bf16[256,768]{1,0:T(8,128)(2,1)S(1)}, bf16[256,768]{1,0:T(8,128)(2,1)S(1)}, u32[]{:S(2)}, u32[]{:S(2)}) collective-permute-start(bf16[256,768]{1,0:T(8,128)(2,1)S(1)} %collective-permute-done.15), channel_id=1, source_target_pairs={{1,0},{2,1},{3,2},{5,4},{6,5},{7,6},{9,8},{10,9},{11,10},{13,12},{... | collective-permute-start | bytes 1179656 | tf_op jit(solution)/shard_map/ppermute | solution.py:77
  119.1 15.1 %collective-permute-start.12 = (bf16[2,4,96,768]{3,2,1,0:T(8,128)(2,1)S(1)}, bf16[2,4,96,768]{3,2,1,0:T(8,128)(2,1)S(1)}, u32[]{:S(2)}, u32[]{:S(2)}) collective-permute-start(bf16[2,4,96,768]{3,2,1,0:T(8,128)(2,1)S(1)} %bitcast.297), channel_id=1, source_target_pairs={{0,4},{4,0},{8,12},{12,8},{16,20},{20,16},{24,28},{28,24},{1,5},{5... | collective-permute-start | bytes 3538952 | tf_op jit(solution)/shard_map/ppermute | solution.py:71
  130.0 39.9 %collective-permute-start.25 = (bf16[1,4,96,3072]{3,2,1,0:T(8,128)(2,1)}, bf16[1,4,96,3072]{3,2,1,0:T(8,128)(2,1)}, u32[]{:S(2)}, u32[]{:S(2)}) collective-permute-start(bf16[1,4,96,3072]{3,2,1,0:T(8,128)(2,1)} %bitcast.33), channel_id=1, source_target_pairs={{0,4},{4,0},{8,12},{12,8},{16,20},{20,16},{24,28},{28,24},{1,5},{5... | collective-permute-start | bytes 7077896 | tf_op jit(solution)/shard_map/ppermute | solution.py:71
  131.7 32.6 %collective-permute-start.22 = (bf16[1,4,96,3072]{3,2,1,0:T(8,128)(2,1)}, bf16[1,4,96,3072]{3,2,1,0:T(8,128)(2,1)}, u32[]{:S(2)}, u32[]{:S(2)}) collective-permute-start(bf16[1,4,96,3072]{3,2,1,0:T(8,128)(2,1)} %pad_maximum_fusion.4), channel_id=1, source_target_pairs={{0,4},{4,0},{8,12},{12,8},{16,20},{20,16},{24,28},{28,24},{1,5},{5... | collective-permute-start | bytes 7077896 | tf_op jit(solution)/shard_map/ppermute | solution.py:71
  180.2 4.1 collective-permute-start.26
  184.3 5.0 %collective-permute-start.27 = (f32[2,8,768]{2,1,0:T(8,128)S(1)}, f32[2,8,768]{2,1,0:T(8,128)S(1)}, u32[]{:S(2)}, u32[]{:S(2)}) collective-permute-start(f32[2,8,768]{2,1,0:T(8,128)S(1)} %add.594), channel_id=1, source_target_pairs={{0,2},{1,3},{2,0},{3,1},{4,6},{5,7},{6,4},{7,5},{8,10},{9,11},{10,... | collective-permute-start | bytes 147464 | tf_op jit(solution)/shard_map/ppermute | solution.py:71
  186.0 3.9 collective-permute-start.32
  191.2 4.2 collective-permute-start.29
  195.4 8.5 %collective-permute-start.30 = (bf16[4,2,8,768]{3,2,0,1:T(8,128)(2,1)S(1)}, bf16[4,2,8,768]{3,2,0,1:T(8,128)(2,1)S(1)}, u32[]{:S(2)}, u32[]{:S(2)}) collective-permute-start(bf16[4,2,8,768]{3,2,0,1:T(8,128)(2,1)S(1)} %pad_maximum_fusion.23), channel_id=1, source_target_pairs={{0,16},{4,20},{8,24},{12,28},{16,0},{20,4},{24,8},{28,12},{1,17},{... | collective-permute-start | bytes 294920 | tf_op jit(solution)/shard_map/ppermute | solution.py:71
  260.5 54.9 %collective-permute-start.38 = (bf16[256,768]{1,0:T(8,128)(2,1)}, bf16[256,768]{1,0:T(8,128)(2,1)}, u32[]{:S(2)}, u32[]{:S(2)}) collective-permute-start(bf16[256,768]{1,0:T(8,128)(2,1)} %get-tuple-element.154), channel_id=1, source_target_pairs={{1,0},{2,1},{3,2},{5,4},{6,5},{7,6},{9,8},{10,9},{11,10},{13,12},{... | collective-permute-start | bytes 1179656 | tf_op jit(solution)/shard_map/ppermute | solution.py:77
  261.8 53.6 %collective-permute-start.40 = (bf16[256,768]{1,0:T(8,128)(2,1)}, bf16[256,768]{1,0:T(8,128)(2,1)}, u32[]{:S(2)}, u32[]{:S(2)}) collective-permute-start(bf16[256,768]{1,0:T(8,128)(2,1)} %get-tuple-element.155), channel_id=1, source_target_pairs={{0,1},{1,2},{2,3},{4,5},{5,6},{6,7},{8,9},{9,10},{10,11},{12,13},{... | collective-permute-start | bytes 1179656 | tf_op jit(solution)/shard_map/ppermute | solution.py:77
  295.4 26.7 %collective-permute-start.34 = (bf16[256,768]{1,0:T(8,128)(2,1)}, bf16[256,768]{1,0:T(8,128)(2,1)S(1)}, u32[]{:S(2)}, u32[]{:S(2)}) collective-permute-start(bf16[256,768]{1,0:T(8,128)(2,1)} %get-tuple-element.152), channel_id=1, source_target_pairs={{1,0},{2,1},{3,2},{5,4},{6,5},{7,6},{9,8},{10,9},{11,10},{13,12},{... | collective-permute-start | bytes 1179656 | tf_op jit(solution)/shard_map/ppermute | solution.py:77
  296.6 25.4 %collective-permute-start.36 = (bf16[256,768]{1,0:T(8,128)(2,1)}, bf16[256,768]{1,0:T(8,128)(2,1)}, u32[]{:S(2)}, u32[]{:S(2)}) collective-permute-start(bf16[256,768]{1,0:T(8,128)(2,1)} %get-tuple-element.153), channel_id=1, source_target_pairs={{0,1},{1,2},{2,3},{4,5},{5,6},{6,7},{8,9},{9,10},{10,11},{12,13},{... | collective-permute-start | bytes 1179656 | tf_op jit(solution)/shard_map/ppermute | solution.py:77
  309.3 35.9 %collective-permute-start.42 = (bf16[2,4,96,768]{3,2,1,0:T(8,128)(2,1)}, bf16[2,4,96,768]{3,2,1,0:T(8,128)(2,1)}, u32[]{:S(2)}, u32[]{:S(2)}) collective-permute-start(bf16[2,4,96,768]{3,2,1,0:T(8,128)(2,1)} %pad_maximum_fusion.8), channel_id=1, source_target_pairs={{0,4},{4,0},{8,12},{12,8},{16,20},{20,16},{24,28},{28,24},{1,5},{5... | collective-permute-start | bytes 3538952 | tf_op jit(solution)/shard_map/ppermute | solution.py:71
  317.2 12.9 %collective-permute-start.41 = (bf16[256,768]{1,0:T(8,128)(2,1)S(1)}, bf16[256,768]{1,0:T(8,128)(2,1)S(1)}, u32[]{:S(2)}, u32[]{:S(2)}) collective-permute-start(bf16[256,768]{1,0:T(8,128)(2,1)S(1)} %get-tuple-element.147), channel_id=1, source_target_pairs={{0,1},{1,2},{2,3},{4,5},{5,6},{6,7},{8,9},{9,10},{10,11},{12,13},{... | collective-permute-start | bytes 1179656 | tf_op jit(solution)/shard_map/ppermute | solution.py:77
  320.7 13.8 %collective-permute-start.39 = (bf16[256,768]{1,0:T(8,128)(2,1)S(1)}, bf16[256,768]{1,0:T(8,128)(2,1)S(1)}, u32[]{:S(2)}, u32[]{:S(2)}) collective-permute-start(bf16[256,768]{1,0:T(8,128)(2,1)S(1)} %get-tuple-element.146), channel_id=1, source_target_pairs={{1,0},{2,1},{3,2},{5,4},{6,5},{7,6},{9,8},{10,9},{11,10},{13,12},{... | collective-permute-start | bytes 1179656 | tf_op jit(solution)/shard_map/ppermute | solution.py:77
  323.3 14.9 %collective-permute-start.37 = (bf16[256,768]{1,0:T(8,128)(2,1)S(1)}, bf16[256,768]{1,0:T(8,128)(2,1)S(1)}, u32[]{:S(2)}, u32[]{:S(2)}) collective-permute-start(bf16[256,768]{1,0:T(8,128)(2,1)S(1)} %get-tuple-element.145), channel_id=1, source_target_pairs={{0,1},{1,2},{2,3},{4,5},{5,6},{6,7},{8,9},{9,10},{10,11},{12,13},{... | collective-permute-start | bytes 1179656 | tf_op jit(solution)/shard_map/ppermute | solution.py:77
  327.8 14.4 %collective-permute-start.35 = (bf16[256,768]{1,0:T(8,128)(2,1)S(1)}, bf16[256,768]{1,0:T(8,128)(2,1)S(1)}, u32[]{:S(2)}, u32[]{:S(2)}) collective-permute-start(bf16[256,768]{1,0:T(8,128)(2,1)S(1)} %get-tuple-element.144), channel_id=1, source_target_pairs={{1,0},{2,1},{3,2},{5,4},{6,5},{7,6},{9,8},{10,9},{11,10},{13,12},{... | collective-permute-start | bytes 1179656 | tf_op jit(solution)/shard_map/ppermute | solution.py:77
  330.1 19.1 %collective-permute-start.45 = (bf16[2,4,96,768]{3,2,0,1:T(8,128)(2,1)S(1)}, bf16[2,4,96,768]{3,2,0,1:T(8,128)(2,1)S(1)}, u32[]{:S(2)}, u32[]{:S(2)}) collective-permute-start(bf16[2,4,96,768]{3,2,0,1:T(8,128)(2,1)S(1)} %pad_maximum_fusion.7), channel_id=1, source_target_pairs={{0,4},{4,0},{8,12},{12,8},{16,20},{20,16},{24,28},{28,24},{1,5},{5... | collective-permute-start | bytes 3538952 | tf_op jit(solution)/shard_map/ppermute | solution.py:71
  334.6 38.5 %collective-permute-start.54 = (bf16[1,4,96,3072]{3,2,1,0:T(8,128)(2,1)S(1)}, bf16[1,4,96,3072]{3,2,1,0:T(8,128)(2,1)S(1)}, u32[]{:S(2)}, u32[]{:S(2)}) collective-permute-start(bf16[1,4,96,3072]{3,2,1,0:T(8,128)(2,1)S(1)} %copy-done.49), channel_id=1, source_target_pairs={{0,4},{4,0},{8,12},{12,8},{16,20},{20,16},{24,28},{28,24},{1,5},{5... | collective-permute-start | bytes 7077896 | tf_op jit(solution)/shard_map/ppermute | solution.py:71
  338.2 37.0 %collective-permute-start.51 = (bf16[1,4,96,3072]{3,2,1,0:T(8,128)(2,1)S(1)}, bf16[1,4,96,3072]{3,2,1,0:T(8,128)(2,1)S(1)}, u32[]{:S(2)}, u32[]{:S(2)}) collective-permute-start(bf16[1,4,96,3072]{3,2,1,0:T(8,128)(2,1)S(1)} %copy-done.48), channel_id=1, source_target_pairs={{0,4},{4,0},{8,12},{12,8},{16,20},{20,16},{24,28},{28,24},{1,5},{5... | collective-permute-start | bytes 7077896 | tf_op jit(solution)/shard_map/ppermute | solution.py:71
  347.0 16.0 %collective-permute-start.43 = (bf16[2,2,96,768]{3,2,1,0:T(8,128)(2,1)S(1)}, bf16[2,2,96,768]{3,2,1,0:T(8,128)(2,1)S(1)}, u32[]{:S(2)}, u32[]{:S(2)}) collective-permute-start(bf16[2,2,96,768]{3,2,1,0:T(8,128)(2,1)S(1)} %fusion.96), channel_id=1, source_target_pairs={{0,8},{4,12},{8,0},{12,4},{16,24},{20,28},{24,16},{28,20},{1,9},{5... | collective-permute-start | bytes 1769480 | tf_op jit(solution)/shard_map/ppermute | solution.py:71
  347.1 15.9 %collective-permute-start.66 = (f32[4,768]{1,0:T(4,128)S(1)}, f32[4,768]{1,0:T(4,128)S(1)}, u32[]{:S(2)}, u32[]{:S(2)}) collective-permute-start(f32[4,768]{1,0:T(4,128)S(1)} %fusion.276), channel_id=1, source_target_pairs={{0,8},{4,12},{8,0},{12,4},{16,24},{20,28},{24,16},{28,20},{1,9},{5... | collective-permute-start | bytes 36872 | tf_op jit(solution)/shard_map/ppermute | solution.py:71
  349.6 15.2 %collective-permute-start.46 = (bf16[2,2,96,768]{3,2,0,1:T(8,128)(2,1)S(1)}, bf16[2,2,96,768]{3,2,0,1:T(8,128)(2,1)S(1)}, u32[]{:S(2)}, u32[]{:S(2)}) collective-permute-start(bf16[2,2,96,768]{3,2,0,1:T(8,128)(2,1)S(1)} %slice.612), channel_id=1, source_target_pairs={{0,16},{4,20},{8,24},{12,28},{16,0},{20,4},{24,8},{28,12},{1,17},{... | collective-permute-start | bytes 1769480 | tf_op jit(solution)/shard_map/ppermute | solution.py:71
  363.3 8.7 %collective-permute-start.44 = (bf16[2,1,96,768]{3,2,0,1:T(8,128)(2,1)S(1)}, bf16[2,1,96,768]{3,2,0,1:T(8,128)(2,1)S(1)}, u32[]{:S(2)}, u32[]{:S(2)}) collective-permute-start(bf16[2,1,96,768]{3,2,0,1:T(8,128)(2,1)S(1)} %fusion.133), channel_id=1, source_target_pairs={{0,16},{4,20},{8,24},{12,28},{16,0},{20,4},{24,8},{28,12},{1,17},{... | collective-permute-start | bytes 884744 | tf_op jit(solution)/shard_map/ppermute | solution.py:71
  365.0 8.0 %collective-permute-start.47 = (bf16[2,1,96,768]{3,2,0,1:T(8,128)(2,1)S(1)}, bf16[2,1,96,768]{3,2,0,1:T(8,128)(2,1)S(1)}, u32[]{:S(2)}, u32[]{:S(2)}) collective-permute-start(bf16[2,1,96,768]{3,2,0,1:T(8,128)(2,1)S(1)} %slice.613), channel_id=1, source_target_pairs={{0,8},{4,12},{8,0},{12,4},{16,24},{20,28},{24,16},{28,20},{1,9},{5... | collective-permute-start | bytes 884744 | tf_op jit(solution)/shard_map/ppermute | solution.py:71
  374.2 26.1 %collective-permute-start.55 = (bf16[1,2,96,3072]{3,2,1,0:T(8,128)(2,1)S(1)}, bf16[1,2,96,3072]{3,2,1,0:T(8,128)(2,1)S(1)}, u32[]{:S(2)}, u32[]{:S(2)}) collective-permute-start(bf16[1,2,96,3072]{3,2,1,0:T(8,128)(2,1)S(1)} %slice.610), channel_id=1, source_target_pairs={{0,16},{4,20},{8,24},{12,28},{16,0},{20,4},{24,8},{28,12},{1,17},{... | collective-permute-start | bytes 3538952 | tf_op jit(solution)/shard_map/ppermute | solution.py:71
  376.2 28.0 %collective-permute-start.52 = (bf16[1,2,96,3072]{3,2,1,0:T(8,128)(2,1)S(1)}, bf16[1,2,96,3072]{3,2,1,0:T(8,128)(2,1)S(1)}, u32[]{:S(2)}, u32[]{:S(2)}) collective-permute-start(bf16[1,2,96,3072]{3,2,1,0:T(8,128)(2,1)S(1)} %fusion.52), channel_id=1, source_target_pairs={{0,8},{4,12},{8,0},{12,4},{16,24},{20,28},{24,16},{28,20},{1,9},{5... | collective-permute-start | bytes 3538952 | tf_op jit(solution)/shard_map/ppermute | solution.py:71
  377.0 40.4 %collective-permute-start.50 = (bf16[4,96,192]{2,1,0:T(8,128)(2,1)S(1)}, bf16[4,96,192]{2,1,0:T(8,128)(2,1)S(1)}, u32[]{:S(2)}, u32[]{:S(2)}) collective-permute-start(bf16[4,96,192]{2,1,0:T(8,128)(2,1)S(1)} %get-tuple-element.178), channel_id=1, source_target_pairs={{0,3},{1,2},{2,1},{3,0},{4,7},{5,6},{6,5},{7,4},{8,11},{9,10},{10,... | collective-permute-start | bytes 442376 | tf_op jit(solution)/shard_map/ppermute | solution.py:71
  377.1 43.1 %collective-permute-start.49 = (bf16[4,96,192]{2,1,0:T(8,128)(2,1)S(1)}, bf16[4,96,192]{2,1,0:T(8,128)(2,1)S(1)}, u32[]{:S(2)}, u32[]{:S(2)}) collective-permute-start(bf16[4,96,192]{2,1,0:T(8,128)(2,1)S(1)} %get-tuple-element.179), channel_id=1, source_target_pairs={{0,2},{1,3},{2,0},{3,1},{4,6},{5,7},{6,4},{7,5},{8,10},{9,11},{10,... | collective-permute-start | bytes 442376 | tf_op jit(solution)/shard_map/ppermute | solution.py:71
  378.8 42.1 %collective-permute-start.48 = (bf16[4,96,192]{2,1,0:T(8,128)(2,1)S(1)}, bf16[4,96,192]{2,1,0:T(8,128)(2,1)S(1)}, u32[]{:S(2)}, u32[]{:S(2)}) collective-permute-start(bf16[4,96,192]{2,1,0:T(8,128)(2,1)S(1)} %get-tuple-element.177), channel_id=1, source_target_pairs={{0,1},{1,0},{2,3},{3,2},{4,5},{5,4},{6,7},{7,6},{8,9},{9,8},{10,11... | collective-permute-start | bytes 442376 | tf_op jit(solution)/shard_map/ppermute | solution.py:71
  400.6 14.4 %collective-permute-start.56 = (bf16[1,1,96,3072]{3,2,1,0:T(8,128)(2,1)S(1)}, bf16[1,1,96,3072]{3,2,1,0:T(8,128)(2,1)S(1)}, u32[]{:S(2)}, u32[]{:S(2)}) collective-permute-start(bf16[1,1,96,3072]{3,2,1,0:T(8,128)(2,1)S(1)} %slice.611), channel_id=1, source_target_pairs={{0,8},{4,12},{8,0},{12,4},{16,24},{20,28},{24,16},{28,20},{1,9},{5... | collective-permute-start | bytes 1769480 | tf_op jit(solution)/shard_map/ppermute | solution.py:71
  404.5 10.8 %collective-permute-start.53 = (bf16[1,1,96,3072]{3,2,1,0:T(8,128)(2,1)S(1)}, bf16[1,1,96,3072]{3,2,1,0:T(8,128)(2,1)S(1)}, u32[]{:S(2)}, u32[]{:S(2)}) collective-permute-start(bf16[1,1,96,3072]{3,2,1,0:T(8,128)(2,1)S(1)} %fusion.97), channel_id=1, source_target_pairs={{0,16},{4,20},{8,24},{12,28},{16,0},{20,4},{24,8},{28,12},{1,17},{... | collective-permute-start | bytes 1769480 | tf_op jit(solution)/shard_map/ppermute | solution.py:71
  415.6 11.9 %collective-permute-start.59 = (bf16[2,96,768]{2,1,0:T(8,128)(2,1)S(1)}, bf16[2,96,768]{2,1,0:T(8,128)(2,1)S(1)}, u32[]{:S(2)}, u32[]{:S(2)}) collective-permute-start(bf16[2,96,768]{2,1,0:T(8,128)(2,1)S(1)} %get-tuple-element.158), channel_id=1, source_target_pairs={{0,3},{1,2},{2,1},{3,0},{4,7},{5,6},{6,5},{7,4},{8,11},{9,10},{10,... | collective-permute-start | bytes 884744 | tf_op jit(solution)/shard_map/ppermute | solution.py:71
  415.7 25.6 %collective-permute-start.58 = (bf16[2,96,768]{2,1,0:T(8,128)(2,1)S(1)}, bf16[2,96,768]{2,1,0:T(8,128)(2,1)S(1)}, u32[]{:S(2)}, u32[]{:S(2)}) collective-permute-start(bf16[2,96,768]{2,1,0:T(8,128)(2,1)S(1)} %get-tuple-element.159), channel_id=1, source_target_pairs={{0,2},{1,3},{2,0},{3,1},{4,6},{5,7},{6,4},{7,5},{8,10},{9,11},{10,... | collective-permute-start | bytes 884744 | tf_op jit(solution)/shard_map/ppermute | solution.py:71
  417.4 23.9 %collective-permute-start.57 = (bf16[2,96,768]{2,1,0:T(8,128)(2,1)S(1)}, bf16[2,96,768]{2,1,0:T(8,128)(2,1)S(1)}, u32[]{:S(2)}, u32[]{:S(2)}) collective-permute-start(bf16[2,96,768]{2,1,0:T(8,128)(2,1)S(1)} %get-tuple-element.157), channel_id=1, source_target_pairs={{0,1},{1,0},{2,3},{3,2},{4,5},{5,4},{6,7},{7,6},{8,9},{9,8},{10,11... | collective-permute-start | bytes 884744 | tf_op jit(solution)/shard_map/ppermute | solution.py:71
  420.2 28.1 %collective-permute-start.67 = (f32[4,768]{1,0:T(4,128)S(1)}, f32[4,768]{1,0:T(4,128)S(1)}, u32[]{:S(2)}, u32[]{:S(2)}) collective-permute-start(f32[4,768]{1,0:T(4,128)S(1)} %add.661), channel_id=1, source_target_pairs={{0,16},{4,20},{8,24},{12,28},{16,0},{20,4},{24,8},{28,12},{1,17},{... | collective-permute-start | bytes 36872 | tf_op jit(solution)/shard_map/ppermute | solution.py:71
  452.0 5.6 %collective-permute-start.69 = (f32[4,768]{1,0:T(4,128)S(1)}, f32[4,768]{1,0:T(4,128)S(1)}, u32[]{:S(2)}, u32[]{:S(2)}) collective-permute-start(f32[4,768]{1,0:T(4,128)S(1)} %add.663), channel_id=1, source_target_pairs={{0,2},{1,3},{2,0},{3,1},{4,6},{5,7},{6,4},{7,5},{8,10},{9,11},{10,... | collective-permute-start | bytes 36872 | tf_op jit(solution)/shard_map/ppermute | solution.py:71
  452.1 5.6 %collective-permute-start.62 = (f32[8,128]{1,0:T(8,128)S(1)}, f32[8,128]{1,0:T(8,128)S(1)}, u32[]{:S(2)}, u32[]{:S(2)}) collective-permute-start(f32[8,128]{1,0:T(8,128)S(1)} %fusion.277), channel_id=1, source_target_pairs={{0,16},{4,20},{8,24},{12,28},{16,0},{20,4},{24,8},{28,12},{1,17},{... | collective-permute-start | bytes 12296 | tf_op jit(solution)/shard_map/ppermute | solution.py:71
  461.3 4.5 collective-permute-start.64
  (107 other events, 947.0 us)
Sparse Core Ops, SparseCore 0:
  20.7 65.3 all-gather.2

commit v2 on v1

--- a/solution.py
+++ b/solution.py
@@ -71,10 +71,22 @@
     return lax.ppermute(values, axis, [(i, i ^ mask) for i in range(count)])
 
 
-def shift(values, axis, step):
-    count = lax.axis_size(axis)
-    pairs = [(i, i + step) for i in range(count) if 0 <= i + step < count]
-    return lax.ppermute(values, axis, pairs)
+def link(values, odd):
+    count = lax.axis_size("mp")
+    pairs = [(i, i + 1) for i in range(int(odd), count - 1, 2)]
+    return lax.ppermute(values, "mp", pairs + [(j, i) for i, j in pairs])
+
+
+def gather_columns_chain(values):
+    bit = 1
+    while bit < lax.axis_size("mp"):
+        values = jnp.concatenate([values, swap(values, "mp", bit)], axis=-1)
+        bit *= 2
+    return values
+
+
+def after(values, *earlier):
+    return lax.optimization_barrier((values,) + earlier)[0]
 
 
 def outer_masks():
@@ -86,55 +98,87 @@
 
 
 def gather_columns(values):
-    count = lax.axis_size("mp")
-    return jnp.concatenate([values] + [swap(values, "mp", k) for k in range(1, count)], axis=-1)
-
-
-def gather_rows(values, low_first):
-    held = values[:, None]
-    order = outer_masks()
-    for mask in order if low_first else order[::-1]:
-        other = swap(held, "dp", mask)
-        if low_first:
-            held = jnp.concatenate([held, other], axis=1)
-        else:
-            c, n, r, w = held.shape
-            held = jnp.stack([held, other], axis=2).reshape(c, 2 * n, r, w)
-    for mask in core_masks():
-        held = jnp.concatenate([held, swap(held, "dp", mask)], axis=1)
-    c, n, r, w = held.shape
-    return held.reshape(c, n * r, w)
-
-
-def reduce_rows(values, low_first):
-    count = lax.axis_size("dp")
-    c, _, w = values.shape
-    held = values.reshape(c, count, D // count, w)
-    for mask in core_masks():
-        half = held.shape[1] // 2
-        other = swap(held[:, half:].astype(BF16), "dp", mask)
-        held = held[:, :half].astype(F32) + other.astype(F32)
-    order = outer_masks()
-    for mask in order if low_first else order[::-1]:
-        half = held.shape[1] // 2
-        if low_first:
-            parts = held.reshape(c, half, 2, D // count, w)
-            stay, leave = parts[:, :, 0], parts[:, :, 1]
-        else:
-            stay, leave = held[:, :half], held[:, half:]
-        other = swap(leave.astype(BF16), "dp", mask)
-        held = stay.astype(F32) + other.astype(F32)
-    return held.reshape(c, D // count, w)
-
-
-def reduce_columns(values):
+    return [swap(values, "mp", k) for k in range(1, lax.axis_size("mp"))]
+
+
+def plane_masks():
+    masks = [0]
+    for mask in outer_masks():
+        masks += [held | mask for held in masks]
+    return masks[1:]
+
+
+def gather_plane(values):
+    return jnp.stack([values] + [swap(values, "dp", mask) for mask in plane_masks()], axis=1)
+
+
+def halves(values):
+    c, n, r, w = values.shape
+    near = values.reshape(c, n * r, w)
+    return near, swap(near, "dp", 1)
+
+
+def to_blocks(values):
+    c, rows, w = values.shape
+    count = lax.axis_size("dp") // 2
+    return values.reshape(c, count, rows // count, w)
+
+
+def add_low(stay, *received):
+    return sum([part.astype(F32) for part in received], stay.astype(F32)).astype(BF16)
+
+
+def split_outer(terms, masks, first):
+    spot = 0 if first else len(masks) - 1
+    n, r, w = terms[0].shape
+    split = [term.reshape(n >> (spot + 1), 2, 1 << spot, r, w) for term in terms]
+    stay, leave = ([term[:, k].reshape(n // 2, r, w) for term in split] for k in range(2))
+    return stay, add_low(*leave), masks[spot], masks[:spot] + masks[spot + 1 :]
+
+
+def gather_outer(part, number, low_first):
+    masks = outer_masks()
+    return swap(part, "dp", masks[number] if low_first else masks[len(masks) - 1 - number])
+
+
+def join_outer(part, received, low_first):
+    if low_first:
+        return jnp.concatenate([part, received], axis=0)
+    n, r, w = part.shape
+    return jnp.stack([part, received], axis=1).reshape(2 * n, r, w)
+
+
+def send_plane(held):
+    return [swap(held[:, number + 1], "dp", mask) for number, mask in enumerate(plane_masks())]
+
+
+def send_columns(values):
     count = lax.axis_size("mp")
     width = values.shape[-1] // count
-    parts = [values[..., k * width : (k + 1) * width] for k in range(count)]
-    total = parts[0].astype(F32)
-    for k in range(1, count):
-        total = total + swap(parts[k].astype(BF16), "mp", k).astype(F32)
-    return total
+    return [swap(values[..., k * width : (k + 1) * width], "mp", k) for k in range(1, count)]
+
+
+def send_columns_chain(values):
+    count = lax.axis_size("mp")
+    if count == 1:
+        return values[..., :0]
+    return swap(values[..., values.shape[-1] // 2 :], "mp", count // 2)
+
+
+def finish_columns_chain(values, received):
+    bit = lax.axis_size("mp") // 2
+    while bit:
+        half = values.shape[-1] // 2
+        values = values[..., :half].astype(F32) + received.astype(F32)
+        bit //= 2
+        if bit:
+            received = swap(values[..., half // 2 :].astype(BF16), "mp", bit)
+    return values
+
+
+def add_columns(values, received):
+    width = values.shape[-1] // lax.axis_size("mp")
+    return sum([part.astype(F32) for part in received], values[..., :width].astype(F32))
 
 
 def sum_over(values, axis):
@@ -189,10 +233,18 @@
     ]
 
 
+def whole_rows(near_ref, far_ref, number):
+    return jnp.concatenate([near_ref[number], far_ref[number]], axis=0)
+
+
 def forward_kernel(reach, range_ref, far_ref, q_ref, k_ref, v_ref, qf_ref, kf_ref, bias_ref, o_ref, log_ref):
     pair = pl.program_id(0)
     rows = q_ref.shape[0]
     score_scale = HD ** (-0.5)
+    low, high = range_ref[0], range_ref[1]
+
+    def slot_of(block):
+        return pl.ds(pl.multiple_of(range_ref[2 + block + reach] * rows, rows), rows)
 
     def work(lo, hi):
         query = q_ref[...] * jnp.asarray(score_scale, BF16)
@@ -203,7 +255,7 @@
             scores = []
             for block in range(-lo, hi + 1):
                 spot = pl.ds((block + reach) * rows, rows)
-                key_low = jnp.where(own_q, k_ref[spot, :], kf_ref[spot, :])
+                key_low = jnp.where(own_q, k_ref[slot_of(block), :], kf_ref[spot, :])
                 score = dot(key_low, query_low, NT)
                 if abs(block) <= 1:
                     score = score + bias_ref[part, block + 1]
@@ -213,9 +265,8 @@
             peak = jnp.max(functools.reduce(jnp.maximum, scores), axis=0, keepdims=True)
             total = jnp.zeros((2 * HD, rows), F32)
             for number, block in enumerate(range(-lo, hi + 1)):
-                spot = pl.ds((block + reach) * rows, rows)
                 probs = jnp.exp(scores[number] - peak).astype(BF16)
-                value_low = jnp.where(own_q, v_ref[spot, :], jnp.ones((), BF16))
+                value_low = jnp.where(own_q, v_ref[slot_of(block), :], jnp.ones((), BF16))
                 total = total + dot(value_low, probs, TN)
             row_sum = total[HD * (1 - part) : HD * (1 - part) + 1, :]
             mixed.append(total[HD * part : HD * (part + 1), :] / row_sum)
@@ -224,16 +275,20 @@
         log_ref[0] = jnp.concatenate(logs + [jnp.zeros((6, rows), F32)], axis=0)
 
     for lo, hi in block_choices(reach):
-        pl.when((range_ref[0] == lo) & (range_ref[1] == hi))(functools.partial(work, lo, hi))
+        pl.when((low == lo) & (high == hi))(functools.partial(work, lo, hi))
 
 
 def backward_kernel(
     reach, range_ref, far_ref, q_ref, k_ref, v_ref, qf_ref, kf_ref, bias_ref, do_ref, o_ref, log_ref,
-    dq_ref, dk_ref, dv_ref, db_ref,
+    dq_ref, dk_ref, dv_ref, bias_grad_ref,
 ):
     pair = pl.program_id(0)
     rows = q_ref.shape[0]
     score_scale = HD ** (-0.5)
+    low, high = range_ref[0], range_ref[1]
+
+    def slot_of(block):
+        return pl.ds(pl.multiple_of(range_ref[2 + block + reach] * rows, rows), rows)
 
     def work(lo, hi):
         query = q_ref[...] * jnp.asarray(score_scale, BF16)
@@ -255,22 +310,22 @@
             near[part] = jnp.zeros((rows, rows), F32)
             far[part] = [jnp.zeros((1, rows), F32), jnp.zeros((1, rows), F32)]
         for block in range(-reach, reach + 1):
+            if not -lo <= block <= hi:
+                dk_ref[slot_of(block), :] = jnp.zeros((rows, 2 * HD), BF16)
+                dv_ref[slot_of(block), :] = jnp.zeros((rows, 2 * HD), BF16)
+                continue
             spot = pl.ds((block + reach) * rows, rows)
-            if not -lo <= block <= hi:
-                dk_ref[spot, :] = jnp.zeros((rows, 2 * HD), BF16)
-                dv_ref[spot, :] = jnp.zeros((rows, 2 * HD), BF16)
-                continue
             dk = jnp.zeros((rows, 2 * HD), F32)
             dv = jnp.zeros((rows, 2 * HD), F32)
             for part in range(2):
-                key = k_ref[spot, :]
+                key = k_ref[slot_of(block), :]
                 score = dot(jnp.where(own[part], key, kf_ref[spot, :]), query_low[part], NT)
                 if abs(block) <= 1:
                     score = score + bias_ref[part, block + 1]
                 else:
                     score = score + far_ref[int(block > 0), 2 * pair + part]
                 probs = jnp.exp(score - log_row[part])
-                dprobs = dot(v_ref[spot, :], up_own[part], NT)
+                dprobs = dot(v_ref[slot_of(block), :], up_own[part], NT)
                 dscore = probs * (dprobs - delta[part])
                 probs_low, dscore_low = probs.astype(BF16), dscore.astype(BF16)
                 dv = dv + dot(probs_low, up_own[part])
@@ -287,8 +342,8 @@
                     far[part][int(block > 0)] += jnp.sum(jnp.where(close, 0.0, dscore), axis=0, keepdims=True)
                 else:
                     far[part][int(block > 0)] += jnp.sum(dscore, axis=0, keepdims=True)
-            dk_ref[spot, :] = dk.astype(BF16)
-            dv_ref[spot, :] = dv.astype(BF16)
+            dk_ref[slot_of(block), :] = dk.astype(BF16)
+            dv_ref[slot_of(block), :] = dv.astype(BF16)
         dq_ref[...] = (
             jnp.concatenate([dq[0][:HD], dq[1][HD:]], axis=0).T * score_scale
         ).astype(BF16)
@@ -300,12 +355,22 @@
             turned = dot(flip, near[part].astype(BF16))
             turned = pltpu.roll(turned, 0, 1, stride=1, stride_axis=0)
             line = jnp.sum(turned, axis=0, keepdims=True)
-            db_ref[0, part] = jnp.concatenate(
+            bias_grad_ref[0, part] = jnp.concatenate(
                 [line, far[part][0], far[part][1], jnp.zeros((5, rows), F32)], axis=0
             )
 
     for lo, hi in block_choices(reach):
-        pl.when((range_ref[0] == lo) & (range_ref[1] == hi))(functools.partial(work, lo, hi))
+        pl.when((low == lo) & (high == hi))(functools.partial(work, lo, hi))
+
+
+def pair_block(*shape):
+    count = len(shape)
+    return pl.BlockSpec(shape, lambda p: (0,) * (count - 1) + (p,))
+
+
+def same_block(*shape):
+    count = len(shape)
+    return pl.BlockSpec(shape, lambda p: (0,) * count)
 
 
 def attention_specs(rows, window, pairs):
@@ -313,42 +378,42 @@
     return [
         smem,
         smem,
-        pl.BlockSpec((rows, 2 * HD), lambda p: (0, p)),
-        pl.BlockSpec((window, 2 * HD), lambda p: (0, p)),
-        pl.BlockSpec((window, 2 * HD), lambda p: (0, p)),
-        pl.BlockSpec((rows, 2 * HD), lambda p: (0, 0)),
-        pl.BlockSpec((window, 2 * HD), lambda p: (0, 0)),
+        pair_block(rows, 2 * HD),
+        pair_block(window, 2 * HD),
+        pl.BlockSpec((window, 2 * HD), lambda p: (0, pairs + p)),
+        same_block(rows, 2 * HD),
+        same_block(window, 2 * HD),
         pl.BlockSpec((2, 3, rows, rows), lambda p: (p, 0, 0, 0)),
     ]
 
 
-def attend(reach, *operands):
-    rows, width = operands[2].shape
-    window = operands[3].shape[0]
+LITTLE = pl.CostEstimate(flops=10**5, bytes_accessed=10**4, transcendentals=0)
+
+
+def attend(reach, ranges, far_bias, queries, both, *operands):
+    rows, width = queries.shape
+    window = both.shape[0]
     pairs = width // (2 * HD)
     return pl.pallas_call(
         functools.partial(forward_kernel, reach),
         grid=(pairs,),
         in_specs=attention_specs(rows, window, pairs),
-        out_specs=[
-            pl.BlockSpec((rows, 2 * HD), lambda p: (0, p)),
-            pl.BlockSpec((1, 8, rows), lambda p: (p, 0, 0)),
-        ],
+        out_specs=[pair_block(rows, 2 * HD), pl.BlockSpec((1, 8, rows), lambda p: (p, 0, 0))],
         out_shape=[
             jax.ShapeDtypeStruct((rows, width), BF16),
             jax.ShapeDtypeStruct((pairs, 8, rows), F32),
         ],
         compiler_params=pltpu.CompilerParams(vmem_limit_bytes=VMEM_LIMIT),
+        cost_estimate=LITTLE,
         name="attend",
-    )(*operands)
-
-
-def attend_back(reach, *operands):
-    rows, width = operands[2].shape
-    window = operands[3].shape[0]
+    )(ranges, far_bias, queries, both, both, *operands)
+
+
+def attend_back(reach, ranges, far_bias, queries, both, *operands):
+    rows, width = queries.shape
+    window = both.shape[0]
     pairs = width // (2 * HD)
-    tall = pl.BlockSpec((window, 2 * HD), lambda p: (0, p))
-    short = pl.BlockSpec((rows, 2 * HD), lambda p: (0, p))
+    tall, short = pair_block(window, 2 * HD), pair_block(rows, 2 * HD)
     return pl.pallas_call(
         functools.partial(backward_kernel, reach),
         grid=(pairs,),
@@ -362,8 +427,202 @@
             jax.ShapeDtypeStruct((pairs, 2, 8, rows), F32),
         ],
         compiler_params=pltpu.CompilerParams(vmem_limit_bytes=VMEM_LIMIT),
+        cost_estimate=LITTLE,
         name="attend_back",
-    )(*operands)
+    )(ranges, far_bias, queries, both, both, *operands)
+
+
+def flatten_kernel(rows_ref, flat_ref):
+    flat_ref[...] = rows_ref[...].T
+
+
+def flatten(window, rows):
+    return pl.pallas_call(
+        flatten_kernel,
+        grid=(window.shape[0] // rows,),
+        in_specs=[pl.BlockSpec((rows, window.shape[1]), lambda n: (n, 0))],
+        out_specs=pair_block(window.shape[1], rows),
+        out_shape=jax.ShapeDtypeStruct(window.shape[::-1], BF16),
+        compiler_params=pltpu.CompilerParams(vmem_limit_bytes=VMEM_LIMIT),
+        cost_estimate=LITTLE,
+        name="flatten",
+    )(window)
+
+
+def collect_kernel(count, *refs):
+    half = refs[-1].shape[1]
+    flat_refs, grad_refs = refs[:count], refs[count : 4 * count]
+    out_part_ref, keep_ref, send_ref = refs[4 * count :]
+    for number in range(3):
+        grad = jnp.zeros((2 * half, keep_ref.shape[2]), F32)
+        for flat_ref, grad_ref in zip(flat_refs, grad_refs[number::3]):
+            grad = grad + dot(flat_ref[:, : grad_ref.shape[0]], grad_ref[...])
+        keep_ref[number] = grad[:half].astype(BF16)
+        send_ref[number] = grad[half:].astype(BF16)
+    keep_ref[3] = out_part_ref[:half, :]
+    send_ref[3] = out_part_ref[half:, :]
+
+
+def collect(windows_flat, grads, out_part):
+    count = len(grads)
+    chunk = 4 * HD
+    flat_grads = [part for grad in grads for part in grad]
+    return pl.pallas_call(
+        functools.partial(collect_kernel, count),
+        grid=(D // chunk,),
+        in_specs=[same_block(*part.shape) for part in windows_flat]
+        + [pair_block(part.shape[0], chunk) for part in (*flat_grads, out_part)],
+        out_specs=[pair_block(4, D // 2, chunk)] * 2,
+        out_shape=[jax.ShapeDtypeStruct((4, D // 2, D), BF16)] * 2,
+        compiler_params=pltpu.CompilerParams(vmem_limit_bytes=VMEM_LIMIT),
+        cost_estimate=LITTLE,
+        name="collect",
+    )(*windows_flat, *flat_grads, out_part)
+
+
+CUBE = 0.044715
+ROOT = (2.0 / 3.141592653589793) ** 0.5
+
+
+def feed_kernel(normed_ref, hidden_ref, near_ref, other_ref, out_ref, act_ref, slope_ref):
+    @pl.when(pl.program_id(0) == 0)
+    def _():
+        out_ref[...] = hidden_ref[...]
+
+    pre = dot(normed_ref[...], whole_rows(near_ref, other_ref, 0))
+    square = pre * pre
+    bend = jnp.tanh(ROOT * pre * (1.0 + CUBE * square))
+    gate = 0.5 * (1.0 + bend)
+    act = (pre * gate).astype(BF16)
+    slope = gate + 0.5 * pre * (1.0 - bend * bend) * (ROOT * (1.0 + 3.0 * CUBE * square))
+    act_ref[...] = act
+    slope_ref[...] = slope.astype(BF16)
+    out_ref[...] += dot(act, whole_rows(near_ref, other_ref, 1), NT)
+
+
+def feed_back_kernel(
+    normed_ref, up_ref, near_ref, other_ref, act_ref, slope_ref, out_ref, keep_ref, send_ref,
+    normed_flat_ref, up_flat_ref,
+):
+    half = keep_ref.shape[1]
+
+    @pl.when(pl.program_id(0) == 0)
+    def _():
+        out_ref[...] = jnp.zeros_like(out_ref)
+        normed_flat_ref[...] = normed_ref[...].T
+        up_flat_ref[...] = up_ref[...].T
+
+    act_grad = dot(up_ref[...], whole_rows(near_ref, other_ref, 1))
+    pre_grad = (act_grad * slope_ref[...].astype(F32)).astype(BF16)
+    out_ref[...] += dot(pre_grad, whole_rows(near_ref, other_ref, 0), NT)
+    for number, grad in enumerate(
+        (dot(normed_flat_ref[...], pre_grad), dot(up_flat_ref[...], act_ref[...]))
+    ):
+        keep_ref[number] = grad[:half].astype(BF16)
+        send_ref[number] = grad[half:].astype(BF16)
+
+
+def unit_chunk(units):
+    return 512 if units % 512 == 0 else units
+
+
+def feed(normed, hidden, near, other):
+    count, width = normed.shape
+    _, half, units = near.shape
+    chunk = unit_chunk(units)
+    weights = pair_block(2, half, chunk)
+    wide = pair_block(count, chunk)
+    return pl.pallas_call(
+        feed_kernel,
+        grid=(units // chunk,),
+        in_specs=[same_block(count, width), same_block(count, width), weights, weights],
+        out_specs=[same_block(count, width), wide, wide],
+        out_shape=[
+            jax.ShapeDtypeStruct((count, width), F32),
+            jax.ShapeDtypeStruct((count, units), BF16),
+            jax.ShapeDtypeStruct((count, units), BF16),
+        ],
+        compiler_params=pltpu.CompilerParams(vmem_limit_bytes=VMEM_LIMIT),
+        cost_estimate=LITTLE,
+        name="feed",
+    )(normed, hidden, near, other)
+
+
+def feed_back(normed, upstream, near, other, act, slope):
+    count, width = normed.shape
+    _, half, units = near.shape
+    chunk = unit_chunk(units)
+    weights = pair_block(2, half, chunk)
+    wide = pair_block(count, chunk)
+    return pl.pallas_call(
+        feed_back_kernel,
+        grid=(units // chunk,),
+        in_specs=[same_block(count, width), same_block(count, width), weights, weights, wide, wide],
+        out_specs=[same_block(count, width), weights, weights],
+        out_shape=[
+            jax.ShapeDtypeStruct((count, width), F32),
+            jax.ShapeDtypeStruct((2, half, units), BF16),
+            jax.ShapeDtypeStruct((2, half, units), BF16),
+        ],
+        scratch_shapes=[pltpu.VMEM((width, count), BF16), pltpu.VMEM((width, count), BF16)],
+        compiler_params=pltpu.CompilerParams(vmem_limit_bytes=VMEM_LIMIT),
+        cost_estimate=LITTLE,
+        name="feed_back",
+    )(normed, upstream, near, other, act, slope)
+
+
+def contrast_kernel(
+    micro_count, segment_count, rank_ref, pooled_ref, near_ref, other_ref, turn_ref, grad_ref, proj_grad_ref
+):
+    every = pooled_ref.shape[0]
+    own = micro_count * segment_count
+
+    def place(axis):
+        number = lax.broadcasted_iota(jnp.int32, (every, every), axis)
+        segment = number % segment_count
+        micro = (number // segment_count) % micro_count
+        owner = rank_ref[0] ^ (number // own)
+        return owner * segment_count + segment, micro
+
+    spot, micro = place(0)
+    other_spot, other_micro = place(1)
+    together = micro == other_micro
+    pooled = dot(pooled_ref[:, :D], turn_ref[...]).astype(BF16)
+    proj = jnp.concatenate([near_ref[...], other_ref[...]], axis=0)
+    marks = pooled_ref[:, D:].astype(F32)
+    target = (marks[:, 0:1] * 16.0 + marks[:, 1:2]).astype(jnp.int32)
+    picked = target + (target >= spot).astype(jnp.int32)
+    chosen = together & (picked == other_spot)
+    embedded = dot(pooled, proj)
+    inverse = lax.rsqrt(jnp.sum(embedded * embedded, axis=1, keepdims=True) + EPS_NORM)
+    unit = (embedded * inverse).astype(BF16)
+    logits = jnp.where(together & (spot != other_spot), SIM_SCALE * dot(unit, unit, NT), NEG_FILL)
+    shifted = jnp.exp(logits - jnp.max(logits, axis=1, keepdims=True))
+    shares = shifted / jnp.sum(shifted, axis=1, keepdims=True)
+    logit_grad = (shares - chosen.astype(F32)).astype(BF16)
+    unit_grad = SIM_SCALE * (dot(logit_grad, unit) + dot(logit_grad, unit, TN))
+    unit_grad = unit_grad.astype(BF16).astype(F32)
+    along = jnp.sum(unit_grad * embedded, axis=1, keepdims=True)
+    embed_grad = inverse * unit_grad - embedded * (inverse * inverse * inverse) * along
+    embed_grad = embed_grad.astype(BF16)
+    grad_ref[...] = dot(embed_grad[:own], proj, NT)
+    proj_grad_ref[...] = dot(pooled, embed_grad, TN)
+
+
+def contrast(rank, pooled, near, other, turn, micro_count, segment_count):
+    vmem = pl.BlockSpec(memory_space=pltpu.VMEM)
+    return pl.pallas_call(
+        functools.partial(contrast_kernel, micro_count, segment_count),
+        in_specs=[pl.BlockSpec(memory_space=pltpu.SMEM), vmem, vmem, vmem, vmem],
+        out_specs=[vmem, vmem],
+        out_shape=[
+            jax.ShapeDtypeStruct((micro_count * segment_count, D), F32),
+            jax.ShapeDtypeStruct((D, D), F32),
+        ],
+        compiler_params=pltpu.CompilerParams(vmem_limit_bytes=VMEM_LIMIT),
+        cost_estimate=LITTLE,
+        name="contrast",
+    )(rank, pooled, near, other, turn)
 
 
 def local(
@@ -416,37 +675,82 @@
     normed_one = (token_rows * factor_one * gains[0]).astype(BF16)
     normed_one = normed_one.reshape(micro_count, rows, D)
 
-    attn_cols = gather_columns(attention_low)
-    attn_qo = gather_rows(jnp.stack([attn_cols[0], attn_cols[3]]), True)
-    attn_kv = gather_rows(attn_cols[1:3], False)
-    w_query, w_out = attn_qo[0], attn_qo[1]
-    w_key, w_value = attn_kv[0], attn_kv[1]
-
-    windows = []
+    head = jnp.arange(bias_table.shape[1], dtype=jnp.int32)
+    head_source = (narrow_rank ^ (head // heads_part)) * heads_part + head % heads_part
+    head_turn = (head[:, None] == head_source[None, :]).astype(F32)
+
+    is_even = narrow_rank % 2 == 0
+
+    def hop(held):
+        return link(held[1], False), link(held[0], True)
+
+    hops = [[] for _ in range(micro_count)]
+
+    def window_of(micro):
+        return jnp.concatenate([normed_one[micro]] + [part for pair in hops[micro] for part in pair])
+
+    def project(micro):
+        return (
+            dot(normed_one[micro], w_query).astype(BF16),
+            dot(windows[micro], w_both).astype(BF16),
+        )
+
+    def finish_hops(micro):
+        while len(hops[micro]) < reach:
+            hops[micro].append(hop(hops[micro][-1]))
+
+    def chain_step(values, bit):
+        return jnp.concatenate([values, swap(values, "mp", bit)], axis=-1)
+
+    bits = []
+    while 1 << len(bits) < narrow_count:
+        bits.append(1 << len(bits))
+    attn_parts = gather_columns(attention_low)
+    ffn_cols = feedforward_low
+    for bit in bits[:1]:
+        ffn_cols = chain_step(ffn_cols, bit)
+    attn_parts, ffn_cols, normed_late = after((attn_parts, ffn_cols, normed_one))
+    segment_ids, bias_late = after((segment_ids, bias_table), *attn_parts)
+    table = dot(bias_late, head_turn, precision=HIGHEST)
+    tiles = bias_tiles(table, rows)
+    attn_held = gather_plane(jnp.concatenate([attention_low] + attn_parts, axis=-1))
+    for bit in bits[1:]:
+        ffn_cols = chain_step(ffn_cols, bit)
+    attn_held, ffn_cols, normed_late, tiles = after((attn_held, ffn_cols, normed_late, tiles))
+    attn_near, attn_other = halves(attn_held)
+    first_hop = hop((normed_late, normed_late))
+    parts = [ffn_cols[0][None], ffn_cols[1][None]]
+
+    def outer_received(number):
+        return [gather_outer(part, number, first) for part, first in zip(parts, (True, False))]
+
+    def outer_joined(received):
+        return [
+            join_outer(part, got, first) for part, got, first in zip(parts, received, (True, False))
+        ]
+
+    outer_count = len(outer_masks())
+    received = outer_received(0)
+    attn_other, first_hop, received = after((attn_other, first_hop, received))
+    parts = outer_joined(received)
+    attn_all = jnp.concatenate([attn_near, attn_other], axis=1)
+    w_query, w_out = attn_all[0], attn_all[3]
+    w_both = jnp.concatenate([attn_all[1], attn_all[2]], axis=1)
     for micro in range(micro_count):
-        left, right = [], []
-        from_left = from_right = normed_one[micro]
-        for _ in range(reach):
-            from_left, from_right = shift(from_left, "mp", 1), shift(from_right, "mp", -1)
-            left.insert(0, from_left)
-            right.append(from_right)
-        windows.append(jnp.concatenate(left + [normed_one[micro]] + right, axis=0))
-
-    ffn_cols = gather_columns(feedforward_low)
-    w_up = gather_rows(ffn_cols[0:1], True)[0]
-    w_down = gather_rows(ffn_cols[1:2], False)[0]
-    proj_all = lax.all_gather(projection_low, ("dp", "mp"), axis=0, tiled=False)
-    proj_all = proj_all.reshape(wide_count, narrow_count, block, D // narrow_count)
-    proj_all = proj_all.transpose(0, 2, 1, 3).reshape(D, D)
-
-    table = jnp.concatenate(
+        hops[micro].append((first_hop[0][micro], first_hop[1][micro]))
+    finish_hops(0)
+    w_both, w_query, hops, parts = after((w_both, w_query, hops, parts))
+    windows = [window_of(0)]
+    projected = [project(0)]
+    slots = jnp.stack(
         [
-            lax.dynamic_slice_in_dim(bias_table, (narrow_rank ^ k) * heads_part, heads_part, 1)
-            for k in range(narrow_count)
-        ],
-        axis=1,
-    )
-    tiles = bias_tiles(table, rows)
+            jnp.int32(0)
+            if n == 0
+            else jnp.where(is_even == (n > 0), 2 * abs(n) - 1, 2 * abs(n)).astype(jnp.int32)
+            for n in range(-reach, reach + 1)
+        ]
+    )
+
     far_bias = jnp.stack([table[15], table[31]])
     lanes = jnp.arange(2 * HD, dtype=jnp.int32) % HD
     padded = jnp.pad(
@@ -467,28 +771,57 @@
         (window_segments[:, (reach + n) * rows] == last).astype(jnp.int32)
         for n in range(1, reach + 1)
     )
-    ranges = jnp.stack([low_count, high_count], axis=1)
+    ranges = jnp.concatenate(
+        [
+            jnp.stack([low_count, high_count], axis=1),
+            jnp.broadcast_to(slots, (micro_count, span)),
+        ],
+        axis=1,
+    )
 
     mixed, kept = [], []
+    proj_parts = []
     for micro in range(micro_count):
-        queries = dot(normed_one[micro], w_query).astype(BF16)
-        keys = dot(windows[micro], w_key).astype(BF16)
-        values = dot(windows[micro], w_value).astype(BF16)
+        came, received = [], []
+        parts, projected[micro] = after((parts, projected[micro]))
+        if micro == 0 and outer_count > 1:
+            received = outer_received(1)
+        if micro + 1 < micro_count:
+            finish_hops(micro + 1)
+            came = hops[micro + 1]
+        else:
+            proj_parts = gather_columns(after(projection_low, projected[micro][0]))
         operands = (
-            ranges[micro], far_bias, queries, keys, values, query_marks[micro], key_marks[micro], tiles
+            ranges[micro], far_bias, *projected[micro], query_marks[micro], key_marks[micro], tiles
         )
         mixed_part, logs = attend(reach, *operands)
+        came, mixed_part, proj_parts = after((came, mixed_part, proj_parts))
+        if came:
+            hops[micro + 1] = came
+            windows.append(window_of(micro + 1))
+            projected.append(project(micro + 1))
+        if received:
+            last_received = received
+        kept.append((operands, mixed_part, logs))
         mixed.append(mixed_part)
-        kept.append((operands, mixed_part, logs))
-    mixed = jnp.concatenate(mixed, axis=0)
-    hidden_one = token_rows + dot(mixed, w_out, NT)
+    if outer_count > 1:
+        last_received, mixed = after((last_received, mixed))
+        parts = outer_joined(last_received)
+    for number in range(2, outer_count):
+        parts = outer_joined(outer_received(number))
+    ffn_near, ffn_other = halves(jnp.stack(parts))
+    hidden_one = token_rows + dot(jnp.concatenate(mixed, axis=0), w_out, NT)
+    proj_held = gather_plane(jnp.concatenate([projection_low] + proj_parts, axis=-1)[None])
+    windows_flat = [flatten(window, rows) for window in windows]
+    hidden_one, ffn_other, proj_held, windows_flat = after(
+        (hidden_one, ffn_other, proj_held, windows_flat)
+    )
+    proj_near, proj_other = halves(proj_held)
 
     factor_two = norm_factor(hidden_one)
     normed_two = (hidden_one * factor_two * gains[1]).astype(BF16)
-    pre_act = dot(normed_two, w_up)
-    activated, gelu_pull = jax.vjp(jax.nn.gelu, pre_act)
-    activated = activated.astype(BF16)
-    hidden_two = hidden_one + dot(activated, w_down, NT)
+    hidden_two, activated, slopes = feed(normed_two, hidden_one, ffn_near, ffn_other)
+    hidden_two, proj_other = after((hidden_two, proj_other))
     output = dot(hidden_two.astype(BF16), turn, NT).astype(BF16)
 
     factor_three = norm_factor(hidden_two)
@@ -504,42 +837,16 @@
     )
     pooled = sum_over(pooled, "mp") / counts
     pooled = dot(pooled.reshape(-1, D).astype(BF16), turn, NT).astype(BF16)
-    pooled_all = gather_near(pooled.reshape(1, micro_count, segment_count, D))
-    targets_all = gather_near(targets[:, 0].astype(F32)[None])
-    every = wide_count * segment_count
-    pooled_all = pooled_all.transpose(1, 0, 2, 3).reshape(micro_count, every, D)
-    owner = wide_rank ^ jnp.arange(wide_count, dtype=jnp.int32)
-    absolute = (owner[:, None] * segment_count + numbers[None, :]).reshape(every)
-    picked = targets_all.astype(jnp.int32).transpose(1, 0, 2).reshape(micro_count, every)
-    picked = picked + (picked >= absolute[None]).astype(jnp.int32)
-    embedded = dot(pooled_all.reshape(-1, D), proj_all).reshape(micro_count, every, D)
-    inverse = lax.rsqrt(jnp.sum(embedded * embedded, axis=2, keepdims=True) + EPS_NORM)
-    unit = (embedded * inverse).astype(BF16)
-    sims = lax.dot_general(
-        unit, unit, (((2,), (2,)), ((0,), (0,))), preferred_element_type=F32
-    )
-    logits = jnp.where(jnp.eye(every, dtype=bool)[None], NEG_FILL, SIM_SCALE * sims)
-    logit_grad = (
-        jax.nn.softmax(logits, axis=-1) - (picked[:, :, None] == absolute[None, None, :]).astype(F32)
-    ).astype(BF16)
-    unit_grad = SIM_SCALE * (
-        lax.dot_general(logit_grad, unit, (((2,), (1,)), ((0,), (0,))), preferred_element_type=F32)
-        + lax.dot_general(logit_grad, unit, (((1,), (1,)), ((0,), (0,))), preferred_element_type=F32)
-    )
-    unit_grad = unit_grad.astype(BF16).astype(F32)
-    along = jnp.sum(unit_grad * embedded, axis=2, keepdims=True)
-    embed_grad = (
-        inverse * unit_grad - embedded * (inverse * inverse * inverse) * along
-    ).astype(BF16)
-    proj_reduced = dot(
-        lax.dynamic_slice_in_dim(pooled_all.reshape(-1, D), wide_rank * block, block, 1),
-        lax.dynamic_slice_in_dim(
-            embed_grad.reshape(-1, D), narrow_rank * projection.shape[1], projection.shape[1], 1
-        ),
-        TN,
-    )
-    pooled_grad = dot(embed_grad[:, :segment_count].reshape(-1, D), proj_all, NT)
-    pooled_grad = dot(pooled_grad, turn_wide, precision=HIGHEST)
+    pooled = pooled.reshape(1, micro_count, segment_count, D)
+    marks = jnp.stack([targets[:, 0] // 16, targets[:, 0] % 16], axis=-1).astype(BF16)
+    marks = jnp.pad(marks[None], ((0, 0), (0, 0), (0, 0), (0, 126)))
+    pooled_all = gather_near(jnp.concatenate([pooled, marks], axis=-1))
+    rank = jnp.stack([wide_rank, narrow_rank]).astype(jnp.int32)
+    pooled_grad, proj_grad = contrast(
+        rank, pooled_all.reshape(-1, pooled_all.shape[-1]), proj_near[0], proj_other[0], turn,
+        micro_count, segment_count,
+    )
+    proj_reduced = proj_grad[:block, : projection.shape[1]]
     pooled_grad = pooled_grad.reshape(micro_count, segment_count, D) / counts
     normed_three_grad = lax.dot_general(
         member, pooled_grad, (((1,), (1,)), ((0,), (0,))), precision=HIGHEST, preferred_element_type=F32
@@ -549,54 +856,106 @@
     upstream = dot(cotangent.reshape(micro_count * rows, D), turn)
     hidden_two_grad = upstream + norm_back(hidden_two, factor_three, normed_three_grad * gains[2])
     hidden_two_low = hidden_two_grad.astype(BF16)
-    act_grad = dot(hidden_two_low, w_down)
-    pre_grad = gelu_pull(act_grad)[0].astype(BF16)
-    down_part = dot(hidden_two_low, activated, TN).astype(BF16)
-    down_rows = reduce_rows(down_part[None], False)
-    up_part = dot(normed_two, pre_grad, TN).astype(BF16)
-    up_rows = reduce_rows(up_part[None], True)
-    ffn_reduced = reduce_columns(jnp.concatenate([up_rows, down_rows]))
-    normed_two_grad = dot(pre_grad, w_up, NT)
+    normed_two_grad, ffn_keep, ffn_send = feed_back(
+        normed_two, hidden_two_low, ffn_near, ffn_other, activated, slopes
+    )
+    ffn_received = swap(ffn_send, "dp", 1)
     gain_two = jnp.sum(normed_two_grad * hidden_one * factor_two, axis=0)
     hidden_one_grad = hidden_two_grad + norm_back(
         hidden_one, factor_two, normed_two_grad * gains[1]
     )
     hidden_one_low = hidden_one_grad.astype(BF16)
     mixed_grad = dot(hidden_one_low, w_out).astype(BF16).reshape(micro_count, rows, D)
-    out_part = dot(hidden_one_low, mixed, TN).astype(BF16)
-
-    query_grads, key_grads, value_grads, bias_parts, normed_one_grads = [], [], [], [], []
+    out_part = dot(hidden_one_low, jnp.concatenate(mixed, axis=0), TN).astype(BF16)
+    ffn_received, mixed_grad, out_part = after((ffn_received, mixed_grad, out_part))
+
+    def outer_split(parts):
+        return [split_outer(terms, masks, first) for (terms, masks), first in zip(parts, (False, True))]
+
+    ffn_blocks = [to_blocks(ffn_keep), to_blocks(ffn_received)]
+    parts = [([held[number] for held in ffn_blocks], outer_masks()) for number in range(2)]
+    grads, owns, bias_parts, flows = [], [], [], []
+
+    def leave(flow, n):
+        even, odd = flow[2 * n - 2], flow[2 * n - 1]
+        return link(even, False), link(odd, True)
+
+    def join(flow, n, came):
+        if n > 0:
+            flow[2 * n - 1] = add_low(flow[2 * n - 1], came[0])
+            flow[2 * n - 2] = add_low(flow[2 * n - 2], came[1])
+
+    def flow_of(dq, dk, dv):
+        partial = dot(dk, w_both[:, :D], NT) + dot(dv, w_both[:, D:], NT)
+        own = partial[:rows] + dot(dq, w_query, NT)
+        low_parts = partial.astype(BF16)
+        return own, [low_parts[n * rows : (n + 1) * rows] for n in range(1, span)]
+
+    came = []
     for micro in range(micro_count):
         operands, mixed_part, logs = kept[micro]
-        dq, dk, dv, db = attend_back(reach, *operands, mixed_grad[micro], mixed_part, logs)
-        query_grads.append(dq)
-        key_grads.append(dk)
-        value_grads.append(dv)
-        bias_parts.append(db)
-        partial = (dot(dk, w_key, NT) + dot(dv, w_value, NT)).reshape(span, rows, D)
-        own = partial[reach] + dot(dq, w_query, NT)
-        to_left = to_right = None
-        for n in range(reach, 0, -1):
-            leave_left, leave_right = partial[reach - n], partial[reach + n]
-            if to_left is not None:
-                leave_left = leave_left + to_left
-                leave_right = leave_right + to_right
-            to_left = shift(leave_left.astype(BF16), "mp", -1).astype(F32)
-            to_right = shift(leave_right.astype(BF16), "mp", 1).astype(F32)
-        normed_one_grads.append(own + to_left + to_right)
-    windows_all = jnp.concatenate(windows, axis=0)
-    query_part = dot(normed_one.reshape(-1, D), jnp.concatenate(query_grads), TN).astype(BF16)
-    key_part = dot(windows_all, jnp.concatenate(key_grads), TN).astype(BF16)
-    value_part = dot(windows_all, jnp.concatenate(value_grads), TN).astype(BF16)
-    qo_rows = reduce_rows(jnp.stack([query_part, out_part]), True)
-    kv_rows = reduce_rows(jnp.stack([key_part, value_part]), False)
-    attn_reduced = reduce_columns(
-        jnp.concatenate([qo_rows[0:1], kv_rows, qo_rows[1:2]])
-    )
-    normed_one_grad = jnp.concatenate(normed_one_grads, axis=0)
+        last = micro == micro_count - 1
+        steps = outer_split(parts) if parts[0][1] else []
+        upstream_low, flows, sent = after(
+            (mixed_grad[micro], flows, [step[1] for step in steps])
+        )
+        received = [swap(leaves, "dp", step[2]) for leaves, step in zip(sent, steps)]
+        came = [leave(flow, reach) for flow in flows]
+        dq, dk, dv, bias_part = attend_back(reach, *operands, upstream_low, mixed_part, logs)
+        flow = None if last else flow_of(dq, dk, dv)
+        received, came, dq, dk, dv, flow = after(
+            (received, came, dq, dk, dv, flow)
+        )
+        if steps:
+            parts = [(step[0] + [got], step[3]) for step, got in zip(steps, received)]
+        grads.append((dq, dk, dv))
+        bias_parts.append(bias_part)
+        if not last:
+            owns.append(flow[0])
+            flows.append(list(flow[1]))
+    while parts[0][1]:
+        parts = [
+            (stay + [swap(leaves, "dp", mask)], masks)
+            for stay, leaves, mask, masks in outer_split(parts)
+        ]
+    others = came
+    for flow, got in zip(flows, others):
+        join(flow, reach - 1, got)
+    ffn_last = [add_low(*terms)[0] for terms, _ in parts]
+    ffn_last, grads = after((ffn_last, grads))
+    up_column = send_columns_chain(ffn_last[0])
+    attn_keep, attn_send = collect(windows_flat, grads, out_part)
+    attn_keep, attn_send, up_column, flows, owns, last_grads = after(
+        (attn_keep, attn_send, up_column, flows, owns, grads[-1])
+    )
+    last = flow_of(*last_grads)
+    owns.append(last[0])
+    last = list(last[1])
+    attn_received = swap(attn_send, "dp", 1)
+    down_column = send_columns_chain(after(ffn_last[1], attn_keep))
+    came = leave(last, reach) if reach > 1 else ()
+    attn_received, down_column, came = after((attn_received, down_column, came))
+    attn_held = to_blocks(add_low(attn_keep, attn_received))
+    if reach > 1:
+        join(last, reach - 1, came)
+    flow = [jnp.stack(pair) for pair in zip(*flows, last)]
+    attn_held, flow = after((attn_held, flow))
+    attn_received = send_plane(attn_held)
+    for n in range(reach - 1, 0, -1):
+        came = leave(flow, n)
+        join(flow, n - 1, came)
+    attn_received, came = after((attn_received, came))
+    attn_last = add_low(attn_held[:, 0], *attn_received)
+    attn_columns = send_columns(attn_last)
+    normed_one_grad = jnp.stack(owns) + came[0].astype(F32) + came[1].astype(F32)
+    normed_one_grad = normed_one_grad.reshape(micro_count * rows, D)
+    ffn_column, ffn_last = after((jnp.stack([up_column, down_column]), jnp.stack(ffn_last)), *attn_received)
+    ffn_reduced = finish_columns_chain(ffn_last, ffn_column)
     gain_one = jnp.sum(normed_one_grad * token_rows * factor_one, axis=0)
     tokens_grad = hidden_one_grad + norm_back(token_rows, factor_one, normed_one_grad * gains[0])
     tokens_grad = dot(tokens_grad, turn_wide, NT, HIGHEST)
+    attn_columns, tokens_grad, gain_one = after((attn_columns, tokens_grad, gain_one))
+    attn_reduced = add_columns(attn_last, attn_columns)
 
     bias_sum = sum(bias_parts)
     heads = table.shape[1]
@@ -613,33 +972,25 @@
         + (buckets == 15).astype(F32)[:, None] * jnp.sum(bias_sum[:, 1], axis=1)[None, :]
         + (buckets == 31).astype(F32)[:, None] * jnp.sum(bias_sum[:, 2], axis=1)[None, :]
     )
-    full_table = jnp.zeros_like(bias_table)
-    for k in range(narrow_count):
-        full_table = lax.dynamic_update_slice_in_dim(
-            full_table,
-            table_grad[:, k * heads_part : (k + 1) * heads_part],
-            (narrow_rank ^ k) * heads_part,
-            1,
-        )
+    full_table = dot(table_grad, head_turn, NT, HIGHEST)
     gains_part = dot(jnp.stack([gain_one, gain_two, gain_three]), turn_wide, NT, HIGHEST)
-    small = jnp.concatenate(
-        [gains_part, jnp.pad(full_table.reshape(1, -1), ((0, 0), (0, D - full_table.size)))]
-    )
-    small = sum_over(sum_over(small, "dp"), "mp")
-    gains_grad = small[:3]
-    table_full_grad = small[3, : full_table.size].reshape(full_table.shape)
     local_squares = (
         jnp.sum(attn_reduced * attn_reduced)
         + jnp.sum(ffn_reduced * ffn_reduced)
         + jnp.sum(proj_reduced * proj_reduced)
     )
-    total_squares = sum_over(
-        sum_over(jnp.broadcast_to(local_squares, (8, 128)), "dp"), "mp"
-    )[0, 0]
+    small = jnp.concatenate(
+        [
+            gains_part,
+            jnp.pad(full_table.reshape(1, -1), ((0, 0), (0, D - full_table.size))),
+            jnp.broadcast_to(local_squares, (4, D)),
+        ]
+    )
+    small = sum_over(sum_over(small, "dp"), "mp")
+    gains_grad = small[:3]
+    table_full_grad = small[3, : full_table.size].reshape(full_table.shape)
     total_squares = (
-        total_squares
-        + jnp.sum(gains_grad * gains_grad)
-        + jnp.sum(table_full_grad * table_full_grad)
+        small[4, 0] + jnp.sum(gains_grad * gains_grad) + jnp.sum(table_full_grad * table_full_grad)
     )
     grad_norm = jnp.sqrt(total_squares)
     factor = jnp.minimum(1.0, CLIP_NORM / (grad_norm + 1e-06))

time: 492 us -> 428 us (0.87)
  matrix products: 82.7 us -> 38.1 us
  waiting for transfers between devices: 152 us -> 111 us
  Pallas kernels: 53.5 us -> 94.3 us
  starting transfers between devices: 102 us -> 73.8 us
  other arithmetic: 45.4 us -> 64 us
  between operations: 22 us -> 8.16 us
    dot_general x37 -> x24, matrix products: 78.7 us -> 36 us  [dot(): lax.dot_general(left, right, dims, precision=precision, preferred_element...]
    pallas_call x0 -> x6, Pallas kernels: none -> 41.5 us  [the longest x1 15.5 us: feed_back(): pl.pallas_call(feed_back_kernel, grid=(units // chunk,), in_specs=[same_b...]
    ppermute x16 -> x12, starting transfers between devices: 51.9 us -> 16.6 us  [link(): return lax.ppermute(values, 'mp', pairs + [(j, i) for i, j in pairs])]
    ppermute x16 -> x12, waiting for transfers between devices: 37.7 us -> 15.6 us  [link(): return lax.ppermute(values, 'mp', pairs + [(j, i) for i, j in pairs])]
    ppermute x54 -> x46, waiting for transfers between devices: 114 us -> 95.8 us  [swap(): return lax.ppermute(values, axis, [(i, i ^ mask) for i in range(count)])]
    convert_element_type x4 -> x10, other arithmetic: 3.09 us -> 15.1 us  [the longest x8 13.8 us: add_low(): sum([part.astype(F32) for part in received], stay.astype(F32)).astype(BF16)]
    unnamed x216 -> x256, local copies, waits for them, and re-layouts: 8.76 us -> 18.6 us
    reshape x4 -> x0, local copies, waits for them, and re-layouts: 7.39 us -> none  [the longest x2 4.68 us: local(): proj_all = proj_all.transpose(0, 2, 1, 3).reshape(D, D)]
  transfers between devices with their start and end apart: 71 -> 58, of which waited for: 30 -> 29; matrix products, arithmetic and copies ran while one was open for 21% -> 18% of each run, Pallas kernels for 8% -> 18%
where the time goes in v2:
time: 428 us; the launch traced here: 420 us
  waiting for transfers between devices  111 us (26%)
  Pallas kernels  94.3 us (22%)
  starting transfers between devices  73.8 us (17%)
  other arithmetic  64 us (15%)
  matrix products  38.1 us (9%)
  local copies, waits for them, and re-layouts  30.7 us (7%)
  between operations  8.16 us (2%)
    ppermute x46, waiting for transfers between devices, swap(): return lax.ppermute(values, axis, [(i, i ^ mask) for i in range(count)])  95.8 us
    ppermute x46, starting transfers between devices, swap(): return lax.ppermute(values, axis, [(i, i ^ mask) for i in range(count)])  57.2 us
    dot_general x24, matrix products, dot(): lax.dot_general(left, right, dims, precision=precision, preferred_element...  36 us
    pallas_call x2, Pallas kernels, attend_back(): pl.pallas_call(functools.partial(backward_kernel, reach), grid=(pairs,),...  26.3 us
    pallas_call x2, Pallas kernels, attend(): pl.pallas_call(functools.partial(forward_kernel, reach), grid=(pairs,), i...  19.1 us
    unnamed x256, local copies, waits for them, and re-layouts  18.6 us
    ppermute x12, starting transfers between devices, link(): return lax.ppermute(values, 'mp', pairs + [(j, i) for i, j in pairs])  16.6 us
    ppermute x12, waiting for transfers between devices, link(): return lax.ppermute(values, 'mp', pairs + [(j, i) for i, j in pairs])  15.6 us
  transfers between devices with their start and end apart: 58, of which 29 were waited for; matrix products, arithmetic and copies ran while one was open for 18% of the time, Pallas kernels for 18%

profile of v2, /device:TPU:0, one launch (start us, length us, event | category | flops | bytes accessed | tf_op | source)
XLA Modules:
  0.0 420.5 jit_solution(12814685822002320920)
XLA Ops:
  1.8 3.1 collective-permute-start
  4.9 2.6 collective-permute-start.1
  7.4 1.8 convert_element_type.523
  11.2 2.1 fusion.12
  18.5 1.9 slice_dynamic-update-slice_fusion
  20.4 4.2 %collective-permute-done.3 = bf16[2,96,768]{2,1,0:T(8,128)(2,1)} collective-permute-done((bf16[2,96,768]{2,1,0:T(8,128)(2,1)}, bf16[2,96,768]{2,1,0:T(8,128)(2,1)}, u32[]{:S(2)}, u32[]{:S(2)}) %collective-permute-start.3) | collective-permute-done | bytes 294944 | tf_op jit(solution)/shard_map/ppermute | solution.py:71
  27.0 2.7 collective-permute-start.6
  30.6 2.8 collective-permute-start.7
  34.1 7.3 %shard_map.322.bias_ref = f32[12,3,256,256]{3,2,1,0:T(8,128)} custom-call(f32[12,3,512]{2,1,0:T(4,128)S(1)} %copy.110.line_ref), custom_call_target="tpu_custom_call" | custom-call | tf_op jit(solution)/shard_map/pallas_call | solution.py:215
  44.3 10.8 %collective-permute-done.5 = bf16[4,96,768]{2,1,0:T(8,128)(2,1)S(1)} collective-permute-done((bf16[4,96,768]{2,1,0:T(8,128)(2,1)S(1)}, bf16[4,96,768]{2,1,0:T(8,128)(2,1)S(1)}, u32[]{:S(2)}, u32[]{:S(2)}) %collective-permute-start.5) | collective-permute-done | bytes 589856 | tf_op jit(solution)/shard_map/ppermute | solution.py:71
  55.1 1.7 pad_maximum_fusion.1
  65.9 12.5 %collective-permute-done.11 = bf16[1,96,3072]{2,1,0:T(8,128)(2,1)S(1)} collective-permute-done((bf16[1,96,3072]{2,1,0:T(8,128)(2,1)S(1)}, bf16[1,96,3072]{2,1,0:T(8,128)(2,1)S(1)}, u32[]{:S(2)}, u32[]{:S(2)}) %collective-permute-start.11) | collective-permute-done | bytes 589856 | tf_op jit(solution)/shard_map/ppermute | solution.py:71
  80.1 2.6 fusion.30
  83.7 4.4 %collective-permute-start.13 = (bf16[256,768]{1,0:T(8,128)(2,1)S(1)}, bf16[256,768]{1,0:T(8,128)(2,1)S(1)}, u32[]{:S(2)}, u32[]{:S(2)}) collective-permute-start(bf16[256,768]{1,0:T(8,128)(2,1)S(1)} %get-tuple-element.180), channel_id=1, source_target_pairs={{0,1},{2,3},{1,0},{3,2},{4,5},{6,7},{5,4},{7,6},{8,9},{10,11},{9,8... | collective-permute-start | bytes 1179656 | tf_op jit(solution)/shard_map/ppermute | solution.py:77
  90.3 6.8 %collective-permute-done.13 = bf16[256,768]{1,0:T(8,128)(2,1)S(1)} collective-permute-done((bf16[256,768]{1,0:T(8,128)(2,1)S(1)}, bf16[256,768]{1,0:T(8,128)(2,1)S(1)}, u32[]{:S(2)}, u32[]{:S(2)}) %collective-permute-start.13) | collective-permute-done | bytes 393248 | tf_op jit(solution)/shard_map/ppermute | solution.py:77
  97.1 3.6 collective-permute-start.17
  102.5 3.4 convolution_convert_fusion.1.k_ref.v_ref
  109.5 8.9 %attend.2 = (bf16[256,768]{1,0:T(8,128)(2,1)S(1)}, f32[6,8,256]{2,1,0:T(8,128)S(1)}) custom-call(s32[7]{0:T(128)S(1)} %get-tuple-element.459.range_ref, f32[2,12]{1,0:T(2,128)S(1)} %pad_maximum_fusion.20.far_ref, bf16[256,768]{1,0:T(8,128)(2,1)S(1)} %convolution_convert_fusion.5.q_ref, bf16[1280,1536]{1,0:T(8,128)(2,1)S(1)} %convolution_convert_fusion.1.k_ref.v_ref, ...), custom_call_target="tpu_custom_call" | custom-call | flops 100000 | bytes 10000 | tf_op jit(solution)/shard_map/attend/pallas_call | solution.py:397
  119.2 1.6 convolution_convert_fusion.4.q_ref
  124.1 3.5 convolution_convert_fusion.k_ref.v_ref
  127.6 2.0 collective-permute-start.19
  132.1 10.2 %attend.3 = (bf16[256,768]{1,0:T(8,128)(2,1)S(1)}, f32[6,8,256]{2,1,0:T(8,128)S(1)}) custom-call(s32[7]{0:T(128)S(1)} %get-tuple-element.458.range_ref, f32[2,12]{1,0:T(2,128)S(1)} %pad_maximum_fusion.20.far_ref, bf16[256,768]{1,0:T(8,128)(2,1)S(1)} %convolution_convert_fusion.4.q_ref, bf16[1280,1536]{1,0:T(8,128)(2,1)S(1)} %convolution_convert_fusion.k_ref.v_ref, ...), custom_call_target="tpu_custom_call" | custom-call | flops 100000 | bytes 10000 | tf_op jit(solution)/shard_map/attend/pallas_call | solution.py:397
  144.1 1.8 pad_maximum_fusion.3
  147.1 2.3 collective-permute-start.24
  154.2 2.6 collective-permute-done.24
  159.0 11.1 %feed.1 = (f32[512,768]{1,0:T(8,128)S(1)}, bf16[512,3072]{1,0:T(8,128)(2,1)}, bf16[512,3072]{1,0:T(8,128)(2,1)}) custom-call(bf16[512,768]{1,0:T(8,128)(2,1)S(1)} %multiply_convert_fusion.normed_ref, f32[512,768]{1,0:T(8,128)S(1)} %bitcast_add_fusion.1.hidden_ref, bf16[2,384,3072]{2,1,0:T(8,128)(2,1)} %copy-done.39, ...), custom_call_target="tpu_custom_call" | custom-call | flops 100000 | bytes 10000 | tf_op jit(solution)/shard_map/feed/pallas_call | solution.py:535
  178.1 1.7 collective-permute-start.28
  180.6 2.5 collective-permute-done.28
  187.0 2.8 collective-permute-done.30
  192.1 2.5 collective-permute-done.31
  194.7 2.8 contrast.1
  200.4 15.5 %feed_back.1 = (f32[512,768]{1,0:T(8,128)S(1)}, bf16[2,384,3072]{2,1,0:T(8,128)(2,1)}, bf16[2,384,3072]{2,1,0:T(8,128)(2,1)}) custom-call(bf16[512,768]{1,0:T(8,128)(2,1)S(1)} %multiply_convert_fusion.normed_ref, bf16[512,768]{1,0:T(8,128)(2,1)S(1)} %get-tuple-element.462.up_ref, bf16[2,384,3072]{2,1,0:T(8,128)(2,1)} %copy-done.39, ...), custom_call_target="tpu_custom_call" | custom-call | flops 100000 | bytes 10000 | tf_op jit(solution)/shard_map/feed_back/pallas_call | solution.py:557
  220.9 3.1 collective-permute-done.32
  224.3 1.8 fusion.22
  230.0 12.0 %attend_back.2 = (bf16[256,768]{1,0:T(8,128)(2,1)S(1)}, bf16[1280,768]{1,0:T(8,128)(2,1)S(1)}, bf16[1280,768]{1,0:T(8,128)(2,1)S(1)}, f32[6,2,8,256]{3,2,1,0:T(8,128)S(1)}) custom-call(s32[7]{0:T(128)S(1)} %get-tuple-element.459.range_ref, f32[2,12]{1,0:T(2,128)S(1)} %pad_maximum_fusion.20.far_ref, bf16[256,768]{1,0:T(8,128)(2,1)S(1)} %copy-done.29, ...), custom_call_target="tpu_custom_call" | custom-call | flops 100000 | bytes 10000 | tf_op jit(solution)/shard_map/attend_back/pallas_call | solution.py:417
  242.0 1.7 fusion.49
  243.9 1.9 fusion.149
  249.8 6.4 %collective-permute-done.33 = bf16[2,96,3072]{2,1,0:T(8,128)(2,1)} collective-permute-done((bf16[2,96,3072]{2,1,0:T(8,128)(2,1)}, bf16[2,96,3072]{2,1,0:T(8,128)(2,1)}, u32[]{:S(2)}, u32[]{:S(2)}) %collective-permute-start.33) | collective-permute-done | bytes 1179680 | tf_op jit(solution)/shard_map/ppermute | solution.py:71
  257.0 2.1 fusion.59
  259.1 2.2 fusion.60
  266.1 14.3 %attend_back.3 = (bf16[256,768]{1,0:T(8,128)(2,1)S(1)}, bf16[1280,768]{1,0:T(8,128)(2,1)S(1)}, bf16[1280,768]{1,0:T(8,128)(2,1)S(1)}, f32[6,2,8,256]{3,2,1,0:T(8,128)S(1)}) custom-call(s32[7]{0:T(128)S(1)} %get-tuple-element.458.range_ref, f32[2,12]{1,0:T(2,128)S(1)} %pad_maximum_fusion.20.far_ref, bf16[256,768]{1,0:T(8,128)(2,1)S(1)} %copy-done.27, ...), custom_call_target="tpu_custom_call" | custom-call | flops 100000 | bytes 10000 | tf_op jit(solution)/shard_map/attend_back/pallas_call | solution.py:417
  284.2 1.8 fusion.62
  286.1 5.4 %collective-permute-start.39 = (bf16[96,1536]{1,0:T(8,128)(2,1)S(1)}, bf16[96,1536]{1,0:T(8,128)(2,1)S(1)}, u32[]{:S(2)}, u32[]{:S(2)}) collective-permute-start(bf16[96,1536]{1,0:T(8,128)(2,1)S(1)} %slice.343), channel_id=1, source_target_pairs={{0,2},{1,3},{2,0},{3,1},{4,6},{5,7},{6,4},{7,5},{8,10},{9,11},{10,... | collective-permute-start | bytes 884744 | tf_op jit(solution)/shard_map/ppermute | solution.py:71
  292.6 10.3 %collect.1 = (bf16[4,384,768]{2,1,0:T(8,128)(2,1)}, bf16[4,384,768]{2,1,0:T(8,128)(2,1)}) custom-call(bf16[768,1280]{1,0:T(8,128)(2,1)S(1)} %copy-done.11, bf16[768,1280]{1,0:T(8,128)(2,1)S(1)} %copy-done.13, bf16[256,768]{1,0:T(8,128)(2,1)S(1)} %get-tuple-element.258.refs_2_, bf16[1280,768]{1,0:T(8,128)(2,1)} %copy-done.7, bf16[1280,768]{1,0:T(8,128)(2,1)} %copy-done.19, ...), custom_call_target="tpu_custom_call" | custom-call | flops 100000 | bytes 10000 | tf_op jit(solution)/shard_map/collect/pallas_call | solution.py:470
  302.9 2.0 add_convert_fusion.7
  308.8 1.7 fusion.47
  310.9 3.7 fusion.150
  317.4 4.5 %collective-permute-done.41 = bf16[96,1536]{1,0:T(8,128)(2,1)} collective-permute-done((bf16[96,1536]{1,0:T(8,128)(2,1)}, bf16[96,1536]{1,0:T(8,128)(2,1)}, u32[]{:S(2)}, u32[]{:S(2)}) %collective-permute-start.41) | collective-permute-done | bytes 294944 | tf_op jit(solution)/shard_map/ppermute | solution.py:71
  321.9 8.2 %collective-permute-done.42 = bf16[256,768]{1,0:T(8,128)(2,1)S(1)} collective-permute-done((bf16[256,768]{1,0:T(8,128)(2,1)}, bf16[256,768]{1,0:T(8,128)(2,1)S(1)}, u32[]{:S(2)}, u32[]{:S(2)}) %collective-permute-start.42) | collective-permute-done | bytes 393248 | tf_op jit(solution)/shard_map/ppermute | solution.py:77
  330.9 2.9 add_convert_fusion
  336.3 2.6 collective-permute-start.46
  340.8 1.7 fusion.53
  343.5 8.1 %collective-permute-done.44 = bf16[4,96,768]{2,1,0:T(8,128)(2,1)S(1)} collective-permute-done((bf16[4,96,768]{2,1,0:T(8,128)(2,1)S(1)}, bf16[4,96,768]{2,1,0:T(8,128)(2,1)S(1)}, u32[]{:S(2)}, u32[]{:S(2)}) %collective-permute-start.44) | collective-permute-done | bytes 589856 | tf_op jit(solution)/shard_map/ppermute | solution.py:71
  351.6 12.3 %collective-permute-done.45 = bf16[4,96,768]{2,1,0:T(8,128)(2,1)S(1)} collective-permute-done((bf16[4,96,768]{2,1,0:T(8,128)(2,1)S(1)}, bf16[4,96,768]{2,1,0:T(8,128)(2,1)S(1)}, u32[]{:S(2)}, u32[]{:S(2)}) %collective-permute-start.45) | collective-permute-done | bytes 589856 | tf_op jit(solution)/shard_map/ppermute | solution.py:71
  364.5 3.2 collective-permute-start.50
  372.2 3.7 fusion.1
  375.9 6.0 %collective-permute-done.50 = bf16[4,96,192]{2,1,0:T(8,128)(2,1)S(1)} collective-permute-done((bf16[4,96,192]{2,1,0:T(8,128)(2,1)S(1)}, bf16[4,96,192]{2,1,0:T(8,128)(2,1)S(1)}, u32[]{:S(2)}, u32[]{:S(2)}) %collective-permute-start.50) | collective-permute-done | bytes 147488 | tf_op jit(solution)/shard_map/ppermute | solution.py:71
  392.4 2.6 collective-permute-done.54
  396.3 2.6 collective-permute-done.55
  400.5 2.2 collective-permute-done.56
  402.7 2.6 collective-permute-start.57
  405.3 1.7 fusion.21
  411.5 2.9 multiply_subtract_fusion.1
  414.4 1.6 multiply_subtract_fusion.2
  (478 shorter events, 126.1 us)
Async XLA Ops:
  0.7 198.7 %copy-start = (bf16[2,1,256,768]{3,2,1,0:T(8,128)(2,1)S(1)}, bf16[2,1,256,768]{3,2,1,0:T(8,128)(2,1)}, u32[]{:S(2)}) copy-start(bf16[2,1,256,768]{3,2,1,0:T(8,128)(2,1)} %param.20) | copy-start | bytes 2359300
  1.8 23.9 %collective-permute-start = (bf16[4,96,192]{2,1,0:T(8,128)(2,1)S(1)}, bf16[4,96,192]{2,1,0:T(8,128)(2,1)S(1)}, u32[]{:S(2)}, u32[]{:S(2)}) collective-permute-start(bf16[4,96,192]{2,1,0:T(8,128)(2,1)S(1)} %convert_element_type.522), channel_id=1, source_target_pairs={{0,1},{1,0},{2,3},{3,2},{4,5},{5,4},{6,7},{7,6},{8,9},{9,8},{10,11... | collective-permute-start | bytes 442376 | tf_op jit(solution)/shard_map/ppermute | solution.py:71
  4.9 20.9 %collective-permute-start.1 = (bf16[4,96,192]{2,1,0:T(8,128)(2,1)S(1)}, bf16[4,96,192]{2,1,0:T(8,128)(2,1)}, u32[]{:S(2)}, u32[]{:S(2)}) collective-permute-start(bf16[4,96,192]{2,1,0:T(8,128)(2,1)S(1)} %convert_element_type.522), channel_id=1, source_target_pairs={{0,2},{1,3},{2,0},{3,1},{4,6},{5,7},{6,4},{7,5},{8,10},{9,11},{10,... | collective-permute-start | bytes 442376 | tf_op jit(solution)/shard_map/ppermute | solution.py:71
  7.4 18.3 %collective-permute-start.2 = (bf16[4,96,192]{2,1,0:T(8,128)(2,1)S(1)}, bf16[4,96,192]{2,1,0:T(8,128)(2,1)}, u32[]{:S(2)}, u32[]{:S(2)}) collective-permute-start(bf16[4,96,192]{2,1,0:T(8,128)(2,1)S(1)} %convert_element_type.522), channel_id=1, source_target_pairs={{0,3},{1,2},{2,1},{3,0},{4,7},{5,6},{6,5},{7,4},{8,11},{9,10},{10,... | collective-permute-start | bytes 442376 | tf_op jit(solution)/shard_map/ppermute | solution.py:71
  9.3 15.4 %collective-permute-start.3 = (bf16[2,96,768]{2,1,0:T(8,128)(2,1)}, bf16[2,96,768]{2,1,0:T(8,128)(2,1)}, u32[]{:S(2)}, u32[]{:S(2)}) collective-permute-start(bf16[2,96,768]{2,1,0:T(8,128)(2,1)} %convert_element_type.523), channel_id=1, source_target_pairs={{0,1},{1,0},{2,3},{3,2},{4,5},{5,4},{6,7},{7,6},{8,9},{9,8},{10,11... | collective-permute-start | bytes 884744 | tf_op jit(solution)/shard_map/ppermute | solution.py:71
  27.0 17.3 %collective-permute-start.6 = (bf16[4,96,768]{2,1,0:T(8,128)(2,1)S(1)}, bf16[4,96,768]{2,1,0:T(8,128)(2,1)S(1)}, u32[]{:S(2)}, u32[]{:S(2)}) collective-permute-start(bf16[4,96,768]{2,1,0:T(8,128)(2,1)S(1)} %pad_maximum_fusion.12), channel_id=1, source_target_pairs={{0,24},{4,28},{8,16},{12,20},{16,8},{20,12},{24,0},{28,4},{1,25},{... | collective-permute-start | bytes 1769480 | tf_op jit(solution)/shard_map/ppermute | solution.py:71
  29.7 25.4 %collective-permute-start.5 = (bf16[4,96,768]{2,1,0:T(8,128)(2,1)S(1)}, bf16[4,96,768]{2,1,0:T(8,128)(2,1)S(1)}, u32[]{:S(2)}, u32[]{:S(2)}) collective-permute-start(bf16[4,96,768]{2,1,0:T(8,128)(2,1)S(1)} %pad_maximum_fusion.12), channel_id=1, source_target_pairs={{0,16},{4,20},{8,24},{12,28},{16,0},{20,4},{24,8},{28,12},{1,17},{... | collective-permute-start | bytes 1769480 | tf_op jit(solution)/shard_map/ppermute | solution.py:71
  30.2 24.9 %collective-permute-start.4 = (bf16[4,96,768]{2,1,0:T(8,128)(2,1)S(1)}, bf16[4,96,768]{2,1,0:T(8,128)(2,1)S(1)}, u32[]{:S(2)}, u32[]{:S(2)}) collective-permute-start(bf16[4,96,768]{2,1,0:T(8,128)(2,1)S(1)} %pad_maximum_fusion.12), channel_id=1, source_target_pairs={{0,8},{4,12},{8,0},{12,4},{16,24},{20,28},{24,16},{28,20},{1,9},{5... | collective-permute-start | bytes 1769480 | tf_op jit(solution)/shard_map/ppermute | solution.py:71
  30.6 27.2 %collective-permute-start.7 = (bf16[2,96,1536]{2,1,0:T(8,128)(2,1)S(1)}, bf16[2,96,1536]{2,1,0:T(8,128)(2,1)S(1)}, u32[]{:S(2)}, u32[]{:S(2)}) collective-permute-start(bf16[2,96,1536]{2,1,0:T(8,128)(2,1)S(1)} %pad_maximum_fusion.11), channel_id=1, source_target_pairs={{0,2},{1,3},{2,0},{3,1},{4,6},{5,7},{6,4},{7,5},{8,10},{9,11},{10,... | collective-permute-start | bytes 1769480 | tf_op jit(solution)/shard_map/ppermute | solution.py:71
  59.0 21.2 %collective-permute-start.8 = (bf16[4,384,768]{2,1,0:T(8,128)(2,1)}, bf16[4,384,768]{2,1,0:T(8,128)(2,1)}, u32[]{:S(2)}, u32[]{:S(2)}) collective-permute-start(bf16[4,384,768]{2,1,0:T(8,128)(2,1)} %bitcast.12), channel_id=1, source_target_pairs={{0,4},{4,0},{8,12},{12,8},{16,20},{20,16},{24,28},{28,24},{1,5},{5... | collective-permute-start | bytes 7077896 | tf_op jit(solution)/shard_map/ppermute | solution.py:71
  59.2 112.4 %copy-start.91 = (s32[2,256]{1,0:T(2,128)}, s32[2,256]{1,0:T(2,128)S(1)}, u32[]{:S(2)}) copy-start(s32[2,256]{1,0:T(2,128)S(1)} %pad_dynamic-slice_fusion) | copy-start | bytes 6148
  59.4 50.1 %copy-start.30 = (bf16[256,128]{1,0:T(8,128)(2,1)}, bf16[256,128]{1,0:T(8,128)(2,1)S(1)}, u32[]{:S(2)}) copy-start(bf16[256,128]{1,0:T(8,128)(2,1)S(1)} %get-tuple-element.444.qf_ref) | copy-start | bytes 196612
  59.9 20.2 %collective-permute-start.9 = (bf16[2,256,768]{2,1,0:T(8,128)(2,1)}, bf16[2,256,768]{2,1,0:T(8,128)(2,1)S(1)}, u32[]{:S(2)}, u32[]{:S(2)}) collective-permute-start(bf16[2,256,768]{2,1,0:T(8,128)(2,1)} %bitcast.270), channel_id=1, source_target_pairs={{0,1},{2,3},{1,0},{3,2},{4,5},{6,7},{5,4},{7,6},{8,9},{10,11},{9,8... | collective-permute-start | bytes 2359304 | tf_op jit(solution)/shard_map/ppermute | solution.py:77
  60.7 19.5 %collective-permute-start.10 = (bf16[2,256,768]{2,1,0:T(8,128)(2,1)}, bf16[2,256,768]{2,1,0:T(8,128)(2,1)S(1)}, u32[]{:S(2)}, u32[]{:S(2)}) collective-permute-start(bf16[2,256,768]{2,1,0:T(8,128)(2,1)} %bitcast.271), channel_id=1, source_target_pairs={{1,2},{2,1},{5,6},{6,5},{9,10},{10,9},{13,14},{14,13},{17,18},{18,... | collective-permute-start | bytes 2359304 | tf_op jit(solution)/shard_map/ppermute | solution.py:77
  62.8 15.5 %collective-permute-start.11 = (bf16[1,96,3072]{2,1,0:T(8,128)(2,1)S(1)}, bf16[1,96,3072]{2,1,0:T(8,128)(2,1)S(1)}, u32[]{:S(2)}, u32[]{:S(2)}) collective-permute-start(bf16[1,96,3072]{2,1,0:T(8,128)(2,1)S(1)} %get-tuple-element.427), channel_id=1, source_target_pairs={{0,8},{4,12},{8,0},{12,4},{16,24},{20,28},{24,16},{28,20},{1,9},{5... | collective-permute-start | bytes 1769480 | tf_op jit(solution)/shard_map/ppermute | solution.py:71
  64.4 15.2 %collective-permute-start.12 = (bf16[1,96,3072]{2,1,0:T(8,128)(2,1)S(1)}, bf16[1,96,3072]{2,1,0:T(8,128)(2,1)S(1)}, u32[]{:S(2)}, u32[]{:S(2)}) collective-permute-start(bf16[1,96,3072]{2,1,0:T(8,128)(2,1)S(1)} %get-tuple-element.426), channel_id=1, source_target_pairs={{0,16},{4,20},{8,24},{12,28},{16,0},{20,4},{24,8},{28,12},{1,17},{... | collective-permute-start | bytes 1769480 | tf_op jit(solution)/shard_map/ppermute | solution.py:71
  65.8 43.7 %copy-start.14 = (bf16[1280,128]{1,0:T(8,128)(2,1)}, bf16[1280,128]{1,0:T(8,128)(2,1)S(1)}, u32[]{:S(2)}) copy-start(bf16[1280,128]{1,0:T(8,128)(2,1)S(1)} %get-tuple-element.437.kf_ref) | copy-start | bytes 983044
  82.7 74.3 %copy-start.57 = (bf16[768,768]{1,0:T(8,128)(2,1)}, bf16[768,768]{1,0:T(8,128)(2,1)S(1)}, u32[]{:S(2)}) copy-start(bf16[768,768]{1,0:T(8,128)(2,1)S(1)} %get-tuple-element.408) | copy-start | bytes 3538948
  83.7 13.4 %collective-permute-start.13 = (bf16[256,768]{1,0:T(8,128)(2,1)S(1)}, bf16[256,768]{1,0:T(8,128)(2,1)S(1)}, u32[]{:S(2)}, u32[]{:S(2)}) collective-permute-start(bf16[256,768]{1,0:T(8,128)(2,1)S(1)} %get-tuple-element.180), channel_id=1, source_target_pairs={{0,1},{2,3},{1,0},{3,2},{4,5},{6,7},{5,4},{7,6},{8,9},{10,11},{9,8... | collective-permute-start | bytes 1179656 | tf_op jit(solution)/shard_map/ppermute | solution.py:77
  88.1 9.0 %collective-permute-start.14 = (bf16[256,768]{1,0:T(8,128)(2,1)S(1)}, bf16[256,768]{1,0:T(8,128)(2,1)S(1)}, u32[]{:S(2)}, u32[]{:S(2)}) collective-permute-start(bf16[256,768]{1,0:T(8,128)(2,1)S(1)} %get-tuple-element.179), channel_id=1, source_target_pairs={{1,2},{2,1},{5,6},{6,5},{9,10},{10,9},{13,14},{14,13},{17,18},{18,... | collective-permute-start | bytes 1179656 | tf_op jit(solution)/shard_map/ppermute | solution.py:77
  97.1 23.8 %collective-permute-start.17 = (bf16[256,768]{1,0:T(8,128)(2,1)}, bf16[256,768]{1,0:T(8,128)(2,1)}, u32[]{:S(2)}, u32[]{:S(2)}) collective-permute-start(bf16[256,768]{1,0:T(8,128)(2,1)} %get-tuple-element.195), channel_id=1, source_target_pairs={{0,1},{2,3},{1,0},{3,2},{4,5},{6,7},{5,4},{7,6},{8,9},{10,11},{9,8... | collective-permute-start | bytes 1179656 | tf_op jit(solution)/shard_map/ppermute | solution.py:77
  100.7 20.2 %collective-permute-start.18 = (bf16[256,768]{1,0:T(8,128)(2,1)S(1)}, bf16[256,768]{1,0:T(8,128)(2,1)}, u32[]{:S(2)}, u32[]{:S(2)}) collective-permute-start(bf16[256,768]{1,0:T(8,128)(2,1)S(1)} %get-tuple-element.194), channel_id=1, source_target_pairs={{1,2},{2,1},{5,6},{6,5},{9,10},{10,9},{13,14},{14,13},{17,18},{18,... | collective-permute-start | bytes 1179656 | tf_op jit(solution)/shard_map/ppermute | solution.py:77
  106.4 35.9 %collective-permute-start.15 = (bf16[2,96,3072]{2,1,0:T(8,128)(2,1)}, bf16[2,96,3072]{2,1,0:T(8,128)(2,1)}, u32[]{:S(2)}, u32[]{:S(2)}) collective-permute-start(bf16[2,96,3072]{2,1,0:T(8,128)(2,1)} %pad_maximum_fusion.7), channel_id=1, source_target_pairs={{0,16},{4,20},{8,24},{12,28},{16,0},{20,4},{24,8},{28,12},{1,17},{... | collective-permute-start | bytes 3538952 | tf_op jit(solution)/shard_map/ppermute | solution.py:71
  108.0 34.3 %collective-permute-start.16 = (bf16[2,96,3072]{2,1,0:T(8,128)(2,1)S(1)}, bf16[2,96,3072]{2,1,0:T(8,128)(2,1)}, u32[]{:S(2)}, u32[]{:S(2)}) collective-permute-start(bf16[2,96,3072]{2,1,0:T(8,128)(2,1)S(1)} %maximum_bitcast_fusion), channel_id=1, source_target_pairs={{0,8},{4,12},{8,0},{12,4},{16,24},{20,28},{24,16},{28,20},{1,9},{5... | collective-permute-start | bytes 3538952 | tf_op jit(solution)/shard_map/ppermute | solution.py:71
  119.2 37.7 %copy-start.24 = (bf16[256,768]{1,0:T(8,128)(2,1)}, bf16[256,768]{1,0:T(8,128)(2,1)S(1)}, u32[]{:S(2)}) copy-start(bf16[256,768]{1,0:T(8,128)(2,1)S(1)} %get-tuple-element.203.o_ref) | copy-start | bytes 1179652
  127.6 14.7 %collective-permute-start.19 = (bf16[96,192]{1,0:T(8,128)(2,1)S(1)}, bf16[96,192]{1,0:T(8,128)(2,1)S(1)}, u32[]{:S(2)}, u32[]{:S(2)}) collective-permute-start(bf16[96,192]{1,0:T(8,128)(2,1)S(1)} %copy-done.81), channel_id=1, source_target_pairs={{0,1},{1,0},{2,3},{3,2},{4,5},{5,4},{6,7},{7,6},{8,9},{9,8},{10,11... | collective-permute-start | bytes 110600 | tf_op jit(solution)/shard_map/ppermute | solution.py:71
  129.6 12.7 %collective-permute-start.20 = (bf16[96,192]{1,0:T(8,128)(2,1)S(1)}, bf16[96,192]{1,0:T(8,128)(2,1)S(1)}, u32[]{:S(2)}, u32[]{:S(2)}) collective-permute-start(bf16[96,192]{1,0:T(8,128)(2,1)S(1)} %copy-done.81), channel_id=1, source_target_pairs={{0,2},{1,3},{2,0},{3,1},{4,6},{5,7},{6,4},{7,5},{8,10},{9,11},{10,... | collective-permute-start | bytes 110600 | tf_op jit(solution)/shard_map/ppermute | solution.py:71
  130.6 11.7 %collective-permute-start.21 = (bf16[96,192]{1,0:T(8,128)(2,1)S(1)}, bf16[96,192]{1,0:T(8,128)(2,1)S(1)}, u32[]{:S(2)}, u32[]{:S(2)}) collective-permute-start(bf16[96,192]{1,0:T(8,128)(2,1)S(1)} %copy-done.81), channel_id=1, source_target_pairs={{0,3},{1,2},{2,1},{3,0},{4,7},{5,6},{6,5},{7,4},{8,11},{9,10},{10,... | collective-permute-start | bytes 110600 | tf_op jit(solution)/shard_map/ppermute | solution.py:71
  146.4 11.7 %collective-permute-start.22 = (bf16[2,384,3072]{2,1,0:T(8,128)(2,1)S(1)}, bf16[2,384,3072]{2,1,0:T(8,128)(2,1)}, u32[]{:S(2)}, u32[]{:S(2)}) collective-permute-start(bf16[2,384,3072]{2,1,0:T(8,128)(2,1)S(1)} %pad_maximum_fusion.near_ref), channel_id=1, source_target_pairs={{0,4},{4,0},{8,12},{12,8},{16,20},{20,16},{24,28},{28,24},{1,5},{5... | collective-permute-start | bytes 14155784 | tf_op jit(solution)/shard_map/ppermute | solution.py:71
  146.6 7.7 %collective-permute-start.25 = (bf16[1,96,768]{2,1,0:T(8,128)(2,1)S(1)}, bf16[1,96,768]{2,1,0:T(8,128)(2,1)S(1)}, u32[]{:S(2)}, u32[]{:S(2)}) collective-permute-start(bf16[1,96,768]{2,1,0:T(8,128)(2,1)S(1)} %get-tuple-element.442), channel_id=1, source_target_pairs={{0,24},{4,28},{8,16},{12,20},{16,8},{20,12},{24,0},{28,4},{1,25},{... | collective-permute-start | bytes 442376 | tf_op jit(solution)/shard_map/ppermute | solution.py:71
  147.1 9.7 %collective-permute-start.24 = (bf16[1,96,768]{2,1,0:T(8,128)(2,1)S(1)}, bf16[1,96,768]{2,1,0:T(8,128)(2,1)S(1)}, u32[]{:S(2)}, u32[]{:S(2)}) collective-permute-start(bf16[1,96,768]{2,1,0:T(8,128)(2,1)S(1)} %get-tuple-element.442), channel_id=1, source_target_pairs={{0,16},{4,20},{8,24},{12,28},{16,0},{20,4},{24,8},{28,12},{1,17},{... | collective-permute-start | bytes 442376 | tf_op jit(solution)/shard_map/ppermute | solution.py:71
  149.5 7.4 %collective-permute-start.23 = (bf16[1,96,768]{2,1,0:T(8,128)(2,1)S(1)}, bf16[1,96,768]{2,1,0:T(8,128)(2,1)S(1)}, u32[]{:S(2)}, u32[]{:S(2)}) collective-permute-start(bf16[1,96,768]{2,1,0:T(8,128)(2,1)S(1)} %get-tuple-element.442), channel_id=1, source_target_pairs={{0,8},{4,12},{8,0},{12,4},{16,24},{20,28},{24,16},{28,20},{1,9},{5... | collective-permute-start | bytes 442376 | tf_op jit(solution)/shard_map/ppermute | solution.py:71
  158.1 12.1 %collective-permute-start.26 = (bf16[1,384,768]{2,1,0:T(8,128)(2,1)S(1)}, bf16[1,384,768]{2,1,0:T(8,128)(2,1)S(1)}, u32[]{:S(2)}, u32[]{:S(2)}) collective-permute-start(bf16[1,384,768]{2,1,0:T(8,128)(2,1)S(1)} %bitcast.247), channel_id=1, source_target_pairs={{0,4},{4,0},{8,12},{12,8},{16,20},{20,16},{24,28},{28,24},{1,5},{5... | collective-permute-start | bytes 1769480 | tf_op jit(solution)/shard_map/ppermute | solution.py:71
  172.8 4.5 %collective-permute-start.27 = (f32[2,8,768]{2,1,0:T(8,128)}, f32[2,8,768]{2,1,0:T(8,128)}, u32[]{:S(2)}, u32[]{:S(2)}) collective-permute-start(f32[2,8,768]{2,1,0:T(8,128)} %fusion.84), channel_id=1, source_target_pairs={{0,1},{1,0},{2,3},{3,2},{4,5},{5,4},{6,7},{7,6},{8,9},{9,8},{10,11... | collective-permute-start | bytes 147464 | tf_op jit(solution)/shard_map/ppermute | solution.py:71
  178.1 5.0 %collective-permute-start.28 = (f32[2,8,768]{2,1,0:T(8,128)S(1)}, f32[2,8,768]{2,1,0:T(8,128)S(1)}, u32[]{:S(2)}, u32[]{:S(2)}) collective-permute-start(f32[2,8,768]{2,1,0:T(8,128)S(1)} %add.637), channel_id=1, source_target_pairs={{0,2},{1,3},{2,0},{3,1},{4,6},{5,7},{6,4},{7,5},{8,10},{9,11},{10,... | collective-permute-start | bytes 147464 | tf_op jit(solution)/shard_map/ppermute | solution.py:71
  184.3 1.2 collective-permute-start.29
  185.5 4.2 collective-permute-start.30
  189.7 4.9 %collective-permute-start.31 = (bf16[4,2,8,896]{3,2,1,0:T(8,128)(2,1)S(1)}, bf16[4,2,8,896]{3,2,1,0:T(8,128)(2,1)S(1)}, u32[]{:S(2)}, u32[]{:S(2)}) collective-permute-start(bf16[4,2,8,896]{3,2,1,0:T(8,128)(2,1)S(1)} %pad_maximum_fusion.17), channel_id=1, source_target_pairs={{0,16},{4,20},{8,24},{12,28},{16,0},{20,4},{24,8},{28,12},{1,17},{... | collective-permute-start | bytes 344072 | tf_op jit(solution)/shard_map/ppermute | solution.py:71
  215.9 8.1 %collective-permute-start.32 = (bf16[2,384,3072]{2,1,0:T(8,128)(2,1)}, bf16[2,384,3072]{2,1,0:T(8,128)(2,1)S(1)}, u32[]{:S(2)}, u32[]{:S(2)}) collective-permute-start(bf16[2,384,3072]{2,1,0:T(8,128)(2,1)} %get-tuple-element.224), channel_id=1, source_target_pairs={{0,4},{4,0},{8,12},{12,8},{16,20},{20,16},{24,28},{28,24},{1,5},{5... | collective-permute-start | bytes 14155784 | tf_op jit(solution)/shard_map/ppermute | solution.py:71
  227.9 28.3 %collective-permute-start.33 = (bf16[2,96,3072]{2,1,0:T(8,128)(2,1)}, bf16[2,96,3072]{2,1,0:T(8,128)(2,1)}, u32[]{:S(2)}, u32[]{:S(2)}) collective-permute-start(bf16[2,96,3072]{2,1,0:T(8,128)(2,1)} %fusion.22), channel_id=1, source_target_pairs={{0,16},{4,20},{8,24},{12,28},{16,0},{20,4},{24,8},{28,12},{1,17},{... | collective-permute-start | bytes 3538952 | tf_op jit(solution)/shard_map/ppermute | solution.py:71
  229.0 28.0 %collective-permute-start.34 = (bf16[2,96,3072]{2,1,0:T(8,128)(2,1)}, bf16[2,96,3072]{2,1,0:T(8,128)(2,1)}, u32[]{:S(2)}, u32[]{:S(2)}) collective-permute-start(bf16[2,96,3072]{2,1,0:T(8,128)(2,1)} %fusion.23), channel_id=1, source_target_pairs={{0,8},{4,12},{8,0},{12,4},{16,24},{20,28},{24,16},{28,20},{1,9},{5... | collective-permute-start | bytes 3538952 | tf_op jit(solution)/shard_map/ppermute | solution.py:71
  261.3 20.5 %collective-permute-start.35 = (bf16[1,96,3072]{2,1,0:T(8,128)(2,1)}, bf16[1,96,3072]{2,1,0:T(8,128)(2,1)S(1)}, u32[]{:S(2)}, u32[]{:S(2)}) collective-permute-start(bf16[1,96,3072]{2,1,0:T(8,128)(2,1)} %fusion.59), channel_id=1, source_target_pairs={{0,8},{4,12},{8,0},{12,4},{16,24},{20,28},{24,16},{28,20},{1,9},{5... | collective-permute-start | bytes 1769480 | tf_op jit(solution)/shard_map/ppermute | solution.py:71
  262.2 19.6 %collective-permute-start.36 = (bf16[1,96,3072]{2,1,0:T(8,128)(2,1)}, bf16[1,96,3072]{2,1,0:T(8,128)(2,1)S(1)}, u32[]{:S(2)}, u32[]{:S(2)}) collective-permute-start(bf16[1,96,3072]{2,1,0:T(8,128)(2,1)} %fusion.60), channel_id=1, source_target_pairs={{0,16},{4,20},{8,24},{12,28},{16,0},{20,4},{24,8},{28,12},{1,17},{... | collective-permute-start | bytes 1769480 | tf_op jit(solution)/shard_map/ppermute | solution.py:71
  263.6 18.1 %collective-permute-start.37 = (bf16[256,768]{1,0:T(8,128)(2,1)}, bf16[256,768]{1,0:T(8,128)(2,1)}, u32[]{:S(2)}, u32[]{:S(2)}) collective-permute-start(bf16[256,768]{1,0:T(8,128)(2,1)} %get-tuple-element.243), channel_id=1, source_target_pairs={{0,1},{2,3},{1,0},{3,2},{4,5},{6,7},{5,4},{7,6},{8,9},{10,11},{9,8... | collective-permute-start | bytes 1179656 | tf_op jit(solution)/shard_map/ppermute | solution.py:77
  264.7 17.1 %collective-permute-start.38 = (bf16[256,768]{1,0:T(8,128)(2,1)}, bf16[256,768]{1,0:T(8,128)(2,1)}, u32[]{:S(2)}, u32[]{:S(2)}) collective-permute-start(bf16[256,768]{1,0:T(8,128)(2,1)} %get-tuple-element.244), channel_id=1, source_target_pairs={{1,2},{2,1},{5,6},{6,5},{9,10},{10,9},{13,14},{14,13},{17,18},{18,... | collective-permute-start | bytes 1179656 | tf_op jit(solution)/shard_map/ppermute | solution.py:77
  286.1 18.9 %collective-permute-start.39 = (bf16[96,1536]{1,0:T(8,128)(2,1)S(1)}, bf16[96,1536]{1,0:T(8,128)(2,1)S(1)}, u32[]{:S(2)}, u32[]{:S(2)}) collective-permute-start(bf16[96,1536]{1,0:T(8,128)(2,1)S(1)} %slice.343), channel_id=1, source_target_pairs={{0,2},{1,3},{2,0},{3,1},{4,6},{5,7},{6,4},{7,5},{8,10},{9,11},{10,... | collective-permute-start | bytes 884744 | tf_op jit(solution)/shard_map/ppermute | solution.py:71
  304.9 25.2 %collective-permute-start.40 = (bf16[4,384,768]{2,1,0:T(8,128)(2,1)}, bf16[4,384,768]{2,1,0:T(8,128)(2,1)}, u32[]{:S(2)}, u32[]{:S(2)}) collective-permute-start(bf16[4,384,768]{2,1,0:T(8,128)(2,1)} %get-tuple-element.274), channel_id=1, source_target_pairs={{0,4},{4,0},{8,12},{12,8},{16,20},{20,16},{24,28},{28,24},{1,5},{5... | collective-permute-start | bytes 7077896 | tf_op jit(solution)/shard_map/ppermute | solution.py:71
  308.6 13.2 %collective-permute-start.41 = (bf16[96,1536]{1,0:T(8,128)(2,1)}, bf16[96,1536]{1,0:T(8,128)(2,1)}, u32[]{:S(2)}, u32[]{:S(2)}) collective-permute-start(bf16[96,1536]{1,0:T(8,128)(2,1)} %slice.344), channel_id=1, source_target_pairs={{0,2},{1,3},{2,0},{3,1},{4,6},{5,7},{6,4},{7,5},{8,10},{9,11},{10,... | collective-permute-start | bytes 884744 | tf_op jit(solution)/shard_map/ppermute | solution.py:71
  315.5 14.6 %collective-permute-start.42 = (bf16[256,768]{1,0:T(8,128)(2,1)}, bf16[256,768]{1,0:T(8,128)(2,1)S(1)}, u32[]{:S(2)}, u32[]{:S(2)}) collective-permute-start(bf16[256,768]{1,0:T(8,128)(2,1)} %get-tuple-element.418), channel_id=1, source_target_pairs={{0,1},{2,3},{1,0},{3,2},{4,5},{6,7},{5,4},{7,6},{8,9},{10,11},{9,8... | collective-permute-start | bytes 1179656 | tf_op jit(solution)/shard_map/ppermute | solution.py:77
  315.5 14.6 %collective-permute-start.43 = (bf16[256,768]{1,0:T(8,128)(2,1)}, bf16[256,768]{1,0:T(8,128)(2,1)S(1)}, u32[]{:S(2)}, u32[]{:S(2)}) collective-permute-start(bf16[256,768]{1,0:T(8,128)(2,1)} %get-tuple-element.417), channel_id=1, source_target_pairs={{1,2},{2,1},{5,6},{6,5},{9,10},{10,9},{13,14},{14,13},{17,18},{18,... | collective-permute-start | bytes 1179656 | tf_op jit(solution)/shard_map/ppermute | solution.py:77
  335.4 16.2 %collective-permute-start.44 = (bf16[4,96,768]{2,1,0:T(8,128)(2,1)S(1)}, bf16[4,96,768]{2,1,0:T(8,128)(2,1)S(1)}, u32[]{:S(2)}, u32[]{:S(2)}) collective-permute-start(bf16[4,96,768]{2,1,0:T(8,128)(2,1)S(1)} %get-tuple-element.414), channel_id=1, source_target_pairs={{0,8},{4,12},{8,0},{12,4},{16,24},{20,28},{24,16},{28,20},{1,9},{5... | collective-permute-start | bytes 1769480 | tf_op jit(solution)/shard_map/ppermute | solution.py:71
  336.3 27.7 %collective-permute-start.45 = (bf16[4,96,768]{2,1,0:T(8,128)(2,1)S(1)}, bf16[4,96,768]{2,1,0:T(8,128)(2,1)S(1)}, u32[]{:S(2)}, u32[]{:S(2)}) collective-permute-start(bf16[4,96,768]{2,1,0:T(8,128)(2,1)S(1)} %get-tuple-element.413), channel_id=1, source_target_pairs={{0,16},{4,20},{8,24},{12,28},{16,0},{20,4},{24,8},{28,12},{1,17},{... | collective-permute-start | bytes 1769480 | tf_op jit(solution)/shard_map/ppermute | solution.py:71
  336.3 27.7 %collective-permute-start.46 = (bf16[4,96,768]{2,1,0:T(8,128)(2,1)S(1)}, bf16[4,96,768]{2,1,0:T(8,128)(2,1)S(1)}, u32[]{:S(2)}, u32[]{:S(2)}) collective-permute-start(bf16[4,96,768]{2,1,0:T(8,128)(2,1)S(1)} %get-tuple-element.412), channel_id=1, source_target_pairs={{0,24},{4,28},{8,16},{12,20},{16,8},{20,12},{24,0},{28,4},{1,25},{... | collective-permute-start | bytes 1769480 | tf_op jit(solution)/shard_map/ppermute | solution.py:71
  338.9 25.0 %collective-permute-start.47 = (bf16[2,256,768]{2,1,0:T(8,128)(2,1)S(1)}, bf16[2,256,768]{2,1,0:T(8,128)(2,1)S(1)}, u32[]{:S(2)}, u32[]{:S(2)}) collective-permute-start(bf16[2,256,768]{2,1,0:T(8,128)(2,1)S(1)} %pad_maximum_fusion.9), channel_id=1, source_target_pairs={{0,1},{2,3},{1,0},{3,2},{4,5},{6,7},{5,4},{7,6},{8,9},{10,11},{9,8... | collective-permute-start | bytes 2359304 | tf_op jit(solution)/shard_map/ppermute | solution.py:77
  339.7 24.3 %collective-permute-start.48 = (bf16[2,256,768]{2,1,0:T(8,128)(2,1)S(1)}, bf16[2,256,768]{2,1,0:T(8,128)(2,1)S(1)}, u32[]{:S(2)}, u32[]{:S(2)}) collective-permute-start(bf16[2,256,768]{2,1,0:T(8,128)(2,1)S(1)} %pad_maximum_fusion.10), channel_id=1, source_target_pairs={{1,2},{2,1},{5,6},{6,5},{9,10},{10,9},{13,14},{14,13},{17,18},{18,... | collective-permute-start | bytes 2359304 | tf_op jit(solution)/shard_map/ppermute | solution.py:77
  364.5 11.5 %collective-permute-start.49 = (bf16[4,96,192]{2,1,0:T(8,128)(2,1)S(1)}, bf16[4,96,192]{2,1,0:T(8,128)(2,1)S(1)}, u32[]{:S(2)}, u32[]{:S(2)}) collective-permute-start(bf16[4,96,192]{2,1,0:T(8,128)(2,1)S(1)} %get-tuple-element.440), channel_id=1, source_target_pairs={{0,1},{1,0},{2,3},{3,2},{4,5},{5,4},{6,7},{7,6},{8,9},{9,8},{10,11... | collective-permute-start | bytes 442376 | tf_op jit(solution)/shard_map/ppermute | solution.py:71
  364.5 17.4 %collective-permute-start.50 = (bf16[4,96,192]{2,1,0:T(8,128)(2,1)S(1)}, bf16[4,96,192]{2,1,0:T(8,128)(2,1)S(1)}, u32[]{:S(2)}, u32[]{:S(2)}) collective-permute-start(bf16[4,96,192]{2,1,0:T(8,128)(2,1)S(1)} %get-tuple-element.439), channel_id=1, source_target_pairs={{0,2},{1,3},{2,0},{3,1},{4,6},{5,7},{6,4},{7,5},{8,10},{9,11},{10,... | collective-permute-start | bytes 442376 | tf_op jit(solution)/shard_map/ppermute | solution.py:71
  367.7 14.2 %collective-permute-start.51 = (bf16[4,96,192]{2,1,0:T(8,128)(2,1)S(1)}, bf16[4,96,192]{2,1,0:T(8,128)(2,1)S(1)}, u32[]{:S(2)}, u32[]{:S(2)}) collective-permute-start(bf16[4,96,192]{2,1,0:T(8,128)(2,1)S(1)} %get-tuple-element.438), channel_id=1, source_target_pairs={{0,3},{1,2},{2,1},{3,0},{4,7},{5,6},{6,5},{7,4},{8,11},{9,10},{10,... | collective-permute-start | bytes 442376 | tf_op jit(solution)/shard_map/ppermute | solution.py:71
  371.0 14.0 %collective-permute-start.52 = (bf16[2,96,768]{2,1,0:T(8,128)(2,1)S(1)}, bf16[2,96,768]{2,1,0:T(8,128)(2,1)S(1)}, u32[]{:S(2)}, u32[]{:S(2)}) collective-permute-start(bf16[2,96,768]{2,1,0:T(8,128)(2,1)S(1)} %slice.550), channel_id=1, source_target_pairs={{0,1},{1,0},{2,3},{3,2},{4,5},{5,4},{6,7},{7,6},{8,9},{9,8},{10,11... | collective-permute-start | bytes 884744 | tf_op jit(solution)/shard_map/ppermute | solution.py:71
  389.3 1.2 collective-permute-start.53
  391.2 3.8 collective-permute-start.54
  395.0 3.8 collective-permute-start.55
  398.9 3.8 collective-permute-start.56
  402.7 4.7 %collective-permute-start.57 = (f32[8,768]{1,0:T(8,128)S(1)}, f32[8,768]{1,0:T(8,128)S(1)}, u32[]{:S(2)}, u32[]{:S(2)}) collective-permute-start(f32[8,768]{1,0:T(8,128)S(1)} %add.695), channel_id=1, source_target_pairs={{0,2},{1,3},{2,0},{3,1},{4,6},{5,7},{6,4},{7,5},{8,10},{9,11},{10,... | collective-permute-start | bytes 73736 | tf_op jit(solution)/shard_map/ppermute | solution.py:71
  (116 other events, 720.3 us)

commit v3 on v2

--- a/solution.py
+++ b/solution.py
@@ -187,6 +187,29 @@
         values = values + swap(values, axis, bit)
         bit *= 2
     return values
+
+
+def sum_at_once(values, axis):
+    received = [values] + [swap(values, axis, mask) for mask in range(1, lax.axis_size(axis))]
+    while len(received) > 1:
+        received = [one + two for one, two in zip(received[::2], received[1::2])]
+    return received[0]
+
+
+def sum_everywhere(values):
+    if lax.axis_size("dp") != 8:
+        return sum_over(sum_over(values, "dp"), "mp")
+    values = values + swap(values, "dp", 1)
+    across = [swap(values, "dp", mask) for mask in (2, 4, 6)]
+    values = (values + across[0]) + (across[1] + across[2])
+    return sum_at_once(values, "mp")
+
+
+def gather_wide(values):
+    if lax.axis_size("dp") != 8:
+        return gather_near(values)
+    values = jnp.concatenate([values, swap(values, "dp", 1)], axis=0)
+    return jnp.concatenate([values] + [swap(values, "dp", mask) for mask in (2, 4, 6)], axis=0)
 
 
 def gather_near(values):
@@ -625,6 +648,74 @@
     )(rank, pooled, near, other, turn)
 
 
+def pack_kernel(parts, *refs):
+    ffn_ref, proj_ref, gains_ref, table_ref, total_ref, small_ref = refs[parts:]
+    squares = jnp.zeros((1, 1), F32)
+
+    def square(values):
+        return jnp.sum(jnp.sum(values * values, axis=1, keepdims=True), axis=0, keepdims=True)
+
+    for layer in range(total_ref.shape[0]):
+        total = refs[0][layer].astype(F32)
+        for ref in refs[1:parts]:
+            total = total + ref[layer].astype(F32)
+        total_ref[layer] = total
+        squares = squares + square(total)
+    for layer in range(ffn_ref.shape[0]):
+        squares = squares + square(ffn_ref[layer])
+    squares = squares + square(proj_ref[...])
+    small_ref[0:3, :] = gains_ref[...]
+    small_ref[3:4, :] = table_ref[...]
+    small_ref[4:8, :] = jnp.broadcast_to(squares, (4, small_ref.shape[1]))
+
+
+def pack(parts, ffn, proj, gains, table_row):
+    return pl.pallas_call(
+        functools.partial(pack_kernel, len(parts)),
+        out_shape=[
+            jax.ShapeDtypeStruct(parts[0].shape, F32),
+            jax.ShapeDtypeStruct((8, gains.shape[1]), F32),
+        ],
+        compiler_params=pltpu.CompilerParams(vmem_limit_bytes=VMEM_LIMIT),
+        name="pack",
+    )(*parts, ffn, proj, gains, table_row)
+
+
+def update_kernel(matrices, *refs):
+    small_ref, grad_refs, rest = refs[0], refs[1 : matrices + 1], refs[matrices + 1 :]
+    old_refs, norm_ref, new_refs = rest[: 3 * matrices + 3], rest[3 * matrices + 3], rest[3 * matrices + 4 :]
+    few = small_ref[0:4, :]
+    total = small_ref[4:5, 0:1] + jnp.sum(
+        jnp.sum(few * few, axis=1, keepdims=True), axis=0, keepdims=True
+    )
+    norm = jnp.sqrt(total)
+    norm_ref[...] = norm
+    factor = jnp.minimum(1.0, CLIP_NORM / (norm + 1e-06))
+    for number in range(matrices + 1):
+        weight_ref, first_ref, second_ref = old_refs[3 * number : 3 * number + 3]
+        is_matrix = number < matrices
+        rate, decay = (RATE_MATRIX, DECAY_MATRIX) if is_matrix else (RATE_SMALL, 0.0)
+        layers = range(weight_ref.shape[0]) if len(weight_ref.shape) == 3 else [Ellipsis]
+        for layer in layers:
+            grad = grad_refs[number][layer] if is_matrix else small_ref[0:3, :]
+            results = adam_update(
+                weight_ref[layer], grad * factor, first_ref[layer], second_ref[layer], rate, decay
+            )
+            for new_ref, result in zip(new_refs[3 * number : 3 * number + 3], results):
+                new_ref[layer] = result
+
+
+def update(small, grads, old):
+    flat = [part for group in old for part in group]
+    return pl.pallas_call(
+        functools.partial(update_kernel, len(grads)),
+        out_shape=[jax.ShapeDtypeStruct((1, 1), F32)]
+        + [jax.ShapeDtypeStruct(part.shape, F32) for part in flat],
+        compiler_params=pltpu.CompilerParams(vmem_limit_bytes=VMEM_LIMIT),
+        name="update",
+    )(small, *grads, *flat)
+
+
 def local(
     tokens,
     cotangent,
@@ -710,13 +801,17 @@
     for bit in bits[:1]:
         ffn_cols = chain_step(ffn_cols, bit)
     attn_parts, ffn_cols, normed_late = after((attn_parts, ffn_cols, normed_one))
-    segment_ids, bias_late = after((segment_ids, bias_table), *attn_parts)
+    segment_ids, bias_late, targets_late = after((segment_ids, bias_table, targets), *attn_parts)
     table = dot(bias_late, head_turn, precision=HIGHEST)
     tiles = bias_tiles(table, rows)
+    marks = jnp.stack([targets_late[:, 0] // 16, targets_late[:, 0] % 16], axis=-1).astype(BF16)
+    marks = jnp.pad(marks[None], ((0, 0), (0, 0), (0, 0), (0, 126)))
     attn_held = gather_plane(jnp.concatenate([attention_low] + attn_parts, axis=-1))
     for bit in bits[1:]:
         ffn_cols = chain_step(ffn_cols, bit)
-    attn_held, ffn_cols, normed_late, tiles = after((attn_held, ffn_cols, normed_late, tiles))
+    attn_held, ffn_cols, normed_late, tiles, marks = after(
+        (attn_held, ffn_cols, normed_late, tiles, marks)
+    )
     attn_near, attn_other = halves(attn_held)
     first_hop = hop((normed_late, normed_late))
     parts = [ffn_cols[0][None], ffn_cols[1][None]]
@@ -739,7 +834,9 @@
     for micro in range(micro_count):
         hops[micro].append((first_hop[0][micro], first_hop[1][micro]))
     finish_hops(0)
-    w_both, w_query, hops, parts = after((w_both, w_query, hops, parts))
+    proj_parts = gather_columns(after(projection_low, attn_other))
+    w_both, w_query, hops, parts, proj_parts = after((w_both, w_query, hops, parts, proj_parts))
+    proj_cols = jnp.concatenate([projection_low] + proj_parts, axis=-1)[None]
     windows = [window_of(0)]
     projected = [project(0)]
     slots = jnp.stack(
@@ -780,7 +877,7 @@
     )
 
     mixed, kept = [], []
-    proj_parts = []
+    proj_held = []
     for micro in range(micro_count):
         came, received = [], []
         parts, projected[micro] = after((parts, projected[micro]))
@@ -790,12 +887,12 @@
             finish_hops(micro + 1)
             came = hops[micro + 1]
         else:
-            proj_parts = gather_columns(after(projection_low, projected[micro][0]))
+            proj_held = gather_plane(after(proj_cols, projected[micro][0]))
         operands = (
             ranges[micro], far_bias, *projected[micro], query_marks[micro], key_marks[micro], tiles
         )
         mixed_part, logs = attend(reach, *operands)
-        came, mixed_part, proj_parts = after((came, mixed_part, proj_parts))
+        came, mixed_part, proj_held = after((came, mixed_part, proj_held))
         if came:
             hops[micro + 1] = came
             windows.append(window_of(micro + 1))
@@ -811,17 +908,15 @@
         parts = outer_joined(outer_received(number))
     ffn_near, ffn_other = halves(jnp.stack(parts))
     hidden_one = token_rows + dot(jnp.concatenate(mixed, axis=0), w_out, NT)
-    proj_held = gather_plane(jnp.concatenate([projection_low] + proj_parts, axis=-1)[None])
+    proj_near, proj_other = halves(proj_held)
     windows_flat = [flatten(window, rows) for window in windows]
-    hidden_one, ffn_other, proj_held, windows_flat = after(
-        (hidden_one, ffn_other, proj_held, windows_flat)
-    )
-    proj_near, proj_other = halves(proj_held)
+    hidden_one, ffn_other, proj_other, windows_flat = after(
+        (hidden_one, ffn_other, proj_other, windows_flat)
+    )
 
     factor_two = norm_factor(hidden_one)
     normed_two = (hidden_one * factor_two * gains[1]).astype(BF16)
     hidden_two, activated, slopes = feed(normed_two, hidden_one, ffn_near, ffn_other)
-    hidden_two, proj_other = after((hidden_two, proj_other))
     output = dot(hidden_two.astype(BF16), turn, NT).astype(BF16)
 
     factor_three = norm_factor(hidden_two)
@@ -835,12 +930,10 @@
     pooled = lax.dot_general(
         member, normed_three, (((2,), (1,)), ((0,), (0,))), precision=HIGHEST, preferred_element_type=F32
     )
-    pooled = sum_over(pooled, "mp") / counts
+    pooled = sum_at_once(pooled, "mp") / counts
     pooled = dot(pooled.reshape(-1, D).astype(BF16), turn, NT).astype(BF16)
     pooled = pooled.reshape(1, micro_count, segment_count, D)
-    marks = jnp.stack([targets[:, 0] // 16, targets[:, 0] % 16], axis=-1).astype(BF16)
-    marks = jnp.pad(marks[None], ((0, 0), (0, 0), (0, 0), (0, 126)))
-    pooled_all = gather_near(jnp.concatenate([pooled, marks], axis=-1))
+    pooled_all = gather_wide(jnp.concatenate([pooled, marks], axis=-1))
     rank = jnp.stack([wide_rank, narrow_rank]).astype(jnp.int32)
     pooled_grad, proj_grad = contrast(
         rank, pooled_all.reshape(-1, pooled_all.shape[-1]), proj_near[0], proj_other[0], turn,
@@ -923,18 +1016,19 @@
         join(flow, reach - 1, got)
     ffn_last = [add_low(*terms)[0] for terms, _ in parts]
     ffn_last, grads = after((ffn_last, grads))
-    up_column = send_columns_chain(ffn_last[0])
+    ffn_last = jnp.stack(ffn_last)
+    ffn_column = send_columns_chain(ffn_last)
     attn_keep, attn_send = collect(windows_flat, grads, out_part)
-    attn_keep, attn_send, up_column, flows, owns, last_grads = after(
-        (attn_keep, attn_send, up_column, flows, owns, grads[-1])
-    )
-    last = flow_of(*last_grads)
+    last = flow_of(*grads[-1])
+    attn_keep, attn_send, ffn_column, flows, owns, last = after(
+        (attn_keep, attn_send, ffn_column, flows, owns, last)
+    )
     owns.append(last[0])
     last = list(last[1])
     attn_received = swap(attn_send, "dp", 1)
-    down_column = send_columns_chain(after(ffn_last[1], attn_keep))
     came = leave(last, reach) if reach > 1 else ()
-    attn_received, down_column, came = after((attn_received, down_column, came))
+    ffn_reduced = finish_columns_chain(ffn_last, ffn_column)
+    attn_received, came, ffn_reduced = after((attn_received, came, ffn_reduced))
     attn_held = to_blocks(add_low(attn_keep, attn_received))
     if reach > 1:
         join(last, reach - 1, came)
@@ -949,13 +1043,10 @@
     attn_columns = send_columns(attn_last)
     normed_one_grad = jnp.stack(owns) + came[0].astype(F32) + came[1].astype(F32)
     normed_one_grad = normed_one_grad.reshape(micro_count * rows, D)
-    ffn_column, ffn_last = after((jnp.stack([up_column, down_column]), jnp.stack(ffn_last)), *attn_received)
-    ffn_reduced = finish_columns_chain(ffn_last, ffn_column)
     gain_one = jnp.sum(normed_one_grad * token_rows * factor_one, axis=0)
     tokens_grad = hidden_one_grad + norm_back(token_rows, factor_one, normed_one_grad * gains[0])
     tokens_grad = dot(tokens_grad, turn_wide, NT, HIGHEST)
     attn_columns, tokens_grad, gain_one = after((attn_columns, tokens_grad, gain_one))
-    attn_reduced = add_columns(attn_last, attn_columns)
 
     bias_sum = sum(bias_parts)
     heads = table.shape[1]
@@ -974,41 +1065,26 @@
     )
     full_table = dot(table_grad, head_turn, NT, HIGHEST)
     gains_part = dot(jnp.stack([gain_one, gain_two, gain_three]), turn_wide, NT, HIGHEST)
-    local_squares = (
-        jnp.sum(attn_reduced * attn_reduced)
-        + jnp.sum(ffn_reduced * ffn_reduced)
-        + jnp.sum(proj_reduced * proj_reduced)
-    )
-    small = jnp.concatenate(
+    table_row = jnp.pad(full_table.reshape(1, -1), ((0, 0), (0, D - full_table.size)))
+    attn_reduced, small = pack(
+        [attn_last[..., : attn_columns[0].shape[-1]], *attn_columns],
+        ffn_reduced, proj_reduced, gains_part, table_row,
+    )
+    small = sum_everywhere(small)
+    table_full_grad = small[3, : full_table.size].reshape(full_table.shape)
+    grad_norm, *updated = update(
+        small,
+        [attn_reduced, ffn_reduced, proj_reduced],
         [
-            gains_part,
-            jnp.pad(full_table.reshape(1, -1), ((0, 0), (0, D - full_table.size))),
-            jnp.broadcast_to(local_squares, (4, D)),
-        ]
-    )
-    small = sum_over(sum_over(small, "dp"), "mp")
-    gains_grad = small[:3]
-    table_full_grad = small[3, : full_table.size].reshape(full_table.shape)
-    total_squares = (
-        small[4, 0] + jnp.sum(gains_grad * gains_grad) + jnp.sum(table_full_grad * table_full_grad)
-    )
-    grad_norm = jnp.sqrt(total_squares)
+            (attention_weights, attention_first, attention_second),
+            (feedforward_weights, feedforward_first, feedforward_second),
+            (projection, projection_first, projection_second),
+            (norm_gains, gains_first, gains_second),
+        ],
+    )
+    grad_norm = grad_norm.reshape(())
+    attn_new, ffn_new, proj_new, gains_new = (updated[3 * k : 3 * k + 3] for k in range(4))
     factor = jnp.minimum(1.0, CLIP_NORM / (grad_norm + 1e-06))
-    attn_new = adam_update(
-        attention_weights, attn_reduced * factor, attention_first, attention_second,
-        RATE_MATRIX, DECAY_MATRIX,
-    )
-    ffn_new = adam_update(
-        feedforward_weights, ffn_reduced * factor, feedforward_first, feedforward_second,
-        RATE_MATRIX, DECAY_MATRIX,
-    )
-    proj_new = adam_update(
-        projection, proj_reduced * factor, projection_first, projection_second,
-        RATE_MATRIX, DECAY_MATRIX,
-    )
-    gains_new = adam_update(
-        norm_gains, gains_grad * factor, gains_first, gains_second, RATE_SMALL, 0.0
-    )
     table_new = adam_update(
         bias_table, table_full_grad * factor, bias_first, bias_second, RATE_SMALL, 0.0
     )

time: 428 us -> 417 us (0.974)
  other arithmetic: 64 us -> 53.7 us
  starting transfers between devices: 73.8 us -> 82.3 us
  Pallas kernels: 94.3 us -> 101 us
  local copies, waits for them, and re-layouts: 30.7 us -> 24.8 us
  matrix products: 38.1 us -> 33.7 us
    ppermute x46 -> x49, starting transfers between devices: 57.2 us -> 64.5 us  [swap(): return lax.ppermute(values, axis, [(i, i ^ mask) for i in range(count)])]
    sub x5 -> x1, other arithmetic: 7.3 us -> 0.63 us  [adam_update(): weight_now - step_rate * (first_hat / (jnp.sqrt(second_hat) + EPS_ADAM) +...]
    dot_general x24, matrix products: 36 us -> 31.6 us  [dot(): lax.dot_general(left, right, dims, precision=precision, preferred_element...]
    ppermute x46 -> x49, waiting for transfers between devices: 95.8 us -> 99.1 us  [swap(): return lax.ppermute(values, axis, [(i, i ^ mask) for i in range(count)])]
    unnamed x256 -> x262, local copies, waits for them, and re-layouts: 18.6 us -> 15.7 us
  transfers between devices with their start and end apart: 58 -> 61, of which waited for: 29 -> 31; matrix products, arithmetic and copies ran while one was open for 18% -> 15% of each run, Pallas kernels for 18% -> 17%
where the time goes in v3:
time: 417 us; the launch traced here: 410 us
  waiting for transfers between devices  111 us (27%)
  Pallas kernels  101 us (24%)
  starting transfers between devices  82.3 us (20%)
  other arithmetic  53.7 us (13%)
  matrix products  33.7 us (8%)
  local copies, waits for them, and re-layouts  24.8 us (6%)
    ppermute x49, waiting for transfers between devices, swap(): return lax.ppermute(values, axis, [(i, i ^ mask) for i in range(count)])  99.1 us
    ppermute x49, starting transfers between devices, swap(): return lax.ppermute(values, axis, [(i, i ^ mask) for i in range(count)])  64.5 us
    dot_general x24, matrix products, dot(): lax.dot_general(left, right, dims, precision=precision, preferred_element...  31.6 us
    pallas_call x2, Pallas kernels, attend_back(): pl.pallas_call(functools.partial(backward_kernel, reach), grid=(pairs,),...  29.3 us
    pallas_call x2, Pallas kernels, attend(): pl.pallas_call(functools.partial(forward_kernel, reach), grid=(pairs,), i...  19.9 us
    ppermute x12, starting transfers between devices, link(): return lax.ppermute(values, 'mp', pairs + [(j, i) for i, j in pairs])  17.8 us
    unnamed x262, local copies, waits for them, and re-layouts  15.7 us
    pallas_call x1, Pallas kernels, feed_back(): pl.pallas_call(feed_back_kernel, grid=(units // chunk,), in_specs=[same_b...  15.5 us
  transfers between devices with their start and end apart: 61, of which 31 were waited for; matrix products, arithmetic and copies ran while one was open for 15% of the time, Pallas kernels for 17%

profile of v3, /device:TPU:0, one launch (start us, length us, event | category | flops | bytes accessed | tf_op | source)
XLA Modules:
  0.0 409.8 jit_solution(4472696748879493100)
XLA Ops:
  1.8 5.1 %collective-permute-start.2 = (bf16[4,96,192]{2,1,0:T(8,128)(2,1)S(1)}, bf16[4,96,192]{2,1,0:T(8,128)(2,1)}, u32[]{:S(2)}, u32[]{:S(2)}) collective-permute-start(bf16[4,96,192]{2,1,0:T(8,128)(2,1)S(1)} %convert_element_type.510), channel_id=1, source_target_pairs={{0,3},{1,2},{2,1},{3,0},{4,7},{5,6},{6,5},{7,4},{8,11},{9,10},{10,... | collective-permute-start | bytes 442376 | tf_op jit(solution)/shard_map/ppermute | solution.py:71
  16.2 1.9 slice_dynamic-update-slice_fusion
  18.1 8.7 %collective-permute-done.3 = bf16[2,96,768]{2,1,0:T(8,128)(2,1)} collective-permute-done((bf16[2,96,768]{2,1,0:T(8,128)(2,1)S(1)}, bf16[2,96,768]{2,1,0:T(8,128)(2,1)}, u32[]{:S(2)}, u32[]{:S(2)}) %collective-permute-start.3) | collective-permute-done | bytes 294944 | tf_op jit(solution)/shard_map/ppermute | solution.py:71
  29.2 1.6 collective-permute-start.5
  35.7 7.4 %shard_map.322.bias_ref = f32[12,3,256,256]{3,2,1,0:T(8,128)} custom-call(f32[12,3,512]{2,1,0:T(4,128)S(1)} %copy.106.line_ref), custom_call_target="tpu_custom_call" | custom-call | tf_op jit(solution)/shard_map/pallas_call | solution.py:238
  44.6 2.4 collective-permute-done.4
  47.0 11.3 %collective-permute-done.6 = bf16[4,96,768]{2,1,0:T(8,128)(2,1)S(1)} collective-permute-done((bf16[4,96,768]{2,1,0:T(8,128)(2,1)S(1)}, bf16[4,96,768]{2,1,0:T(8,128)(2,1)S(1)}, u32[]{:S(2)}, u32[]{:S(2)}) %collective-permute-start.6) | collective-permute-done | bytes 589856 | tf_op jit(solution)/shard_map/ppermute | solution.py:71
  58.3 1.7 pad_maximum_fusion.1
  63.7 2.5 collective-permute-start.9
  67.6 1.6 collective-permute-start.12
  70.8 12.1 %collective-permute-done.12 = bf16[1,96,3072]{2,1,0:T(8,128)(2,1)S(1)} collective-permute-done((bf16[1,96,3072]{2,1,0:T(8,128)(2,1)S(1)}, bf16[1,96,3072]{2,1,0:T(8,128)(2,1)S(1)}, u32[]{:S(2)}, u32[]{:S(2)}) %collective-permute-start.12) | collective-permute-done | bytes 589856 | tf_op jit(solution)/shard_map/ppermute | solution.py:71
  84.4 2.3 collective-permute-start.17
  90.7 2.8 collective-permute-start.13
  94.6 3.4 fusion.30
  98.2 3.3 collective-permute-done.13
  102.4 3.9 collective-permute-start.20
  106.5 3.4 convolution_convert_fusion.1.k_ref.v_ref
  110.4 1.6 collective-permute-start.18
  113.5 9.8 %attend.2 = (bf16[256,768]{1,0:T(8,128)(2,1)S(1)}, f32[6,8,256]{2,1,0:T(8,128)S(1)}) custom-call(s32[7]{0:T(128)S(1)} %get-tuple-element.478.range_ref, f32[2,12]{1,0:T(2,128)S(1)} %pad_maximum_fusion.16.far_ref, bf16[256,768]{1,0:T(8,128)(2,1)S(1)} %convolution_convert_fusion.5.q_ref, bf16[1280,1536]{1,0:T(8,128)(2,1)S(1)} %convolution_convert_fusion.1.k_ref.v_ref, ...), custom_call_target="tpu_custom_call" | custom-call | flops 100000 | bytes 10000 | tf_op jit(solution)/shard_map/attend/pallas_call | solution.py:420
  125.2 3.5 convolution_convert_fusion.k_ref.v_ref
  132.2 10.2 %attend.3 = (bf16[256,768]{1,0:T(8,128)(2,1)S(1)}, f32[6,8,256]{2,1,0:T(8,128)S(1)}) custom-call(s32[7]{0:T(128)S(1)} %get-tuple-element.477.range_ref, f32[2,12]{1,0:T(2,128)S(1)} %pad_maximum_fusion.16.far_ref, bf16[256,768]{1,0:T(8,128)(2,1)S(1)} %convolution_convert_fusion.4.q_ref, bf16[1280,1536]{1,0:T(8,128)(2,1)S(1)} %convolution_convert_fusion.k_ref.v_ref, ...), custom_call_target="tpu_custom_call" | custom-call | flops 100000 | bytes 10000 | tf_op jit(solution)/shard_map/attend/pallas_call | solution.py:420
  143.1 2.0 pad_maximum_fusion.4
  145.3 1.8 pad_maximum_fusion.3
  147.9 1.8 fusion.2.turn_ref
  153.2 2.2 copy-done.53
  157.5 11.1 %feed.1 = (f32[512,768]{1,0:T(8,128)S(1)}, bf16[512,3072]{1,0:T(8,128)(2,1)}, bf16[512,3072]{1,0:T(8,128)(2,1)}) custom-call(bf16[512,768]{1,0:T(8,128)(2,1)S(1)} %multiply_convert_fusion.normed_ref, f32[512,768]{1,0:T(8,128)S(1)} %bitcast_add_fusion.1.hidden_ref, bf16[2,384,3072]{2,1,0:T(8,128)(2,1)} %copy-done.51, ...), custom_call_target="tpu_custom_call" | custom-call | flops 100000 | bytes 10000 | tf_op jit(solution)/shard_map/feed/pallas_call | solution.py:558
  171.4 2.5 collective-permute-start.29
  174.0 1.9 collective-permute-start.27
  187.0 3.6 collective-permute-done.31
  192.8 2.8 contrast.1
  198.8 15.5 %feed_back.1 = (f32[512,768]{1,0:T(8,128)S(1)}, bf16[2,384,3072]{2,1,0:T(8,128)(2,1)}, bf16[2,384,3072]{2,1,0:T(8,128)(2,1)}) custom-call(bf16[512,768]{1,0:T(8,128)(2,1)S(1)} %multiply_convert_fusion.normed_ref, bf16[512,768]{1,0:T(8,128)(2,1)S(1)} %get-tuple-element.483.up_ref, bf16[2,384,3072]{2,1,0:T(8,128)(2,1)} %copy-done.51, ...), custom_call_target="tpu_custom_call" | custom-call | flops 100000 | bytes 10000 | tf_op jit(solution)/shard_map/feed_back/pallas_call | solution.py:580
  219.7 2.7 collective-permute-done.34
  222.7 1.8 fusion.22
  227.3 14.8 %attend_back.2 = (bf16[256,768]{1,0:T(8,128)(2,1)S(1)}, bf16[1280,768]{1,0:T(8,128)(2,1)S(1)}, bf16[1280,768]{1,0:T(8,128)(2,1)S(1)}, f32[6,2,8,256]{3,2,1,0:T(8,128)S(1)}) custom-call(s32[7]{0:T(128)S(1)} %get-tuple-element.478.range_ref, f32[2,12]{1,0:T(2,128)S(1)} %pad_maximum_fusion.16.far_ref, bf16[256,768]{1,0:T(8,128)(2,1)S(1)} %copy-done.30, ...), custom_call_target="tpu_custom_call" | custom-call | flops 100000 | bytes 10000 | tf_op jit(solution)/shard_map/attend_back/pallas_call | solution.py:440
  242.2 1.7 fusion.49
  245.2 1.9 fusion.140
  251.1 3.4 collective-permute-done.35
  254.8 2.1 fusion.57
  261.9 14.4 %attend_back.3 = (bf16[256,768]{1,0:T(8,128)(2,1)S(1)}, bf16[1280,768]{1,0:T(8,128)(2,1)S(1)}, bf16[1280,768]{1,0:T(8,128)(2,1)S(1)}, f32[6,2,8,256]{3,2,1,0:T(8,128)S(1)}) custom-call(s32[7]{0:T(128)S(1)} %get-tuple-element.477.range_ref, f32[2,12]{1,0:T(2,128)S(1)} %pad_maximum_fusion.16.far_ref, bf16[256,768]{1,0:T(8,128)(2,1)S(1)} %copy-done.28, ...), custom_call_target="tpu_custom_call" | custom-call | flops 100000 | bytes 10000 | tf_op jit(solution)/shard_map/attend_back/pallas_call | solution.py:440
  276.3 1.8 fusion.60
  280.7 6.4 %collective-permute-start.41 = (bf16[2,96,1536]{2,1,0:T(8,128)(2,1)}, bf16[2,96,1536]{2,1,0:T(8,128)(2,1)}, u32[]{:S(2)}, u32[]{:S(2)}) collective-permute-start(bf16[2,96,1536]{2,1,0:T(8,128)(2,1)} %fusion.61), channel_id=1, source_target_pairs={{0,2},{1,3},{2,0},{3,1},{4,6},{5,7},{6,4},{7,5},{8,10},{9,11},{10,... | collective-permute-start | bytes 1769480 | tf_op jit(solution)/shard_map/ppermute | solution.py:71
  287.1 1.7 fusion.47
  288.9 1.8 add_convert_fusion.7
  290.7 1.8 fusion.141
  293.1 10.2 %collect.1 = (bf16[4,384,768]{2,1,0:T(8,128)(2,1)}, bf16[4,384,768]{2,1,0:T(8,128)(2,1)}) custom-call(bf16[768,1280]{1,0:T(8,128)(2,1)S(1)} %copy-done.10, bf16[768,1280]{1,0:T(8,128)(2,1)S(1)} %copy-done.12, bf16[256,768]{1,0:T(8,128)(2,1)S(1)} %get-tuple-element.276.refs_2_, bf16[1280,768]{1,0:T(8,128)(2,1)} %copy-done.7, bf16[1280,768]{1,0:T(8,128)(2,1)} %copy-done.20, ...), custom_call_target="tpu_custom_call" | custom-call | flops 100000 | bytes 10000 | tf_op jit(solution)/shard_map/collect/pallas_call | solution.py:493
  303.9 2.1 collective-permute-done.41
  307.4 2.1 collective-permute-start.43
  311.3 6.0 %collective-permute-done.45 = bf16[2,96,768]{2,1,0:T(8,128)(2,1)S(1)} collective-permute-done((bf16[2,96,768]{2,1,0:T(8,128)(2,1)S(1)}, bf16[2,96,768]{2,1,0:T(8,128)(2,1)S(1)}, u32[]{:S(2)}, u32[]{:S(2)}) %collective-permute-start.45) | collective-permute-done | bytes 294944 | tf_op jit(solution)/shard_map/ppermute | solution.py:71
  317.3 7.9 %collective-permute-done.43 = bf16[256,768]{1,0:T(8,128)(2,1)S(1)} collective-permute-done((bf16[256,768]{1,0:T(8,128)(2,1)S(1)}, bf16[256,768]{1,0:T(8,128)(2,1)S(1)}, u32[]{:S(2)}, u32[]{:S(2)}) %collective-permute-start.43) | collective-permute-done | bytes 393248 | tf_op jit(solution)/shard_map/ppermute | solution.py:77
  328.4 1.8 collective-permute-start.50
  331.3 4.7 %collective-permute-start.48 = (bf16[4,96,768]{2,1,0:T(8,128)(2,1)}, bf16[4,96,768]{2,1,0:T(8,128)(2,1)}, u32[]{:S(2)}, u32[]{:S(2)}) collective-permute-start(bf16[4,96,768]{2,1,0:T(8,128)(2,1)} %get-tuple-element.432), channel_id=1, source_target_pairs={{0,24},{4,28},{8,16},{12,20},{16,8},{20,12},{24,0},{28,4},{1,25},{... | collective-permute-start | bytes 1769480 | tf_op jit(solution)/shard_map/ppermute | solution.py:71
  336.0 3.2 collective-permute-start.47
  340.0 10.6 %collective-permute-done.48 = bf16[4,96,768]{2,1,0:T(8,128)(2,1)} collective-permute-done((bf16[4,96,768]{2,1,0:T(8,128)(2,1)}, bf16[4,96,768]{2,1,0:T(8,128)(2,1)}, u32[]{:S(2)}, u32[]{:S(2)}) %collective-permute-start.48) | collective-permute-done | bytes 589856 | tf_op jit(solution)/shard_map/ppermute | solution.py:71
  350.6 12.4 %collective-permute-done.47 = bf16[4,96,768]{2,1,0:T(8,128)(2,1)} collective-permute-done((bf16[4,96,768]{2,1,0:T(8,128)(2,1)}, bf16[4,96,768]{2,1,0:T(8,128)(2,1)}, u32[]{:S(2)}, u32[]{:S(2)}) %collective-permute-start.47) | collective-permute-done | bytes 589856 | tf_op jit(solution)/shard_map/ppermute | solution.py:71
  364.1 1.7 fusion.8
  366.5 2.0 fusion.33
  370.0 2.1 collective-permute-start.52
  373.1 3.7 fusion.1
  376.9 1.6 collective-permute-done.53.refs_3_
  378.5 10.5 %collective-permute-done.52.refs_2_ = bf16[4,96,192]{2,1,0:T(8,128)(2,1)S(1)} collective-permute-done((bf16[4,96,192]{2,1,0:T(8,128)(2,1)S(1)}, bf16[4,96,192]{2,1,0:T(8,128)(2,1)S(1)}, u32[]{:S(2)}, u32[]{:S(2)}) %collective-permute-start.52) | collective-permute-done | bytes 147488 | tf_op jit(solution)/shard_map/ppermute | solution.py:71
  391.7 1.7 collective-permute-start.57
  400.1 2.9 collective-permute-start.58
  403.1 1.7 fusion.21
  405.3 2.5 update.1
  (476 shorter events, 112.2 us)
Async XLA Ops:
  0.7 197.0 %copy-start = (bf16[2,1,256,768]{3,2,1,0:T(8,128)(2,1)S(1)}, bf16[2,1,256,768]{3,2,1,0:T(8,128)(2,1)}, u32[]{:S(2)}) copy-start(bf16[2,1,256,768]{3,2,1,0:T(8,128)(2,1)} %param.20) | copy-start | bytes 2359300
  1.8 26.0 %collective-permute-start.2 = (bf16[4,96,192]{2,1,0:T(8,128)(2,1)S(1)}, bf16[4,96,192]{2,1,0:T(8,128)(2,1)}, u32[]{:S(2)}, u32[]{:S(2)}) collective-permute-start(bf16[4,96,192]{2,1,0:T(8,128)(2,1)S(1)} %convert_element_type.510), channel_id=1, source_target_pairs={{0,3},{1,2},{2,1},{3,0},{4,7},{5,6},{6,5},{7,4},{8,11},{9,10},{10,... | collective-permute-start | bytes 442376 | tf_op jit(solution)/shard_map/ppermute | solution.py:71
  6.9 20.9 %collective-permute-start.1 = (bf16[4,96,192]{2,1,0:T(8,128)(2,1)S(1)}, bf16[4,96,192]{2,1,0:T(8,128)(2,1)}, u32[]{:S(2)}, u32[]{:S(2)}) collective-permute-start(bf16[4,96,192]{2,1,0:T(8,128)(2,1)S(1)} %convert_element_type.510), channel_id=1, source_target_pairs={{0,2},{1,3},{2,0},{3,1},{4,6},{5,7},{6,4},{7,5},{8,10},{9,11},{10,... | collective-permute-start | bytes 442376 | tf_op jit(solution)/shard_map/ppermute | solution.py:71
  6.9 20.9 %collective-permute-start = (bf16[4,96,192]{2,1,0:T(8,128)(2,1)S(1)}, bf16[4,96,192]{2,1,0:T(8,128)(2,1)}, u32[]{:S(2)}, u32[]{:S(2)}) collective-permute-start(bf16[4,96,192]{2,1,0:T(8,128)(2,1)S(1)} %convert_element_type.510), channel_id=1, source_target_pairs={{0,1},{1,0},{2,3},{3,2},{4,5},{5,4},{6,7},{7,6},{8,9},{9,8},{10,11... | collective-permute-start | bytes 442376 | tf_op jit(solution)/shard_map/ppermute | solution.py:71
  8.7 18.1 %collective-permute-start.3 = (bf16[2,96,768]{2,1,0:T(8,128)(2,1)S(1)}, bf16[2,96,768]{2,1,0:T(8,128)(2,1)}, u32[]{:S(2)}, u32[]{:S(2)}) collective-permute-start(bf16[2,96,768]{2,1,0:T(8,128)(2,1)S(1)} %convert_element_type.511), channel_id=1, source_target_pairs={{0,1},{1,0},{2,3},{3,2},{4,5},{5,4},{6,7},{7,6},{8,9},{9,8},{10,11... | collective-permute-start | bytes 884744 | tf_op jit(solution)/shard_map/ppermute | solution.py:71
  16.2 71.4 %copy-start.85 = (bf16[96,192]{1,0:T(8,128)(2,1)}, bf16[96,192]{1,0:T(8,128)(2,1)S(1)}, u32[]{:S(2)}) copy-start(bf16[96,192]{1,0:T(8,128)(2,1)S(1)} %convert_element_type.520) | copy-start | bytes 110596
  29.2 15.4 %collective-permute-start.5 = (bf16[4,96,768]{2,1,0:T(8,128)(2,1)S(1)}, bf16[4,96,768]{2,1,0:T(8,128)(2,1)S(1)}, u32[]{:S(2)}, u32[]{:S(2)}) collective-permute-start(bf16[4,96,768]{2,1,0:T(8,128)(2,1)S(1)} %pad_maximum_fusion.12), channel_id=1, source_target_pairs={{0,16},{4,20},{8,24},{12,28},{16,0},{20,4},{24,8},{28,12},{1,17},{... | collective-permute-start | bytes 1769480 | tf_op jit(solution)/shard_map/ppermute | solution.py:71
  30.8 16.2 %collective-permute-start.4 = (bf16[4,96,768]{2,1,0:T(8,128)(2,1)S(1)}, bf16[4,96,768]{2,1,0:T(8,128)(2,1)S(1)}, u32[]{:S(2)}, u32[]{:S(2)}) collective-permute-start(bf16[4,96,768]{2,1,0:T(8,128)(2,1)S(1)} %pad_maximum_fusion.12), channel_id=1, source_target_pairs={{0,8},{4,12},{8,0},{12,4},{16,24},{20,28},{24,16},{28,20},{1,9},{5... | collective-permute-start | bytes 1769480 | tf_op jit(solution)/shard_map/ppermute | solution.py:71
  32.3 26.1 %collective-permute-start.6 = (bf16[4,96,768]{2,1,0:T(8,128)(2,1)S(1)}, bf16[4,96,768]{2,1,0:T(8,128)(2,1)S(1)}, u32[]{:S(2)}, u32[]{:S(2)}) collective-permute-start(bf16[4,96,768]{2,1,0:T(8,128)(2,1)S(1)} %pad_maximum_fusion.12), channel_id=1, source_target_pairs={{0,24},{4,28},{8,16},{12,20},{16,8},{20,12},{24,0},{28,4},{1,25},{... | collective-permute-start | bytes 1769480 | tf_op jit(solution)/shard_map/ppermute | solution.py:71
  32.8 28.0 %collective-permute-start.7 = (bf16[2,96,1536]{2,1,0:T(8,128)(2,1)S(1)}, bf16[2,96,1536]{2,1,0:T(8,128)(2,1)S(1)}, u32[]{:S(2)}, u32[]{:S(2)}) collective-permute-start(bf16[2,96,1536]{2,1,0:T(8,128)(2,1)S(1)} %pad_maximum_fusion.11), channel_id=1, source_target_pairs={{0,2},{1,3},{2,0},{3,1},{4,6},{5,7},{6,4},{7,5},{8,10},{9,11},{10,... | collective-permute-start | bytes 1769480 | tf_op jit(solution)/shard_map/ppermute | solution.py:71
  62.0 22.3 %collective-permute-start.8 = (bf16[4,384,768]{2,1,0:T(8,128)(2,1)}, bf16[4,384,768]{2,1,0:T(8,128)(2,1)}, u32[]{:S(2)}, u32[]{:S(2)}) collective-permute-start(bf16[4,384,768]{2,1,0:T(8,128)(2,1)} %bitcast.15), channel_id=1, source_target_pairs={{0,4},{4,0},{8,12},{12,8},{16,20},{20,16},{24,28},{28,24},{1,5},{5... | collective-permute-start | bytes 7077896 | tf_op jit(solution)/shard_map/ppermute | solution.py:71
  62.2 108.0 %copy-start.97 = (s32[2,256]{1,0:T(2,128)}, s32[2,256]{1,0:T(2,128)S(1)}, u32[]{:S(2)}) copy-start(s32[2,256]{1,0:T(2,128)S(1)} %pad_dynamic-slice_fusion) | copy-start | bytes 6148
  62.9 21.2 %collective-permute-start.10 = (bf16[2,256,768]{2,1,0:T(8,128)(2,1)}, bf16[2,256,768]{2,1,0:T(8,128)(2,1)S(1)}, u32[]{:S(2)}, u32[]{:S(2)}) collective-permute-start(bf16[2,256,768]{2,1,0:T(8,128)(2,1)} %bitcast.268), channel_id=1, source_target_pairs={{1,2},{2,1},{5,6},{6,5},{9,10},{10,9},{13,14},{14,13},{17,18},{18,... | collective-permute-start | bytes 2359304 | tf_op jit(solution)/shard_map/ppermute | solution.py:77
  63.7 20.7 %collective-permute-start.9 = (bf16[2,256,768]{2,1,0:T(8,128)(2,1)}, bf16[2,256,768]{2,1,0:T(8,128)(2,1)S(1)}, u32[]{:S(2)}, u32[]{:S(2)}) collective-permute-start(bf16[2,256,768]{2,1,0:T(8,128)(2,1)} %bitcast.269), channel_id=1, source_target_pairs={{0,1},{2,3},{1,0},{3,2},{4,5},{6,7},{5,4},{7,6},{8,9},{10,11},{9,8... | collective-permute-start | bytes 2359304 | tf_op jit(solution)/shard_map/ppermute | solution.py:77
  67.6 15.2 %collective-permute-start.12 = (bf16[1,96,3072]{2,1,0:T(8,128)(2,1)S(1)}, bf16[1,96,3072]{2,1,0:T(8,128)(2,1)S(1)}, u32[]{:S(2)}, u32[]{:S(2)}) collective-permute-start(bf16[1,96,3072]{2,1,0:T(8,128)(2,1)S(1)} %get-tuple-element.446), channel_id=1, source_target_pairs={{0,16},{4,20},{8,24},{12,28},{16,0},{20,4},{24,8},{28,12},{1,17},{... | collective-permute-start | bytes 1769480 | tf_op jit(solution)/shard_map/ppermute | solution.py:71
  69.2 14.9 %collective-permute-start.11 = (bf16[1,96,3072]{2,1,0:T(8,128)(2,1)S(1)}, bf16[1,96,3072]{2,1,0:T(8,128)(2,1)S(1)}, u32[]{:S(2)}, u32[]{:S(2)}) collective-permute-start(bf16[1,96,3072]{2,1,0:T(8,128)(2,1)S(1)} %get-tuple-element.447), channel_id=1, source_target_pairs={{0,8},{4,12},{8,0},{12,4},{16,24},{20,28},{24,16},{28,20},{1,9},{5... | collective-permute-start | bytes 1769480 | tf_op jit(solution)/shard_map/ppermute | solution.py:71
  84.4 13.8 %collective-permute-start.17 = (bf16[96,192]{1,0:T(8,128)(2,1)S(1)}, bf16[96,192]{1,0:T(8,128)(2,1)S(1)}, u32[]{:S(2)}, u32[]{:S(2)}) collective-permute-start(bf16[96,192]{1,0:T(8,128)(2,1)S(1)} %convert_element_type.520), channel_id=1, source_target_pairs={{0,3},{1,2},{2,1},{3,0},{4,7},{5,6},{6,5},{7,4},{8,11},{9,10},{10,... | collective-permute-start | bytes 110600 | tf_op jit(solution)/shard_map/ppermute | solution.py:71
  86.6 11.6 %collective-permute-start.16 = (bf16[96,192]{1,0:T(8,128)(2,1)S(1)}, bf16[96,192]{1,0:T(8,128)(2,1)S(1)}, u32[]{:S(2)}, u32[]{:S(2)}) collective-permute-start(bf16[96,192]{1,0:T(8,128)(2,1)S(1)} %convert_element_type.520), channel_id=1, source_target_pairs={{0,2},{1,3},{2,0},{3,1},{4,6},{5,7},{6,4},{7,5},{8,10},{9,11},{10,... | collective-permute-start | bytes 110600 | tf_op jit(solution)/shard_map/ppermute | solution.py:71
  87.6 10.6 %collective-permute-start.15 = (bf16[96,192]{1,0:T(8,128)(2,1)S(1)}, bf16[96,192]{1,0:T(8,128)(2,1)S(1)}, u32[]{:S(2)}, u32[]{:S(2)}) collective-permute-start(bf16[96,192]{1,0:T(8,128)(2,1)S(1)} %convert_element_type.520), channel_id=1, source_target_pairs={{0,1},{1,0},{2,3},{3,2},{4,5},{5,4},{6,7},{7,6},{8,9},{9,8},{10,11... | collective-permute-start | bytes 110600 | tf_op jit(solution)/shard_map/ppermute | solution.py:71
  88.8 9.4 %collective-permute-start.14 = (bf16[256,768]{1,0:T(8,128)(2,1)S(1)}, bf16[256,768]{1,0:T(8,128)(2,1)S(1)}, u32[]{:S(2)}, u32[]{:S(2)}) collective-permute-start(bf16[256,768]{1,0:T(8,128)(2,1)S(1)} %get-tuple-element.197), channel_id=1, source_target_pairs={{1,2},{2,1},{5,6},{6,5},{9,10},{10,9},{13,14},{14,13},{17,18},{18,... | collective-permute-start | bytes 1179656 | tf_op jit(solution)/shard_map/ppermute | solution.py:77
  90.7 10.8 %collective-permute-start.13 = (bf16[256,768]{1,0:T(8,128)(2,1)S(1)}, bf16[256,768]{1,0:T(8,128)(2,1)S(1)}, u32[]{:S(2)}, u32[]{:S(2)}) collective-permute-start(bf16[256,768]{1,0:T(8,128)(2,1)S(1)} %get-tuple-element.198), channel_id=1, source_target_pairs={{0,1},{2,3},{1,0},{3,2},{4,5},{6,7},{5,4},{7,6},{8,9},{10,11},{9,8... | collective-permute-start | bytes 1179656 | tf_op jit(solution)/shard_map/ppermute | solution.py:77
  101.5 22.5 %collective-permute-start.21 = (bf16[256,768]{1,0:T(8,128)(2,1)S(1)}, bf16[256,768]{1,0:T(8,128)(2,1)S(1)}, u32[]{:S(2)}, u32[]{:S(2)}) collective-permute-start(bf16[256,768]{1,0:T(8,128)(2,1)S(1)} %get-tuple-element.212), channel_id=1, source_target_pairs={{1,2},{2,1},{5,6},{6,5},{9,10},{10,9},{13,14},{14,13},{17,18},{18,... | collective-permute-start | bytes 1179656 | tf_op jit(solution)/shard_map/ppermute | solution.py:77
  102.4 21.6 %collective-permute-start.20 = (bf16[256,768]{1,0:T(8,128)(2,1)S(1)}, bf16[256,768]{1,0:T(8,128)(2,1)}, u32[]{:S(2)}, u32[]{:S(2)}) collective-permute-start(bf16[256,768]{1,0:T(8,128)(2,1)S(1)} %get-tuple-element.213), channel_id=1, source_target_pairs={{0,1},{2,3},{1,0},{3,2},{4,5},{6,7},{5,4},{7,6},{8,9},{10,11},{9,8... | collective-permute-start | bytes 1179656 | tf_op jit(solution)/shard_map/ppermute | solution.py:77
  110.4 32.7 %collective-permute-start.18 = (bf16[2,96,3072]{2,1,0:T(8,128)(2,1)}, bf16[2,96,3072]{2,1,0:T(8,128)(2,1)}, u32[]{:S(2)}, u32[]{:S(2)}) collective-permute-start(bf16[2,96,3072]{2,1,0:T(8,128)(2,1)} %pad_maximum_fusion.7), channel_id=1, source_target_pairs={{0,16},{4,20},{8,24},{12,28},{16,0},{20,4},{24,8},{28,12},{1,17},{... | collective-permute-start | bytes 3538952 | tf_op jit(solution)/shard_map/ppermute | solution.py:71
  112.0 31.1 %collective-permute-start.19 = (bf16[2,96,3072]{2,1,0:T(8,128)(2,1)}, bf16[2,96,3072]{2,1,0:T(8,128)(2,1)}, u32[]{:S(2)}, u32[]{:S(2)}) collective-permute-start(bf16[2,96,3072]{2,1,0:T(8,128)(2,1)} %maximum_bitcast_fusion), channel_id=1, source_target_pairs={{0,8},{4,12},{8,0},{12,4},{16,24},{20,28},{24,16},{28,20},{1,9},{5... | collective-permute-start | bytes 3538952 | tf_op jit(solution)/shard_map/ppermute | solution.py:71
  128.7 13.8 %collective-permute-start.24 = (bf16[1,96,768]{2,1,0:T(8,128)(2,1)S(1)}, bf16[1,96,768]{2,1,0:T(8,128)(2,1)S(1)}, u32[]{:S(2)}, u32[]{:S(2)}) collective-permute-start(bf16[1,96,768]{2,1,0:T(8,128)(2,1)S(1)} %maximum_bitcast_fusion.1), channel_id=1, source_target_pairs={{0,24},{4,28},{8,16},{12,20},{16,8},{20,12},{24,0},{28,4},{1,25},{... | collective-permute-start | bytes 442376 | tf_op jit(solution)/shard_map/ppermute | solution.py:71
  129.2 13.2 %collective-permute-start.23 = (bf16[1,96,768]{2,1,0:T(8,128)(2,1)S(1)}, bf16[1,96,768]{2,1,0:T(8,128)(2,1)S(1)}, u32[]{:S(2)}, u32[]{:S(2)}) collective-permute-start(bf16[1,96,768]{2,1,0:T(8,128)(2,1)S(1)} %maximum_bitcast_fusion.1), channel_id=1, source_target_pairs={{0,16},{4,20},{8,24},{12,28},{16,0},{20,4},{24,8},{28,12},{1,17},{... | collective-permute-start | bytes 442376 | tf_op jit(solution)/shard_map/ppermute | solution.py:71
  130.8 12.3 %collective-permute-start.22 = (bf16[1,96,768]{2,1,0:T(8,128)(2,1)S(1)}, bf16[1,96,768]{2,1,0:T(8,128)(2,1)S(1)}, u32[]{:S(2)}, u32[]{:S(2)}) collective-permute-start(bf16[1,96,768]{2,1,0:T(8,128)(2,1)S(1)} %maximum_bitcast_fusion.1), channel_id=1, source_target_pairs={{0,8},{4,12},{8,0},{12,4},{16,24},{20,28},{24,16},{28,20},{1,9},{5... | collective-permute-start | bytes 442376 | tf_op jit(solution)/shard_map/ppermute | solution.py:71
  147.6 8.8 %collective-permute-start.25 = (bf16[2,384,3072]{2,1,0:T(8,128)(2,1)S(1)}, bf16[2,384,3072]{2,1,0:T(8,128)(2,1)}, u32[]{:S(2)}, u32[]{:S(2)}) collective-permute-start(bf16[2,384,3072]{2,1,0:T(8,128)(2,1)S(1)} %pad_maximum_fusion.near_ref), channel_id=1, source_target_pairs={{0,4},{4,0},{8,12},{12,8},{16,20},{20,16},{24,28},{28,24},{1,5},{5... | collective-permute-start | bytes 14155784 | tf_op jit(solution)/shard_map/ppermute | solution.py:71
  152.9 3.6 collective-permute-start.26
  171.4 6.6 %collective-permute-start.29 = (f32[2,8,768]{2,1,0:T(8,128)}, f32[2,8,768]{2,1,0:T(8,128)}, u32[]{:S(2)}, u32[]{:S(2)}) collective-permute-start(f32[2,8,768]{2,1,0:T(8,128)} %fusion.82), channel_id=1, source_target_pairs={{0,3},{1,2},{2,1},{3,0},{4,7},{5,6},{6,5},{7,4},{8,11},{9,10},{10,... | collective-permute-start | bytes 147464 | tf_op jit(solution)/shard_map/ppermute | solution.py:71
  174.0 5.5 %collective-permute-start.28 = (f32[2,8,768]{2,1,0:T(8,128)}, f32[2,8,768]{2,1,0:T(8,128)}, u32[]{:S(2)}, u32[]{:S(2)}) collective-permute-start(f32[2,8,768]{2,1,0:T(8,128)} %fusion.82), channel_id=1, source_target_pairs={{0,2},{1,3},{2,0},{3,1},{4,6},{5,7},{6,4},{7,5},{8,10},{9,11},{10,... | collective-permute-start | bytes 147464 | tf_op jit(solution)/shard_map/ppermute | solution.py:71
  174.0 5.5 %collective-permute-start.27 = (f32[2,8,768]{2,1,0:T(8,128)}, f32[2,8,768]{2,1,0:T(8,128)}, u32[]{:S(2)}, u32[]{:S(2)}) collective-permute-start(f32[2,8,768]{2,1,0:T(8,128)} %fusion.82), channel_id=1, source_target_pairs={{0,1},{1,0},{2,3},{3,2},{4,5},{5,4},{6,7},{7,6},{8,9},{9,8},{10,11... | collective-permute-start | bytes 147464 | tf_op jit(solution)/shard_map/ppermute | solution.py:71
  181.5 1.3 collective-permute-start.30
  183.5 7.2 %collective-permute-start.33 = (bf16[2,2,8,896]{3,2,1,0:T(8,128)(2,1)S(1)}, bf16[2,2,8,896]{3,2,1,0:T(8,128)(2,1)S(1)}, u32[]{:S(2)}, u32[]{:S(2)}) collective-permute-start(bf16[2,2,8,896]{3,2,1,0:T(8,128)(2,1)S(1)} %pad_maximum_fusion.14), channel_id=1, source_target_pairs={{0,24},{4,28},{8,16},{12,20},{16,8},{20,12},{24,0},{28,4},{1,25},{... | collective-permute-start | bytes 172040 | tf_op jit(solution)/shard_map/ppermute | solution.py:71
  184.9 5.7 %collective-permute-start.32 = (bf16[2,2,8,896]{3,2,1,0:T(8,128)(2,1)S(1)}, bf16[2,2,8,896]{3,2,1,0:T(8,128)(2,1)S(1)}, u32[]{:S(2)}, u32[]{:S(2)}) collective-permute-start(bf16[2,2,8,896]{3,2,1,0:T(8,128)(2,1)S(1)} %pad_maximum_fusion.14), channel_id=1, source_target_pairs={{0,16},{4,20},{8,24},{12,28},{16,0},{20,4},{24,8},{28,12},{1,17},{... | collective-permute-start | bytes 172040 | tf_op jit(solution)/shard_map/ppermute | solution.py:71
  186.5 4.2 %collective-permute-start.31 = (bf16[2,2,8,896]{3,2,1,0:T(8,128)(2,1)S(1)}, bf16[2,2,8,896]{3,2,1,0:T(8,128)(2,1)S(1)}, u32[]{:S(2)}, u32[]{:S(2)}) collective-permute-start(bf16[2,2,8,896]{3,2,1,0:T(8,128)(2,1)S(1)} %pad_maximum_fusion.14), channel_id=1, source_target_pairs={{0,8},{4,12},{8,0},{12,4},{16,24},{20,28},{24,16},{28,20},{1,9},{5... | collective-permute-start | bytes 172040 | tf_op jit(solution)/shard_map/ppermute | solution.py:71
  214.3 8.1 %collective-permute-start.34 = (bf16[2,384,3072]{2,1,0:T(8,128)(2,1)}, bf16[2,384,3072]{2,1,0:T(8,128)(2,1)S(1)}, u32[]{:S(2)}, u32[]{:S(2)}) collective-permute-start(bf16[2,384,3072]{2,1,0:T(8,128)(2,1)} %get-tuple-element.242), channel_id=1, source_target_pairs={{0,4},{4,0},{8,12},{12,8},{16,20},{20,16},{24,28},{28,24},{1,5},{5... | collective-permute-start | bytes 14155784 | tf_op jit(solution)/shard_map/ppermute | solution.py:71
  226.2 28.3 %collective-permute-start.35 = (bf16[2,96,3072]{2,1,0:T(8,128)(2,1)}, bf16[2,96,3072]{2,1,0:T(8,128)(2,1)}, u32[]{:S(2)}, u32[]{:S(2)}) collective-permute-start(bf16[2,96,3072]{2,1,0:T(8,128)(2,1)} %fusion.22), channel_id=1, source_target_pairs={{0,16},{4,20},{8,24},{12,28},{16,0},{20,4},{24,8},{28,12},{1,17},{... | collective-permute-start | bytes 3538952 | tf_op jit(solution)/shard_map/ppermute | solution.py:71
  226.7 28.0 %collective-permute-start.36 = (bf16[2,96,3072]{2,1,0:T(8,128)(2,1)}, bf16[2,96,3072]{2,1,0:T(8,128)(2,1)}, u32[]{:S(2)}, u32[]{:S(2)}) collective-permute-start(bf16[2,96,3072]{2,1,0:T(8,128)(2,1)} %fusion.23), channel_id=1, source_target_pairs={{0,8},{4,12},{8,0},{12,4},{16,24},{20,28},{24,16},{28,20},{1,9},{5... | collective-permute-start | bytes 3538952 | tf_op jit(solution)/shard_map/ppermute | solution.py:71
  258.2 18.1 %collective-permute-start.37 = (bf16[1,96,3072]{2,1,0:T(8,128)(2,1)}, bf16[1,96,3072]{2,1,0:T(8,128)(2,1)S(1)}, u32[]{:S(2)}, u32[]{:S(2)}) collective-permute-start(bf16[1,96,3072]{2,1,0:T(8,128)(2,1)} %fusion.57), channel_id=1, source_target_pairs={{0,8},{4,12},{8,0},{12,4},{16,24},{20,28},{24,16},{28,20},{1,9},{5... | collective-permute-start | bytes 1769480 | tf_op jit(solution)/shard_map/ppermute | solution.py:71
  258.8 17.5 %collective-permute-start.38 = (bf16[1,96,3072]{2,1,0:T(8,128)(2,1)S(1)}, bf16[1,96,3072]{2,1,0:T(8,128)(2,1)S(1)}, u32[]{:S(2)}, u32[]{:S(2)}) collective-permute-start(bf16[1,96,3072]{2,1,0:T(8,128)(2,1)S(1)} %fusion.58), channel_id=1, source_target_pairs={{0,16},{4,20},{8,24},{12,28},{16,0},{20,4},{24,8},{28,12},{1,17},{... | collective-permute-start | bytes 1769480 | tf_op jit(solution)/shard_map/ppermute | solution.py:71
  260.3 15.9 %collective-permute-start.39 = (bf16[256,768]{1,0:T(8,128)(2,1)}, bf16[256,768]{1,0:T(8,128)(2,1)}, u32[]{:S(2)}, u32[]{:S(2)}) collective-permute-start(bf16[256,768]{1,0:T(8,128)(2,1)} %get-tuple-element.261), channel_id=1, source_target_pairs={{0,1},{2,3},{1,0},{3,2},{4,5},{6,7},{5,4},{7,6},{8,9},{10,11},{9,8... | collective-permute-start | bytes 1179656 | tf_op jit(solution)/shard_map/ppermute | solution.py:77
  261.1 15.2 %collective-permute-start.40 = (bf16[256,768]{1,0:T(8,128)(2,1)}, bf16[256,768]{1,0:T(8,128)(2,1)S(1)}, u32[]{:S(2)}, u32[]{:S(2)}) collective-permute-start(bf16[256,768]{1,0:T(8,128)(2,1)} %get-tuple-element.262), channel_id=1, source_target_pairs={{1,2},{2,1},{5,6},{6,5},{9,10},{10,9},{13,14},{14,13},{17,18},{18,... | collective-permute-start | bytes 1179656 | tf_op jit(solution)/shard_map/ppermute | solution.py:77
  280.7 25.3 %collective-permute-start.41 = (bf16[2,96,1536]{2,1,0:T(8,128)(2,1)}, bf16[2,96,1536]{2,1,0:T(8,128)(2,1)}, u32[]{:S(2)}, u32[]{:S(2)}) collective-permute-start(bf16[2,96,1536]{2,1,0:T(8,128)(2,1)} %fusion.61), channel_id=1, source_target_pairs={{0,2},{1,3},{2,0},{3,1},{4,6},{5,7},{6,4},{7,5},{8,10},{9,11},{10,... | collective-permute-start | bytes 1769480 | tf_op jit(solution)/shard_map/ppermute | solution.py:71
  306.1 19.2 %collective-permute-start.42 = (bf16[4,384,768]{2,1,0:T(8,128)(2,1)S(1)}, bf16[4,384,768]{2,1,0:T(8,128)(2,1)S(1)}, u32[]{:S(2)}, u32[]{:S(2)}) collective-permute-start(bf16[4,384,768]{2,1,0:T(8,128)(2,1)S(1)} %copy-done.120), channel_id=1, source_target_pairs={{0,4},{4,0},{8,12},{12,8},{16,20},{20,16},{24,28},{28,24},{1,5},{5... | collective-permute-start | bytes 7077896 | tf_op jit(solution)/shard_map/ppermute | solution.py:71
  307.3 9.9 %collective-permute-start.45 = (bf16[2,96,768]{2,1,0:T(8,128)(2,1)S(1)}, bf16[2,96,768]{2,1,0:T(8,128)(2,1)S(1)}, u32[]{:S(2)}, u32[]{:S(2)}) collective-permute-start(bf16[2,96,768]{2,1,0:T(8,128)(2,1)S(1)} %slice.518), channel_id=1, source_target_pairs={{0,1},{1,0},{2,3},{3,2},{4,5},{5,4},{6,7},{7,6},{8,9},{9,8},{10,11... | collective-permute-start | bytes 884744 | tf_op jit(solution)/shard_map/ppermute | solution.py:71
  307.4 17.8 %collective-permute-start.43 = (bf16[256,768]{1,0:T(8,128)(2,1)S(1)}, bf16[256,768]{1,0:T(8,128)(2,1)S(1)}, u32[]{:S(2)}, u32[]{:S(2)}) collective-permute-start(bf16[256,768]{1,0:T(8,128)(2,1)S(1)} %get-tuple-element.294), channel_id=1, source_target_pairs={{0,1},{2,3},{1,0},{3,2},{4,5},{6,7},{5,4},{7,6},{8,9},{10,11},{9,8... | collective-permute-start | bytes 1179656 | tf_op jit(solution)/shard_map/ppermute | solution.py:77
  309.5 15.7 %collective-permute-start.44 = (bf16[256,768]{1,0:T(8,128)(2,1)S(1)}, bf16[256,768]{1,0:T(8,128)(2,1)S(1)}, u32[]{:S(2)}, u32[]{:S(2)}) collective-permute-start(bf16[256,768]{1,0:T(8,128)(2,1)S(1)} %get-tuple-element.295), channel_id=1, source_target_pairs={{1,2},{2,1},{5,6},{6,5},{9,10},{10,9},{13,14},{14,13},{17,18},{18,... | collective-permute-start | bytes 1179656 | tf_op jit(solution)/shard_map/ppermute | solution.py:77
  328.1 35.9 %collective-permute-start.49 = (bf16[2,256,768]{2,1,0:T(8,128)(2,1)}, bf16[2,256,768]{2,1,0:T(8,128)(2,1)}, u32[]{:S(2)}, u32[]{:S(2)}) collective-permute-start(bf16[2,256,768]{2,1,0:T(8,128)(2,1)} %pad_maximum_fusion.8), channel_id=1, source_target_pairs={{0,1},{2,3},{1,0},{3,2},{4,5},{6,7},{5,4},{7,6},{8,9},{10,11},{9,8... | collective-permute-start | bytes 2359304 | tf_op jit(solution)/shard_map/ppermute | solution.py:77
  328.4 35.7 %collective-permute-start.50 = (bf16[2,256,768]{2,1,0:T(8,128)(2,1)}, bf16[2,256,768]{2,1,0:T(8,128)(2,1)}, u32[]{:S(2)}, u32[]{:S(2)}) collective-permute-start(bf16[2,256,768]{2,1,0:T(8,128)(2,1)} %pad_maximum_fusion.9), channel_id=1, source_target_pairs={{1,2},{2,1},{5,6},{6,5},{9,10},{10,9},{13,14},{14,13},{17,18},{18,... | collective-permute-start | bytes 2359304 | tf_op jit(solution)/shard_map/ppermute | solution.py:77
  331.3 19.2 %collective-permute-start.48 = (bf16[4,96,768]{2,1,0:T(8,128)(2,1)}, bf16[4,96,768]{2,1,0:T(8,128)(2,1)}, u32[]{:S(2)}, u32[]{:S(2)}) collective-permute-start(bf16[4,96,768]{2,1,0:T(8,128)(2,1)} %get-tuple-element.432), channel_id=1, source_target_pairs={{0,24},{4,28},{8,16},{12,20},{16,8},{20,12},{24,0},{28,4},{1,25},{... | collective-permute-start | bytes 1769480 | tf_op jit(solution)/shard_map/ppermute | solution.py:71
  336.0 27.0 %collective-permute-start.47 = (bf16[4,96,768]{2,1,0:T(8,128)(2,1)}, bf16[4,96,768]{2,1,0:T(8,128)(2,1)}, u32[]{:S(2)}, u32[]{:S(2)}) collective-permute-start(bf16[4,96,768]{2,1,0:T(8,128)(2,1)} %get-tuple-element.433), channel_id=1, source_target_pairs={{0,16},{4,20},{8,24},{12,28},{16,0},{20,4},{24,8},{28,12},{1,17},{... | collective-permute-start | bytes 1769480 | tf_op jit(solution)/shard_map/ppermute | solution.py:71
  339.2 24.9 %collective-permute-start.46 = (bf16[4,96,768]{2,1,0:T(8,128)(2,1)S(1)}, bf16[4,96,768]{2,1,0:T(8,128)(2,1)}, u32[]{:S(2)}, u32[]{:S(2)}) collective-permute-start(bf16[4,96,768]{2,1,0:T(8,128)(2,1)S(1)} %get-tuple-element.434), channel_id=1, source_target_pairs={{0,8},{4,12},{8,0},{12,4},{16,24},{20,28},{24,16},{28,20},{1,9},{5... | collective-permute-start | bytes 1769480 | tf_op jit(solution)/shard_map/ppermute | solution.py:71
  368.7 9.8 %collective-permute-start.53 = (bf16[4,96,192]{2,1,0:T(8,128)(2,1)S(1)}, bf16[4,96,192]{2,1,0:T(8,128)(2,1)S(1)}, u32[]{:S(2)}, u32[]{:S(2)}) collective-permute-start(bf16[4,96,192]{2,1,0:T(8,128)(2,1)S(1)} %get-tuple-element.459), channel_id=1, source_target_pairs={{0,3},{1,2},{2,1},{3,0},{4,7},{5,6},{6,5},{7,4},{8,11},{9,10},{10,... | collective-permute-start | bytes 442376 | tf_op jit(solution)/shard_map/ppermute | solution.py:71
  370.0 19.0 %collective-permute-start.52 = (bf16[4,96,192]{2,1,0:T(8,128)(2,1)S(1)}, bf16[4,96,192]{2,1,0:T(8,128)(2,1)S(1)}, u32[]{:S(2)}, u32[]{:S(2)}) collective-permute-start(bf16[4,96,192]{2,1,0:T(8,128)(2,1)S(1)} %get-tuple-element.460), channel_id=1, source_target_pairs={{0,2},{1,3},{2,0},{3,1},{4,6},{5,7},{6,4},{7,5},{8,10},{9,11},{10,... | collective-permute-start | bytes 442376 | tf_op jit(solution)/shard_map/ppermute | solution.py:71
  372.1 16.9 %collective-permute-start.51 = (bf16[4,96,192]{2,1,0:T(8,128)(2,1)S(1)}, bf16[4,96,192]{2,1,0:T(8,128)(2,1)S(1)}, u32[]{:S(2)}, u32[]{:S(2)}) collective-permute-start(bf16[4,96,192]{2,1,0:T(8,128)(2,1)S(1)} %get-tuple-element.461), channel_id=1, source_target_pairs={{0,1},{1,0},{2,3},{3,2},{4,5},{5,4},{6,7},{7,6},{8,9},{9,8},{10,11... | collective-permute-start | bytes 442376 | tf_op jit(solution)/shard_map/ppermute | solution.py:71
  390.4 1.3 collective-permute-start.54
  391.7 4.7 %collective-permute-start.57 = (f32[8,768]{1,0:T(8,128)S(1)}, f32[8,768]{1,0:T(8,128)S(1)}, u32[]{:S(2)}, u32[]{:S(2)}) collective-permute-start(f32[8,768]{1,0:T(8,128)S(1)} %add.616), channel_id=1, source_target_pairs={{0,24},{4,28},{8,16},{12,20},{16,8},{20,12},{24,0},{28,4},{1,25},{... | collective-permute-start | bytes 73736 | tf_op jit(solution)/shard_map/ppermute | solution.py:71
  393.4 3.8 collective-permute-start.56
  394.6 3.8 collective-permute-start.55
  398.6 6.2 %collective-permute-start.60 = (f32[8,768]{1,0:T(8,128)S(1)}, f32[8,768]{1,0:T(8,128)S(1)}, u32[]{:S(2)}, u32[]{:S(2)}) collective-permute-start(f32[8,768]{1,0:T(8,128)S(1)} %add_add_fusion.1), channel_id=1, source_target_pairs={{0,3},{1,2},{2,1},{3,0},{4,7},{5,6},{6,5},{7,4},{8,11},{9,10},{10,... | collective-permute-start | bytes 73736 | tf_op jit(solution)/shard_map/ppermute | solution.py:71
  400.1 4.8 %collective-permute-start.59 = (f32[8,768]{1,0:T(8,128)S(1)}, f32[8,768]{1,0:T(8,128)S(1)}, u32[]{:S(2)}, u32[]{:S(2)}) collective-permute-start(f32[8,768]{1,0:T(8,128)S(1)} %add_add_fusion.1), channel_id=1, source_target_pairs={{0,2},{1,3},{2,0},{3,1},{4,6},{5,7},{6,4},{7,5},{8,10},{9,11},{10,... | collective-permute-start | bytes 73736 | tf_op jit(solution)/shard_map/ppermute | solution.py:71
  400.1 5.0 %collective-permute-start.58 = (f32[8,768]{1,0:T(8,128)S(1)}, f32[8,768]{1,0:T(8,128)S(1)}, u32[]{:S(2)}, u32[]{:S(2)}) collective-permute-start(f32[8,768]{1,0:T(8,128)S(1)} %add_add_fusion.1), channel_id=1, source_target_pairs={{0,1},{1,0},{2,3},{3,2},{4,5},{5,4},{6,7},{7,6},{8,9},{9,8},{10,11... | collective-permute-start | bytes 73736 | tf_op jit(solution)/shard_map/ppermute | solution.py:71
  (121 other events, 922.3 us)

commit v4 on v3

--- a/solution.py
+++ b/solution.py
@@ -130,9 +130,9 @@
 
 def split_outer(terms, masks, first):
     spot = 0 if first else len(masks) - 1
-    n, r, w = terms[0].shape
-    split = [term.reshape(n >> (spot + 1), 2, 1 << spot, r, w) for term in terms]
-    stay, leave = ([term[:, k].reshape(n // 2, r, w) for term in split] for k in range(2))
+    c, n, r, w = terms[0].shape
+    split = [term.reshape(c, n >> (spot + 1), 2, 1 << spot, r, w) for term in terms]
+    stay, leave = ([term[:, :, k].reshape(c, n // 2, r, w) for term in split] for k in range(2))
     return stay, add_low(*leave), masks[spot], masks[:spot] + masks[spot + 1 :]
 
 
@@ -146,10 +146,6 @@
         return jnp.concatenate([part, received], axis=0)
     n, r, w = part.shape
     return jnp.stack([part, received], axis=1).reshape(2 * n, r, w)
-
-
-def send_plane(held):
-    return [swap(held[:, number + 1], "dp", mask) for number, mask in enumerate(plane_masks())]
 
 
 def send_columns(values):
@@ -966,7 +962,9 @@
         return [split_outer(terms, masks, first) for (terms, masks), first in zip(parts, (False, True))]
 
     ffn_blocks = [to_blocks(ffn_keep), to_blocks(ffn_received)]
-    parts = [([held[number] for held in ffn_blocks], outer_masks()) for number in range(2)]
+    parts = [
+        ([held[number : number + 1] for held in ffn_blocks], outer_masks()) for number in range(2)
+    ]
     grads, owns, bias_parts, flows = [], [], [], []
 
     def leave(flow, n):
@@ -1014,7 +1012,7 @@
     others = came
     for flow, got in zip(flows, others):
         join(flow, reach - 1, got)
-    ffn_last = [add_low(*terms)[0] for terms, _ in parts]
+    ffn_last = [add_low(*terms)[0, 0] for terms, _ in parts]
     ffn_last, grads = after((ffn_last, grads))
     ffn_last = jnp.stack(ffn_last)
     ffn_column = send_columns_chain(ffn_last)
@@ -1027,22 +1025,30 @@
     last = list(last[1])
     attn_received = swap(attn_send, "dp", 1)
     came = leave(last, reach) if reach > 1 else ()
-    ffn_reduced = finish_columns_chain(ffn_last, ffn_column)
-    attn_received, came, ffn_reduced = after((attn_received, came, ffn_reduced))
-    attn_held = to_blocks(add_low(attn_keep, attn_received))
+    others = [leave(flow, 1) for flow in flows]
+    attn_received, came, others, ffn_column = after((attn_received, came, others, ffn_column))
+    attn_blocks = [to_blocks(attn_keep), to_blocks(attn_received)]
+    attn_parts = [([held[k : k + 2] for held in attn_blocks], outer_masks()) for k in (0, 2)]
     if reach > 1:
         join(last, reach - 1, came)
-    flow = [jnp.stack(pair) for pair in zip(*flows, last)]
-    attn_held, flow = after((attn_held, flow))
-    attn_received = send_plane(attn_held)
-    for n in range(reach - 1, 0, -1):
-        came = leave(flow, n)
-        join(flow, n - 1, came)
-    attn_received, came = after((attn_received, came))
-    attn_last = add_low(attn_held[:, 0], *attn_received)
+    hopped, ffn_reduced = (), None
+    while attn_parts[0][1]:
+        steps = outer_split(attn_parts)
+        sent, last = after(([step[1] for step in steps], last))
+        received = [swap(leaves, "dp", step[2]) for leaves, step in zip(sent, steps)]
+        if ffn_reduced is None:
+            hopped = leave(last, 1)
+            ffn_reduced = finish_columns_chain(ffn_last, ffn_column)
+        received, hopped, ffn_reduced = after((received, hopped, ffn_reduced))
+        attn_parts = [(step[0] + [got], step[3]) for step, got in zip(steps, received)]
+    attn_last = jnp.concatenate([add_low(*terms) for terms, _ in attn_parts])[:, 0]
     attn_columns = send_columns(attn_last)
-    normed_one_grad = jnp.stack(owns) + came[0].astype(F32) + came[1].astype(F32)
-    normed_one_grad = normed_one_grad.reshape(micro_count * rows, D)
+    normed_one_grad = jnp.concatenate(
+        [
+            own + even.astype(F32) + odd.astype(F32)
+            for own, (even, odd) in zip(owns, [*others, hopped])
+        ]
+    )
     gain_one = jnp.sum(normed_one_grad * token_rows * factor_one, axis=0)
     tokens_grad = hidden_one_grad + norm_back(token_rows, factor_one, normed_one_grad * gains[0])
     tokens_grad = dot(tokens_grad, turn_wide, NT, HIGHEST)

time: 417 us -> 411 us (0.986)
  waiting for transfers between devices: 111 us -> 100 us
  starting transfers between devices: 82.3 us -> 87.2 us
    ppermute x49 -> x50, waiting for transfers between devices: 99.1 us -> 77.5 us  [swap(): return lax.ppermute(values, axis, [(i, i ^ mask) for i in range(count)])]
    ppermute x12 -> x14, waiting for transfers between devices: 11.5 us -> 23 us  [link(): return lax.ppermute(values, 'mp', pairs + [(j, i) for i, j in pairs])]
    ppermute x12 -> x14, starting transfers between devices: 17.8 us -> 22.2 us  [link(): return lax.ppermute(values, 'mp', pairs + [(j, i) for i, j in pairs])]
    convert_element_type x8 -> x14, other arithmetic: 11.1 us -> 13.4 us  [add_low(): sum([part.astype(F32) for part in received], stay.astype(F32)).astype(BF16)]
    ppermute x49 -> x50, starting transfers between devices: 64.5 us -> 65 us  [swap(): return lax.ppermute(values, axis, [(i, i ^ mask) for i in range(count)])]
    unnamed x262 -> x288, local copies, waits for them, and re-layouts: 15.7 us -> 15.5 us
  transfers between devices with their start and end apart: 61 -> 64, of which waited for: 31 -> 29; matrix products, arithmetic and copies ran while one was open for 15% -> 15% of each run, Pallas kernels for 17% -> 17%
where the time goes in v4:
time: 411 us; the launch traced here: 403 us
  Pallas kernels  101 us (25%)
  waiting for transfers between devices  100 us (24%)
  starting transfers between devices  87.2 us (21%)
  other arithmetic  52.8 us (13%)
  matrix products  33.7 us (8%)
  local copies, waits for them, and re-layouts  24 us (6%)
  between operations  4.19 us (1%)
    ppermute x50, waiting for transfers between devices, swap(): return lax.ppermute(values, axis, [(i, i ^ mask) for i in range(count)])  77.5 us
    ppermute x50, starting transfers between devices, swap(): return lax.ppermute(values, axis, [(i, i ^ mask) for i in range(count)])  65 us
    dot_general x24, matrix products, dot(): lax.dot_general(left, right, dims, precision=precision, preferred_element...  31.6 us
    pallas_call x2, Pallas kernels, attend_back(): pl.pallas_call(functools.partial(backward_kernel, reach), grid=(pairs,),...  29.2 us
    ppermute x14, waiting for transfers between devices, link(): return lax.ppermute(values, 'mp', pairs + [(j, i) for i, j in pairs])  23 us
    ppermute x14, starting transfers between devices, link(): return lax.ppermute(values, 'mp', pairs + [(j, i) for i, j in pairs])  22.2 us
    pallas_call x2, Pallas kernels, attend(): pl.pallas_call(functools.partial(forward_kernel, reach), grid=(pairs,), i...  19.9 us
    unnamed x288, local copies, waits for them, and re-layouts  15.5 us
  transfers between devices with their start and end apart: 64, of which 29 were waited for; matrix products, arithmetic and copies ran while one was open for 15% of the time, Pallas kernels for 17%

profile of v4, /device:TPU:0, one launch (start us, length us, event | category | flops | bytes accessed | tf_op | source)
XLA Modules:
  0.0 403.2 jit_solution(17999051902188028945)
XLA Ops:
  1.8 5.1 %collective-permute-start.2 = (bf16[4,96,192]{2,1,0:T(8,128)(2,1)S(1)}, bf16[4,96,192]{2,1,0:T(8,128)(2,1)}, u32[]{:S(2)}, u32[]{:S(2)}) collective-permute-start(bf16[4,96,192]{2,1,0:T(8,128)(2,1)S(1)} %convert_element_type.749), channel_id=1, source_target_pairs={{0,3},{1,2},{2,1},{3,0},{4,7},{5,6},{6,5},{7,4},{8,11},{9,10},{10,... | collective-permute-start | bytes 442376 | tf_op jit(solution)/shard_map/ppermute | solution.py:71
  15.7 1.9 slice_dynamic-update-slice_fusion
  17.6 9.2 %collective-permute-done.3 = bf16[2,96,768]{2,1,0:T(8,128)(2,1)} collective-permute-done((bf16[2,96,768]{2,1,0:T(8,128)(2,1)S(1)}, bf16[2,96,768]{2,1,0:T(8,128)(2,1)}, u32[]{:S(2)}, u32[]{:S(2)}) %collective-permute-start.3) | collective-permute-done | bytes 294944 | tf_op jit(solution)/shard_map/ppermute | solution.py:71
  29.2 1.6 collective-permute-start.5
  32.8 1.6 collective-permute-start.7
  35.7 7.4 %shard_map.322.bias_ref = f32[12,3,256,256]{3,2,1,0:T(8,128)} custom-call(f32[12,3,512]{2,1,0:T(4,128)S(1)} %copy.114.line_ref), custom_call_target="tpu_custom_call" | custom-call | tf_op jit(solution)/shard_map/pallas_call | solution.py:234
  44.6 2.4 collective-permute-done.4
  47.0 11.3 %collective-permute-done.6 = bf16[4,96,768]{2,1,0:T(8,128)(2,1)S(1)} collective-permute-done((bf16[4,96,768]{2,1,0:T(8,128)(2,1)S(1)}, bf16[4,96,768]{2,1,0:T(8,128)(2,1)S(1)}, u32[]{:S(2)}, u32[]{:S(2)}) %collective-permute-start.6) | collective-permute-done | bytes 589856 | tf_op jit(solution)/shard_map/ppermute | solution.py:71
  58.3 1.7 pad_maximum_fusion.1
  63.7 2.5 collective-permute-start.9
  67.6 1.6 collective-permute-start.12
  70.8 12.1 %collective-permute-done.12 = bf16[1,96,3072]{2,1,0:T(8,128)(2,1)S(1)} collective-permute-done((bf16[1,96,3072]{2,1,0:T(8,128)(2,1)S(1)}, bf16[1,96,3072]{2,1,0:T(8,128)(2,1)S(1)}, u32[]{:S(2)}, u32[]{:S(2)}) %collective-permute-start.12) | collective-permute-done | bytes 589856 | tf_op jit(solution)/shard_map/ppermute | solution.py:71
  84.3 2.3 collective-permute-start.17
  90.7 2.8 collective-permute-start.13
  94.6 3.4 fusion.30
  98.3 3.3 collective-permute-done.13
  102.4 3.9 collective-permute-start.20
  106.5 3.4 convolution_convert_fusion.1.k_ref.v_ref
  110.5 1.6 collective-permute-start.18
  113.6 9.8 %attend.2 = (bf16[256,768]{1,0:T(8,128)(2,1)S(1)}, f32[6,8,256]{2,1,0:T(8,128)S(1)}) custom-call(s32[7]{0:T(128)S(1)} %get-tuple-element.506.range_ref, f32[2,12]{1,0:T(2,128)S(1)} %pad_maximum_fusion.16.far_ref, bf16[256,768]{1,0:T(8,128)(2,1)S(1)} %convolution_convert_fusion.5.q_ref, bf16[1280,1536]{1,0:T(8,128)(2,1)S(1)} %convolution_convert_fusion.1.k_ref.v_ref, ...), custom_call_target="tpu_custom_call" | custom-call | flops 100000 | bytes 10000 | tf_op jit(solution)/shard_map/attend/pallas_call | solution.py:416
  125.2 3.5 convolution_convert_fusion.k_ref.v_ref
  129.2 1.5 collective-permute-start.23
  132.3 10.2 %attend.3 = (bf16[256,768]{1,0:T(8,128)(2,1)S(1)}, f32[6,8,256]{2,1,0:T(8,128)S(1)}) custom-call(s32[7]{0:T(128)S(1)} %get-tuple-element.505.range_ref, f32[2,12]{1,0:T(2,128)S(1)} %pad_maximum_fusion.16.far_ref, bf16[256,768]{1,0:T(8,128)(2,1)S(1)} %convolution_convert_fusion.4.q_ref, bf16[1280,1536]{1,0:T(8,128)(2,1)S(1)} %convolution_convert_fusion.k_ref.v_ref, ...), custom_call_target="tpu_custom_call" | custom-call | flops 100000 | bytes 10000 | tf_op jit(solution)/shard_map/attend/pallas_call | solution.py:416
  143.1 2.0 pad_maximum_fusion.4
  145.4 1.8 pad_maximum_fusion.3
  147.9 1.9 fusion.2.turn_ref
  153.3 2.2 copy-done.53
  157.5 11.1 %feed.1 = (f32[512,768]{1,0:T(8,128)S(1)}, bf16[512,3072]{1,0:T(8,128)(2,1)}, bf16[512,3072]{1,0:T(8,128)(2,1)}) custom-call(bf16[512,768]{1,0:T(8,128)(2,1)S(1)} %multiply_convert_fusion.normed_ref, f32[512,768]{1,0:T(8,128)S(1)} %bitcast_add_fusion.1.hidden_ref, bf16[2,384,3072]{2,1,0:T(8,128)(2,1)} %copy-done.51, ...), custom_call_target="tpu_custom_call" | custom-call | flops 100000 | bytes 10000 | tf_op jit(solution)/shard_map/feed/pallas_call | solution.py:554
  171.4 2.5 collective-permute-start.29
  173.9 1.9 collective-permute-start.27
  184.9 1.5 collective-permute-start.32
  186.9 3.6 collective-permute-done.31
  192.8 2.8 contrast.1
  198.6 15.5 %feed_back.1 = (f32[512,768]{1,0:T(8,128)S(1)}, bf16[2,384,3072]{2,1,0:T(8,128)(2,1)}, bf16[2,384,3072]{2,1,0:T(8,128)(2,1)}) custom-call(bf16[512,768]{1,0:T(8,128)(2,1)S(1)} %multiply_convert_fusion.normed_ref, bf16[512,768]{1,0:T(8,128)(2,1)S(1)} %get-tuple-element.511.up_ref, bf16[2,384,3072]{2,1,0:T(8,128)(2,1)} %copy-done.51, ...), custom_call_target="tpu_custom_call" | custom-call | flops 100000 | bytes 10000 | tf_op jit(solution)/shard_map/feed_back/pallas_call | solution.py:576
  219.4 2.7 collective-permute-done.34
  222.5 1.7 fusion.22
  227.0 14.9 %attend_back.2 = (bf16[256,768]{1,0:T(8,128)(2,1)S(1)}, bf16[1280,768]{1,0:T(8,128)(2,1)S(1)}, bf16[1280,768]{1,0:T(8,128)(2,1)S(1)}, f32[6,2,8,256]{3,2,1,0:T(8,128)S(1)}) custom-call(s32[7]{0:T(128)S(1)} %get-tuple-element.506.range_ref, f32[2,12]{1,0:T(2,128)S(1)} %pad_maximum_fusion.16.far_ref, bf16[256,768]{1,0:T(8,128)(2,1)S(1)} %copy-done.30, ...), custom_call_target="tpu_custom_call" | custom-call | flops 100000 | bytes 10000 | tf_op jit(solution)/shard_map/attend_back/pallas_call | solution.py:436
  241.9 1.7 fusion.46
  245.0 1.9 fusion.149
  250.8 3.4 collective-permute-done.35
  257.8 1.5 collective-permute-start.38
  261.5 14.4 %attend_back.3 = (bf16[256,768]{1,0:T(8,128)(2,1)S(1)}, bf16[1280,768]{1,0:T(8,128)(2,1)S(1)}, bf16[1280,768]{1,0:T(8,128)(2,1)S(1)}, f32[6,2,8,256]{3,2,1,0:T(8,128)S(1)}) custom-call(s32[7]{0:T(128)S(1)} %get-tuple-element.505.range_ref, f32[2,12]{1,0:T(2,128)S(1)} %pad_maximum_fusion.16.far_ref, bf16[256,768]{1,0:T(8,128)(2,1)S(1)} %copy-done.28, ...), custom_call_target="tpu_custom_call" | custom-call | flops 100000 | bytes 10000 | tf_op jit(solution)/shard_map/attend_back/pallas_call | solution.py:436
  275.9 1.9 fusion.60
  277.8 1.6 fusion.59
  280.3 5.7 %collective-permute-start.41 = (bf16[2,96,1536]{2,1,0:T(8,128)(2,1)}, bf16[2,96,1536]{2,1,0:T(8,128)(2,1)}, u32[]{:S(2)}, u32[]{:S(2)}) collective-permute-start(bf16[2,96,1536]{2,1,0:T(8,128)(2,1)} %fusion.61), channel_id=1, source_target_pairs={{0,2},{1,3},{2,0},{3,1},{4,6},{5,7},{6,4},{7,5},{8,10},{9,11},{10,... | collective-permute-start | bytes 1769480 | tf_op jit(solution)/shard_map/ppermute | solution.py:71
  286.1 1.7 fusion.44
  287.8 1.8 add_convert_fusion.8
  289.7 1.9 fusion.150
  292.7 10.2 %collect.1 = (bf16[4,384,768]{2,1,0:T(8,128)(2,1)}, bf16[4,384,768]{2,1,0:T(8,128)(2,1)}) custom-call(bf16[768,1280]{1,0:T(8,128)(2,1)S(1)} %copy-done.10, bf16[768,1280]{1,0:T(8,128)(2,1)S(1)} %copy-done.12, bf16[256,768]{1,0:T(8,128)(2,1)S(1)} %get-tuple-element.286.refs_2_, bf16[1280,768]{1,0:T(8,128)(2,1)} %copy-done.7, bf16[1280,768]{1,0:T(8,128)(2,1)} %copy-done.20, ...), custom_call_target="tpu_custom_call" | custom-call | flops 100000 | bytes 10000 | tf_op jit(solution)/shard_map/collect/pallas_call | solution.py:489
  303.5 4.2 %collective-permute-done.41 = bf16[2,96,1536]{2,1,0:T(8,128)(2,1)} collective-permute-done((bf16[2,96,1536]{2,1,0:T(8,128)(2,1)}, bf16[2,96,1536]{2,1,0:T(8,128)(2,1)}, u32[]{:S(2)}, u32[]{:S(2)}) %collective-permute-start.41) | collective-permute-done | bytes 589856 | tf_op jit(solution)/shard_map/ppermute | solution.py:71
  310.3 5.2 %collective-permute-start.43 = (bf16[256,768]{1,0:T(8,128)(2,1)S(1)}, bf16[256,768]{1,0:T(8,128)(2,1)S(1)}, u32[]{:S(2)}, u32[]{:S(2)}) collective-permute-start(bf16[256,768]{1,0:T(8,128)(2,1)S(1)} %get-tuple-element.304), channel_id=1, source_target_pairs={{0,1},{2,3},{1,0},{3,2},{4,5},{6,7},{5,4},{7,6},{8,9},{10,11},{9,8... | collective-permute-start | bytes 1179656 | tf_op jit(solution)/shard_map/ppermute | solution.py:77
  316.6 4.1 %collective-permute-done.45 = bf16[256,768]{1,0:T(8,128)(2,1)S(1)} collective-permute-done((bf16[256,768]{1,0:T(8,128)(2,1)S(1)}, bf16[256,768]{1,0:T(8,128)(2,1)S(1)}, u32[]{:S(2)}, u32[]{:S(2)}) %collective-permute-start.45) | collective-permute-done | bytes 393248 | tf_op jit(solution)/shard_map/ppermute | solution.py:77
  320.7 8.0 %collective-permute-done.43 = bf16[256,768]{1,0:T(8,128)(2,1)S(1)} collective-permute-done((bf16[256,768]{1,0:T(8,128)(2,1)S(1)}, bf16[256,768]{1,0:T(8,128)(2,1)S(1)}, u32[]{:S(2)}, u32[]{:S(2)}) %collective-permute-start.43) | collective-permute-done | bytes 393248 | tf_op jit(solution)/shard_map/ppermute | solution.py:77
  330.8 4.6 %collective-permute-start.51 = (bf16[2,96,768]{2,1,0:T(8,128)(2,1)S(1)}, bf16[2,96,768]{2,1,0:T(8,128)(2,1)S(1)}, u32[]{:S(2)}, u32[]{:S(2)}) collective-permute-start(bf16[2,96,768]{2,1,0:T(8,128)(2,1)S(1)} %slice.624), channel_id=1, source_target_pairs={{0,1},{1,0},{2,3},{3,2},{4,5},{5,4},{6,7},{7,6},{8,9},{9,8},{10,11... | collective-permute-start | bytes 884744 | tf_op jit(solution)/shard_map/ppermute | solution.py:71
  339.3 4.0 %collective-permute-done.51 = bf16[2,96,768]{2,1,0:T(8,128)(2,1)S(1)} collective-permute-done((bf16[2,96,768]{2,1,0:T(8,128)(2,1)S(1)}, bf16[2,96,768]{2,1,0:T(8,128)(2,1)S(1)}, u32[]{:S(2)}, u32[]{:S(2)}) %collective-permute-start.51) | collective-permute-done | bytes 294944 | tf_op jit(solution)/shard_map/ppermute | solution.py:71
  343.4 7.3 %collective-permute-done.49 = bf16[256,768]{1,0:T(8,128)(2,1)S(1)} collective-permute-done((bf16[256,768]{1,0:T(8,128)(2,1)S(1)}, bf16[256,768]{1,0:T(8,128)(2,1)S(1)}, u32[]{:S(2)}, u32[]{:S(2)}) %collective-permute-start.49) | collective-permute-done | bytes 393248 | tf_op jit(solution)/shard_map/ppermute | solution.py:77
  356.7 4.1 %collective-permute-done.52 = bf16[2,1,96,768]{3,2,0,1:T(8,128)(2,1)} collective-permute-done((bf16[2,1,96,768]{3,2,0,1:T(8,128)(2,1)}, bf16[2,1,96,768]{3,2,0,1:T(8,128)(2,1)}, u32[]{:S(2)}, u32[]{:S(2)}) %collective-permute-start.52) | collective-permute-done | bytes 294944 | tf_op jit(solution)/shard_map/ppermute | solution.py:71
  365.5 2.0 collective-permute-start.56
  369.9 3.8 fusion.1
  375.2 8.2 %collective-permute-done.55.refs_2_ = bf16[4,96,192]{2,1,0:T(8,128)(2,1)S(1)} collective-permute-done((bf16[4,96,192]{2,1,0:T(8,128)(2,1)S(1)}, bf16[4,96,192]{2,1,0:T(8,128)(2,1)S(1)}, u32[]{:S(2)}, u32[]{:S(2)}) %collective-permute-start.55) | collective-permute-done | bytes 147488 | tf_op jit(solution)/shard_map/ppermute | solution.py:71
  392.1 1.7 collective-permute-start.63
  393.8 2.8 collective-permute-start.61
  396.5 1.7 fusion.21
  398.8 2.5 update.1
  (517 shorter events, 117.0 us)
Async XLA Ops:
  1.8 26.0 %collective-permute-start.2 = (bf16[4,96,192]{2,1,0:T(8,128)(2,1)S(1)}, bf16[4,96,192]{2,1,0:T(8,128)(2,1)}, u32[]{:S(2)}, u32[]{:S(2)}) collective-permute-start(bf16[4,96,192]{2,1,0:T(8,128)(2,1)S(1)} %convert_element_type.749), channel_id=1, source_target_pairs={{0,3},{1,2},{2,1},{3,0},{4,7},{5,6},{6,5},{7,4},{8,11},{9,10},{10,... | collective-permute-start | bytes 442376 | tf_op jit(solution)/shard_map/ppermute | solution.py:71
  6.9 20.9 %collective-permute-start.1 = (bf16[4,96,192]{2,1,0:T(8,128)(2,1)S(1)}, bf16[4,96,192]{2,1,0:T(8,128)(2,1)}, u32[]{:S(2)}, u32[]{:S(2)}) collective-permute-start(bf16[4,96,192]{2,1,0:T(8,128)(2,1)S(1)} %convert_element_type.749), channel_id=1, source_target_pairs={{0,2},{1,3},{2,0},{3,1},{4,6},{5,7},{6,4},{7,5},{8,10},{9,11},{10,... | collective-permute-start | bytes 442376 | tf_op jit(solution)/shard_map/ppermute | solution.py:71
  6.9 20.9 %collective-permute-start = (bf16[4,96,192]{2,1,0:T(8,128)(2,1)S(1)}, bf16[4,96,192]{2,1,0:T(8,128)(2,1)}, u32[]{:S(2)}, u32[]{:S(2)}) collective-permute-start(bf16[4,96,192]{2,1,0:T(8,128)(2,1)S(1)} %convert_element_type.749), channel_id=1, source_target_pairs={{0,1},{1,0},{2,3},{3,2},{4,5},{5,4},{6,7},{7,6},{8,9},{9,8},{10,11... | collective-permute-start | bytes 442376 | tf_op jit(solution)/shard_map/ppermute | solution.py:71
  8.7 18.1 %collective-permute-start.3 = (bf16[2,96,768]{2,1,0:T(8,128)(2,1)S(1)}, bf16[2,96,768]{2,1,0:T(8,128)(2,1)}, u32[]{:S(2)}, u32[]{:S(2)}) collective-permute-start(bf16[2,96,768]{2,1,0:T(8,128)(2,1)S(1)} %convert_element_type.750), channel_id=1, source_target_pairs={{0,1},{1,0},{2,3},{3,2},{4,5},{5,4},{6,7},{7,6},{8,9},{9,8},{10,11... | collective-permute-start | bytes 884744 | tf_op jit(solution)/shard_map/ppermute | solution.py:71
  29.2 15.4 %collective-permute-start.5 = (bf16[4,96,768]{2,1,0:T(8,128)(2,1)S(1)}, bf16[4,96,768]{2,1,0:T(8,128)(2,1)S(1)}, u32[]{:S(2)}, u32[]{:S(2)}) collective-permute-start(bf16[4,96,768]{2,1,0:T(8,128)(2,1)S(1)} %pad_maximum_fusion.12), channel_id=1, source_target_pairs={{0,16},{4,20},{8,24},{12,28},{16,0},{20,4},{24,8},{28,12},{1,17},{... | collective-permute-start | bytes 1769480 | tf_op jit(solution)/shard_map/ppermute | solution.py:71
  30.8 16.2 %collective-permute-start.4 = (bf16[4,96,768]{2,1,0:T(8,128)(2,1)S(1)}, bf16[4,96,768]{2,1,0:T(8,128)(2,1)S(1)}, u32[]{:S(2)}, u32[]{:S(2)}) collective-permute-start(bf16[4,96,768]{2,1,0:T(8,128)(2,1)S(1)} %pad_maximum_fusion.12), channel_id=1, source_target_pairs={{0,8},{4,12},{8,0},{12,4},{16,24},{20,28},{24,16},{28,20},{1,9},{5... | collective-permute-start | bytes 1769480 | tf_op jit(solution)/shard_map/ppermute | solution.py:71
  32.3 26.1 %collective-permute-start.6 = (bf16[4,96,768]{2,1,0:T(8,128)(2,1)S(1)}, bf16[4,96,768]{2,1,0:T(8,128)(2,1)S(1)}, u32[]{:S(2)}, u32[]{:S(2)}) collective-permute-start(bf16[4,96,768]{2,1,0:T(8,128)(2,1)S(1)} %pad_maximum_fusion.12), channel_id=1, source_target_pairs={{0,24},{4,28},{8,16},{12,20},{16,8},{20,12},{24,0},{28,4},{1,25},{... | collective-permute-start | bytes 1769480 | tf_op jit(solution)/shard_map/ppermute | solution.py:71
  32.8 28.0 %collective-permute-start.7 = (bf16[2,96,1536]{2,1,0:T(8,128)(2,1)S(1)}, bf16[2,96,1536]{2,1,0:T(8,128)(2,1)S(1)}, u32[]{:S(2)}, u32[]{:S(2)}) collective-permute-start(bf16[2,96,1536]{2,1,0:T(8,128)(2,1)S(1)} %pad_maximum_fusion.11), channel_id=1, source_target_pairs={{0,2},{1,3},{2,0},{3,1},{4,6},{5,7},{6,4},{7,5},{8,10},{9,11},{10,... | collective-permute-start | bytes 1769480 | tf_op jit(solution)/shard_map/ppermute | solution.py:71
  62.0 22.3 %collective-permute-start.8 = (bf16[4,384,768]{2,1,0:T(8,128)(2,1)}, bf16[4,384,768]{2,1,0:T(8,128)(2,1)}, u32[]{:S(2)}, u32[]{:S(2)}) collective-permute-start(bf16[4,384,768]{2,1,0:T(8,128)(2,1)} %bitcast.15), channel_id=1, source_target_pairs={{0,4},{4,0},{8,12},{12,8},{16,20},{20,16},{24,28},{28,24},{1,5},{5... | collective-permute-start | bytes 7077896 | tf_op jit(solution)/shard_map/ppermute | solution.py:71
  62.9 21.2 %collective-permute-start.10 = (bf16[2,256,768]{2,1,0:T(8,128)(2,1)}, bf16[2,256,768]{2,1,0:T(8,128)(2,1)S(1)}, u32[]{:S(2)}, u32[]{:S(2)}) collective-permute-start(bf16[2,256,768]{2,1,0:T(8,128)(2,1)} %bitcast.279), channel_id=1, source_target_pairs={{1,2},{2,1},{5,6},{6,5},{9,10},{10,9},{13,14},{14,13},{17,18},{18,... | collective-permute-start | bytes 2359304 | tf_op jit(solution)/shard_map/ppermute | solution.py:77
  63.7 20.7 %collective-permute-start.9 = (bf16[2,256,768]{2,1,0:T(8,128)(2,1)}, bf16[2,256,768]{2,1,0:T(8,128)(2,1)S(1)}, u32[]{:S(2)}, u32[]{:S(2)}) collective-permute-start(bf16[2,256,768]{2,1,0:T(8,128)(2,1)} %bitcast.280), channel_id=1, source_target_pairs={{0,1},{2,3},{1,0},{3,2},{4,5},{6,7},{5,4},{7,6},{8,9},{10,11},{9,8... | collective-permute-start | bytes 2359304 | tf_op jit(solution)/shard_map/ppermute | solution.py:77
  67.6 15.2 %collective-permute-start.12 = (bf16[1,96,3072]{2,1,0:T(8,128)(2,1)S(1)}, bf16[1,96,3072]{2,1,0:T(8,128)(2,1)S(1)}, u32[]{:S(2)}, u32[]{:S(2)}) collective-permute-start(bf16[1,96,3072]{2,1,0:T(8,128)(2,1)S(1)} %get-tuple-element.474), channel_id=1, source_target_pairs={{0,16},{4,20},{8,24},{12,28},{16,0},{20,4},{24,8},{28,12},{1,17},{... | collective-permute-start | bytes 1769480 | tf_op jit(solution)/shard_map/ppermute | solution.py:71
  69.2 14.9 %collective-permute-start.11 = (bf16[1,96,3072]{2,1,0:T(8,128)(2,1)S(1)}, bf16[1,96,3072]{2,1,0:T(8,128)(2,1)S(1)}, u32[]{:S(2)}, u32[]{:S(2)}) collective-permute-start(bf16[1,96,3072]{2,1,0:T(8,128)(2,1)S(1)} %get-tuple-element.475), channel_id=1, source_target_pairs={{0,8},{4,12},{8,0},{12,4},{16,24},{20,28},{24,16},{28,20},{1,9},{5... | collective-permute-start | bytes 1769480 | tf_op jit(solution)/shard_map/ppermute | solution.py:71
  84.3 13.9 %collective-permute-start.17 = (bf16[96,192]{1,0:T(8,128)(2,1)S(1)}, bf16[96,192]{1,0:T(8,128)(2,1)S(1)}, u32[]{:S(2)}, u32[]{:S(2)}) collective-permute-start(bf16[96,192]{1,0:T(8,128)(2,1)S(1)} %convert_element_type.759), channel_id=1, source_target_pairs={{0,3},{1,2},{2,1},{3,0},{4,7},{5,6},{6,5},{7,4},{8,11},{9,10},{10,... | collective-permute-start | bytes 110600 | tf_op jit(solution)/shard_map/ppermute | solution.py:71
  86.6 11.6 %collective-permute-start.16 = (bf16[96,192]{1,0:T(8,128)(2,1)S(1)}, bf16[96,192]{1,0:T(8,128)(2,1)S(1)}, u32[]{:S(2)}, u32[]{:S(2)}) collective-permute-start(bf16[96,192]{1,0:T(8,128)(2,1)S(1)} %convert_element_type.759), channel_id=1, source_target_pairs={{0,2},{1,3},{2,0},{3,1},{4,6},{5,7},{6,4},{7,5},{8,10},{9,11},{10,... | collective-permute-start | bytes 110600 | tf_op jit(solution)/shard_map/ppermute | solution.py:71
  87.5 10.7 %collective-permute-start.15 = (bf16[96,192]{1,0:T(8,128)(2,1)S(1)}, bf16[96,192]{1,0:T(8,128)(2,1)S(1)}, u32[]{:S(2)}, u32[]{:S(2)}) collective-permute-start(bf16[96,192]{1,0:T(8,128)(2,1)S(1)} %convert_element_type.759), channel_id=1, source_target_pairs={{0,1},{1,0},{2,3},{3,2},{4,5},{5,4},{6,7},{7,6},{8,9},{9,8},{10,11... | collective-permute-start | bytes 110600 | tf_op jit(solution)/shard_map/ppermute | solution.py:71
  88.8 9.5 %collective-permute-start.14 = (bf16[256,768]{1,0:T(8,128)(2,1)S(1)}, bf16[256,768]{1,0:T(8,128)(2,1)S(1)}, u32[]{:S(2)}, u32[]{:S(2)}) collective-permute-start(bf16[256,768]{1,0:T(8,128)(2,1)S(1)} %get-tuple-element.207), channel_id=1, source_target_pairs={{1,2},{2,1},{5,6},{6,5},{9,10},{10,9},{13,14},{14,13},{17,18},{18,... | collective-permute-start | bytes 1179656 | tf_op jit(solution)/shard_map/ppermute | solution.py:77
  90.7 10.8 %collective-permute-start.13 = (bf16[256,768]{1,0:T(8,128)(2,1)S(1)}, bf16[256,768]{1,0:T(8,128)(2,1)S(1)}, u32[]{:S(2)}, u32[]{:S(2)}) collective-permute-start(bf16[256,768]{1,0:T(8,128)(2,1)S(1)} %get-tuple-element.208), channel_id=1, source_target_pairs={{0,1},{2,3},{1,0},{3,2},{4,5},{6,7},{5,4},{7,6},{8,9},{10,11},{9,8... | collective-permute-start | bytes 1179656 | tf_op jit(solution)/shard_map/ppermute | solution.py:77
  101.5 22.5 %collective-permute-start.21 = (bf16[256,768]{1,0:T(8,128)(2,1)S(1)}, bf16[256,768]{1,0:T(8,128)(2,1)S(1)}, u32[]{:S(2)}, u32[]{:S(2)}) collective-permute-start(bf16[256,768]{1,0:T(8,128)(2,1)S(1)} %get-tuple-element.222), channel_id=1, source_target_pairs={{1,2},{2,1},{5,6},{6,5},{9,10},{10,9},{13,14},{14,13},{17,18},{18,... | collective-permute-start | bytes 1179656 | tf_op jit(solution)/shard_map/ppermute | solution.py:77
  102.4 21.6 %collective-permute-start.20 = (bf16[256,768]{1,0:T(8,128)(2,1)S(1)}, bf16[256,768]{1,0:T(8,128)(2,1)}, u32[]{:S(2)}, u32[]{:S(2)}) collective-permute-start(bf16[256,768]{1,0:T(8,128)(2,1)S(1)} %get-tuple-element.223), channel_id=1, source_target_pairs={{0,1},{2,3},{1,0},{3,2},{4,5},{6,7},{5,4},{7,6},{8,9},{10,11},{9,8... | collective-permute-start | bytes 1179656 | tf_op jit(solution)/shard_map/ppermute | solution.py:77
  110.5 32.7 %collective-permute-start.18 = (bf16[2,96,3072]{2,1,0:T(8,128)(2,1)}, bf16[2,96,3072]{2,1,0:T(8,128)(2,1)}, u32[]{:S(2)}, u32[]{:S(2)}) collective-permute-start(bf16[2,96,3072]{2,1,0:T(8,128)(2,1)} %pad_maximum_fusion.8), channel_id=1, source_target_pairs={{0,16},{4,20},{8,24},{12,28},{16,0},{20,4},{24,8},{28,12},{1,17},{... | collective-permute-start | bytes 3538952 | tf_op jit(solution)/shard_map/ppermute | solution.py:71
  112.0 31.1 %collective-permute-start.19 = (bf16[2,96,3072]{2,1,0:T(8,128)(2,1)}, bf16[2,96,3072]{2,1,0:T(8,128)(2,1)}, u32[]{:S(2)}, u32[]{:S(2)}) collective-permute-start(bf16[2,96,3072]{2,1,0:T(8,128)(2,1)} %maximum_bitcast_fusion), channel_id=1, source_target_pairs={{0,8},{4,12},{8,0},{12,4},{16,24},{20,28},{24,16},{28,20},{1,9},{5... | collective-permute-start | bytes 3538952 | tf_op jit(solution)/shard_map/ppermute | solution.py:71
  128.7 13.8 %collective-permute-start.24 = (bf16[1,96,768]{2,1,0:T(8,128)(2,1)S(1)}, bf16[1,96,768]{2,1,0:T(8,128)(2,1)S(1)}, u32[]{:S(2)}, u32[]{:S(2)}) collective-permute-start(bf16[1,96,768]{2,1,0:T(8,128)(2,1)S(1)} %maximum_bitcast_fusion.2), channel_id=1, source_target_pairs={{0,24},{4,28},{8,16},{12,20},{16,8},{20,12},{24,0},{28,4},{1,25},{... | collective-permute-start | bytes 442376 | tf_op jit(solution)/shard_map/ppermute | solution.py:71
  129.2 13.2 %collective-permute-start.23 = (bf16[1,96,768]{2,1,0:T(8,128)(2,1)S(1)}, bf16[1,96,768]{2,1,0:T(8,128)(2,1)S(1)}, u32[]{:S(2)}, u32[]{:S(2)}) collective-permute-start(bf16[1,96,768]{2,1,0:T(8,128)(2,1)S(1)} %maximum_bitcast_fusion.2), channel_id=1, source_target_pairs={{0,16},{4,20},{8,24},{12,28},{16,0},{20,4},{24,8},{28,12},{1,17},{... | collective-permute-start | bytes 442376 | tf_op jit(solution)/shard_map/ppermute | solution.py:71
  130.8 12.3 %collective-permute-start.22 = (bf16[1,96,768]{2,1,0:T(8,128)(2,1)S(1)}, bf16[1,96,768]{2,1,0:T(8,128)(2,1)S(1)}, u32[]{:S(2)}, u32[]{:S(2)}) collective-permute-start(bf16[1,96,768]{2,1,0:T(8,128)(2,1)S(1)} %maximum_bitcast_fusion.2), channel_id=1, source_target_pairs={{0,8},{4,12},{8,0},{12,4},{16,24},{20,28},{24,16},{28,20},{1,9},{5... | collective-permute-start | bytes 442376 | tf_op jit(solution)/shard_map/ppermute | solution.py:71
  147.7 8.8 %collective-permute-start.25 = (bf16[2,384,3072]{2,1,0:T(8,128)(2,1)S(1)}, bf16[2,384,3072]{2,1,0:T(8,128)(2,1)}, u32[]{:S(2)}, u32[]{:S(2)}) collective-permute-start(bf16[2,384,3072]{2,1,0:T(8,128)(2,1)S(1)} %pad_maximum_fusion.near_ref), channel_id=1, source_target_pairs={{0,4},{4,0},{8,12},{12,8},{16,20},{20,16},{24,28},{28,24},{1,5},{5... | collective-permute-start | bytes 14155784 | tf_op jit(solution)/shard_map/ppermute | solution.py:71
  153.0 3.5 collective-permute-start.26
  171.4 6.6 %collective-permute-start.29 = (f32[2,8,768]{2,1,0:T(8,128)}, f32[2,8,768]{2,1,0:T(8,128)}, u32[]{:S(2)}, u32[]{:S(2)}) collective-permute-start(f32[2,8,768]{2,1,0:T(8,128)} %fusion.84), channel_id=1, source_target_pairs={{0,3},{1,2},{2,1},{3,0},{4,7},{5,6},{6,5},{7,4},{8,11},{9,10},{10,... | collective-permute-start | bytes 147464 | tf_op jit(solution)/shard_map/ppermute | solution.py:71
  173.9 5.5 %collective-permute-start.28 = (f32[2,8,768]{2,1,0:T(8,128)}, f32[2,8,768]{2,1,0:T(8,128)}, u32[]{:S(2)}, u32[]{:S(2)}) collective-permute-start(f32[2,8,768]{2,1,0:T(8,128)} %fusion.84), channel_id=1, source_target_pairs={{0,2},{1,3},{2,0},{3,1},{4,6},{5,7},{6,4},{7,5},{8,10},{9,11},{10,... | collective-permute-start | bytes 147464 | tf_op jit(solution)/shard_map/ppermute | solution.py:71
  173.9 5.5 %collective-permute-start.27 = (f32[2,8,768]{2,1,0:T(8,128)}, f32[2,8,768]{2,1,0:T(8,128)}, u32[]{:S(2)}, u32[]{:S(2)}) collective-permute-start(f32[2,8,768]{2,1,0:T(8,128)} %fusion.84), channel_id=1, source_target_pairs={{0,1},{1,0},{2,3},{3,2},{4,5},{5,4},{6,7},{7,6},{8,9},{9,8},{10,11... | collective-permute-start | bytes 147464 | tf_op jit(solution)/shard_map/ppermute | solution.py:71
  181.5 1.3 collective-permute-start.30
  183.4 7.2 %collective-permute-start.33 = (bf16[2,2,8,896]{3,2,1,0:T(8,128)(2,1)S(1)}, bf16[2,2,8,896]{3,2,1,0:T(8,128)(2,1)S(1)}, u32[]{:S(2)}, u32[]{:S(2)}) collective-permute-start(bf16[2,2,8,896]{3,2,1,0:T(8,128)(2,1)S(1)} %pad_maximum_fusion.14), channel_id=1, source_target_pairs={{0,24},{4,28},{8,16},{12,20},{16,8},{20,12},{24,0},{28,4},{1,25},{... | collective-permute-start | bytes 172040 | tf_op jit(solution)/shard_map/ppermute | solution.py:71
  184.9 5.7 %collective-permute-start.32 = (bf16[2,2,8,896]{3,2,1,0:T(8,128)(2,1)S(1)}, bf16[2,2,8,896]{3,2,1,0:T(8,128)(2,1)S(1)}, u32[]{:S(2)}, u32[]{:S(2)}) collective-permute-start(bf16[2,2,8,896]{3,2,1,0:T(8,128)(2,1)S(1)} %pad_maximum_fusion.14), channel_id=1, source_target_pairs={{0,16},{4,20},{8,24},{12,28},{16,0},{20,4},{24,8},{28,12},{1,17},{... | collective-permute-start | bytes 172040 | tf_op jit(solution)/shard_map/ppermute | solution.py:71
  186.4 4.2 %collective-permute-start.31 = (bf16[2,2,8,896]{3,2,1,0:T(8,128)(2,1)S(1)}, bf16[2,2,8,896]{3,2,1,0:T(8,128)(2,1)S(1)}, u32[]{:S(2)}, u32[]{:S(2)}) collective-permute-start(bf16[2,2,8,896]{3,2,1,0:T(8,128)(2,1)S(1)} %pad_maximum_fusion.14), channel_id=1, source_target_pairs={{0,8},{4,12},{8,0},{12,4},{16,24},{20,28},{24,16},{28,20},{1,9},{5... | collective-permute-start | bytes 172040 | tf_op jit(solution)/shard_map/ppermute | solution.py:71
  214.0 8.1 %collective-permute-start.34 = (bf16[2,384,3072]{2,1,0:T(8,128)(2,1)}, bf16[2,384,3072]{2,1,0:T(8,128)(2,1)S(1)}, u32[]{:S(2)}, u32[]{:S(2)}) collective-permute-start(bf16[2,384,3072]{2,1,0:T(8,128)(2,1)} %get-tuple-element.252), channel_id=1, source_target_pairs={{0,4},{4,0},{8,12},{12,8},{16,20},{20,16},{24,28},{28,24},{1,5},{5... | collective-permute-start | bytes 14155784 | tf_op jit(solution)/shard_map/ppermute | solution.py:71
  225.9 28.3 %collective-permute-start.35 = (bf16[1,2,96,3072]{3,2,1,0:T(8,128)(2,1)}, bf16[1,2,96,3072]{3,2,1,0:T(8,128)(2,1)}, u32[]{:S(2)}, u32[]{:S(2)}) collective-permute-start(bf16[1,2,96,3072]{3,2,1,0:T(8,128)(2,1)} %fusion.22), channel_id=1, source_target_pairs={{0,16},{4,20},{8,24},{12,28},{16,0},{20,4},{24,8},{28,12},{1,17},{... | collective-permute-start | bytes 3538952 | tf_op jit(solution)/shard_map/ppermute | solution.py:71
  226.4 28.0 %collective-permute-start.36 = (bf16[1,2,96,3072]{3,2,1,0:T(8,128)(2,1)}, bf16[1,2,96,3072]{3,2,1,0:T(8,128)(2,1)}, u32[]{:S(2)}, u32[]{:S(2)}) collective-permute-start(bf16[1,2,96,3072]{3,2,1,0:T(8,128)(2,1)} %fusion.23), channel_id=1, source_target_pairs={{0,8},{4,12},{8,0},{12,4},{16,24},{20,28},{24,16},{28,20},{1,9},{5... | collective-permute-start | bytes 3538952 | tf_op jit(solution)/shard_map/ppermute | solution.py:71
  257.2 18.8 %collective-permute-start.37 = (bf16[1,1,96,3072]{3,2,1,0:T(8,128)(2,1)S(1)}, bf16[1,1,96,3072]{3,2,1,0:T(8,128)(2,1)S(1)}, u32[]{:S(2)}, u32[]{:S(2)}) collective-permute-start(bf16[1,1,96,3072]{3,2,1,0:T(8,128)(2,1)S(1)} %fusion.55), channel_id=1, source_target_pairs={{0,8},{4,12},{8,0},{12,4},{16,24},{20,28},{24,16},{28,20},{1,9},{5... | collective-permute-start | bytes 1769480 | tf_op jit(solution)/shard_map/ppermute | solution.py:71
  257.8 18.2 %collective-permute-start.38 = (bf16[1,1,96,3072]{3,2,1,0:T(8,128)(2,1)S(1)}, bf16[1,1,96,3072]{3,2,1,0:T(8,128)(2,1)S(1)}, u32[]{:S(2)}, u32[]{:S(2)}) collective-permute-start(bf16[1,1,96,3072]{3,2,1,0:T(8,128)(2,1)S(1)} %fusion.56), channel_id=1, source_target_pairs={{0,16},{4,20},{8,24},{12,28},{16,0},{20,4},{24,8},{28,12},{1,17},{... | collective-permute-start | bytes 1769480 | tf_op jit(solution)/shard_map/ppermute | solution.py:71
  259.3 16.6 %collective-permute-start.39 = (bf16[256,768]{1,0:T(8,128)(2,1)}, bf16[256,768]{1,0:T(8,128)(2,1)}, u32[]{:S(2)}, u32[]{:S(2)}) collective-permute-start(bf16[256,768]{1,0:T(8,128)(2,1)} %get-tuple-element.271), channel_id=1, source_target_pairs={{0,1},{2,3},{1,0},{3,2},{4,5},{6,7},{5,4},{7,6},{8,9},{10,11},{9,8... | collective-permute-start | bytes 1179656 | tf_op jit(solution)/shard_map/ppermute | solution.py:77
  260.1 15.8 %collective-permute-start.40 = (bf16[256,768]{1,0:T(8,128)(2,1)}, bf16[256,768]{1,0:T(8,128)(2,1)}, u32[]{:S(2)}, u32[]{:S(2)}) collective-permute-start(bf16[256,768]{1,0:T(8,128)(2,1)} %get-tuple-element.272), channel_id=1, source_target_pairs={{1,2},{2,1},{5,6},{6,5},{9,10},{10,9},{13,14},{14,13},{17,18},{18,... | collective-permute-start | bytes 1179656 | tf_op jit(solution)/shard_map/ppermute | solution.py:77
  280.3 27.4 %collective-permute-start.41 = (bf16[2,96,1536]{2,1,0:T(8,128)(2,1)}, bf16[2,96,1536]{2,1,0:T(8,128)(2,1)}, u32[]{:S(2)}, u32[]{:S(2)}) collective-permute-start(bf16[2,96,1536]{2,1,0:T(8,128)(2,1)} %fusion.61), channel_id=1, source_target_pairs={{0,2},{1,3},{2,0},{3,1},{4,6},{5,7},{6,4},{7,5},{8,10},{9,11},{10,... | collective-permute-start | bytes 1769480 | tf_op jit(solution)/shard_map/ppermute | solution.py:71
  307.7 21.0 %collective-permute-start.42 = (bf16[4,384,768]{2,1,0:T(8,128)(2,1)S(1)}, bf16[4,384,768]{2,1,0:T(8,128)(2,1)S(1)}, u32[]{:S(2)}, u32[]{:S(2)}) collective-permute-start(bf16[4,384,768]{2,1,0:T(8,128)(2,1)S(1)} %copy-done.131), channel_id=1, source_target_pairs={{0,4},{4,0},{8,12},{12,8},{16,20},{20,16},{24,28},{28,24},{1,5},{5... | collective-permute-start | bytes 7077896 | tf_op jit(solution)/shard_map/ppermute | solution.py:71
  308.7 12.0 %collective-permute-start.45 = (bf16[256,768]{1,0:T(8,128)(2,1)S(1)}, bf16[256,768]{1,0:T(8,128)(2,1)S(1)}, u32[]{:S(2)}, u32[]{:S(2)}) collective-permute-start(bf16[256,768]{1,0:T(8,128)(2,1)S(1)} %add_convert_fusion.9), channel_id=1, source_target_pairs={{0,1},{2,3},{1,0},{3,2},{4,5},{6,7},{5,4},{7,6},{8,9},{10,11},{9,8... | collective-permute-start | bytes 1179656 | tf_op jit(solution)/shard_map/ppermute | solution.py:77
  309.6 11.1 %collective-permute-start.46 = (bf16[256,768]{1,0:T(8,128)(2,1)S(1)}, bf16[256,768]{1,0:T(8,128)(2,1)S(1)}, u32[]{:S(2)}, u32[]{:S(2)}) collective-permute-start(bf16[256,768]{1,0:T(8,128)(2,1)S(1)} %copy-done.94), channel_id=1, source_target_pairs={{1,2},{2,1},{5,6},{6,5},{9,10},{10,9},{13,14},{14,13},{17,18},{18,... | collective-permute-start | bytes 1179656 | tf_op jit(solution)/shard_map/ppermute | solution.py:77
  310.3 18.4 %collective-permute-start.43 = (bf16[256,768]{1,0:T(8,128)(2,1)S(1)}, bf16[256,768]{1,0:T(8,128)(2,1)S(1)}, u32[]{:S(2)}, u32[]{:S(2)}) collective-permute-start(bf16[256,768]{1,0:T(8,128)(2,1)S(1)} %get-tuple-element.304), channel_id=1, source_target_pairs={{0,1},{2,3},{1,0},{3,2},{4,5},{6,7},{5,4},{7,6},{8,9},{10,11},{9,8... | collective-permute-start | bytes 1179656 | tf_op jit(solution)/shard_map/ppermute | solution.py:77
  315.5 13.2 %collective-permute-start.44 = (bf16[256,768]{1,0:T(8,128)(2,1)S(1)}, bf16[256,768]{1,0:T(8,128)(2,1)S(1)}, u32[]{:S(2)}, u32[]{:S(2)}) collective-permute-start(bf16[256,768]{1,0:T(8,128)(2,1)S(1)} %get-tuple-element.305), channel_id=1, source_target_pairs={{1,2},{2,1},{5,6},{6,5},{9,10},{10,9},{13,14},{14,13},{17,18},{18,... | collective-permute-start | bytes 1179656 | tf_op jit(solution)/shard_map/ppermute | solution.py:77
  330.8 12.5 %collective-permute-start.51 = (bf16[2,96,768]{2,1,0:T(8,128)(2,1)S(1)}, bf16[2,96,768]{2,1,0:T(8,128)(2,1)S(1)}, u32[]{:S(2)}, u32[]{:S(2)}) collective-permute-start(bf16[2,96,768]{2,1,0:T(8,128)(2,1)S(1)} %slice.624), channel_id=1, source_target_pairs={{0,1},{1,0},{2,3},{3,2},{4,5},{5,4},{6,7},{7,6},{8,9},{9,8},{10,11... | collective-permute-start | bytes 884744 | tf_op jit(solution)/shard_map/ppermute | solution.py:71
  335.5 15.2 %collective-permute-start.47 = (bf16[2,2,96,768]{3,2,0,1:T(8,128)(2,1)S(1)}, bf16[2,2,96,768]{3,2,0,1:T(8,128)(2,1)S(1)}, u32[]{:S(2)}, u32[]{:S(2)}) collective-permute-start(bf16[2,2,96,768]{3,2,0,1:T(8,128)(2,1)S(1)} %fusion.57), channel_id=1, source_target_pairs={{0,16},{4,20},{8,24},{12,28},{16,0},{20,4},{24,8},{28,12},{1,17},{... | collective-permute-start | bytes 1769480 | tf_op jit(solution)/shard_map/ppermute | solution.py:71
  336.1 14.7 %collective-permute-start.48 = (bf16[2,2,96,768]{3,2,0,1:T(8,128)(2,1)S(1)}, bf16[2,2,96,768]{3,2,0,1:T(8,128)(2,1)S(1)}, u32[]{:S(2)}, u32[]{:S(2)}) collective-permute-start(bf16[2,2,96,768]{3,2,0,1:T(8,128)(2,1)S(1)} %fusion.58), channel_id=1, source_target_pairs={{0,8},{4,12},{8,0},{12,4},{16,24},{20,28},{24,16},{28,20},{1,9},{5... | collective-permute-start | bytes 1769480 | tf_op jit(solution)/shard_map/ppermute | solution.py:71
  337.7 13.0 %collective-permute-start.49 = (bf16[256,768]{1,0:T(8,128)(2,1)S(1)}, bf16[256,768]{1,0:T(8,128)(2,1)S(1)}, u32[]{:S(2)}, u32[]{:S(2)}) collective-permute-start(bf16[256,768]{1,0:T(8,128)(2,1)S(1)} %add_convert_fusion.7), channel_id=1, source_target_pairs={{0,1},{2,3},{1,0},{3,2},{4,5},{6,7},{5,4},{7,6},{8,9},{10,11},{9,8... | collective-permute-start | bytes 1179656 | tf_op jit(solution)/shard_map/ppermute | solution.py:77
  337.8 12.9 %collective-permute-start.50 = (bf16[256,768]{1,0:T(8,128)(2,1)S(1)}, bf16[256,768]{1,0:T(8,128)(2,1)S(1)}, u32[]{:S(2)}, u32[]{:S(2)}) collective-permute-start(bf16[256,768]{1,0:T(8,128)(2,1)S(1)} %add_convert_fusion.6), channel_id=1, source_target_pairs={{1,2},{2,1},{5,6},{6,5},{9,10},{10,9},{13,14},{14,13},{17,18},{18,... | collective-permute-start | bytes 1179656 | tf_op jit(solution)/shard_map/ppermute | solution.py:77
  352.6 8.3 %collective-permute-start.52 = (bf16[2,1,96,768]{3,2,0,1:T(8,128)(2,1)}, bf16[2,1,96,768]{3,2,0,1:T(8,128)(2,1)}, u32[]{:S(2)}, u32[]{:S(2)}) collective-permute-start(bf16[2,1,96,768]{3,2,0,1:T(8,128)(2,1)} %fusion.68), channel_id=1, source_target_pairs={{0,8},{4,12},{8,0},{12,4},{16,24},{20,28},{24,16},{28,20},{1,9},{5... | collective-permute-start | bytes 884744 | tf_op jit(solution)/shard_map/ppermute | solution.py:71
  354.0 8.0 %collective-permute-start.53 = (bf16[2,1,96,768]{3,2,0,1:T(8,128)(2,1)}, bf16[2,1,96,768]{3,2,0,1:T(8,128)(2,1)}, u32[]{:S(2)}, u32[]{:S(2)}) collective-permute-start(bf16[2,1,96,768]{3,2,0,1:T(8,128)(2,1)} %fusion.69), channel_id=1, source_target_pairs={{0,16},{4,20},{8,24},{12,28},{16,0},{20,4},{24,8},{28,12},{1,17},{... | collective-permute-start | bytes 884744 | tf_op jit(solution)/shard_map/ppermute | solution.py:71
  365.5 9.7 %collective-permute-start.56 = (bf16[4,96,192]{2,1,0:T(8,128)(2,1)S(1)}, bf16[4,96,192]{2,1,0:T(8,128)(2,1)S(1)}, u32[]{:S(2)}, u32[]{:S(2)}) collective-permute-start(bf16[4,96,192]{2,1,0:T(8,128)(2,1)S(1)} %get-tuple-element.487), channel_id=1, source_target_pairs={{0,3},{1,2},{2,1},{3,0},{4,7},{5,6},{6,5},{7,4},{8,11},{9,10},{10,... | collective-permute-start | bytes 442376 | tf_op jit(solution)/shard_map/ppermute | solution.py:71
  367.5 15.9 %collective-permute-start.55 = (bf16[4,96,192]{2,1,0:T(8,128)(2,1)S(1)}, bf16[4,96,192]{2,1,0:T(8,128)(2,1)S(1)}, u32[]{:S(2)}, u32[]{:S(2)}) collective-permute-start(bf16[4,96,192]{2,1,0:T(8,128)(2,1)S(1)} %get-tuple-element.488), channel_id=1, source_target_pairs={{0,2},{1,3},{2,0},{3,1},{4,6},{5,7},{6,4},{7,5},{8,10},{9,11},{10,... | collective-permute-start | bytes 442376 | tf_op jit(solution)/shard_map/ppermute | solution.py:71
  368.4 15.0 %collective-permute-start.54 = (bf16[4,96,192]{2,1,0:T(8,128)(2,1)S(1)}, bf16[4,96,192]{2,1,0:T(8,128)(2,1)S(1)}, u32[]{:S(2)}, u32[]{:S(2)}) collective-permute-start(bf16[4,96,192]{2,1,0:T(8,128)(2,1)S(1)} %get-tuple-element.489), channel_id=1, source_target_pairs={{0,1},{1,0},{2,3},{3,2},{4,5},{5,4},{6,7},{7,6},{8,9},{9,8},{10,11... | collective-permute-start | bytes 442376 | tf_op jit(solution)/shard_map/ppermute | solution.py:71
  384.8 1.3 collective-permute-start.57
  386.1 5.0 %collective-permute-start.60 = (f32[8,768]{1,0:T(8,128)S(1)}, f32[8,768]{1,0:T(8,128)S(1)}, u32[]{:S(2)}, u32[]{:S(2)}) collective-permute-start(f32[8,768]{1,0:T(8,128)S(1)} %add.752), channel_id=1, source_target_pairs={{0,24},{4,28},{8,16},{12,20},{16,8},{20,12},{24,0},{28,4},{1,25},{... | collective-permute-start | bytes 73736 | tf_op jit(solution)/shard_map/ppermute | solution.py:71
  386.9 4.1 %collective-permute-start.59 = (f32[8,768]{1,0:T(8,128)S(1)}, f32[8,768]{1,0:T(8,128)S(1)}, u32[]{:S(2)}, u32[]{:S(2)}) collective-permute-start(f32[8,768]{1,0:T(8,128)S(1)} %add.752), channel_id=1, source_target_pairs={{0,16},{4,20},{8,24},{12,28},{16,0},{20,4},{24,8},{28,12},{1,17},{... | collective-permute-start | bytes 73736 | tf_op jit(solution)/shard_map/ppermute | solution.py:71
  388.1 3.8 collective-permute-start.58
  392.1 6.2 %collective-permute-start.63 = (f32[8,768]{1,0:T(8,128)S(1)}, f32[8,768]{1,0:T(8,128)S(1)}, u32[]{:S(2)}, u32[]{:S(2)}) collective-permute-start(f32[8,768]{1,0:T(8,128)S(1)} %add_add_fusion.1), channel_id=1, source_target_pairs={{0,3},{1,2},{2,1},{3,0},{4,7},{5,6},{6,5},{7,4},{8,11},{9,10},{10,... | collective-permute-start | bytes 73736 | tf_op jit(solution)/shard_map/ppermute | solution.py:71
  393.8 4.8 %collective-permute-start.62 = (f32[8,768]{1,0:T(8,128)S(1)}, f32[8,768]{1,0:T(8,128)S(1)}, u32[]{:S(2)}, u32[]{:S(2)}) collective-permute-start(f32[8,768]{1,0:T(8,128)S(1)} %add_add_fusion.1), channel_id=1, source_target_pairs={{0,2},{1,3},{2,0},{3,1},{4,6},{5,7},{6,4},{7,5},{8,10},{9,11},{10,... | collective-permute-start | bytes 73736 | tf_op jit(solution)/shard_map/ppermute | solution.py:71
  393.8 4.8 %collective-permute-start.61 = (f32[8,768]{1,0:T(8,128)S(1)}, f32[8,768]{1,0:T(8,128)S(1)}, u32[]{:S(2)}, u32[]{:S(2)}) collective-permute-start(f32[8,768]{1,0:T(8,128)S(1)} %add_add_fusion.1), channel_id=1, source_target_pairs={{0,1},{1,0},{2,3},{3,2},{4,5},{5,4},{6,7},{7,6},{8,9},{9,8},{10,11... | collective-permute-start | bytes 73736 | tf_op jit(solution)/shard_map/ppermute | solution.py:71
  (135 other events, 1392.1 us)

commit v5 on v4

--- a/solution.py
+++ b/solution.py
@@ -508,15 +508,18 @@
     def _():
         out_ref[...] = hidden_ref[...]
 
-    pre = dot(normed_ref[...], whole_rows(near_ref, other_ref, 0))
-    square = pre * pre
-    bend = jnp.tanh(ROOT * pre * (1.0 + CUBE * square))
-    gate = 0.5 * (1.0 + bend)
-    act = (pre * gate).astype(BF16)
-    slope = gate + 0.5 * pre * (1.0 - bend * bend) * (ROOT * (1.0 + 3.0 * CUBE * square))
-    act_ref[...] = act
-    slope_ref[...] = slope.astype(BF16)
-    out_ref[...] += dot(act, whole_rows(near_ref, other_ref, 1), NT)
+    w_up = whole_rows(near_ref, other_ref, 0)
+    chunk = act_ref.shape[1]
+    step = 256 if chunk % 256 == 0 else chunk
+    for start in range(0, chunk, step):
+        pre = dot(normed_ref[...], w_up[:, start : start + step])
+        square = pre * pre
+        gate = 0.5 + 0.5 * jnp.tanh(pre * (ROOT + (ROOT * CUBE) * square))
+        act = pre * gate
+        slope = gate + act * ((1.0 - gate) * (2.0 * ROOT + (6.0 * ROOT * CUBE) * square))
+        act_ref[:, start : start + step] = act.astype(BF16)
+        slope_ref[:, start : start + step] = slope.astype(BF16)
+    out_ref[...] += dot(act_ref[...], whole_rows(near_ref, other_ref, 1), NT)
 
 
 def feed_back_kernel(
@@ -542,7 +545,7 @@
 
 
 def unit_chunk(units):
-    return 512 if units % 512 == 0 else units
+    return 1024 if units % 1024 == 0 else units
 
 
 def feed(normed, hidden, near, other):

time: 411 us -> 410 us (level)
  Pallas kernels: 101 us -> 96.6 us
  transfers between devices with their start and end apart: 64 -> 64, of which waited for: 29 -> 30; matrix products, arithmetic and copies ran while one was open for 15% -> 15% of each run, Pallas kernels for 17% -> 16%
where the time goes in v5:
time: 410 us; the launch traced here: 404 us
  waiting for transfers between devices  104 us (25%)
  Pallas kernels  96.6 us (24%)
  starting transfers between devices  88.3 us (22%)
  other arithmetic  52.8 us (13%)
  matrix products  33.7 us (8%)
  local copies, waits for them, and re-layouts  24 us (6%)
  between operations  4.18 us (1%)
    ppermute x50, waiting for transfers between devices, swap(): return lax.ppermute(values, axis, [(i, i ^ mask) for i in range(count)])  80.5 us
    ppermute x50, starting transfers between devices, swap(): return lax.ppermute(values, axis, [(i, i ^ mask) for i in range(count)])  66.9 us
    dot_general x24, matrix products, dot(): lax.dot_general(left, right, dims, precision=precision, preferred_element...  31.6 us
    pallas_call x2, Pallas kernels, attend_back(): pl.pallas_call(functools.partial(backward_kernel, reach), grid=(pairs,),...  26.3 us
    ppermute x14, waiting for transfers between devices, link(): return lax.ppermute(values, 'mp', pairs + [(j, i) for i, j in pairs])  23.5 us
    ppermute x14, starting transfers between devices, link(): return lax.ppermute(values, 'mp', pairs + [(j, i) for i, j in pairs])  21.4 us
    pallas_call x2, Pallas kernels, attend(): pl.pallas_call(functools.partial(forward_kernel, reach), grid=(pairs,), i...  19.2 us
    unnamed x288, local copies, waits for them, and re-layouts  15.5 us
  transfers between devices with their start and end apart: 64, of which 30 were waited for; matrix products, arithmetic and copies ran while one was open for 15% of the time, Pallas kernels for 16%

profile of v5, /device:TPU:0, one launch (start us, length us, event | category | flops | bytes accessed | tf_op | source)
XLA Modules:
  0.0 403.5 jit_solution(18049917030317538887)
XLA Ops:
  1.8 5.1 %collective-permute-start.2 = (bf16[4,96,192]{2,1,0:T(8,128)(2,1)S(1)}, bf16[4,96,192]{2,1,0:T(8,128)(2,1)}, u32[]{:S(2)}, u32[]{:S(2)}) collective-permute-start(bf16[4,96,192]{2,1,0:T(8,128)(2,1)S(1)} %convert_element_type.749), channel_id=1, source_target_pairs={{0,3},{1,2},{2,1},{3,0},{4,7},{5,6},{6,5},{7,4},{8,11},{9,10},{10,... | collective-permute-start | bytes 442376 | tf_op jit(solution)/shard_map/ppermute | solution.py:71
  15.7 1.9 slice_dynamic-update-slice_fusion
  17.6 9.2 %collective-permute-done.3 = bf16[2,96,768]{2,1,0:T(8,128)(2,1)} collective-permute-done((bf16[2,96,768]{2,1,0:T(8,128)(2,1)S(1)}, bf16[2,96,768]{2,1,0:T(8,128)(2,1)}, u32[]{:S(2)}, u32[]{:S(2)}) %collective-permute-start.3) | collective-permute-done | bytes 294944 | tf_op jit(solution)/shard_map/ppermute | solution.py:71
  29.2 1.6 collective-permute-start.5
  35.7 7.4 %shard_map.322.bias_ref = f32[12,3,256,256]{3,2,1,0:T(8,128)} custom-call(f32[12,3,512]{2,1,0:T(4,128)S(1)} %copy.114.line_ref), custom_call_target="tpu_custom_call" | custom-call | tf_op jit(solution)/shard_map/pallas_call | solution.py:234
  44.6 2.4 collective-permute-done.4
  47.0 11.3 %collective-permute-done.6 = bf16[4,96,768]{2,1,0:T(8,128)(2,1)S(1)} collective-permute-done((bf16[4,96,768]{2,1,0:T(8,128)(2,1)S(1)}, bf16[4,96,768]{2,1,0:T(8,128)(2,1)S(1)}, u32[]{:S(2)}, u32[]{:S(2)}) %collective-permute-start.6) | collective-permute-done | bytes 589856 | tf_op jit(solution)/shard_map/ppermute | solution.py:71
  58.3 1.7 pad_maximum_fusion.1
  63.7 2.5 collective-permute-start.9
  70.8 12.1 %collective-permute-done.12 = bf16[1,96,3072]{2,1,0:T(8,128)(2,1)S(1)} collective-permute-done((bf16[1,96,3072]{2,1,0:T(8,128)(2,1)S(1)}, bf16[1,96,3072]{2,1,0:T(8,128)(2,1)S(1)}, u32[]{:S(2)}, u32[]{:S(2)}) %collective-permute-start.12) | collective-permute-done | bytes 589856 | tf_op jit(solution)/shard_map/ppermute | solution.py:71
  84.3 2.3 collective-permute-start.17
  90.7 2.8 collective-permute-start.13
  94.6 3.4 fusion.30
  98.3 3.3 collective-permute-done.13
  102.4 3.9 collective-permute-start.20
  106.5 3.4 convolution_convert_fusion.1.k_ref.v_ref
  110.5 1.6 collective-permute-start.18
  113.6 9.8 %attend.2 = (bf16[256,768]{1,0:T(8,128)(2,1)S(1)}, f32[6,8,256]{2,1,0:T(8,128)S(1)}) custom-call(s32[7]{0:T(128)S(1)} %get-tuple-element.506.range_ref, f32[2,12]{1,0:T(2,128)S(1)} %pad_maximum_fusion.16.far_ref, bf16[256,768]{1,0:T(8,128)(2,1)S(1)} %convolution_convert_fusion.5.q_ref, bf16[1280,1536]{1,0:T(8,128)(2,1)S(1)} %convolution_convert_fusion.1.k_ref.v_ref, ...), custom_call_target="tpu_custom_call" | custom-call | flops 100000 | bytes 10000 | tf_op jit(solution)/shard_map/attend/pallas_call | solution.py:416
  125.2 3.5 convolution_convert_fusion.k_ref.v_ref
  128.8 2.0 collective-permute-start.23
  132.3 9.4 %attend.3 = (bf16[256,768]{1,0:T(8,128)(2,1)S(1)}, f32[6,8,256]{2,1,0:T(8,128)S(1)}) custom-call(s32[7]{0:T(128)S(1)} %get-tuple-element.505.range_ref, f32[2,12]{1,0:T(2,128)S(1)} %pad_maximum_fusion.16.far_ref, bf16[256,768]{1,0:T(8,128)(2,1)S(1)} %convolution_convert_fusion.4.q_ref, bf16[1280,1536]{1,0:T(8,128)(2,1)S(1)} %convolution_convert_fusion.k_ref.v_ref, ...), custom_call_target="tpu_custom_call" | custom-call | flops 100000 | bytes 10000 | tf_op jit(solution)/shard_map/attend/pallas_call | solution.py:416
  143.1 2.0 pad_maximum_fusion.4
  145.4 1.8 pad_maximum_fusion.3
  147.9 1.9 fusion.2.turn_ref
  153.3 2.2 copy-done.53
  157.5 10.9 %feed.1 = (f32[512,768]{1,0:T(8,128)S(1)}, bf16[512,3072]{1,0:T(8,128)(2,1)}, bf16[512,3072]{1,0:T(8,128)(2,1)}) custom-call(bf16[512,768]{1,0:T(8,128)(2,1)S(1)} %multiply_convert_fusion.normed_ref, f32[512,768]{1,0:T(8,128)S(1)} %bitcast_add_fusion.1.hidden_ref, bf16[2,384,3072]{2,1,0:T(8,128)(2,1)} %copy-done.51, ...), custom_call_target="tpu_custom_call" | custom-call | flops 100000 | bytes 10000 | tf_op jit(solution)/shard_map/feed/pallas_call | solution.py:557
  171.1 2.5 collective-permute-start.29
  173.6 1.9 collective-permute-start.27
  186.7 3.6 collective-permute-done.31
  192.5 2.8 contrast.1
  198.3 15.1 %feed_back.1 = (f32[512,768]{1,0:T(8,128)S(1)}, bf16[2,384,3072]{2,1,0:T(8,128)(2,1)}, bf16[2,384,3072]{2,1,0:T(8,128)(2,1)}) custom-call(bf16[512,768]{1,0:T(8,128)(2,1)S(1)} %multiply_convert_fusion.normed_ref, bf16[512,768]{1,0:T(8,128)(2,1)S(1)} %get-tuple-element.511.up_ref, bf16[2,384,3072]{2,1,0:T(8,128)(2,1)} %copy-done.51, ...), custom_call_target="tpu_custom_call" | custom-call | flops 100000 | bytes 10000 | tf_op jit(solution)/shard_map/feed_back/pallas_call | solution.py:579
  218.9 2.7 collective-permute-done.34
  221.9 1.7 fusion.22
  226.4 14.8 %attend_back.2 = (bf16[256,768]{1,0:T(8,128)(2,1)S(1)}, bf16[1280,768]{1,0:T(8,128)(2,1)S(1)}, bf16[1280,768]{1,0:T(8,128)(2,1)S(1)}, f32[6,2,8,256]{3,2,1,0:T(8,128)S(1)}) custom-call(s32[7]{0:T(128)S(1)} %get-tuple-element.506.range_ref, f32[2,12]{1,0:T(2,128)S(1)} %pad_maximum_fusion.16.far_ref, bf16[256,768]{1,0:T(8,128)(2,1)S(1)} %copy-done.30, ...), custom_call_target="tpu_custom_call" | custom-call | flops 100000 | bytes 10000 | tf_op jit(solution)/shard_map/attend_back/pallas_call | solution.py:436
  241.3 1.7 fusion.46
  244.4 1.9 fusion.149
  250.2 3.4 collective-permute-done.35
  261.0 11.5 %attend_back.3 = (bf16[256,768]{1,0:T(8,128)(2,1)S(1)}, bf16[1280,768]{1,0:T(8,128)(2,1)S(1)}, bf16[1280,768]{1,0:T(8,128)(2,1)S(1)}, f32[6,2,8,256]{3,2,1,0:T(8,128)S(1)}) custom-call(s32[7]{0:T(128)S(1)} %get-tuple-element.505.range_ref, f32[2,12]{1,0:T(2,128)S(1)} %pad_maximum_fusion.16.far_ref, bf16[256,768]{1,0:T(8,128)(2,1)S(1)} %copy-done.28, ...), custom_call_target="tpu_custom_call" | custom-call | flops 100000 | bytes 10000 | tf_op jit(solution)/shard_map/attend_back/pallas_call | solution.py:436
  272.6 1.9 fusion.60
  277.0 3.1 collective-permute-start.41
  280.1 1.7 fusion.44
  281.8 1.8 add_convert_fusion.8
  283.7 1.9 fusion.150
  286.7 10.2 %collect.1 = (bf16[4,384,768]{2,1,0:T(8,128)(2,1)}, bf16[4,384,768]{2,1,0:T(8,128)(2,1)}) custom-call(bf16[768,1280]{1,0:T(8,128)(2,1)S(1)} %copy-done.10, bf16[768,1280]{1,0:T(8,128)(2,1)S(1)} %copy-done.12, bf16[256,768]{1,0:T(8,128)(2,1)S(1)} %get-tuple-element.286.refs_2_, bf16[1280,768]{1,0:T(8,128)(2,1)} %copy-done.7, bf16[1280,768]{1,0:T(8,128)(2,1)} %copy-done.20, ...), custom_call_target="tpu_custom_call" | custom-call | flops 100000 | bytes 10000 | tf_op jit(solution)/shard_map/collect/pallas_call | solution.py:489
  297.6 7.3 %collective-permute-done.41 = bf16[2,96,1536]{2,1,0:T(8,128)(2,1)} collective-permute-done((bf16[2,96,1536]{2,1,0:T(8,128)(2,1)}, bf16[2,96,1536]{2,1,0:T(8,128)(2,1)}, u32[]{:S(2)}, u32[]{:S(2)}) %collective-permute-start.41) | collective-permute-done | bytes 589856 | tf_op jit(solution)/shard_map/ppermute | solution.py:71
  304.9 2.1 collective-permute-start.42
  308.8 5.0 %collective-permute-start.43 = (bf16[256,768]{1,0:T(8,128)(2,1)S(1)}, bf16[256,768]{1,0:T(8,128)(2,1)S(1)}, u32[]{:S(2)}, u32[]{:S(2)}) collective-permute-start(bf16[256,768]{1,0:T(8,128)(2,1)S(1)} %get-tuple-element.304), channel_id=1, source_target_pairs={{0,1},{2,3},{1,0},{3,2},{4,5},{6,7},{5,4},{7,6},{8,9},{10,11},{9,8... | collective-permute-start | bytes 1179656 | tf_op jit(solution)/shard_map/ppermute | solution.py:77
  314.9 5.2 %collective-permute-done.45 = bf16[256,768]{1,0:T(8,128)(2,1)S(1)} collective-permute-done((bf16[256,768]{1,0:T(8,128)(2,1)S(1)}, bf16[256,768]{1,0:T(8,128)(2,1)S(1)}, u32[]{:S(2)}, u32[]{:S(2)}) %collective-permute-start.45) | collective-permute-done | bytes 393248 | tf_op jit(solution)/shard_map/ppermute | solution.py:77
  320.1 7.5 %collective-permute-done.43 = bf16[256,768]{1,0:T(8,128)(2,1)S(1)} collective-permute-done((bf16[256,768]{1,0:T(8,128)(2,1)S(1)}, bf16[256,768]{1,0:T(8,128)(2,1)S(1)}, u32[]{:S(2)}, u32[]{:S(2)}) %collective-permute-start.43) | collective-permute-done | bytes 393248 | tf_op jit(solution)/shard_map/ppermute | solution.py:77
  329.7 4.2 %collective-permute-start.51 = (bf16[2,96,768]{2,1,0:T(8,128)(2,1)S(1)}, bf16[2,96,768]{2,1,0:T(8,128)(2,1)S(1)}, u32[]{:S(2)}, u32[]{:S(2)}) collective-permute-start(bf16[2,96,768]{2,1,0:T(8,128)(2,1)S(1)} %slice.624), channel_id=1, source_target_pairs={{0,1},{1,0},{2,3},{3,2},{4,5},{5,4},{6,7},{7,6},{8,9},{9,8},{10,11... | collective-permute-start | bytes 884744 | tf_op jit(solution)/shard_map/ppermute | solution.py:71
  333.8 1.7 collective-permute-start.47
  335.5 2.2 collective-permute-start.48
  339.5 1.9 collective-permute-done.51
  341.5 7.3 %collective-permute-done.49 = bf16[256,768]{1,0:T(8,128)(2,1)S(1)} collective-permute-done((bf16[256,768]{1,0:T(8,128)(2,1)S(1)}, bf16[256,768]{1,0:T(8,128)(2,1)S(1)}, u32[]{:S(2)}, u32[]{:S(2)}) %collective-permute-start.49) | collective-permute-done | bytes 393248 | tf_op jit(solution)/shard_map/ppermute | solution.py:77
  352.0 2.5 collective-permute-start.52
  357.1 3.5 collective-permute-done.52
  365.5 1.9 collective-permute-start.56
  370.0 3.8 fusion.1
  375.2 7.9 %collective-permute-done.55.refs_2_ = bf16[4,96,192]{2,1,0:T(8,128)(2,1)S(1)} collective-permute-done((bf16[4,96,192]{2,1,0:T(8,128)(2,1)S(1)}, bf16[4,96,192]{2,1,0:T(8,128)(2,1)S(1)}, u32[]{:S(2)}, u32[]{:S(2)}) %collective-permute-start.55) | collective-permute-done | bytes 147488 | tf_op jit(solution)/shard_map/ppermute | solution.py:71
  385.8 2.1 collective-permute-start.59
  391.9 2.3 collective-permute-start.63
  394.1 2.2 collective-permute-start.61
  396.3 1.7 fusion.21
  399.1 2.5 update.1
  (517 shorter events, 120.9 us)
Async XLA Ops:
  1.8 26.0 %collective-permute-start.2 = (bf16[4,96,192]{2,1,0:T(8,128)(2,1)S(1)}, bf16[4,96,192]{2,1,0:T(8,128)(2,1)}, u32[]{:S(2)}, u32[]{:S(2)}) collective-permute-start(bf16[4,96,192]{2,1,0:T(8,128)(2,1)S(1)} %convert_element_type.749), channel_id=1, source_target_pairs={{0,3},{1,2},{2,1},{3,0},{4,7},{5,6},{6,5},{7,4},{8,11},{9,10},{10,... | collective-permute-start | bytes 442376 | tf_op jit(solution)/shard_map/ppermute | solution.py:71
  6.9 20.9 %collective-permute-start.1 = (bf16[4,96,192]{2,1,0:T(8,128)(2,1)S(1)}, bf16[4,96,192]{2,1,0:T(8,128)(2,1)}, u32[]{:S(2)}, u32[]{:S(2)}) collective-permute-start(bf16[4,96,192]{2,1,0:T(8,128)(2,1)S(1)} %convert_element_type.749), channel_id=1, source_target_pairs={{0,2},{1,3},{2,0},{3,1},{4,6},{5,7},{6,4},{7,5},{8,10},{9,11},{10,... | collective-permute-start | bytes 442376 | tf_op jit(solution)/shard_map/ppermute | solution.py:71
  6.9 20.9 %collective-permute-start = (bf16[4,96,192]{2,1,0:T(8,128)(2,1)S(1)}, bf16[4,96,192]{2,1,0:T(8,128)(2,1)}, u32[]{:S(2)}, u32[]{:S(2)}) collective-permute-start(bf16[4,96,192]{2,1,0:T(8,128)(2,1)S(1)} %convert_element_type.749), channel_id=1, source_target_pairs={{0,1},{1,0},{2,3},{3,2},{4,5},{5,4},{6,7},{7,6},{8,9},{9,8},{10,11... | collective-permute-start | bytes 442376 | tf_op jit(solution)/shard_map/ppermute | solution.py:71
  8.7 18.1 %collective-permute-start.3 = (bf16[2,96,768]{2,1,0:T(8,128)(2,1)S(1)}, bf16[2,96,768]{2,1,0:T(8,128)(2,1)}, u32[]{:S(2)}, u32[]{:S(2)}) collective-permute-start(bf16[2,96,768]{2,1,0:T(8,128)(2,1)S(1)} %convert_element_type.750), channel_id=1, source_target_pairs={{0,1},{1,0},{2,3},{3,2},{4,5},{5,4},{6,7},{7,6},{8,9},{9,8},{10,11... | collective-permute-start | bytes 884744 | tf_op jit(solution)/shard_map/ppermute | solution.py:71
  29.2 15.4 %collective-permute-start.5 = (bf16[4,96,768]{2,1,0:T(8,128)(2,1)S(1)}, bf16[4,96,768]{2,1,0:T(8,128)(2,1)S(1)}, u32[]{:S(2)}, u32[]{:S(2)}) collective-permute-start(bf16[4,96,768]{2,1,0:T(8,128)(2,1)S(1)} %pad_maximum_fusion.12), channel_id=1, source_target_pairs={{0,16},{4,20},{8,24},{12,28},{16,0},{20,4},{24,8},{28,12},{1,17},{... | collective-permute-start | bytes 1769480 | tf_op jit(solution)/shard_map/ppermute | solution.py:71
  30.8 16.2 %collective-permute-start.4 = (bf16[4,96,768]{2,1,0:T(8,128)(2,1)S(1)}, bf16[4,96,768]{2,1,0:T(8,128)(2,1)S(1)}, u32[]{:S(2)}, u32[]{:S(2)}) collective-permute-start(bf16[4,96,768]{2,1,0:T(8,128)(2,1)S(1)} %pad_maximum_fusion.12), channel_id=1, source_target_pairs={{0,8},{4,12},{8,0},{12,4},{16,24},{20,28},{24,16},{28,20},{1,9},{5... | collective-permute-start | bytes 1769480 | tf_op jit(solution)/shard_map/ppermute | solution.py:71
  32.3 26.1 %collective-permute-start.6 = (bf16[4,96,768]{2,1,0:T(8,128)(2,1)S(1)}, bf16[4,96,768]{2,1,0:T(8,128)(2,1)S(1)}, u32[]{:S(2)}, u32[]{:S(2)}) collective-permute-start(bf16[4,96,768]{2,1,0:T(8,128)(2,1)S(1)} %pad_maximum_fusion.12), channel_id=1, source_target_pairs={{0,24},{4,28},{8,16},{12,20},{16,8},{20,12},{24,0},{28,4},{1,25},{... | collective-permute-start | bytes 1769480 | tf_op jit(solution)/shard_map/ppermute | solution.py:71
  32.8 28.0 %collective-permute-start.7 = (bf16[2,96,1536]{2,1,0:T(8,128)(2,1)S(1)}, bf16[2,96,1536]{2,1,0:T(8,128)(2,1)S(1)}, u32[]{:S(2)}, u32[]{:S(2)}) collective-permute-start(bf16[2,96,1536]{2,1,0:T(8,128)(2,1)S(1)} %pad_maximum_fusion.11), channel_id=1, source_target_pairs={{0,2},{1,3},{2,0},{3,1},{4,6},{5,7},{6,4},{7,5},{8,10},{9,11},{10,... | collective-permute-start | bytes 1769480 | tf_op jit(solution)/shard_map/ppermute | solution.py:71
  62.0 22.3 %collective-permute-start.8 = (bf16[4,384,768]{2,1,0:T(8,128)(2,1)}, bf16[4,384,768]{2,1,0:T(8,128)(2,1)}, u32[]{:S(2)}, u32[]{:S(2)}) collective-permute-start(bf16[4,384,768]{2,1,0:T(8,128)(2,1)} %bitcast.15), channel_id=1, source_target_pairs={{0,4},{4,0},{8,12},{12,8},{16,20},{20,16},{24,28},{28,24},{1,5},{5... | collective-permute-start | bytes 7077896 | tf_op jit(solution)/shard_map/ppermute | solution.py:71
  62.9 21.2 %collective-permute-start.10 = (bf16[2,256,768]{2,1,0:T(8,128)(2,1)}, bf16[2,256,768]{2,1,0:T(8,128)(2,1)S(1)}, u32[]{:S(2)}, u32[]{:S(2)}) collective-permute-start(bf16[2,256,768]{2,1,0:T(8,128)(2,1)} %bitcast.279), channel_id=1, source_target_pairs={{1,2},{2,1},{5,6},{6,5},{9,10},{10,9},{13,14},{14,13},{17,18},{18,... | collective-permute-start | bytes 2359304 | tf_op jit(solution)/shard_map/ppermute | solution.py:77
  63.7 20.7 %collective-permute-start.9 = (bf16[2,256,768]{2,1,0:T(8,128)(2,1)}, bf16[2,256,768]{2,1,0:T(8,128)(2,1)S(1)}, u32[]{:S(2)}, u32[]{:S(2)}) collective-permute-start(bf16[2,256,768]{2,1,0:T(8,128)(2,1)} %bitcast.280), channel_id=1, source_target_pairs={{0,1},{2,3},{1,0},{3,2},{4,5},{6,7},{5,4},{7,6},{8,9},{10,11},{9,8... | collective-permute-start | bytes 2359304 | tf_op jit(solution)/shard_map/ppermute | solution.py:77
  67.6 15.2 %collective-permute-start.12 = (bf16[1,96,3072]{2,1,0:T(8,128)(2,1)S(1)}, bf16[1,96,3072]{2,1,0:T(8,128)(2,1)S(1)}, u32[]{:S(2)}, u32[]{:S(2)}) collective-permute-start(bf16[1,96,3072]{2,1,0:T(8,128)(2,1)S(1)} %get-tuple-element.474), channel_id=1, source_target_pairs={{0,16},{4,20},{8,24},{12,28},{16,0},{20,4},{24,8},{28,12},{1,17},{... | collective-permute-start | bytes 1769480 | tf_op jit(solution)/shard_map/ppermute | solution.py:71
  69.2 14.9 %collective-permute-start.11 = (bf16[1,96,3072]{2,1,0:T(8,128)(2,1)S(1)}, bf16[1,96,3072]{2,1,0:T(8,128)(2,1)S(1)}, u32[]{:S(2)}, u32[]{:S(2)}) collective-permute-start(bf16[1,96,3072]{2,1,0:T(8,128)(2,1)S(1)} %get-tuple-element.475), channel_id=1, source_target_pairs={{0,8},{4,12},{8,0},{12,4},{16,24},{20,28},{24,16},{28,20},{1,9},{5... | collective-permute-start | bytes 1769480 | tf_op jit(solution)/shard_map/ppermute | solution.py:71
  84.3 13.9 %collective-permute-start.17 = (bf16[96,192]{1,0:T(8,128)(2,1)S(1)}, bf16[96,192]{1,0:T(8,128)(2,1)S(1)}, u32[]{:S(2)}, u32[]{:S(2)}) collective-permute-start(bf16[96,192]{1,0:T(8,128)(2,1)S(1)} %convert_element_type.759), channel_id=1, source_target_pairs={{0,3},{1,2},{2,1},{3,0},{4,7},{5,6},{6,5},{7,4},{8,11},{9,10},{10,... | collective-permute-start | bytes 110600 | tf_op jit(solution)/shard_map/ppermute | solution.py:71
  86.6 11.6 %collective-permute-start.16 = (bf16[96,192]{1,0:T(8,128)(2,1)S(1)}, bf16[96,192]{1,0:T(8,128)(2,1)S(1)}, u32[]{:S(2)}, u32[]{:S(2)}) collective-permute-start(bf16[96,192]{1,0:T(8,128)(2,1)S(1)} %convert_element_type.759), channel_id=1, source_target_pairs={{0,2},{1,3},{2,0},{3,1},{4,6},{5,7},{6,4},{7,5},{8,10},{9,11},{10,... | collective-permute-start | bytes 110600 | tf_op jit(solution)/shard_map/ppermute | solution.py:71
  87.5 10.7 %collective-permute-start.15 = (bf16[96,192]{1,0:T(8,128)(2,1)S(1)}, bf16[96,192]{1,0:T(8,128)(2,1)S(1)}, u32[]{:S(2)}, u32[]{:S(2)}) collective-permute-start(bf16[96,192]{1,0:T(8,128)(2,1)S(1)} %convert_element_type.759), channel_id=1, source_target_pairs={{0,1},{1,0},{2,3},{3,2},{4,5},{5,4},{6,7},{7,6},{8,9},{9,8},{10,11... | collective-permute-start | bytes 110600 | tf_op jit(solution)/shard_map/ppermute | solution.py:71
  88.8 9.5 %collective-permute-start.14 = (bf16[256,768]{1,0:T(8,128)(2,1)S(1)}, bf16[256,768]{1,0:T(8,128)(2,1)S(1)}, u32[]{:S(2)}, u32[]{:S(2)}) collective-permute-start(bf16[256,768]{1,0:T(8,128)(2,1)S(1)} %get-tuple-element.207), channel_id=1, source_target_pairs={{1,2},{2,1},{5,6},{6,5},{9,10},{10,9},{13,14},{14,13},{17,18},{18,... | collective-permute-start | bytes 1179656 | tf_op jit(solution)/shard_map/ppermute | solution.py:77
  90.7 10.8 %collective-permute-start.13 = (bf16[256,768]{1,0:T(8,128)(2,1)S(1)}, bf16[256,768]{1,0:T(8,128)(2,1)S(1)}, u32[]{:S(2)}, u32[]{:S(2)}) collective-permute-start(bf16[256,768]{1,0:T(8,128)(2,1)S(1)} %get-tuple-element.208), channel_id=1, source_target_pairs={{0,1},{2,3},{1,0},{3,2},{4,5},{6,7},{5,4},{7,6},{8,9},{10,11},{9,8... | collective-permute-start | bytes 1179656 | tf_op jit(solution)/shard_map/ppermute | solution.py:77
  101.5 22.5 %collective-permute-start.21 = (bf16[256,768]{1,0:T(8,128)(2,1)S(1)}, bf16[256,768]{1,0:T(8,128)(2,1)S(1)}, u32[]{:S(2)}, u32[]{:S(2)}) collective-permute-start(bf16[256,768]{1,0:T(8,128)(2,1)S(1)} %get-tuple-element.222), channel_id=1, source_target_pairs={{1,2},{2,1},{5,6},{6,5},{9,10},{10,9},{13,14},{14,13},{17,18},{18,... | collective-permute-start | bytes 1179656 | tf_op jit(solution)/shard_map/ppermute | solution.py:77
  102.4 21.6 %collective-permute-start.20 = (bf16[256,768]{1,0:T(8,128)(2,1)S(1)}, bf16[256,768]{1,0:T(8,128)(2,1)}, u32[]{:S(2)}, u32[]{:S(2)}) collective-permute-start(bf16[256,768]{1,0:T(8,128)(2,1)S(1)} %get-tuple-element.223), channel_id=1, source_target_pairs={{0,1},{2,3},{1,0},{3,2},{4,5},{6,7},{5,4},{7,6},{8,9},{10,11},{9,8... | collective-permute-start | bytes 1179656 | tf_op jit(solution)/shard_map/ppermute | solution.py:77
  110.5 32.7 %collective-permute-start.18 = (bf16[2,96,3072]{2,1,0:T(8,128)(2,1)}, bf16[2,96,3072]{2,1,0:T(8,128)(2,1)}, u32[]{:S(2)}, u32[]{:S(2)}) collective-permute-start(bf16[2,96,3072]{2,1,0:T(8,128)(2,1)} %pad_maximum_fusion.8), channel_id=1, source_target_pairs={{0,16},{4,20},{8,24},{12,28},{16,0},{20,4},{24,8},{28,12},{1,17},{... | collective-permute-start | bytes 3538952 | tf_op jit(solution)/shard_map/ppermute | solution.py:71
  112.1 31.1 %collective-permute-start.19 = (bf16[2,96,3072]{2,1,0:T(8,128)(2,1)}, bf16[2,96,3072]{2,1,0:T(8,128)(2,1)}, u32[]{:S(2)}, u32[]{:S(2)}) collective-permute-start(bf16[2,96,3072]{2,1,0:T(8,128)(2,1)} %maximum_bitcast_fusion), channel_id=1, source_target_pairs={{0,8},{4,12},{8,0},{12,4},{16,24},{20,28},{24,16},{28,20},{1,9},{5... | collective-permute-start | bytes 3538952 | tf_op jit(solution)/shard_map/ppermute | solution.py:71
  128.7 13.0 %collective-permute-start.24 = (bf16[1,96,768]{2,1,0:T(8,128)(2,1)S(1)}, bf16[1,96,768]{2,1,0:T(8,128)(2,1)S(1)}, u32[]{:S(2)}, u32[]{:S(2)}) collective-permute-start(bf16[1,96,768]{2,1,0:T(8,128)(2,1)S(1)} %maximum_bitcast_fusion.2), channel_id=1, source_target_pairs={{0,24},{4,28},{8,16},{12,20},{16,8},{20,12},{24,0},{28,4},{1,25},{... | collective-permute-start | bytes 442376 | tf_op jit(solution)/shard_map/ppermute | solution.py:71
  128.8 13.0 %collective-permute-start.23 = (bf16[1,96,768]{2,1,0:T(8,128)(2,1)S(1)}, bf16[1,96,768]{2,1,0:T(8,128)(2,1)S(1)}, u32[]{:S(2)}, u32[]{:S(2)}) collective-permute-start(bf16[1,96,768]{2,1,0:T(8,128)(2,1)S(1)} %maximum_bitcast_fusion.2), channel_id=1, source_target_pairs={{0,16},{4,20},{8,24},{12,28},{16,0},{20,4},{24,8},{28,12},{1,17},{... | collective-permute-start | bytes 442376 | tf_op jit(solution)/shard_map/ppermute | solution.py:71
  130.8 12.3 %collective-permute-start.22 = (bf16[1,96,768]{2,1,0:T(8,128)(2,1)S(1)}, bf16[1,96,768]{2,1,0:T(8,128)(2,1)S(1)}, u32[]{:S(2)}, u32[]{:S(2)}) collective-permute-start(bf16[1,96,768]{2,1,0:T(8,128)(2,1)S(1)} %maximum_bitcast_fusion.2), channel_id=1, source_target_pairs={{0,8},{4,12},{8,0},{12,4},{16,24},{20,28},{24,16},{28,20},{1,9},{5... | collective-permute-start | bytes 442376 | tf_op jit(solution)/shard_map/ppermute | solution.py:71
  147.7 8.8 %collective-permute-start.25 = (bf16[2,384,3072]{2,1,0:T(8,128)(2,1)S(1)}, bf16[2,384,3072]{2,1,0:T(8,128)(2,1)}, u32[]{:S(2)}, u32[]{:S(2)}) collective-permute-start(bf16[2,384,3072]{2,1,0:T(8,128)(2,1)S(1)} %pad_maximum_fusion.near_ref), channel_id=1, source_target_pairs={{0,4},{4,0},{8,12},{12,8},{16,20},{20,16},{24,28},{28,24},{1,5},{5... | collective-permute-start | bytes 14155784 | tf_op jit(solution)/shard_map/ppermute | solution.py:71
  153.0 3.5 collective-permute-start.26
  171.1 6.6 %collective-permute-start.29 = (f32[2,8,768]{2,1,0:T(8,128)}, f32[2,8,768]{2,1,0:T(8,128)}, u32[]{:S(2)}, u32[]{:S(2)}) collective-permute-start(f32[2,8,768]{2,1,0:T(8,128)} %fusion.84), channel_id=1, source_target_pairs={{0,3},{1,2},{2,1},{3,0},{4,7},{5,6},{6,5},{7,4},{8,11},{9,10},{10,... | collective-permute-start | bytes 147464 | tf_op jit(solution)/shard_map/ppermute | solution.py:71
  173.6 5.5 %collective-permute-start.28 = (f32[2,8,768]{2,1,0:T(8,128)}, f32[2,8,768]{2,1,0:T(8,128)}, u32[]{:S(2)}, u32[]{:S(2)}) collective-permute-start(f32[2,8,768]{2,1,0:T(8,128)} %fusion.84), channel_id=1, source_target_pairs={{0,2},{1,3},{2,0},{3,1},{4,6},{5,7},{6,4},{7,5},{8,10},{9,11},{10,... | collective-permute-start | bytes 147464 | tf_op jit(solution)/shard_map/ppermute | solution.py:71
  173.6 5.5 %collective-permute-start.27 = (f32[2,8,768]{2,1,0:T(8,128)}, f32[2,8,768]{2,1,0:T(8,128)}, u32[]{:S(2)}, u32[]{:S(2)}) collective-permute-start(f32[2,8,768]{2,1,0:T(8,128)} %fusion.84), channel_id=1, source_target_pairs={{0,1},{1,0},{2,3},{3,2},{4,5},{5,4},{6,7},{7,6},{8,9},{9,8},{10,11... | collective-permute-start | bytes 147464 | tf_op jit(solution)/shard_map/ppermute | solution.py:71
  181.2 1.3 collective-permute-start.30
  183.2 7.2 %collective-permute-start.33 = (bf16[2,2,8,896]{3,2,1,0:T(8,128)(2,1)S(1)}, bf16[2,2,8,896]{3,2,1,0:T(8,128)(2,1)S(1)}, u32[]{:S(2)}, u32[]{:S(2)}) collective-permute-start(bf16[2,2,8,896]{3,2,1,0:T(8,128)(2,1)S(1)} %pad_maximum_fusion.14), channel_id=1, source_target_pairs={{0,24},{4,28},{8,16},{12,20},{16,8},{20,12},{24,0},{28,4},{1,25},{... | collective-permute-start | bytes 172040 | tf_op jit(solution)/shard_map/ppermute | solution.py:71
  184.6 5.7 %collective-permute-start.32 = (bf16[2,2,8,896]{3,2,1,0:T(8,128)(2,1)S(1)}, bf16[2,2,8,896]{3,2,1,0:T(8,128)(2,1)S(1)}, u32[]{:S(2)}, u32[]{:S(2)}) collective-permute-start(bf16[2,2,8,896]{3,2,1,0:T(8,128)(2,1)S(1)} %pad_maximum_fusion.14), channel_id=1, source_target_pairs={{0,16},{4,20},{8,24},{12,28},{16,0},{20,4},{24,8},{28,12},{1,17},{... | collective-permute-start | bytes 172040 | tf_op jit(solution)/shard_map/ppermute | solution.py:71
  186.1 4.2 %collective-permute-start.31 = (bf16[2,2,8,896]{3,2,1,0:T(8,128)(2,1)S(1)}, bf16[2,2,8,896]{3,2,1,0:T(8,128)(2,1)S(1)}, u32[]{:S(2)}, u32[]{:S(2)}) collective-permute-start(bf16[2,2,8,896]{3,2,1,0:T(8,128)(2,1)S(1)} %pad_maximum_fusion.14), channel_id=1, source_target_pairs={{0,8},{4,12},{8,0},{12,4},{16,24},{20,28},{24,16},{28,20},{1,9},{5... | collective-permute-start | bytes 172040 | tf_op jit(solution)/shard_map/ppermute | solution.py:71
  213.4 8.1 %collective-permute-start.34 = (bf16[2,384,3072]{2,1,0:T(8,128)(2,1)}, bf16[2,384,3072]{2,1,0:T(8,128)(2,1)S(1)}, u32[]{:S(2)}, u32[]{:S(2)}) collective-permute-start(bf16[2,384,3072]{2,1,0:T(8,128)(2,1)} %get-tuple-element.252), channel_id=1, source_target_pairs={{0,4},{4,0},{8,12},{12,8},{16,20},{20,16},{24,28},{28,24},{1,5},{5... | collective-permute-start | bytes 14155784 | tf_op jit(solution)/shard_map/ppermute | solution.py:71
  225.3 28.3 %collective-permute-start.35 = (bf16[1,2,96,3072]{3,2,1,0:T(8,128)(2,1)}, bf16[1,2,96,3072]{3,2,1,0:T(8,128)(2,1)}, u32[]{:S(2)}, u32[]{:S(2)}) collective-permute-start(bf16[1,2,96,3072]{3,2,1,0:T(8,128)(2,1)} %fusion.22), channel_id=1, source_target_pairs={{0,16},{4,20},{8,24},{12,28},{16,0},{20,4},{24,8},{28,12},{1,17},{... | collective-permute-start | bytes 3538952 | tf_op jit(solution)/shard_map/ppermute | solution.py:71
  225.8 28.0 %collective-permute-start.36 = (bf16[1,2,96,3072]{3,2,1,0:T(8,128)(2,1)}, bf16[1,2,96,3072]{3,2,1,0:T(8,128)(2,1)}, u32[]{:S(2)}, u32[]{:S(2)}) collective-permute-start(bf16[1,2,96,3072]{3,2,1,0:T(8,128)(2,1)} %fusion.23), channel_id=1, source_target_pairs={{0,8},{4,12},{8,0},{12,4},{16,24},{20,28},{24,16},{28,20},{1,9},{5... | collective-permute-start | bytes 3538952 | tf_op jit(solution)/shard_map/ppermute | solution.py:71
  256.6 16.0 %collective-permute-start.37 = (bf16[1,1,96,3072]{3,2,1,0:T(8,128)(2,1)S(1)}, bf16[1,1,96,3072]{3,2,1,0:T(8,128)(2,1)S(1)}, u32[]{:S(2)}, u32[]{:S(2)}) collective-permute-start(bf16[1,1,96,3072]{3,2,1,0:T(8,128)(2,1)S(1)} %fusion.55), channel_id=1, source_target_pairs={{0,8},{4,12},{8,0},{12,4},{16,24},{20,28},{24,16},{28,20},{1,9},{5... | collective-permute-start | bytes 1769480 | tf_op jit(solution)/shard_map/ppermute | solution.py:71
  257.2 15.4 %collective-permute-start.38 = (bf16[1,1,96,3072]{3,2,1,0:T(8,128)(2,1)S(1)}, bf16[1,1,96,3072]{3,2,1,0:T(8,128)(2,1)S(1)}, u32[]{:S(2)}, u32[]{:S(2)}) collective-permute-start(bf16[1,1,96,3072]{3,2,1,0:T(8,128)(2,1)S(1)} %fusion.56), channel_id=1, source_target_pairs={{0,16},{4,20},{8,24},{12,28},{16,0},{20,4},{24,8},{28,12},{1,17},{... | collective-permute-start | bytes 1769480 | tf_op jit(solution)/shard_map/ppermute | solution.py:71
  258.7 13.8 %collective-permute-start.39 = (bf16[256,768]{1,0:T(8,128)(2,1)}, bf16[256,768]{1,0:T(8,128)(2,1)}, u32[]{:S(2)}, u32[]{:S(2)}) collective-permute-start(bf16[256,768]{1,0:T(8,128)(2,1)} %get-tuple-element.271), channel_id=1, source_target_pairs={{0,1},{2,3},{1,0},{3,2},{4,5},{6,7},{5,4},{7,6},{8,9},{10,11},{9,8... | collective-permute-start | bytes 1179656 | tf_op jit(solution)/shard_map/ppermute | solution.py:77
  259.6 12.9 %collective-permute-start.40 = (bf16[256,768]{1,0:T(8,128)(2,1)}, bf16[256,768]{1,0:T(8,128)(2,1)}, u32[]{:S(2)}, u32[]{:S(2)}) collective-permute-start(bf16[256,768]{1,0:T(8,128)(2,1)} %get-tuple-element.272), channel_id=1, source_target_pairs={{1,2},{2,1},{5,6},{6,5},{9,10},{10,9},{13,14},{14,13},{17,18},{18,... | collective-permute-start | bytes 1179656 | tf_op jit(solution)/shard_map/ppermute | solution.py:77
  277.0 27.9 %collective-permute-start.41 = (bf16[2,96,1536]{2,1,0:T(8,128)(2,1)}, bf16[2,96,1536]{2,1,0:T(8,128)(2,1)}, u32[]{:S(2)}, u32[]{:S(2)}) collective-permute-start(bf16[2,96,1536]{2,1,0:T(8,128)(2,1)} %fusion.61), channel_id=1, source_target_pairs={{0,2},{1,3},{2,0},{3,1},{4,6},{5,7},{6,4},{7,5},{8,10},{9,11},{10,... | collective-permute-start | bytes 1769480 | tf_op jit(solution)/shard_map/ppermute | solution.py:71
  304.9 22.6 %collective-permute-start.42 = (bf16[4,384,768]{2,1,0:T(8,128)(2,1)S(1)}, bf16[4,384,768]{2,1,0:T(8,128)(2,1)S(1)}, u32[]{:S(2)}, u32[]{:S(2)}) collective-permute-start(bf16[4,384,768]{2,1,0:T(8,128)(2,1)S(1)} %copy-done.131), channel_id=1, source_target_pairs={{0,4},{4,0},{8,12},{12,8},{16,20},{20,16},{24,28},{28,24},{1,5},{5... | collective-permute-start | bytes 7077896 | tf_op jit(solution)/shard_map/ppermute | solution.py:71
  308.0 12.0 %collective-permute-start.45 = (bf16[256,768]{1,0:T(8,128)(2,1)S(1)}, bf16[256,768]{1,0:T(8,128)(2,1)S(1)}, u32[]{:S(2)}, u32[]{:S(2)}) collective-permute-start(bf16[256,768]{1,0:T(8,128)(2,1)S(1)} %add_convert_fusion.9), channel_id=1, source_target_pairs={{0,1},{2,3},{1,0},{3,2},{4,5},{6,7},{5,4},{7,6},{8,9},{10,11},{9,8... | collective-permute-start | bytes 1179656 | tf_op jit(solution)/shard_map/ppermute | solution.py:77
  308.1 12.0 %collective-permute-start.46 = (bf16[256,768]{1,0:T(8,128)(2,1)S(1)}, bf16[256,768]{1,0:T(8,128)(2,1)S(1)}, u32[]{:S(2)}, u32[]{:S(2)}) collective-permute-start(bf16[256,768]{1,0:T(8,128)(2,1)S(1)} %copy-done.94), channel_id=1, source_target_pairs={{1,2},{2,1},{5,6},{6,5},{9,10},{10,9},{13,14},{14,13},{17,18},{18,... | collective-permute-start | bytes 1179656 | tf_op jit(solution)/shard_map/ppermute | solution.py:77
  308.8 18.7 %collective-permute-start.43 = (bf16[256,768]{1,0:T(8,128)(2,1)S(1)}, bf16[256,768]{1,0:T(8,128)(2,1)S(1)}, u32[]{:S(2)}, u32[]{:S(2)}) collective-permute-start(bf16[256,768]{1,0:T(8,128)(2,1)S(1)} %get-tuple-element.304), channel_id=1, source_target_pairs={{0,1},{2,3},{1,0},{3,2},{4,5},{6,7},{5,4},{7,6},{8,9},{10,11},{9,8... | collective-permute-start | bytes 1179656 | tf_op jit(solution)/shard_map/ppermute | solution.py:77
  313.9 13.7 %collective-permute-start.44 = (bf16[256,768]{1,0:T(8,128)(2,1)S(1)}, bf16[256,768]{1,0:T(8,128)(2,1)S(1)}, u32[]{:S(2)}, u32[]{:S(2)}) collective-permute-start(bf16[256,768]{1,0:T(8,128)(2,1)S(1)} %get-tuple-element.305), channel_id=1, source_target_pairs={{1,2},{2,1},{5,6},{6,5},{9,10},{10,9},{13,14},{14,13},{17,18},{18,... | collective-permute-start | bytes 1179656 | tf_op jit(solution)/shard_map/ppermute | solution.py:77
  329.7 11.7 %collective-permute-start.51 = (bf16[2,96,768]{2,1,0:T(8,128)(2,1)S(1)}, bf16[2,96,768]{2,1,0:T(8,128)(2,1)S(1)}, u32[]{:S(2)}, u32[]{:S(2)}) collective-permute-start(bf16[2,96,768]{2,1,0:T(8,128)(2,1)S(1)} %slice.624), channel_id=1, source_target_pairs={{0,1},{1,0},{2,3},{3,2},{4,5},{5,4},{6,7},{7,6},{8,9},{9,8},{10,11... | collective-permute-start | bytes 884744 | tf_op jit(solution)/shard_map/ppermute | solution.py:71
  333.8 15.0 %collective-permute-start.47 = (bf16[2,2,96,768]{3,2,0,1:T(8,128)(2,1)S(1)}, bf16[2,2,96,768]{3,2,0,1:T(8,128)(2,1)S(1)}, u32[]{:S(2)}, u32[]{:S(2)}) collective-permute-start(bf16[2,2,96,768]{3,2,0,1:T(8,128)(2,1)S(1)} %fusion.57), channel_id=1, source_target_pairs={{0,16},{4,20},{8,24},{12,28},{16,0},{20,4},{24,8},{28,12},{1,17},{... | collective-permute-start | bytes 1769480 | tf_op jit(solution)/shard_map/ppermute | solution.py:71
  335.5 14.7 %collective-permute-start.48 = (bf16[2,2,96,768]{3,2,0,1:T(8,128)(2,1)S(1)}, bf16[2,2,96,768]{3,2,0,1:T(8,128)(2,1)S(1)}, u32[]{:S(2)}, u32[]{:S(2)}) collective-permute-start(bf16[2,2,96,768]{3,2,0,1:T(8,128)(2,1)S(1)} %fusion.58), channel_id=1, source_target_pairs={{0,8},{4,12},{8,0},{12,4},{16,24},{20,28},{24,16},{28,20},{1,9},{5... | collective-permute-start | bytes 1769480 | tf_op jit(solution)/shard_map/ppermute | solution.py:71
  337.9 10.9 %collective-permute-start.49 = (bf16[256,768]{1,0:T(8,128)(2,1)S(1)}, bf16[256,768]{1,0:T(8,128)(2,1)S(1)}, u32[]{:S(2)}, u32[]{:S(2)}) collective-permute-start(bf16[256,768]{1,0:T(8,128)(2,1)S(1)} %add_convert_fusion.7), channel_id=1, source_target_pairs={{0,1},{2,3},{1,0},{3,2},{4,5},{6,7},{5,4},{7,6},{8,9},{10,11},{9,8... | collective-permute-start | bytes 1179656 | tf_op jit(solution)/shard_map/ppermute | solution.py:77
  338.1 10.7 %collective-permute-start.50 = (bf16[256,768]{1,0:T(8,128)(2,1)S(1)}, bf16[256,768]{1,0:T(8,128)(2,1)S(1)}, u32[]{:S(2)}, u32[]{:S(2)}) collective-permute-start(bf16[256,768]{1,0:T(8,128)(2,1)S(1)} %add_convert_fusion.6), channel_id=1, source_target_pairs={{1,2},{2,1},{5,6},{6,5},{9,10},{10,9},{13,14},{14,13},{17,18},{18,... | collective-permute-start | bytes 1179656 | tf_op jit(solution)/shard_map/ppermute | solution.py:77
  352.0 8.7 %collective-permute-start.52 = (bf16[2,1,96,768]{3,2,0,1:T(8,128)(2,1)}, bf16[2,1,96,768]{3,2,0,1:T(8,128)(2,1)}, u32[]{:S(2)}, u32[]{:S(2)}) collective-permute-start(bf16[2,1,96,768]{3,2,0,1:T(8,128)(2,1)} %fusion.68), channel_id=1, source_target_pairs={{0,8},{4,12},{8,0},{12,4},{16,24},{20,28},{24,16},{28,20},{1,9},{5... | collective-permute-start | bytes 884744 | tf_op jit(solution)/shard_map/ppermute | solution.py:71
  354.5 7.6 %collective-permute-start.53 = (bf16[2,1,96,768]{3,2,0,1:T(8,128)(2,1)}, bf16[2,1,96,768]{3,2,0,1:T(8,128)(2,1)}, u32[]{:S(2)}, u32[]{:S(2)}) collective-permute-start(bf16[2,1,96,768]{3,2,0,1:T(8,128)(2,1)} %fusion.69), channel_id=1, source_target_pairs={{0,16},{4,20},{8,24},{12,28},{16,0},{20,4},{24,8},{28,12},{1,17},{... | collective-permute-start | bytes 884744 | tf_op jit(solution)/shard_map/ppermute | solution.py:71
  365.5 9.7 %collective-permute-start.56 = (bf16[4,96,192]{2,1,0:T(8,128)(2,1)S(1)}, bf16[4,96,192]{2,1,0:T(8,128)(2,1)S(1)}, u32[]{:S(2)}, u32[]{:S(2)}) collective-permute-start(bf16[4,96,192]{2,1,0:T(8,128)(2,1)S(1)} %get-tuple-element.487), channel_id=1, source_target_pairs={{0,3},{1,2},{2,1},{3,0},{4,7},{5,6},{6,5},{7,4},{8,11},{9,10},{10,... | collective-permute-start | bytes 442376 | tf_op jit(solution)/shard_map/ppermute | solution.py:71
  367.5 15.7 %collective-permute-start.55 = (bf16[4,96,192]{2,1,0:T(8,128)(2,1)S(1)}, bf16[4,96,192]{2,1,0:T(8,128)(2,1)S(1)}, u32[]{:S(2)}, u32[]{:S(2)}) collective-permute-start(bf16[4,96,192]{2,1,0:T(8,128)(2,1)S(1)} %get-tuple-element.488), channel_id=1, source_target_pairs={{0,2},{1,3},{2,0},{3,1},{4,6},{5,7},{6,4},{7,5},{8,10},{9,11},{10,... | collective-permute-start | bytes 442376 | tf_op jit(solution)/shard_map/ppermute | solution.py:71
  368.5 14.6 %collective-permute-start.54 = (bf16[4,96,192]{2,1,0:T(8,128)(2,1)S(1)}, bf16[4,96,192]{2,1,0:T(8,128)(2,1)S(1)}, u32[]{:S(2)}, u32[]{:S(2)}) collective-permute-start(bf16[4,96,192]{2,1,0:T(8,128)(2,1)S(1)} %get-tuple-element.489), channel_id=1, source_target_pairs={{0,1},{1,0},{2,3},{3,2},{4,5},{5,4},{6,7},{7,6},{8,9},{9,8},{10,11... | collective-permute-start | bytes 442376 | tf_op jit(solution)/shard_map/ppermute | solution.py:71
  384.5 1.3 collective-permute-start.57
  385.8 4.7 %collective-permute-start.60 = (f32[8,768]{1,0:T(8,128)S(1)}, f32[8,768]{1,0:T(8,128)S(1)}, u32[]{:S(2)}, u32[]{:S(2)}) collective-permute-start(f32[8,768]{1,0:T(8,128)S(1)} %add.752), channel_id=1, source_target_pairs={{0,24},{4,28},{8,16},{12,20},{16,8},{20,12},{24,0},{28,4},{1,25},{... | collective-permute-start | bytes 73736 | tf_op jit(solution)/shard_map/ppermute | solution.py:71
  385.8 4.7 %collective-permute-start.59 = (f32[8,768]{1,0:T(8,128)S(1)}, f32[8,768]{1,0:T(8,128)S(1)}, u32[]{:S(2)}, u32[]{:S(2)}) collective-permute-start(f32[8,768]{1,0:T(8,128)S(1)} %add.752), channel_id=1, source_target_pairs={{0,16},{4,20},{8,24},{12,28},{16,0},{20,4},{24,8},{28,12},{1,17},{... | collective-permute-start | bytes 73736 | tf_op jit(solution)/shard_map/ppermute | solution.py:71
  387.9 3.8 collective-permute-start.58
  391.9 6.2 %collective-permute-start.63 = (f32[8,768]{1,0:T(8,128)S(1)}, f32[8,768]{1,0:T(8,128)S(1)}, u32[]{:S(2)}, u32[]{:S(2)}) collective-permute-start(f32[8,768]{1,0:T(8,128)S(1)} %add_add_fusion.1), channel_id=1, source_target_pairs={{0,3},{1,2},{2,1},{3,0},{4,7},{5,6},{6,5},{7,4},{8,11},{9,10},{10,... | collective-permute-start | bytes 73736 | tf_op jit(solution)/shard_map/ppermute | solution.py:71
  394.1 4.7 %collective-permute-start.62 = (f32[8,768]{1,0:T(8,128)S(1)}, f32[8,768]{1,0:T(8,128)S(1)}, u32[]{:S(2)}, u32[]{:S(2)}) collective-permute-start(f32[8,768]{1,0:T(8,128)S(1)} %add_add_fusion.1), channel_id=1, source_target_pairs={{0,2},{1,3},{2,0},{3,1},{4,6},{5,7},{6,4},{7,5},{8,10},{9,11},{10,... | collective-permute-start | bytes 73736 | tf_op jit(solution)/shard_map/ppermute | solution.py:71
  394.1 4.7 %collective-permute-start.61 = (f32[8,768]{1,0:T(8,128)S(1)}, f32[8,768]{1,0:T(8,128)S(1)}, u32[]{:S(2)}, u32[]{:S(2)}) collective-permute-start(f32[8,768]{1,0:T(8,128)S(1)} %add_add_fusion.1), channel_id=1, source_target_pairs={{0,1},{1,0},{2,3},{3,2},{4,5},{5,4},{6,7},{7,6},{8,9},{9,8},{10,11... | collective-permute-start | bytes 73736 | tf_op jit(solution)/shard_map/ppermute | solution.py:71
  (135 other events, 1411.4 us)
